TPU v7x, 32 devices: a whole 2x2x4 slice. The times are simulated.
32 devices in a mesh: grp: 2 (over y), sets: 16 (over z, x, core).
Axes of the slice: x: 2, y: 2, z: 4, core: 2. Of those that a mesh axis runs over, the one named last changes fastest.
Arguments:
- exposure_adjoint: bfloat16 [7680, 2048], P(('grp', 'sets')), parts along dimension 0, may hold values from -6 to 6
- positive_bits: int32 [512, 2048], P(('grp', 'sets')), parts along dimension 0, may hold values from 0 to 32704
- currencies: int32 [7680, 4], P(('grp', 'sets')), parts along dimension 0, may hold values from 0 to 39, all different within a row
- mix_count: int32 [7680], P(('grp', 'sets')), parts along dimension 0, may hold values from 1 to 4
- notional: float32 [7680, 4], P(('grp', 'sets')), parts along dimension 0, may hold values from -0.375 to 0.375
- fx_paths: float32 [80, 2048], P('grp', 'sets'), parts along dimension 0, may hold values from 0.5 to 2
- short_rates: float32 [80, 2048], P('grp', 'sets'), parts along dimension 0, may hold values from -0.05 to 0.25
- start_integral: float32 [80, 256], P('grp', 'sets'), parts along dimension 0, may hold values from 0 to 2
Outputs:
- fx_adjoint: float32 [80, 2048], P('grp', 'sets'), parts along dimension 0
- rate_adjoint: float32 [80, 2048], P('grp', 'sets'), parts along dimension 0
- notional_adjoint: float32 [7680, 4], P(('grp', 'sets')), parts along dimension 0
There are 2 independent parts, one for each index of `grp`. A program takes and returns all parts, laid end to end along the dimension named above; each array names one. Nothing has to cross between parts.
Inputs may be any that keep to these rules, and one draw needn't show every extreme that they name: The 4 currencies of a set are distinct.
All inputs are finite; a program needn't handle non-finite values.
Results may differ from a plain program's by a relative error of at most 0.003.
Values may be sent and summed in bfloat16 or wider, within the bound.
No kernel may reach another device: no remote copies, remote signals or barrier semaphores. Data moves between devices by JAX's collectives and lax.ppermute only.
A program may use at most 128 MiB of HBM per device.

v0:
```python
import math

import jax
import jax.numpy as jnp
from jax import lax
from jax.sharding import PartitionSpec as P

step_years = 0.25


def unpack(packed, exposure):
    shifts = jnp.arange(15, dtype=jnp.int32)
    flags = jnp.right_shift(packed[:, None, :], shifts[None, :, None]) & 1
    flags = flags.reshape(exposure.shape)
    return jnp.where(flags == 1, exposure, jnp.zeros((), jnp.bfloat16))


def body(
    exposure_adjoint,
    positive_bits,
    currencies,
    mix_count,
    notional,
    fx_paths,
    short_rates,
    start_integral,
):
    currency_count = fx_paths.shape[0]
    owned_columns = fx_paths.shape[1]
    owned_paths = start_integral.shape[1]
    dates_here = owned_columns // owned_paths
    all_columns = exposure_adjoint.shape[1]
    rates_cube = short_rates.reshape(currency_count, owned_paths, dates_here)
    integral = start_integral[:, :, None] + step_years * jnp.cumsum(rates_cube, axis=2)
    discount = jnp.exp(-integral).reshape(currency_count, owned_columns)
    carried = (fx_paths * discount).astype(jnp.bfloat16)
    slot_index = jnp.arange(currencies.shape[1], dtype=jnp.int32)
    active = slot_index[None, :] < mix_count[:, None]
    onehot = currencies[:, :, None] == jnp.arange(currency_count, dtype=jnp.int32)[None, None, :]
    chosen = jnp.logical_and(active[:, :, None], onehot)
    mix_weights = jnp.sum(jnp.where(chosen, notional[:, :, None], jnp.float32(0.0)), axis=1).astype(
        jnp.bfloat16
    )
    masked = unpack(positive_bits, exposure_adjoint)
    projected = lax.dot_general(
        masked,
        lax.all_gather(carried, "sets", axis=1, tiled=True),
        (((1,), (1,)), ((), ())),
        preferred_element_type=jnp.float32,
    )
    whole_term = lax.dot_general(
        mix_weights, masked, (((0,), (0,)), ((), ())), preferred_element_type=jnp.float32
    )
    summed = lax.psum(whole_term, "sets")
    aggregate = lax.dynamic_slice_in_dim(
        summed, lax.axis_index("sets") * owned_columns, owned_columns, 1
    )
    fx_adjoint = aggregate * discount
    sensitivity = (aggregate * fx_paths * discount).reshape(currency_count, owned_paths, dates_here)
    tail_sums = jnp.flip(jnp.cumsum(jnp.flip(sensitivity, axis=2), axis=2), axis=2)
    rate_adjoint = (-step_years * tail_sums).reshape(currency_count, owned_columns)
    picked = jnp.sum(jnp.where(chosen, projected[:, None, :], jnp.float32(0.0)), axis=2)
    notional_adjoint = picked * (1.0 / math.sqrt(all_columns))
    return (fx_adjoint, rate_adjoint, notional_adjoint)


def solution(mesh):
    in_specs = (
        P(("grp", "sets"), None),
        P(("grp", "sets"), None),
        P(("grp", "sets"), None),
        P(("grp", "sets")),
        P(("grp", "sets"), None),
        P("grp", "sets"),
        P("grp", "sets"),
        P("grp", "sets"),
    )
    out_specs = (P("grp", "sets"), P("grp", "sets"), P(("grp", "sets"), None))
    return jax.shard_map(body, mesh=mesh, in_specs=in_specs, out_specs=out_specs, check_vma=False)
```

profile of v0, /device:TPU:0, one launch (start us, length us, event | category | flops | bytes accessed | tf_op | source)
XLA Modules:
  0.0 133.5 jit_solution(6520200351247154760)
XLA Ops:
  7.2 0.0 all-reduce.2.cloned.1.call-start
  7.2 1.1 shift_right_arithmetic.20
  8.4 0.0 copy-start.2
  8.4 0.0 copy-start.1
  8.4 0.0 copy-start.3
  8.4 0.0 copy-start.6
  8.4 0.0 copy-start
  8.4 1.5 %shift_right_arithmetic.21 = s32[240,2048]{1,0:T(8,128)} reshape(s32[16,15,2048]{2,1,0:T(8,128)S(1)} %shift_right_arithmetic.20) | data formatting | bytes 3932160 | tf_op jit(solution)/shard_map/shift_right_arithmetic | solution.py:13
  10.0 0.1 shift_right_arithmetic.23
  10.0 0.0 copy-done.2
  10.1 0.1 copy.24
  10.1 0.0 copy-done.1
  10.2 0.1 copy.28
  10.3 0.1 reduce_window_sum.17
  10.3 0.0 copy-done.3
  10.4 24.6 %all_gather.3 = bf16[40,2048]{0,1:T(8,128)(2,1)S(1)} all-gather(bf16[40,128]{0,1:T(8,128)(2,1)S(1)} %get-tuple-element.11), channel_id=1, replica_groups=mesh['grp'=2,'sets'=16] {'sets'}, dimensions={1}, use_global_device_ids=true | all-gather | bytes 174080 | tf_op jit(solution)/shard_map/all_gather | solution.py:47
  35.0 0.0 copy-done.6
  35.0 0.0 copy-done
  35.0 0.0 copy-start.4
  35.0 0.0 copy-start.5
  35.0 2.0 %fusion = bf16[240,2048]{1,0:T(8,128)(2,1)S(1)} fusion(bf16[240,2048]{1,0:T(8,128)(2,1)S(1)} %copy-done, s32[240,2048]{1,0:T(8,128)} %shift_right_arithmetic.21, s32[240]{0:T(256)S(1)} %shift_right_arithmetic.23), kind=kLoop, calls=%fused_computation.1 | loop fusion | flops 1966080 | bytes 3933120 | tf_op jit(solution)/shard_map/jit(_where)/select_n | solution.py:15
  37.0 0.4 fusion.4
  37.4 0.0 copy-done.4
  37.4 0.0 copy-done.5
  37.4 0.1 select_reduce_fusion
  37.5 1.0 fusion.5
  38.5 0.0 all-reduce.2.cloned.1.call-update
  38.6 0.1 copy.25
  38.6 0.6 broadcast_multiply_fusion
  39.2 85.2 %all-reduce.2.cloned.1.call-done = f32[40,2048]{1,0:T(8,128)} async-done(((f32[40,2048]{1,0:T(8,128)}), f32[40,2048]{1,0:T(8,128)}) %all-reduce.2.cloned.1.call-update) | async-done | bytes 327696 | tf_op jit(solution)/shard_map/psum | solution.py:54
  124.4 1.3 %multiply_multiply_fusion = (f32[40,128]{1,0:T(8,128)S(1)}, f32[40,128]{1,0:T(8,128)}) fusion(f32[40,128]{1,0:T(8,128)S(1)} %copy.25, f32[40,128]{1,0:T(8,128)S(1)} %copy-done.1, f32[40,2048]{1,0:T(8,128)} %all-reduce.2.cloned.1.call-done, s32[]{:T(128)S(6)} %select_n.17), kind=kLoop, calls=%fused_computation.9 | loop fusion | flops 15360 | bytes 102404 | tf_op jit(solution)/shard_map/mul | solution.py:59
  125.8 0.1 copy.27
  125.9 0.1 reduce_window_sum.18
  126.0 0.7 copy.29
  (6 shorter events, 0.1 us)
Async XLA Ops:
  7.2 117.3 %all-reduce.2.cloned.1.call-start = ((), (), s32[]{:S(2)}) async-start(), calls=%async_computation | async-start | bytes 655360 | tf_op jit(solution)/shard_map/psum | solution.py:54
  8.4 1.7 %copy-start.2 = (f32[40,128]{1,0:T(8,128)S(1)}, f32[40,128]{1,0:T(8,128)}, u32[]{:S(2)}) copy-start(f32[40,128]{1,0:T(8,128)} %param.14) | copy-start | bytes 61444
  8.4 1.8 %copy-start.1 = (f32[40,128]{1,0:T(8,128)S(1)}, f32[40,128]{1,0:T(8,128)}, u32[]{:S(2)}) copy-start(f32[40,128]{1,0:T(8,128)} %param.13) | copy-start | bytes 61444
  8.4 1.9 %copy-start.3 = (f32[40,16]{0,1:T(8,128)S(1)}, f32[40,16]{0,1:T(8,128)}, u32[]{:S(2)}) copy-start(f32[40,16]{0,1:T(8,128)} %param.15) | copy-start | bytes 7684
  8.4 26.6 %copy-start.6 = (s32[240]{0:T(256)S(1)}, s32[240]{0:T(256)}, u32[]{:S(2)}) copy-start(s32[240]{0:T(256)} %param.11) | copy-start | bytes 2884
  8.4 26.6 %copy-start = (bf16[240,2048]{1,0:T(8,128)(2,1)S(1)}, bf16[240,2048]{1,0:T(8,128)(2,1)}, u32[]{:S(2)}) copy-start(bf16[240,2048]{1,0:T(8,128)(2,1)} %param.8) | copy-start | bytes 2949124
  35.0 2.5 %copy-start.4 = (s32[240,4]{0,1:T(4,128)S(1)}, s32[240,4]{0,1:T(4,128)}, u32[]{:S(2)}) copy-start(s32[240,4]{0,1:T(4,128)} %param.10) | copy-start | bytes 11524
  35.0 2.5 %copy-start.5 = (f32[240,4]{0,1:T(4,128)S(1)}, f32[240,4]{0,1:T(4,128)}, u32[]{:S(2)}) copy-start(f32[240,4]{0,1:T(4,128)} %param.12) | copy-start | bytes 11524
Sparse Core Ops, SparseCore 0:
  38.7 85.7 all-reduce.1
where the time goes:
time: 134 us
  waiting for transfers between devices  85.2 us (64%)
  blocking collectives  24.6 us (18%)
  between operations  14.2 us (11%)
  other arithmetic  4.21 us (3%)
  local copies, waits for them, and re-layouts  3.86 us (3%)
  matrix products  1.43 us (1%)
    psum x1, waiting for transfers between devices, body(): summed = lax.psum(whole_term, 'sets')  85.2 us
    all_gather x1, blocking collectives, body(): lax.all_gather(carried, 'sets', axis=1, tiled=True)  24.6 us
    shift_right_arithmetic x4, local copies, waits for them, and re-layouts, unpack(): flags = jnp.right_shift(packed[:, None, :], shifts[None, :, None]) & 1  2.76 us
  transfers between devices with their start and end apart: 1, of which 1 were waited for; matrix products, arithmetic and copies ran while one was open for 1% of the time, Pallas kernels for 0%

commit v1 on v0

--- a/solution.py
+++ b/solution.py
@@ -42,19 +42,27 @@
         jnp.bfloat16
     )
     masked = unpack(positive_bits, exposure_adjoint)
+    whole_term = lax.dot_general(
+        mix_weights, masked, (((0,), (0,)), ((), ())), preferred_element_type=jnp.float32
+    )
+    peers = all_columns // owned_columns
+    parts = whole_term.astype(jnp.bfloat16).reshape(currency_count, peers, owned_columns)
+    outgoing = jnp.concatenate(
+        [
+            jnp.broadcast_to(carried[None], (peers, currency_count, owned_columns)),
+            parts.transpose(1, 0, 2),
+        ],
+        axis=1,
+    )
+    arrived = lax.all_to_all(outgoing, "sets", 0, 0, tiled=True)
+    carried_all = arrived[:, :currency_count]
     projected = lax.dot_general(
         masked,
-        lax.all_gather(carried, "sets", axis=1, tiled=True),
+        carried_all.transpose(1, 0, 2).reshape(currency_count, all_columns),
         (((1,), (1,)), ((), ())),
         preferred_element_type=jnp.float32,
     )
-    whole_term = lax.dot_general(
-        mix_weights, masked, (((0,), (0,)), ((), ())), preferred_element_type=jnp.float32
-    )
-    summed = lax.psum(whole_term, "sets")
-    aggregate = lax.dynamic_slice_in_dim(
-        summed, lax.axis_index("sets") * owned_columns, owned_columns, 1
-    )
+    aggregate = jnp.sum(arrived[:, currency_count:].astype(jnp.float32), axis=0)
     fx_adjoint = aggregate * discount
     sensitivity = (aggregate * fx_paths * discount).reshape(currency_count, owned_paths, dates_here)
     tail_sums = jnp.flip(jnp.cumsum(jnp.flip(sensitivity, axis=2), axis=2), axis=2)

time: 134 us -> 27.5 us (0.21)
  waiting for transfers between devices: 85.2 us -> 0 us
  between operations: 14.2 us -> 0.84 us
  blocking collectives: 24.6 us -> 18.3 us
    psum x1 -> x0, waiting for transfers between devices: 85.2 us -> none  [body(): summed = lax.psum(whole_term, 'sets')]
    all_gather x1 -> x0, blocking collectives: 24.6 us -> none  [body(): lax.all_gather(carried, 'sets', axis=1, tiled=True)]
    all_to_all x0 -> x1, blocking collectives: none -> 18.3 us  [body(): arrived = lax.all_to_all(outgoing, 'sets', 0, 0, tiled=True)]
  transfers between devices with their start and end apart: 1 -> 0, of which waited for: 1 -> 0; matrix products, arithmetic and copies ran while one was open for 1% -> 0% of each run, Pallas kernels for 0% -> 0%
where the time goes in v1:
time: 27.5 us; the launch traced here: 27.2 us
  blocking collectives  18.3 us (67%)
  local copies, waits for them, and re-layouts  3.88 us (14%)
  other arithmetic  3.54 us (13%)
  between operations  0.84 us (3%)
  matrix products  0.69 us (3%)
    all_to_all x1, blocking collectives, body(): arrived = lax.all_to_all(outgoing, 'sets', 0, 0, tiled=True)  18.3 us
    shift_right_arithmetic x4, local copies, waits for them, and re-layouts, unpack(): flags = jnp.right_shift(packed[:, None, :], shifts[None, :, None]) & 1  2.76 us
    select_n x1, other arithmetic, unpack(): return jnp.where(flags == 1, exposure, jnp.zeros((), jnp.bfloat16))  2 us
    unnamed x16, local copies, waits for them, and re-layouts  0.89 us
    mul x1, other arithmetic, body(): aggregate * fx_paths * discount  0.61 us
    mul x1, other arithmetic, body(): notional_adjoint = picked * (1.0 / math.sqrt(all_columns))  0.6 us

profile of v1, /device:TPU:0, one launch (start us, length us, event | category | flops | bytes accessed | tf_op | source)
XLA Modules:
  0.0 27.2 jit_solution(7403609997367622149)
XLA Ops:
  0.6 1.1 %shift_right_arithmetic.20 = s32[16,15,2048]{2,1,0:T(8,128)S(1)} broadcast(s32[16,2048]{1,0:T(8,128)} %param.9), dimensions={0,2} | broadcast | bytes 2097152 | tf_op jit(solution)/shard_map/shift_right_arithmetic | solution.py:13
  1.8 0.0 copy-start.6
  1.8 0.0 copy-start
  1.8 1.5 %shift_right_arithmetic.21 = s32[240,2048]{1,0:T(8,128)} reshape(s32[16,15,2048]{2,1,0:T(8,128)S(1)} %shift_right_arithmetic.20) | data formatting | bytes 3932160 | tf_op jit(solution)/shard_map/shift_right_arithmetic | solution.py:13
  3.3 0.1 shift_right_arithmetic.23
  3.4 0.0 copy-done.6
  3.4 0.0 copy-done
  3.5 0.0 copy-start.3
  3.5 0.0 copy-start.5
  3.5 0.0 copy-start.2
  3.5 0.0 copy-start.4
  3.5 2.0 %fusion = bf16[240,2048]{1,0:T(8,128)(2,1)S(1)} fusion(bf16[240,2048]{1,0:T(8,128)(2,1)S(1)} %copy-done, s32[240,2048]{1,0:T(8,128)} %shift_right_arithmetic.21, s32[240]{0:T(256)S(1)} %shift_right_arithmetic.23), kind=kLoop, calls=%fused_computation.2 | loop fusion | flops 1966080 | bytes 3933120 | tf_op jit(solution)/shard_map/jit(_where)/select_n | solution.py:15
  5.5 0.0 copy-done.3
  5.5 0.0 copy-done.5
  5.5 0.0 copy-start.1
  5.6 0.3 %fusion.1 = bf16[5,16,8,128]{3,2,1,0:T(8,128)(2,1)S(1)} fusion(bf16[240,2048]{1,0:T(8,128)(2,1)S(1)} %fusion, bf16[240,40]{0,1:T(8,128)(2,1)S(1)} %select_reduce_fusion.1), kind=kOutput, calls=%fused_computation.3 | convolution fusion | flops 39403520 | bytes 1166080 | tf_op jit(solution)/shard_map/dot_general | solution.py:45
  5.9 0.0 copy-done.2
  5.9 0.1 copy.59
  6.0 0.1 reduce_window_sum.17
  6.1 0.0 copy-done.4
  6.1 0.1 copy.60
  6.2 0.1 copy-done.1
  6.3 18.3 %all_to_all.5 = bf16[16,80,128]{2,1,0:T(8,128)(2,1)S(1)} all-to-all(bf16[16,80,128]{2,1,0:T(8,128)(2,1)S(1)} %pad_maximum_fusion), channel_id=1, replica_groups=mesh['grp'=2,'sets'=16] {'sets'}, dimensions={0} | all-to-all | bytes 655360 | tf_op jit(solution)/shard_map/all_to_all | solution.py:57
  24.6 0.4 %fusion.2 = f32[240,40]{0,1:T(8,128)S(1)} fusion(bf16[240,2048]{1,0:T(8,128)(2,1)S(1)} %fusion, bf16[16,80,128]{2,1,0:T(8,128)(2,1)S(1)} %all_to_all.5), kind=kOutput, calls=%fused_computation.6 | convolution fusion | flops 39321600 | bytes 1185280 | tf_op jit(solution)/shard_map/dot_general | solution.py:59
  25.0 0.1 select_reduce_fusion
  25.1 0.6 %broadcast_multiply_fusion = f32[240,4]{0,1:T(4,128)} fusion(f32[240,4]{0,1:T(4,128)S(1)} %select_reduce_fusion), kind=kLoop, calls=%fused_computation.21 | loop fusion | flops 960 | bytes 7680 | tf_op jit(solution)/shard_map/mul | solution.py:71
  25.7 0.6 %multiply_multiply_fusion = (f32[40,128]{1,0:T(8,128)S(1)}, f32[40,128]{1,0:T(8,128)}) fusion(f32[40,128]{1,0:T(8,128)S(1)} %copy.60, f32[40,128]{1,0:T(8,128)S(1)} %convert_reduce_fusion, f32[40,128]{1,0:T(8,128)S(1)} %copy-done.1), kind=kLoop, calls=%fused_computation.17 | loop fusion | flops 15360 | bytes 102400 | tf_op jit(solution)/shard_map/mul | solution.py:67
  26.3 0.1 copy.65
  26.4 0.1 reduce_window_sum.18
  26.5 0.7 %copy.67 = f32[40,128]{1,0:T(8,128)} copy(f32[40,128]{0,1:T(8,128)S(1)} %multiply_bitcast_fusion) | data formatting | bytes 40960
  (12 shorter events, 0.2 us)
Async XLA Ops:
  1.8 1.6 %copy-start.6 = (s32[240]{0:T(256)S(1)}, s32[240]{0:T(256)}, u32[]{:S(2)}) copy-start(s32[240]{0:T(256)} %param.11) | copy-start | bytes 2884
  1.8 1.7 %copy-start = (bf16[240,2048]{1,0:T(8,128)(2,1)S(1)}, bf16[240,2048]{1,0:T(8,128)(2,1)}, u32[]{:S(2)}) copy-start(bf16[240,2048]{1,0:T(8,128)(2,1)} %param.8) | copy-start | bytes 2949124
  3.5 2.1 %copy-start.3 = (s32[240,4]{0,1:T(4,128)S(1)}, s32[240,4]{0,1:T(4,128)}, u32[]{:S(2)}) copy-start(s32[240,4]{0,1:T(4,128)} %param.10) | copy-start | bytes 11524
  3.5 2.1 %copy-start.5 = (f32[240,4]{0,1:T(4,128)S(1)}, f32[240,4]{0,1:T(4,128)}, u32[]{:S(2)}) copy-start(f32[240,4]{0,1:T(4,128)} %param.12) | copy-start | bytes 11524
  3.5 2.4 %copy-start.2 = (f32[40,128]{1,0:T(8,128)S(1)}, f32[40,128]{1,0:T(8,128)}, u32[]{:S(2)}) copy-start(f32[40,128]{1,0:T(8,128)} %param.14) | copy-start | bytes 61444
  3.5 2.6 %copy-start.4 = (f32[40,16]{0,1:T(8,128)S(1)}, f32[40,16]{0,1:T(8,128)}, u32[]{:S(2)}) copy-start(f32[40,16]{0,1:T(8,128)} %param.15) | copy-start | bytes 7684
  5.5 0.7 %copy-start.1 = (f32[40,128]{1,0:T(8,128)S(1)}, f32[40,128]{1,0:T(8,128)}, u32[]{:S(2)}) copy-start(f32[40,128]{1,0:T(8,128)} %param.13) | copy-start | bytes 61444

commit v2 on v0

v2 whole, which is shorter than its diff:
```python
import functools
import math

import jax
import jax.numpy as jnp
from jax import lax
from jax.experimental import pallas as pl
from jax.experimental.pallas import tpu as pltpu
from jax.sharding import PartitionSpec as P

step_years = 0.25
bits_per_row = 15
lanes = 128
chunks = 8


def spread_paths(values, dates):
    paths, columns = values.shape[0], values.shape[0] * dates
    path_of = lax.broadcasted_iota(jnp.int32, (paths, columns), 1) // dates
    own = lax.broadcasted_iota(jnp.int32, (paths, columns), 0)
    return lax.dot_general(
        values,
        (path_of == own).astype(jnp.float32),
        (((0,), (0,)), ((), ())),
        precision=lax.Precision.HIGHEST,
        preferred_element_type=jnp.float32,
    )


def sums_to_date(values, dates):
    width = values.shape[1]
    date = lax.broadcasted_iota(jnp.int32, values.shape, 1) % dates
    step = 1
    while step < dates:
        values = values + jnp.where(date >= step, pltpu.roll(values, step, 1), 0.0)
        step *= 2
    return values


def sums_from_date(values, dates):
    width = values.shape[1]
    date = lax.broadcasted_iota(jnp.int32, values.shape, 1) % dates
    step = 1
    while step < dates:
        values = values + jnp.where(date < dates - step, pltpu.roll(values, width - step, 1), 0.0)
        step *= 2
    return values


def used_currencies(currencies, counts):
    slot = lax.broadcasted_iota(jnp.int32, currencies.shape, 0)
    return jnp.where(slot < counts, currencies, -1)


def local_kernel(
    dates,
    exposure_hbm,
    bits_hbm,
    currencies_ref,
    counts_ref,
    notional_ref,
    fx_ref,
    rates_ref,
    start_ref,
    outgoing_ref,
    masked_hbm,
    discount_ref,
    exposure,
    bits,
    masked,
    in_sems,
    bits_sems,
    out_sems,
):
    sets, columns = exposure.shape
    currency_count, owned = fx_ref.shape
    peers = columns // owned
    width = columns // chunks

    def exposure_copy(index):
        part = pl.ds(index * width, width)
        return pltpu.make_async_copy(
            exposure_hbm.at[:, part], exposure.at[:, part], in_sems.at[index]
        )

    def bits_copy(index):
        part = pl.ds(index * width, width)
        return pltpu.make_async_copy(bits_hbm.at[:, part], bits.at[:, part], bits_sems.at[index])

    def masked_copy(index):
        part = pl.ds(index * width, width)
        return pltpu.make_async_copy(masked.at[:, part], masked_hbm.at[:, part], out_sems.at[index])

    for index in range(chunks):
        bits_copy(index).start()
        exposure_copy(index).start()

    integral = spread_paths(start_ref[...], dates) + step_years * sums_to_date(rates_ref[...], dates)
    discount = jnp.exp(-integral)
    discount_ref[...] = discount
    carried = (fx_ref[...] * discount).astype(jnp.bfloat16)
    for peer in range(peers):
        outgoing_ref[peer, 0:currency_count, :] = carried

    used = used_currencies(currencies_ref[...], counts_ref[...])
    notional = notional_ref[...]
    currency = lax.broadcasted_iota(jnp.int32, (currency_count, sets), 0)
    weights = jnp.zeros((currency_count, sets), jnp.float32)
    for slot in range(used.shape[0]):
        weights = weights + jnp.where(
            currency == used[slot : slot + 1], notional[slot : slot + 1], 0.0
        )
    weights = weights.astype(jnp.bfloat16)

    row = lax.broadcasted_iota(jnp.int32, (8, lanes), 0)

    def flag_of(tile):
        shift = row + (8 * tile) % bits_per_row
        shift = jnp.where(shift >= bits_per_row, shift - bits_per_row, shift)
        return jnp.left_shift(jnp.int32(1), shift)

    def mask_columns(first, count):
        for pair in range(sets // 16):
            flags = [flag_of(2 * pair), flag_of(2 * pair + 1)]
            for block in range(count):
                part = pl.ds(first + block * lanes, lanes)
                values = exposure[16 * pair : 16 * pair + 16, part].astype(jnp.float32)
                kept = []
                for half in range(2):
                    top = 16 * pair + 8 * half
                    group = top // bits_per_row
                    left = bits_per_row * (group + 1) - top
                    packed = jnp.broadcast_to(bits[group : group + 1, part], (8, lanes))
                    if left < 8:
                        following = jnp.broadcast_to(bits[group + 1 : group + 2, part], (8, lanes))
                        packed = jnp.where(row < left, packed, following)
                    kept.append(
                        jnp.where(
                            (packed & flags[half]) != 0, values[8 * half : 8 * half + 8], 0.0
                        )
                    )
                masked[16 * pair : 16 * pair + 16, part] = jnp.concatenate(kept, axis=0).astype(
                    jnp.bfloat16
                )

    group_width = min(width, 256)

    for index in range(chunks):
        bits_copy(index).wait()
        exposure_copy(index).wait()

        def some_columns(step, _):
            first = index * width + step * group_width
            if not isinstance(first, int):
                first = pl.multiple_of(first, group_width)
            mask_columns(first, group_width // lanes)
            terms = jnp.dot(
                weights, masked[:, pl.ds(first, group_width)], preferred_element_type=jnp.float32
            ).astype(jnp.bfloat16)
            for block in range(group_width // owned):
                outgoing_ref[first // owned + block, currency_count:, :] = terms[
                    :, block * owned : (block + 1) * owned
                ]

        if width == group_width:
            some_columns(0, None)
        else:
            pl.loop(0, width // group_width)(lambda step: some_columns(step, None))
        masked_copy(index).start()
    for index in range(chunks):
        masked_copy(index).wait()


def final_kernel(
    dates,
    arrived_ref,
    masked_hbm,
    currencies_ref,
    counts_ref,
    fx_ref,
    discount_ref,
    fx_adjoint_ref,
    rate_adjoint_ref,
    notional_adjoint_ref,
    masked,
    in_sems,
):
    sets, columns = masked.shape
    currency_count, owned = fx_ref.shape
    peers = columns // owned
    width = columns // chunks

    def masked_copy(index):
        part = pl.ds(index * width, width)
        return pltpu.make_async_copy(masked_hbm.at[:, part], masked.at[:, part], in_sems.at[index])

    for index in range(chunks):
        masked_copy(index).start()

    aggregate = arrived_ref[0, currency_count:, :].astype(jnp.float32)
    for peer in range(1, peers):
        aggregate = aggregate + arrived_ref[peer, currency_count:, :].astype(jnp.float32)
    fx_adjoint = aggregate * discount_ref[...]
    fx_adjoint_ref[...] = fx_adjoint
    rate_adjoint_ref[...] = -step_years * sums_from_date(fx_adjoint * fx_ref[...], dates)

    projected = jnp.zeros((sets, currency_count), jnp.float32)
    for index in range(chunks):
        masked_copy(index).wait()
        per_chunk = width // owned
        carried = jnp.concatenate(
            [
                arrived_ref[index * per_chunk + block, 0:currency_count, :]
                for block in range(per_chunk)
            ],
            axis=1,
        )
        projected = projected + lax.dot_general(
            masked[:, index * width : (index + 1) * width],
            carried,
            (((1,), (1,)), ((), ())),
            preferred_element_type=jnp.float32,
        )
    projected = projected.T
    used = used_currencies(currencies_ref[...], counts_ref[...])
    currency = lax.broadcasted_iota(jnp.int32, (currency_count, sets), 0)
    for slot in range(used.shape[0]):
        picked = jnp.sum(
            jnp.where(currency == used[slot : slot + 1], projected, 0.0), axis=0, keepdims=True
        )
        notional_adjoint_ref[slot : slot + 1, :] = picked * (1.0 / math.sqrt(columns))


def body(
    exposure_adjoint,
    positive_bits,
    currencies,
    mix_count,
    notional,
    fx_paths,
    short_rates,
    start_integral,
):
    sets, columns = exposure_adjoint.shape
    currency_count, owned = fx_paths.shape
    dates = owned // start_integral.shape[1]
    peers = columns // owned
    slots = currencies.shape[1]
    in_vmem = pl.BlockSpec(memory_space=pltpu.VMEM)
    anywhere = pl.BlockSpec(memory_space=pl.ANY)
    slot_currencies = currencies.T
    counts = mix_count.reshape(1, sets)
    outgoing, masked, discount = pl.pallas_call(
        functools.partial(local_kernel, dates),
        out_shape=(
            jax.ShapeDtypeStruct((peers, 2 * currency_count, owned), jnp.bfloat16),
            jax.ShapeDtypeStruct((sets, columns), jnp.bfloat16),
            jax.ShapeDtypeStruct((currency_count, owned), jnp.float32),
        ),
        in_specs=[anywhere] * 2 + [in_vmem] * 6,
        out_specs=(in_vmem, anywhere, in_vmem),
        scratch_shapes=[
            pltpu.VMEM((sets, columns), jnp.bfloat16),
            pltpu.VMEM(positive_bits.shape, jnp.int32),
            pltpu.VMEM((sets, columns), jnp.bfloat16),
            pltpu.SemaphoreType.DMA((chunks,)),
            pltpu.SemaphoreType.DMA((chunks,)),
            pltpu.SemaphoreType.DMA((chunks,)),
        ],
        compiler_params=pltpu.CompilerParams(vmem_limit_bytes=32 * 2**20),
        name="local",
    )(
        exposure_adjoint,
        positive_bits,
        slot_currencies,
        counts,
        notional.T,
        fx_paths,
        short_rates,
        start_integral.T,
    )
    arrived = lax.all_to_all(outgoing, "sets", 0, 0, tiled=True)
    fx_adjoint, rate_adjoint, notional_adjoint = pl.pallas_call(
        functools.partial(final_kernel, dates),
        out_shape=(
            jax.ShapeDtypeStruct((currency_count, owned), jnp.float32),
            jax.ShapeDtypeStruct((currency_count, owned), jnp.float32),
            jax.ShapeDtypeStruct((slots, sets), jnp.float32),
        ),
        in_specs=[in_vmem, anywhere] + [in_vmem] * 4,
        out_specs=(in_vmem,) * 3,
        scratch_shapes=[
            pltpu.VMEM((sets, columns), jnp.bfloat16),
            pltpu.SemaphoreType.DMA((chunks,)),
        ],
        compiler_params=pltpu.CompilerParams(vmem_limit_bytes=32 * 2**20),
        name="final",
    )(arrived, masked, slot_currencies, counts, fx_paths, discount)
    return fx_adjoint, rate_adjoint, notional_adjoint.T


def solution(mesh):
    in_specs = (
        P(("grp", "sets"), None),
        P(("grp", "sets"), None),
        P(("grp", "sets"), None),
        P(("grp", "sets")),
        P(("grp", "sets"), None),
        P("grp", "sets"),
        P("grp", "sets"),
        P("grp", "sets"),
    )
    out_specs = (P("grp", "sets"), P("grp", "sets"), P(("grp", "sets"), None))
    return jax.shard_map(body, mesh=mesh, in_specs=in_specs, out_specs=out_specs, check_vma=False)
```

time: 134 us -> 29.5 us (0.22)
  waiting for transfers between devices: 85.2 us -> 0 us
  between operations: 14.2 us -> 0.67 us
  blocking collectives: 24.6 us -> 18.3 us
  Pallas kernels: 0 us -> 4.42 us
  other arithmetic: 4.21 us -> 0 us
  local copies, waits for them, and re-layouts: 3.86 us -> 5.63 us
  matrix products: 1.43 us -> 0 us
    psum x1 -> x0, waiting for transfers between devices: 85.2 us -> none  [body(): summed = lax.psum(whole_term, 'sets')]
    all_gather x1 -> x0, blocking collectives: 24.6 us -> none  [body(): lax.all_gather(carried, 'sets', axis=1, tiled=True)]
    all_to_all x0 -> x1, blocking collectives: none -> 18.3 us  [body(): arrived = lax.all_to_all(outgoing, 'sets', 0, 0, tiled=True)]
    unnamed x17 -> x18, local copies, waits for them, and re-layouts: 0.92 us -> 5.63 us
    pallas_call x0 -> x2, Pallas kernels: none -> 4.42 us  [the longest x1 2.49 us: body(): pl.pallas_call(functools.partial(local_kernel, dates), out_shape=(jax.Sha...]
    shift_right_arithmetic x4 -> x0, local copies, waits for them, and re-layouts: 2.76 us -> none  [unpack(): flags = jnp.right_shift(packed[:, None, :], shifts[None, :, None]) & 1]
    select_n x1 -> x0, other arithmetic: 2.01 us -> none  [unpack(): return jnp.where(flags == 1, exposure, jnp.zeros((), jnp.bfloat16))]
    mul x2 -> x0, other arithmetic: 1.96 us -> none  [the longest x1 1.34 us: body(): aggregate * fx_paths * discount]
  transfers between devices with their start and end apart: 1 -> 0, of which waited for: 1 -> 0; matrix products, arithmetic and copies ran while one was open for 1% -> 0% of each run, Pallas kernels for 0% -> 0%
where the time goes in v2:
time: 29.5 us; the launch traced here: 29 us
  blocking collectives  18.3 us (62%)
  local copies, waits for them, and re-layouts  5.63 us (19%)
  Pallas kernels  4.42 us (15%)
  between operations  0.67 us (2%)
    all_to_all x1, blocking collectives, body(): arrived = lax.all_to_all(outgoing, 'sets', 0, 0, tiled=True)  18.3 us
    unnamed x18, local copies, waits for them, and re-layouts  5.63 us
    pallas_call x1, Pallas kernels, body(): pl.pallas_call(functools.partial(local_kernel, dates), out_shape=(jax.Sha...  2.49 us
    pallas_call x1, Pallas kernels, body(): pl.pallas_call(functools.partial(final_kernel, dates), out_shape=(jax.Sha...  1.93 us

profile of v2, /device:TPU:0, one launch (start us, length us, event | category | flops | bytes accessed | tf_op | source)
XLA Modules:
  0.0 29.0 jit_solution(15894007058037817381)
XLA Ops:
  0.6 0.0 copy-start.5
  0.6 0.0 copy-start.8
  0.7 0.7 %copy-done.5 = s32[240,4]{0,1:T(4,128)S(1)} copy-done((s32[240,4]{0,1:T(4,128)S(1)}, s32[240,4]{0,1:T(4,128)}, u32[]{:S(2)}) %copy-start.5) | copy-done | bytes 3864
  1.3 0.0 copy-done.8
  1.3 0.0 copy-start
  1.3 1.2 %copy-done = bf16[240,2048]{1,0:T(8,128)(2,1)S(1)} copy-done((bf16[240,2048]{1,0:T(8,128)(2,1)S(1)}, bf16[240,2048]{1,0:T(8,128)(2,1)}, u32[]{:S(2)}) %copy-start) | copy-done | bytes 983064
  2.5 0.0 copy-start.1
  2.5 0.9 %copy-done.1 = s32[16,2048]{1,0:T(8,128)S(1)} copy-done((s32[16,2048]{1,0:T(8,128)S(1)}, s32[16,2048]{1,0:T(8,128)}, u32[]{:S(2)}) %copy-start.1) | copy-done | bytes 131096
  3.4 0.0 copy-start.2
  3.4 0.7 %copy-done.2 = f32[40,128]{1,0:T(8,128)S(1)} copy-done((f32[40,128]{1,0:T(8,128)S(1)}, f32[40,128]{1,0:T(8,128)}, u32[]{:S(2)}) %copy-start.2) | copy-done | bytes 20504
  4.2 0.0 copy-start.4
  4.2 0.7 %copy-done.4 = f32[40,128]{1,0:T(8,128)S(1)} copy-done((f32[40,128]{1,0:T(8,128)S(1)}, f32[40,128]{1,0:T(8,128)}, u32[]{:S(2)}) %copy-start.4) | copy-done | bytes 20504
  4.9 0.0 copy-start.6
  4.9 0.7 %copy-done.6 = f32[40,16]{0,1:T(8,128)S(1)} copy-done((f32[40,16]{0,1:T(8,128)S(1)}, f32[40,16]{0,1:T(8,128)}, u32[]{:S(2)}) %copy-start.6) | copy-done | bytes 2584
  5.6 0.0 copy-start.7
  5.6 0.7 %copy-done.7 = f32[240,4]{0,1:T(4,128)S(1)} copy-done((f32[240,4]{0,1:T(4,128)S(1)}, f32[240,4]{0,1:T(4,128)}, u32[]{:S(2)}) %copy-start.7) | copy-done | bytes 3864
  6.3 2.5 %local.1 = (bf16[16,80,128]{2,1,0:T(8,128)(2,1)S(1)}, bf16[240,2048]{1,0:T(8,128)(2,1)S(1)}, f32[40,128]{1,0:T(8,128)S(1)}) custom-call(bf16[240,2048]{1,0:T(8,128)(2,1)S(1)} %copy-done, s32[16,2048]{1,0:T(8,128)S(1)} %copy-done.1, s32[4,240]{1,0:T(4,128)S(1)} %bitcast.5, s32[1,240]{1,0:T(1,128)S(1)} %bitcast.9, f32[4,240]{1,0:T(4,128)S(1)} %bitcast.8, ...), custom_call_target="tpu_custom_call" | custom-call | tf_op jit(solution)/shard_map/local/pallas_call | solution.py:253
  8.8 0.0 copy-start.3
  8.8 18.3 %all_to_all.5.arrived_ref = bf16[16,80,128]{2,1,0:T(8,128)(2,1)S(1)} all-to-all(bf16[16,80,128]{2,1,0:T(8,128)(2,1)S(1)} %get-tuple-element.9), channel_id=1, replica_groups=mesh['grp'=2,'sets'=16] {'sets'}, dimensions={0} | all-to-all | bytes 655360 | tf_op jit(solution)/shard_map/all_to_all | solution.py:282
  27.0 0.0 copy-done.3
  27.0 1.9 %final.1 = (f32[40,128]{1,0:T(8,128)}, f32[40,128]{1,0:T(8,128)}, f32[4,240]{1,0:T(4,128)}) custom-call(bf16[16,80,128]{2,1,0:T(8,128)(2,1)S(1)} %all_to_all.5.arrived_ref, bf16[240,2048]{1,0:T(8,128)(2,1)S(1)} %get-tuple-element.10.masked_hbm, s32[4,240]{1,0:T(4,128)S(1)} %bitcast.6, s32[1,240]{1,0:T(1,128)S(1)} %bitcast.10, f32[40,128]{1,0:T(8,128)S(1)} %copy-done.3, ...), custom_call_target="tpu_custom_call" | custom-call | tf_op jit(solution)/shard_map/final/pallas_call | solution.py:283
Async XLA Ops:
  0.6 0.7 %copy-start.5 = (s32[240,4]{0,1:T(4,128)S(1)}, s32[240,4]{0,1:T(4,128)}, u32[]{:S(2)}) copy-start(s32[240,4]{0,1:T(4,128)} %param.10) | copy-start | bytes 11524
  0.6 0.7 %copy-start.8 = (s32[240]{0:T(256)S(1)}, s32[240]{0:T(256)}, u32[]{:S(2)}) copy-start(s32[240]{0:T(256)} %param.11) | copy-start | bytes 2884
  1.3 1.2 %copy-start = (bf16[240,2048]{1,0:T(8,128)(2,1)S(1)}, bf16[240,2048]{1,0:T(8,128)(2,1)}, u32[]{:S(2)}) copy-start(bf16[240,2048]{1,0:T(8,128)(2,1)} %exposure_hbm.1) | copy-start | bytes 2949124
  2.5 0.9 %copy-start.1 = (s32[16,2048]{1,0:T(8,128)S(1)}, s32[16,2048]{1,0:T(8,128)}, u32[]{:S(2)}) copy-start(s32[16,2048]{1,0:T(8,128)} %bits_hbm.1) | copy-start | bytes 393220
  3.4 0.7 %copy-start.2 = (f32[40,128]{1,0:T(8,128)S(1)}, f32[40,128]{1,0:T(8,128)}, u32[]{:S(2)}) copy-start(f32[40,128]{1,0:T(8,128)} %fx_ref.3) | copy-start | bytes 61444
  4.2 0.7 %copy-start.4 = (f32[40,128]{1,0:T(8,128)S(1)}, f32[40,128]{1,0:T(8,128)}, u32[]{:S(2)}) copy-start(f32[40,128]{1,0:T(8,128)} %rates_ref.1) | copy-start | bytes 61444
  4.9 0.7 %copy-start.6 = (f32[40,16]{0,1:T(8,128)S(1)}, f32[40,16]{0,1:T(8,128)}, u32[]{:S(2)}) copy-start(f32[40,16]{0,1:T(8,128)} %param.15) | copy-start | bytes 7684
  5.6 0.7 %copy-start.7 = (f32[240,4]{0,1:T(4,128)S(1)}, f32[240,4]{0,1:T(4,128)}, u32[]{:S(2)}) copy-start(f32[240,4]{0,1:T(4,128)} %param.12) | copy-start | bytes 11524
  8.8 18.3 %copy-start.3 = (f32[40,128]{1,0:T(8,128)S(1)}, f32[40,128]{1,0:T(8,128)}, u32[]{:S(2)}) copy-start(f32[40,128]{1,0:T(8,128)} %fx_ref.3) | copy-start | bytes 61444

commit v3 on v2

--- a/solution.py
+++ b/solution.py
@@ -63,14 +63,12 @@
     rates_ref,
     start_ref,
     outgoing_ref,
-    masked_hbm,
+    masked,
     discount_ref,
     exposure,
     bits,
-    masked,
     in_sems,
     bits_sems,
-    out_sems,
 ):
     sets, columns = exposure.shape
     currency_count, owned = fx_ref.shape
@@ -86,10 +84,6 @@
     def bits_copy(index):
         part = pl.ds(index * width, width)
         return pltpu.make_async_copy(bits_hbm.at[:, part], bits.at[:, part], bits_sems.at[index])
-
-    def masked_copy(index):
-        part = pl.ds(index * width, width)
-        return pltpu.make_async_copy(masked.at[:, part], masked_hbm.at[:, part], out_sems.at[index])
 
     for index in range(chunks):
         bits_copy(index).start()
@@ -166,15 +160,12 @@
             some_columns(0, None)
         else:
             pl.loop(0, width // group_width)(lambda step: some_columns(step, None))
-        masked_copy(index).start()
-    for index in range(chunks):
-        masked_copy(index).wait()
 
 
 def final_kernel(
     dates,
     arrived_ref,
-    masked_hbm,
+    masked,
     currencies_ref,
     counts_ref,
     fx_ref,
@@ -182,20 +173,11 @@
     fx_adjoint_ref,
     rate_adjoint_ref,
     notional_adjoint_ref,
-    masked,
-    in_sems,
 ):
     sets, columns = masked.shape
     currency_count, owned = fx_ref.shape
     peers = columns // owned
     width = columns // chunks
-
-    def masked_copy(index):
-        part = pl.ds(index * width, width)
-        return pltpu.make_async_copy(masked_hbm.at[:, part], masked.at[:, part], in_sems.at[index])
-
-    for index in range(chunks):
-        masked_copy(index).start()
 
     aggregate = arrived_ref[0, currency_count:, :].astype(jnp.float32)
     for peer in range(1, peers):
@@ -206,7 +188,6 @@
 
     projected = jnp.zeros((sets, currency_count), jnp.float32)
     for index in range(chunks):
-        masked_copy(index).wait()
         per_chunk = width // owned
         carried = jnp.concatenate(
             [
@@ -253,31 +234,34 @@
     outgoing, masked, discount = pl.pallas_call(
         functools.partial(local_kernel, dates),
         out_shape=(
-            jax.ShapeDtypeStruct((peers, 2 * currency_count, owned), jnp.bfloat16),
-            jax.ShapeDtypeStruct((sets, columns), jnp.bfloat16),
+            pltpu.VMEM((peers, 2 * currency_count, owned), jnp.bfloat16),
+            pltpu.VMEM((sets, columns), jnp.bfloat16),
             jax.ShapeDtypeStruct((currency_count, owned), jnp.float32),
         ),
         in_specs=[anywhere] * 2 + [in_vmem] * 6,
-        out_specs=(in_vmem, anywhere, in_vmem),
+        out_specs=(in_vmem,) * 3,
         scratch_shapes=[
             pltpu.VMEM((sets, columns), jnp.bfloat16),
             pltpu.VMEM(positive_bits.shape, jnp.int32),
-            pltpu.VMEM((sets, columns), jnp.bfloat16),
-            pltpu.SemaphoreType.DMA((chunks,)),
             pltpu.SemaphoreType.DMA((chunks,)),
             pltpu.SemaphoreType.DMA((chunks,)),
         ],
         compiler_params=pltpu.CompilerParams(vmem_limit_bytes=32 * 2**20),
         name="local",
     )(
-        exposure_adjoint,
-        positive_bits,
-        slot_currencies,
-        counts,
-        notional.T,
-        fx_paths,
-        short_rates,
-        start_integral.T,
+        *[
+            pltpu.with_memory_space_constraint(value, pltpu.HBM)
+            for value in (
+                exposure_adjoint,
+                positive_bits,
+                slot_currencies,
+                counts,
+                notional.T,
+                fx_paths,
+                short_rates,
+                start_integral.T,
+            )
+        ]
     )
     arrived = lax.all_to_all(outgoing, "sets", 0, 0, tiled=True)
     fx_adjoint, rate_adjoint, notional_adjoint = pl.pallas_call(
@@ -287,12 +271,8 @@
             jax.ShapeDtypeStruct((currency_count, owned), jnp.float32),
             jax.ShapeDtypeStruct((slots, sets), jnp.float32),
         ),
-        in_specs=[in_vmem, anywhere] + [in_vmem] * 4,
+        in_specs=[in_vmem] * 6,
         out_specs=(in_vmem,) * 3,
-        scratch_shapes=[
-            pltpu.VMEM((sets, columns), jnp.bfloat16),
-            pltpu.SemaphoreType.DMA((chunks,)),
-        ],
         compiler_params=pltpu.CompilerParams(vmem_limit_bytes=32 * 2**20),
         name="final",
     )(arrived, masked, slot_currencies, counts, fx_paths, discount)

time: 29.5 us -> 24.4 us (0.83)
  local copies, waits for them, and re-layouts: 5.63 us -> 0.69 us
    unnamed x18 -> x6, local copies, waits for them, and re-layouts: 5.63 us -> 0.69 us
    pallas_call x1, Pallas kernels: 2.49 us -> 3.47 us  [body(): pl.pallas_call(functools.partial(local_kernel, dates), out_shape=(pltpu.V...]
    pallas_call x1, Pallas kernels: 1.93 us -> 1.06 us  [body(): pl.pallas_call(functools.partial(final_kernel, dates), out_shape=(jax.Sha...]
where the time goes in v3:
time: 24.4 us; the launch traced here: 24.1 us
  blocking collectives  18.3 us (75%)
  Pallas kernels  4.52 us (19%)
  local copies, waits for them, and re-layouts  0.69 us (3%)
  between operations  0.66 us (3%)
    all_to_all x1, blocking collectives, body(): arrived = lax.all_to_all(outgoing, 'sets', 0, 0, tiled=True)  18.3 us
    pallas_call x1, Pallas kernels, body(): pl.pallas_call(functools.partial(local_kernel, dates), out_shape=(pltpu.V...  3.47 us
    pallas_call x1, Pallas kernels, body(): pl.pallas_call(functools.partial(final_kernel, dates), out_shape=(jax.Sha...  1.06 us
    unnamed x6, local copies, waits for them, and re-layouts  0.69 us

profile of v3, /device:TPU:0, one launch (start us, length us, event | category | flops | bytes accessed | tf_op | source)
XLA Modules:
  0.0 24.1 jit_solution(2265975373964418735)
XLA Ops:
  0.6 3.5 %local.1 = (bf16[16,80,128]{2,1,0:T(8,128)(2,1)S(1)}, bf16[240,2048]{1,0:T(8,128)(2,1)S(1)}, f32[40,128]{1,0:T(8,128)S(1)}) custom-call(bf16[240,2048]{1,0:T(8,128)(2,1)} %exposure_hbm.1, s32[16,2048]{1,0:T(8,128)} %bits_hbm.1, s32[4,240]{1,0:T(4,128)} %bitcast.5, s32[1,240]{1,0:T(1,128)} %bitcast.7, f32[4,240]{1,0:T(4,128)} %bitcast.10, f32[40,128]{1,0:T(8,128)} %fx_ref.3, ...), custom_call_target="tpu_custom_call" | custom-call | tf_op jit(solution)/shard_map/local/pallas_call | solution.py:234
  4.1 0.0 copy-start
  4.1 0.0 copy-start.1
  4.1 18.3 %all_to_all.5.arrived_ref = bf16[16,80,128]{2,1,0:T(8,128)(2,1)S(1)} all-to-all(bf16[16,80,128]{2,1,0:T(8,128)(2,1)S(1)} %get-tuple-element.9), channel_id=1, replica_groups=mesh['grp'=2,'sets'=16] {'sets'}, dimensions={0} | all-to-all | bytes 655360 | tf_op jit(solution)/shard_map/all_to_all | solution.py:266
  22.4 0.0 copy-start.2
  22.4 0.0 copy-done
  22.4 0.0 copy-done.1
  22.4 0.7 %copy-done.2 = s32[240]{0:T(256)S(1)} copy-done((s32[240]{0:T(256)S(1)}, s32[240]{0:T(256)}, u32[]{:S(2)}) %copy-start.2) | copy-done | bytes 984
  23.1 1.1 %final.1 = (f32[40,128]{1,0:T(8,128)}, f32[40,128]{1,0:T(8,128)}, f32[4,240]{1,0:T(4,128)}) custom-call(bf16[16,80,128]{2,1,0:T(8,128)(2,1)S(1)} %all_to_all.5.arrived_ref, bf16[240,2048]{1,0:T(8,128)(2,1)S(1)} %get-tuple-element.10.masked, s32[4,240]{1,0:T(4,128)S(1)} %bitcast.6, s32[1,240]{1,0:T(1,128)S(1)} %bitcast.8, f32[40,128]{1,0:T(8,128)S(1)} %copy-done, ...), custom_call_target="tpu_custom_call" | custom-call | tf_op jit(solution)/shard_map/final/pallas_call | solution.py:267
Async XLA Ops:
  4.1 18.3 %copy-start = (f32[40,128]{1,0:T(8,128)S(1)}, f32[40,128]{1,0:T(8,128)}, u32[]{:S(2)}) copy-start(f32[40,128]{1,0:T(8,128)} %fx_ref.3) | copy-start | bytes 61444
  4.1 18.3 %copy-start.1 = (s32[240,4]{0,1:T(4,128)S(1)}, s32[240,4]{0,1:T(4,128)}, u32[]{:S(2)}) copy-start(s32[240,4]{0,1:T(4,128)} %param.10) | copy-start | bytes 11524
  22.4 0.7 %copy-start.2 = (s32[240]{0:T(256)S(1)}, s32[240]{0:T(256)}, u32[]{:S(2)}) copy-start(s32[240]{0:T(256)} %param.11) | copy-start | bytes 2884

commit v4 on v3

--- a/solution.py
+++ b/solution.py
@@ -52,27 +52,29 @@
     return jnp.where(slot < counts, currencies, -1)
 
 
+def carry_kernel(dates, fx_ref, rates_ref, start_ref, carried_ref, discount_ref):
+    integral = spread_paths(start_ref[...], dates) + step_years * sums_to_date(rates_ref[...], dates)
+    discount = jnp.exp(-integral)
+    discount_ref[...] = discount
+    carried_ref[...] = (fx_ref[...] * discount).astype(jnp.bfloat16)
+
+
 def local_kernel(
-    dates,
     exposure_hbm,
     bits_hbm,
     currencies_ref,
     counts_ref,
     notional_ref,
-    fx_ref,
-    rates_ref,
-    start_ref,
-    outgoing_ref,
     masked,
-    discount_ref,
+    terms_ref,
+    used_ref,
     exposure,
     bits,
     in_sems,
     bits_sems,
 ):
     sets, columns = exposure.shape
-    currency_count, owned = fx_ref.shape
-    peers = columns // owned
+    blocks, currency_count, owned = terms_ref.shape
     width = columns // chunks
 
     def exposure_copy(index):
@@ -89,14 +91,8 @@
         bits_copy(index).start()
         exposure_copy(index).start()
 
-    integral = spread_paths(start_ref[...], dates) + step_years * sums_to_date(rates_ref[...], dates)
-    discount = jnp.exp(-integral)
-    discount_ref[...] = discount
-    carried = (fx_ref[...] * discount).astype(jnp.bfloat16)
-    for peer in range(peers):
-        outgoing_ref[peer, 0:currency_count, :] = carried
-
     used = used_currencies(currencies_ref[...], counts_ref[...])
+    used_ref[...] = used
     notional = notional_ref[...]
     currency = lax.broadcasted_iota(jnp.int32, (currency_count, sets), 0)
     weights = jnp.zeros((currency_count, sets), jnp.float32)
@@ -143,7 +139,7 @@
         bits_copy(index).wait()
         exposure_copy(index).wait()
 
-        def some_columns(step, _):
+        def some_columns(step):
             first = index * width + step * group_width
             if not isinstance(first, int):
                 first = pl.multiple_of(first, group_width)
@@ -152,64 +148,74 @@
                 weights, masked[:, pl.ds(first, group_width)], preferred_element_type=jnp.float32
             ).astype(jnp.bfloat16)
             for block in range(group_width // owned):
-                outgoing_ref[first // owned + block, currency_count:, :] = terms[
-                    :, block * owned : (block + 1) * owned
-                ]
+                terms_ref[first // owned + block] = terms[:, block * owned : (block + 1) * owned]
 
         if width == group_width:
-            some_columns(0, None)
+            some_columns(0)
         else:
-            pl.loop(0, width // group_width)(lambda step: some_columns(step, None))
-
-
-def final_kernel(
-    dates,
-    arrived_ref,
-    masked,
-    currencies_ref,
-    counts_ref,
-    fx_ref,
-    discount_ref,
-    fx_adjoint_ref,
-    rate_adjoint_ref,
-    notional_adjoint_ref,
-):
+            pl.loop(0, width // group_width)(some_columns)
+
+
+def packing_kernel(planes, near, *refs):
+    carried_refs, terms_ref = refs[:planes], refs[planes]
+    out_refs = refs[planes + 1 :]
+    currency_count = terms_ref.shape[1]
+    mine = lax.axis_index("sets") % near
+    for offset, out_ref in enumerate(out_refs):
+        for plane in range(planes):
+            out_ref[plane, currency_count:, :] = terms_ref[plane * near + (mine ^ offset)]
+            if offset:
+                out_ref[plane, 0:currency_count, :] = carried_refs[plane][...]
+
+
+def plane_kernel(planes, near, *refs):
+    in_refs, out_refs, summed = refs[:near], refs[near:-1], refs[-1]
+    currency_count = summed.shape[1]
+    for plane in range(planes):
+        total = in_refs[0][plane, currency_count:, :].astype(jnp.float32)
+        for ref in in_refs[1:]:
+            total = total + ref[plane, currency_count:, :].astype(jnp.float32)
+        summed[plane] = total
+    mine = lax.axis_index("sets") // near
+    for offset, out_ref in enumerate(out_refs):
+        out_ref[...] = summed[mine ^ offset]
+
+
+def projection_kernel(planes, near, *refs):
+    carried_refs, stacked_refs = refs[:planes], refs[planes : planes + near - 1]
+    masked, used_ref, notional_adjoint_ref, carried = refs[planes + near - 1 :]
     sets, columns = masked.shape
-    currency_count, owned = fx_ref.shape
-    peers = columns // owned
-    width = columns // chunks
-
-    aggregate = arrived_ref[0, currency_count:, :].astype(jnp.float32)
-    for peer in range(1, peers):
-        aggregate = aggregate + arrived_ref[peer, currency_count:, :].astype(jnp.float32)
-    fx_adjoint = aggregate * discount_ref[...]
-    fx_adjoint_ref[...] = fx_adjoint
-    rate_adjoint_ref[...] = -step_years * sums_from_date(fx_adjoint * fx_ref[...], dates)
-
-    projected = jnp.zeros((sets, currency_count), jnp.float32)
-    for index in range(chunks):
-        per_chunk = width // owned
-        carried = jnp.concatenate(
-            [
-                arrived_ref[index * per_chunk + block, 0:currency_count, :]
-                for block in range(per_chunk)
-            ],
-            axis=1,
-        )
-        projected = projected + lax.dot_general(
-            masked[:, index * width : (index + 1) * width],
-            carried,
-            (((1,), (1,)), ((), ())),
-            preferred_element_type=jnp.float32,
-        )
-    projected = projected.T
-    used = used_currencies(currencies_ref[...], counts_ref[...])
+    currency_count, owned = carried_refs[0].shape
+    me = lax.axis_index("sets")
+    for offset in range(near):
+        for plane in range(planes):
+            block = (
+                stacked_refs[offset - 1][plane, 0:currency_count, :]
+                if offset
+                else carried_refs[plane][...]
+            )
+            source = me ^ (plane * near + offset)
+            carried[:, pl.ds(pl.multiple_of(source * owned, owned), owned)] = block
+    projected = lax.dot_general(
+        masked[...], carried[...], (((1,), (1,)), ((), ())), preferred_element_type=jnp.float32
+    ).T
+    used = used_ref[...]
     currency = lax.broadcasted_iota(jnp.int32, (currency_count, sets), 0)
     for slot in range(used.shape[0]):
         picked = jnp.sum(
             jnp.where(currency == used[slot : slot + 1], projected, 0.0), axis=0, keepdims=True
         )
         notional_adjoint_ref[slot : slot + 1, :] = picked * (1.0 / math.sqrt(columns))
+
+
+def final_kernel(dates, planes, *refs):
+    part_refs, (fx_ref, discount_ref, fx_adjoint_ref, rate_adjoint_ref) = refs[:planes], refs[planes:]
+    aggregate = part_refs[0][...]
+    for ref in part_refs[1:]:
+        aggregate = aggregate + ref[...]
+    fx_adjoint = aggregate * discount_ref[...]
+    fx_adjoint_ref[...] = fx_adjoint
+    rate_adjoint_ref[...] = -step_years * sums_from_date(fx_adjoint * fx_ref[...], dates)
 
 
 def body(
@@ -227,18 +233,36 @@
     dates = owned // start_integral.shape[1]
     peers = columns // owned
     slots = currencies.shape[1]
+    near = 2 ** ((peers.bit_length() - 1) // 2)
+    planes = peers // near
     in_vmem = pl.BlockSpec(memory_space=pltpu.VMEM)
     anywhere = pl.BlockSpec(memory_space=pl.ANY)
-    slot_currencies = currencies.T
-    counts = mix_count.reshape(1, sets)
-    outgoing, masked, discount = pl.pallas_call(
-        functools.partial(local_kernel, dates),
+    params = pltpu.CompilerParams(vmem_limit_bytes=32 * 2**20)
+
+    def in_hbm(value):
+        return pltpu.with_memory_space_constraint(value, pltpu.HBM)
+
+    def exchange(value, offset):
+        return lax.ppermute(value, "sets", [(peer, peer ^ offset) for peer in range(peers)])
+
+    block = (currency_count, owned)
+    carried, discount = pl.pallas_call(
+        functools.partial(carry_kernel, dates),
+        out_shape=(pltpu.VMEM(block, jnp.bfloat16), pltpu.VMEM(block, jnp.float32)),
+        in_specs=[in_vmem] * 3,
+        out_specs=(in_vmem,) * 2,
+        compiler_params=params,
+        name="carry",
+    )(in_hbm(fx_paths), in_hbm(short_rates), in_hbm(start_integral.T))
+    along = [carried] + [exchange(carried, near * offset) for offset in range(1, planes)]
+    masked, terms, used = pl.pallas_call(
+        local_kernel,
         out_shape=(
-            pltpu.VMEM((peers, 2 * currency_count, owned), jnp.bfloat16),
             pltpu.VMEM((sets, columns), jnp.bfloat16),
-            jax.ShapeDtypeStruct((currency_count, owned), jnp.float32),
+            pltpu.VMEM((peers,) + block, jnp.bfloat16),
+            pltpu.VMEM((slots, sets), jnp.int32),
         ),
-        in_specs=[anywhere] * 2 + [in_vmem] * 6,
+        in_specs=[anywhere] * 2 + [in_vmem] * 3,
         out_specs=(in_vmem,) * 3,
         scratch_shapes=[
             pltpu.VMEM((sets, columns), jnp.bfloat16),
@@ -246,36 +270,51 @@
             pltpu.SemaphoreType.DMA((chunks,)),
             pltpu.SemaphoreType.DMA((chunks,)),
         ],
-        compiler_params=pltpu.CompilerParams(vmem_limit_bytes=32 * 2**20),
+        compiler_params=params,
         name="local",
     )(
-        *[
-            pltpu.with_memory_space_constraint(value, pltpu.HBM)
-            for value in (
-                exposure_adjoint,
-                positive_bits,
-                slot_currencies,
-                counts,
-                notional.T,
-                fx_paths,
-                short_rates,
-                start_integral.T,
-            )
-        ]
+        in_hbm(exposure_adjoint),
+        in_hbm(positive_bits),
+        in_hbm(currencies.T),
+        in_hbm(mix_count.reshape(1, sets)),
+        in_hbm(notional.T),
     )
-    arrived = lax.all_to_all(outgoing, "sets", 0, 0, tiled=True)
-    fx_adjoint, rate_adjoint, notional_adjoint = pl.pallas_call(
-        functools.partial(final_kernel, dates),
-        out_shape=(
-            jax.ShapeDtypeStruct((currency_count, owned), jnp.float32),
-            jax.ShapeDtypeStruct((currency_count, owned), jnp.float32),
-            jax.ShapeDtypeStruct((slots, sets), jnp.float32),
-        ),
-        in_specs=[in_vmem] * 6,
-        out_specs=(in_vmem,) * 3,
-        compiler_params=pltpu.CompilerParams(vmem_limit_bytes=32 * 2**20),
+    outgoing = pl.pallas_call(
+        functools.partial(packing_kernel, planes, near),
+        out_shape=(pltpu.VMEM((planes, 2 * currency_count, owned), jnp.bfloat16),) * near,
+        in_specs=[in_vmem] * (planes + 1),
+        out_specs=(in_vmem,) * near,
+        compiler_params=params,
+        name="packing",
+    )(*along, terms)
+    arrived = [exchange(outgoing[offset], offset) for offset in range(1, near)]
+    summed = pl.pallas_call(
+        functools.partial(plane_kernel, planes, near),
+        out_shape=(pltpu.VMEM(block, jnp.float32),) * planes,
+        in_specs=[in_vmem] * near,
+        out_specs=(in_vmem,) * planes,
+        scratch_shapes=[pltpu.VMEM((planes,) + block, jnp.float32)],
+        compiler_params=params,
+        name="plane",
+    )(outgoing[0], *arrived)
+    parts = [summed[0]] + [exchange(summed[offset], near * offset) for offset in range(1, planes)]
+    notional_adjoint = pl.pallas_call(
+        functools.partial(projection_kernel, planes, near),
+        out_shape=jax.ShapeDtypeStruct((slots, sets), jnp.float32),
+        in_specs=[in_vmem] * (planes + near + 1),
+        out_specs=in_vmem,
+        scratch_shapes=[pltpu.VMEM((currency_count, columns), jnp.bfloat16)],
+        compiler_params=params,
+        name="projection",
+    )(*along, *arrived, masked, used)
+    fx_adjoint, rate_adjoint = pl.pallas_call(
+        functools.partial(final_kernel, dates, planes),
+        out_shape=(jax.ShapeDtypeStruct(block, jnp.float32),) * 2,
+        in_specs=[in_vmem] * (planes + 2),
+        out_specs=(in_vmem,) * 2,
+        compiler_params=params,
         name="final",
-    )(arrived, masked, slot_currencies, counts, fx_paths, discount)
+    )(*parts, fx_paths, discount)
     return fx_adjoint, rate_adjoint, notional_adjoint.T
 
 

time: 24.4 us -> 28.3 us (1.16)
  blocking collectives: 18.3 us -> 0 us
  starting transfers between devices: 0 us -> 12.1 us
  waiting for transfers between devices: 0 us -> 8.84 us
  Pallas kernels: 4.52 us -> 6.38 us
  local copies, waits for them, and re-layouts: 0.69 us -> 0.01 us
    all_to_all x1 -> x0, blocking collectives: 18.3 us -> none  [body(): arrived = lax.all_to_all(outgoing, 'sets', 0, 0, tiled=True)]
    ppermute x0 -> x9, starting transfers between devices: none -> 12.1 us  [exchange(): lax.ppermute(value, 'sets', [(peer, peer ^ offset) for peer in range(peer...]
    ppermute x0 -> x9, waiting for transfers between devices: none -> 8.84 us  [exchange(): lax.ppermute(value, 'sets', [(peer, peer ^ offset) for peer in range(peer...]
    pallas_call x2 -> x6, Pallas kernels: 4.52 us -> 6.38 us  [the longest x1 3.39 us: body(): pl.pallas_call(local_kernel, out_shape=(pltpu.VMEM((sets, columns), jnp.b...]
    unnamed x6 -> x2, local copies, waits for them, and re-layouts: 0.69 us -> 0.01 us
  transfers between devices with their start and end apart: 0 -> 9, of which waited for: 0 -> 5; matrix products, arithmetic and copies ran while one was open for 0% -> 0% of each run, Pallas kernels for 0% -> 16%
where the time goes in v4:
time: 28.3 us; the launch traced here: 28 us
  starting transfers between devices  12.1 us (43%)
  waiting for transfers between devices  8.84 us (31%)
  Pallas kernels  6.38 us (23%)
  between operations  0.68 us (2%)
    ppermute x9, starting transfers between devices, exchange(): lax.ppermute(value, 'sets', [(peer, peer ^ offset) for peer in range(peer...  12.1 us
    ppermute x9, waiting for transfers between devices, exchange(): lax.ppermute(value, 'sets', [(peer, peer ^ offset) for peer in range(peer...  8.84 us
    pallas_call x1, Pallas kernels, body(): pl.pallas_call(local_kernel, out_shape=(pltpu.VMEM((sets, columns), jnp.b...  3.39 us
    pallas_call x1, Pallas kernels, body(): pl.pallas_call(functools.partial(projection_kernel, planes, near), out_sh...  1.1 us
    pallas_call x1, Pallas kernels, body(): pl.pallas_call(functools.partial(carry_kernel, dates), out_shape=(pltpu.V...  1 us
    pallas_call x1, Pallas kernels, body(): pl.pallas_call(functools.partial(final_kernel, dates, planes), out_shape=...  0.83 us
  transfers between devices with their start and end apart: 9, of which 5 were waited for; matrix products, arithmetic and copies ran while one was open for 0% of the time, Pallas kernels for 16%

profile of v4, /device:TPU:0, one launch (start us, length us, event | category | flops | bytes accessed | tf_op | source)
XLA Modules:
  0.0 28.0 jit_solution(2584363749256020698)
XLA Ops:
  0.6 1.0 %carry.1 = (bf16[40,128]{1,0:T(8,128)(2,1)S(1)}, f32[40,128]{1,0:T(8,128)S(1)}) custom-call(f32[40,128]{1,0:T(8,128)} %refs_4_.1, f32[40,128]{1,0:T(8,128)} %rates_ref.1, f32[16,40]{1,0:T(8,128)} %bitcast.5), custom_call_target="tpu_custom_call" | custom-call | tf_op jit(solution)/shard_map/carry/pallas_call | solution.py:249
  1.6 5.1 %collective-permute-start.2 = (bf16[40,128]{1,0:T(8,128)(2,1)S(1)}, bf16[40,128]{1,0:T(8,128)(2,1)S(1)}, u32[]{:S(2)}, u32[]{:S(2)}) collective-permute-start(bf16[40,128]{1,0:T(8,128)(2,1)S(1)} %get-tuple-element.18.refs_0_), channel_id=1, source_target_pairs={{0,12},{1,13},{2,14},{3,15},{4,8},{5,9},{6,10},{7,11},{8,4},{9,5},... | collective-permute-start | bytes 30728 | tf_op jit(solution)/shard_map/ppermute | solution.py:246
  6.8 0.0 collective-permute-start.1
  6.8 0.6 %collective-permute-start = (bf16[40,128]{1,0:T(8,128)(2,1)S(1)}, bf16[40,128]{1,0:T(8,128)(2,1)S(1)}, u32[]{:S(2)}, u32[]{:S(2)}) collective-permute-start(bf16[40,128]{1,0:T(8,128)(2,1)S(1)} %get-tuple-element.18.refs_0_), channel_id=1, source_target_pairs={{0,4},{1,5},{2,6},{3,7},{4,0},{5,1},{6,2},{7,3},{8,12},{9,13},{10,... | collective-permute-start | bytes 30728 | tf_op jit(solution)/shard_map/ppermute | solution.py:246
  7.4 3.4 %local.1 = (bf16[240,2048]{1,0:T(8,128)(2,1)S(1)}, bf16[16,40,128]{2,1,0:T(8,128)(2,1)S(1)}, s32[4,240]{1,0:T(4,128)S(1)}) custom-call(bf16[240,2048]{1,0:T(8,128)(2,1)} %exposure_hbm.1, s32[16,2048]{1,0:T(8,128)} %bits_hbm.1, s32[4,240]{1,0:T(4,128)} %bitcast.6, s32[1,240]{1,0:T(1,128)} %bitcast.9, f32[4,240]{1,0:T(4,128)} %bitcast.7), custom_call_target="tpu_custom_call" | custom-call | tf_op jit(solution)/shard_map/local/pallas_call | solution.py:258
  10.8 0.0 collective-permute-done.2.refs_3_
  10.8 0.5 %collective-permute-done.1.refs_2_ = bf16[40,128]{1,0:T(8,128)(2,1)S(1)} collective-permute-done((bf16[40,128]{1,0:T(8,128)(2,1)S(1)}, bf16[40,128]{1,0:T(8,128)(2,1)S(1)}, u32[]{:S(2)}, u32[]{:S(2)}) %collective-permute-start.1) | collective-permute-done | bytes 10272 | tf_op jit(solution)/shard_map/ppermute | solution.py:246
  11.3 0.0 collective-permute-done.refs_1_
  11.4 0.1 collective-permute-start.3
  11.4 1.6 %collective-permute-start.4 = (bf16[4,80,128]{2,1,0:T(8,128)(2,1)S(1)}, bf16[4,80,128]{2,1,0:T(8,128)(2,1)S(1)}, u32[]{:S(2)}, u32[]{:S(2)}) collective-permute-start(bf16[4,80,128]{2,1,0:T(8,128)(2,1)S(1)} %get-tuple-element.22), channel_id=1, source_target_pairs={{0,2},{1,3},{2,0},{3,1},{4,6},{5,7},{6,4},{7,5},{8,10},{9,11},{10,... | collective-permute-start | bytes 245768 | tf_op jit(solution)/shard_map/ppermute | solution.py:246
  13.0 0.3 %collective-permute-start.5 = (bf16[4,80,128]{2,1,0:T(8,128)(2,1)S(1)}, bf16[4,80,128]{2,1,0:T(8,128)(2,1)S(1)}, u32[]{:S(2)}, u32[]{:S(2)}) collective-permute-start(bf16[4,80,128]{2,1,0:T(8,128)(2,1)S(1)} %get-tuple-element.23), channel_id=1, source_target_pairs={{0,3},{1,2},{2,1},{3,0},{4,7},{5,6},{6,5},{7,4},{8,11},{9,10},{10,... | collective-permute-start | bytes 245768 | tf_op jit(solution)/shard_map/ppermute | solution.py:246
  13.3 0.0 collective-permute-done.3.refs_1_.refs_4_
  13.3 3.3 %collective-permute-done.4.refs_2_.refs_5_ = bf16[4,80,128]{2,1,0:T(8,128)(2,1)S(1)} collective-permute-done((bf16[4,80,128]{2,1,0:T(8,128)(2,1)S(1)}, bf16[4,80,128]{2,1,0:T(8,128)(2,1)S(1)}, u32[]{:S(2)}, u32[]{:S(2)}) %collective-permute-start.4) | collective-permute-done | bytes 81952 | tf_op jit(solution)/shard_map/ppermute | solution.py:246
  16.6 1.1 %collective-permute-done.5.refs_3_.refs_6_ = bf16[4,80,128]{2,1,0:T(8,128)(2,1)S(1)} collective-permute-done((bf16[4,80,128]{2,1,0:T(8,128)(2,1)S(1)}, bf16[4,80,128]{2,1,0:T(8,128)(2,1)S(1)}, u32[]{:S(2)}, u32[]{:S(2)}) %collective-permute-start.5) | collective-permute-done | bytes 81952 | tf_op jit(solution)/shard_map/ppermute | solution.py:246
  17.8 1.0 %collective-permute-start.6 = (f32[40,128]{1,0:T(8,128)S(1)}, f32[40,128]{1,0:T(8,128)S(1)}, u32[]{:S(2)}, u32[]{:S(2)}) collective-permute-start(f32[40,128]{1,0:T(8,128)S(1)} %get-tuple-element.25), channel_id=1, source_target_pairs={{0,4},{1,5},{2,6},{3,7},{4,0},{5,1},{6,2},{7,3},{8,12},{9,13},{10,... | collective-permute-start | bytes 61448 | tf_op jit(solution)/shard_map/ppermute | solution.py:246
  18.7 2.9 %collective-permute-start.7 = (f32[40,128]{1,0:T(8,128)S(1)}, f32[40,128]{1,0:T(8,128)S(1)}, u32[]{:S(2)}, u32[]{:S(2)}) collective-permute-start(f32[40,128]{1,0:T(8,128)S(1)} %get-tuple-element.26), channel_id=1, source_target_pairs={{0,8},{1,9},{2,10},{3,11},{4,12},{5,13},{6,14},{7,15},{8,0},{9,1},... | collective-permute-start | bytes 61448 | tf_op jit(solution)/shard_map/ppermute | solution.py:246
  21.6 0.6 %collective-permute-start.8 = (f32[40,128]{1,0:T(8,128)S(1)}, f32[40,128]{1,0:T(8,128)S(1)}, u32[]{:S(2)}, u32[]{:S(2)}) collective-permute-start(f32[40,128]{1,0:T(8,128)S(1)} %get-tuple-element.27), channel_id=1, source_target_pairs={{0,12},{1,13},{2,14},{3,15},{4,8},{5,9},{6,10},{7,11},{8,4},{9,5},... | collective-permute-start | bytes 61448 | tf_op jit(solution)/shard_map/ppermute | solution.py:246
  22.2 0.0 copy-start
  22.2 1.1 %projection.1 = f32[4,240]{1,0:T(4,128)} custom-call(bf16[40,128]{1,0:T(8,128)(2,1)S(1)} %get-tuple-element.18.refs_0_, bf16[40,128]{1,0:T(8,128)(2,1)S(1)} %collective-permute-done.refs_1_, bf16[40,128]{1,0:T(8,128)(2,1)S(1)} %collective-permute-done.1.refs_2_, bf16[40,128]{1,0:T(8,128)(2,1)S(1)} %collective-permute-done.2.refs_3_, ...), custom_call_target="tpu_custom_call" | custom-call | tf_op jit(solution)/shard_map/projection/pallas_call | solution.py:301
  23.3 0.0 collective-permute-done.6.refs_1_
  23.3 0.1 collective-permute-done.7.refs_2_
  23.4 3.8 %collective-permute-done.8.refs_3_ = f32[40,128]{1,0:T(8,128)S(1)} collective-permute-done((f32[40,128]{1,0:T(8,128)S(1)}, f32[40,128]{1,0:T(8,128)S(1)}, u32[]{:S(2)}, u32[]{:S(2)}) %collective-permute-start.8) | collective-permute-done | bytes 20512 | tf_op jit(solution)/shard_map/ppermute | solution.py:246
  27.2 0.0 copy-done
  27.2 0.8 %final.1 = (f32[40,128]{1,0:T(8,128)}, f32[40,128]{1,0:T(8,128)}) custom-call(f32[40,128]{1,0:T(8,128)S(1)} %get-tuple-element.24.refs_0_, f32[40,128]{1,0:T(8,128)S(1)} %collective-permute-done.6.refs_1_, f32[40,128]{1,0:T(8,128)S(1)} %collective-permute-done.7.refs_2_, f32[40,128]{1,0:T(8,128)S(1)} %collective-permute-done.8.refs_3_, ...), custom_call_target="tpu_custom_call" | custom-call | tf_op jit(solution)/shard_map/final/pallas_call | solution.py:310
  (2 shorter events, 0.1 us)
Async XLA Ops:
  1.6 9.2 %collective-permute-start.2 = (bf16[40,128]{1,0:T(8,128)(2,1)S(1)}, bf16[40,128]{1,0:T(8,128)(2,1)S(1)}, u32[]{:S(2)}, u32[]{:S(2)}) collective-permute-start(bf16[40,128]{1,0:T(8,128)(2,1)S(1)} %get-tuple-element.18.refs_0_), channel_id=1, source_target_pairs={{0,12},{1,13},{2,14},{3,15},{4,8},{5,9},{6,10},{7,11},{8,4},{9,5},... | collective-permute-start | bytes 30728 | tf_op jit(solution)/shard_map/ppermute | solution.py:246
  6.8 4.6 %collective-permute-start.1 = (bf16[40,128]{1,0:T(8,128)(2,1)S(1)}, bf16[40,128]{1,0:T(8,128)(2,1)S(1)}, u32[]{:S(2)}, u32[]{:S(2)}) collective-permute-start(bf16[40,128]{1,0:T(8,128)(2,1)S(1)} %get-tuple-element.18.refs_0_), channel_id=1, source_target_pairs={{0,8},{1,9},{2,10},{3,11},{4,12},{5,13},{6,14},{7,15},{8,0},{9,1},... | collective-permute-start | bytes 30728 | tf_op jit(solution)/shard_map/ppermute | solution.py:246
  6.8 4.6 %collective-permute-start = (bf16[40,128]{1,0:T(8,128)(2,1)S(1)}, bf16[40,128]{1,0:T(8,128)(2,1)S(1)}, u32[]{:S(2)}, u32[]{:S(2)}) collective-permute-start(bf16[40,128]{1,0:T(8,128)(2,1)S(1)} %get-tuple-element.18.refs_0_), channel_id=1, source_target_pairs={{0,4},{1,5},{2,6},{3,7},{4,0},{5,1},{6,2},{7,3},{8,12},{9,13},{10,... | collective-permute-start | bytes 30728 | tf_op jit(solution)/shard_map/ppermute | solution.py:246
  11.4 1.9 %collective-permute-start.3 = (bf16[4,80,128]{2,1,0:T(8,128)(2,1)S(1)}, bf16[4,80,128]{2,1,0:T(8,128)(2,1)S(1)}, u32[]{:S(2)}, u32[]{:S(2)}) collective-permute-start(bf16[4,80,128]{2,1,0:T(8,128)(2,1)S(1)} %get-tuple-element.21), channel_id=1, source_target_pairs={{0,1},{1,0},{2,3},{3,2},{4,5},{5,4},{6,7},{7,6},{8,9},{9,8},{10,11... | collective-permute-start | bytes 245768 | tf_op jit(solution)/shard_map/ppermute | solution.py:246
  11.4 5.2 %collective-permute-start.4 = (bf16[4,80,128]{2,1,0:T(8,128)(2,1)S(1)}, bf16[4,80,128]{2,1,0:T(8,128)(2,1)S(1)}, u32[]{:S(2)}, u32[]{:S(2)}) collective-permute-start(bf16[4,80,128]{2,1,0:T(8,128)(2,1)S(1)} %get-tuple-element.22), channel_id=1, source_target_pairs={{0,2},{1,3},{2,0},{3,1},{4,6},{5,7},{6,4},{7,5},{8,10},{9,11},{10,... | collective-permute-start | bytes 245768 | tf_op jit(solution)/shard_map/ppermute | solution.py:246
  13.0 4.7 %collective-permute-start.5 = (bf16[4,80,128]{2,1,0:T(8,128)(2,1)S(1)}, bf16[4,80,128]{2,1,0:T(8,128)(2,1)S(1)}, u32[]{:S(2)}, u32[]{:S(2)}) collective-permute-start(bf16[4,80,128]{2,1,0:T(8,128)(2,1)S(1)} %get-tuple-element.23), channel_id=1, source_target_pairs={{0,3},{1,2},{2,1},{3,0},{4,7},{5,6},{6,5},{7,4},{8,11},{9,10},{10,... | collective-permute-start | bytes 245768 | tf_op jit(solution)/shard_map/ppermute | solution.py:246
  17.8 5.6 %collective-permute-start.6 = (f32[40,128]{1,0:T(8,128)S(1)}, f32[40,128]{1,0:T(8,128)S(1)}, u32[]{:S(2)}, u32[]{:S(2)}) collective-permute-start(f32[40,128]{1,0:T(8,128)S(1)} %get-tuple-element.25), channel_id=1, source_target_pairs={{0,4},{1,5},{2,6},{3,7},{4,0},{5,1},{6,2},{7,3},{8,12},{9,13},{10,... | collective-permute-start | bytes 61448 | tf_op jit(solution)/shard_map/ppermute | solution.py:246
  18.7 4.7 %collective-permute-start.7 = (f32[40,128]{1,0:T(8,128)S(1)}, f32[40,128]{1,0:T(8,128)S(1)}, u32[]{:S(2)}, u32[]{:S(2)}) collective-permute-start(f32[40,128]{1,0:T(8,128)S(1)} %get-tuple-element.26), channel_id=1, source_target_pairs={{0,8},{1,9},{2,10},{3,11},{4,12},{5,13},{6,14},{7,15},{8,0},{9,1},... | collective-permute-start | bytes 61448 | tf_op jit(solution)/shard_map/ppermute | solution.py:246
  21.6 5.6 %collective-permute-start.8 = (f32[40,128]{1,0:T(8,128)S(1)}, f32[40,128]{1,0:T(8,128)S(1)}, u32[]{:S(2)}, u32[]{:S(2)}) collective-permute-start(f32[40,128]{1,0:T(8,128)S(1)} %get-tuple-element.27), channel_id=1, source_target_pairs={{0,12},{1,13},{2,14},{3,15},{4,8},{5,9},{6,10},{7,11},{8,4},{9,5},... | collective-permute-start | bytes 61448 | tf_op jit(solution)/shard_map/ppermute | solution.py:246
  22.2 5.0 %copy-start = (f32[40,128]{1,0:T(8,128)S(1)}, f32[40,128]{1,0:T(8,128)}, u32[]{:S(2)}) copy-start(f32[40,128]{1,0:T(8,128)} %refs_4_.1) | copy-start | bytes 61444

commit v5 on v4

--- a/solution.py
+++ b/solution.py
@@ -56,7 +56,9 @@
     integral = spread_paths(start_ref[...], dates) + step_years * sums_to_date(rates_ref[...], dates)
     discount = jnp.exp(-integral)
     discount_ref[...] = discount
-    carried_ref[...] = (fx_ref[...] * discount).astype(jnp.bfloat16)
+    carried = (fx_ref[...] * discount).astype(jnp.bfloat16)
+    for peer in range(carried_ref.shape[0]):
+        carried_ref[peer] = carried
 
 
 def local_kernel(
@@ -156,49 +158,21 @@
             pl.loop(0, width // group_width)(some_columns)
 
 
-def packing_kernel(planes, near, *refs):
-    carried_refs, terms_ref = refs[:planes], refs[planes]
-    out_refs = refs[planes + 1 :]
-    currency_count = terms_ref.shape[1]
-    mine = lax.axis_index("sets") % near
-    for offset, out_ref in enumerate(out_refs):
-        for plane in range(planes):
-            out_ref[plane, currency_count:, :] = terms_ref[plane * near + (mine ^ offset)]
-            if offset:
-                out_ref[plane, 0:currency_count, :] = carried_refs[plane][...]
-
-
-def plane_kernel(planes, near, *refs):
-    in_refs, out_refs, summed = refs[:near], refs[near:-1], refs[-1]
-    currency_count = summed.shape[1]
-    for plane in range(planes):
-        total = in_refs[0][plane, currency_count:, :].astype(jnp.float32)
-        for ref in in_refs[1:]:
-            total = total + ref[plane, currency_count:, :].astype(jnp.float32)
-        summed[plane] = total
-    mine = lax.axis_index("sets") // near
-    for offset, out_ref in enumerate(out_refs):
-        out_ref[...] = summed[mine ^ offset]
-
-
-def projection_kernel(planes, near, *refs):
-    carried_refs, stacked_refs = refs[:planes], refs[planes : planes + near - 1]
-    masked, used_ref, notional_adjoint_ref, carried = refs[planes + near - 1 :]
+def projection_kernel(carried_ref, masked, used_ref, notional_adjoint_ref):
     sets, columns = masked.shape
-    currency_count, owned = carried_refs[0].shape
-    me = lax.axis_index("sets")
-    for offset in range(near):
-        for plane in range(planes):
-            block = (
-                stacked_refs[offset - 1][plane, 0:currency_count, :]
-                if offset
-                else carried_refs[plane][...]
-            )
-            source = me ^ (plane * near + offset)
-            carried[:, pl.ds(pl.multiple_of(source * owned, owned), owned)] = block
-    projected = lax.dot_general(
-        masked[...], carried[...], (((1,), (1,)), ((), ())), preferred_element_type=jnp.float32
-    ).T
+    blocks, currency_count, owned = carried_ref.shape
+    width = columns // chunks
+    projected = jnp.zeros((sets, currency_count), jnp.float32)
+    for index in range(chunks):
+        here = width // owned
+        carried = jnp.concatenate([carried_ref[index * here + b] for b in range(here)], axis=1)
+        projected = projected + lax.dot_general(
+            masked[:, index * width : (index + 1) * width],
+            carried,
+            (((1,), (1,)), ((), ())),
+            preferred_element_type=jnp.float32,
+        )
+    projected = projected.T
     used = used_ref[...]
     currency = lax.broadcasted_iota(jnp.int32, (currency_count, sets), 0)
     for slot in range(used.shape[0]):
@@ -208,11 +182,10 @@
         notional_adjoint_ref[slot : slot + 1, :] = picked * (1.0 / math.sqrt(columns))
 
 
-def final_kernel(dates, planes, *refs):
-    part_refs, (fx_ref, discount_ref, fx_adjoint_ref, rate_adjoint_ref) = refs[:planes], refs[planes:]
-    aggregate = part_refs[0][...]
-    for ref in part_refs[1:]:
-        aggregate = aggregate + ref[...]
+def final_kernel(dates, parts_ref, fx_ref, discount_ref, fx_adjoint_ref, rate_adjoint_ref):
+    aggregate = parts_ref[0].astype(jnp.float32)
+    for peer in range(1, parts_ref.shape[0]):
+        aggregate = aggregate + parts_ref[peer].astype(jnp.float32)
     fx_adjoint = aggregate * discount_ref[...]
     fx_adjoint_ref[...] = fx_adjoint
     rate_adjoint_ref[...] = -step_years * sums_from_date(fx_adjoint * fx_ref[...], dates)
@@ -233,8 +206,6 @@
     dates = owned // start_integral.shape[1]
     peers = columns // owned
     slots = currencies.shape[1]
-    near = 2 ** ((peers.bit_length() - 1) // 2)
-    planes = peers // near
     in_vmem = pl.BlockSpec(memory_space=pltpu.VMEM)
     anywhere = pl.BlockSpec(memory_space=pl.ANY)
     params = pltpu.CompilerParams(vmem_limit_bytes=32 * 2**20)
@@ -242,19 +213,19 @@
     def in_hbm(value):
         return pltpu.with_memory_space_constraint(value, pltpu.HBM)
 
-    def exchange(value, offset):
-        return lax.ppermute(value, "sets", [(peer, peer ^ offset) for peer in range(peers)])
-
     block = (currency_count, owned)
     carried, discount = pl.pallas_call(
         functools.partial(carry_kernel, dates),
-        out_shape=(pltpu.VMEM(block, jnp.bfloat16), pltpu.VMEM(block, jnp.float32)),
+        out_shape=(
+            pltpu.VMEM((peers,) + block, jnp.bfloat16),
+            pltpu.VMEM(block, jnp.float32),
+        ),
         in_specs=[in_vmem] * 3,
         out_specs=(in_vmem,) * 2,
         compiler_params=params,
         name="carry",
     )(in_hbm(fx_paths), in_hbm(short_rates), in_hbm(start_integral.T))
-    along = [carried] + [exchange(carried, near * offset) for offset in range(1, planes)]
+    carried = lax.all_to_all(carried, "sets", 0, 0, tiled=True)
     masked, terms, used = pl.pallas_call(
         local_kernel,
         out_shape=(
@@ -279,42 +250,23 @@
         in_hbm(mix_count.reshape(1, sets)),
         in_hbm(notional.T),
     )
-    outgoing = pl.pallas_call(
-        functools.partial(packing_kernel, planes, near),
-        out_shape=(pltpu.VMEM((planes, 2 * currency_count, owned), jnp.bfloat16),) * near,
-        in_specs=[in_vmem] * (planes + 1),
-        out_specs=(in_vmem,) * near,
-        compiler_params=params,
-        name="packing",
-    )(*along, terms)
-    arrived = [exchange(outgoing[offset], offset) for offset in range(1, near)]
-    summed = pl.pallas_call(
-        functools.partial(plane_kernel, planes, near),
-        out_shape=(pltpu.VMEM(block, jnp.float32),) * planes,
-        in_specs=[in_vmem] * near,
-        out_specs=(in_vmem,) * planes,
-        scratch_shapes=[pltpu.VMEM((planes,) + block, jnp.float32)],
-        compiler_params=params,
-        name="plane",
-    )(outgoing[0], *arrived)
-    parts = [summed[0]] + [exchange(summed[offset], near * offset) for offset in range(1, planes)]
+    parts = lax.all_to_all(terms, "sets", 0, 0, tiled=True)
     notional_adjoint = pl.pallas_call(
-        functools.partial(projection_kernel, planes, near),
+        projection_kernel,
         out_shape=jax.ShapeDtypeStruct((slots, sets), jnp.float32),
-        in_specs=[in_vmem] * (planes + near + 1),
+        in_specs=[in_vmem] * 3,
         out_specs=in_vmem,
-        scratch_shapes=[pltpu.VMEM((currency_count, columns), jnp.bfloat16)],
         compiler_params=params,
         name="projection",
-    )(*along, *arrived, masked, used)
+    )(carried, masked, used)
     fx_adjoint, rate_adjoint = pl.pallas_call(
-        functools.partial(final_kernel, dates, planes),
+        functools.partial(final_kernel, dates),
         out_shape=(jax.ShapeDtypeStruct(block, jnp.float32),) * 2,
-        in_specs=[in_vmem] * (planes + 2),
+        in_specs=[in_vmem] * 3,
         out_specs=(in_vmem,) * 2,
         compiler_params=params,
         name="final",
-    )(*parts, fx_paths, discount)
+    )(parts, fx_paths, discount)
     return fx_adjoint, rate_adjoint, notional_adjoint.T
 
 

time: 28.3 us -> 34.1 us (1.20)
  waiting for transfers between devices: 8.84 us -> 14.3 us
  Pallas kernels: 6.38 us -> 7.62 us
  starting transfers between devices: 12.1 us -> 11 us
    all_to_all x0 -> x2, waiting for transfers between devices: none -> 14.3 us  [the longest x1 7.57 us: body(): carried = lax.all_to_all(carried, 'sets', 0, 0, tiled=True)]
    ppermute x9 -> x0, starting transfers between devices: 12.1 us -> none  [exchange(): lax.ppermute(value, 'sets', [(peer, peer ^ offset) for peer in range(peer...]
    all_to_all x0 -> x2, starting transfers between devices: none -> 11 us  [the longest x1 7.37 us: body(): parts = lax.all_to_all(terms, 'sets', 0, 0, tiled=True)]
    ppermute x9 -> x0, waiting for transfers between devices: 8.84 us -> none  [exchange(): lax.ppermute(value, 'sets', [(peer, peer ^ offset) for peer in range(peer...]
    pallas_call x1, Pallas kernels: 1 us -> 1.69 us  [body(): pl.pallas_call(functools.partial(carry_kernel, dates), out_shape=(pltpu.V...]
    pallas_call x1, Pallas kernels: 3.39 us -> 4.04 us  [body(): pl.pallas_call(local_kernel, out_shape=(pltpu.VMEM((sets, columns), jnp.b...]
    pallas_call x4 -> x2, Pallas kernels: 1.99 us -> 1.89 us  [the longest x1 1.04 us: body(): pl.pallas_call(projection_kernel, out_shape=jax.ShapeDtypeStruct((slots,...]
  transfers between devices with their start and end apart: 9 -> 2, of which waited for: 5 -> 2; matrix products, arithmetic and copies ran while one was open for 0% -> 0% of each run, Pallas kernels for 16% -> 8%
where the time goes in v5:
time: 34.1 us; the launch traced here: 33.6 us
  waiting for transfers between devices  14.3 us (42%)
  starting transfers between devices  11 us (32%)
  Pallas kernels  7.62 us (22%)
  between operations  0.67 us (2%)
    all_to_all x1, waiting for transfers between devices, body(): carried = lax.all_to_all(carried, 'sets', 0, 0, tiled=True)  7.57 us
    all_to_all x1, starting transfers between devices, body(): parts = lax.all_to_all(terms, 'sets', 0, 0, tiled=True)  7.37 us
    all_to_all x1, waiting for transfers between devices, body(): parts = lax.all_to_all(terms, 'sets', 0, 0, tiled=True)  6.77 us
    pallas_call x1, Pallas kernels, body(): pl.pallas_call(local_kernel, out_shape=(pltpu.VMEM((sets, columns), jnp.b...  4.04 us
    all_to_all x1, starting transfers between devices, body(): carried = lax.all_to_all(carried, 'sets', 0, 0, tiled=True)  3.65 us
    pallas_call x1, Pallas kernels, body(): pl.pallas_call(functools.partial(carry_kernel, dates), out_shape=(pltpu.V...  1.69 us
    pallas_call x1, Pallas kernels, body(): pl.pallas_call(projection_kernel, out_shape=jax.ShapeDtypeStruct((slots,...  1.04 us
    pallas_call x1, Pallas kernels, body(): pl.pallas_call(functools.partial(final_kernel, dates), out_shape=(jax.Sha...  0.85 us
  transfers between devices with their start and end apart: 2, of which 2 were waited for; matrix products, arithmetic and copies ran while one was open for 0% of the time, Pallas kernels for 8%

profile of v5, /device:TPU:0, one launch (start us, length us, event | category | flops | bytes accessed | tf_op | source)
XLA Modules:
  0.0 33.6 jit_solution(15111960464606272204)
XLA Ops:
  0.6 4.0 %local.1 = (bf16[240,2048]{1,0:T(8,128)(2,1)S(1)}, bf16[16,40,128]{2,1,0:T(8,128)(2,1)}, s32[4,240]{1,0:T(4,128)S(1)}) custom-call(bf16[240,2048]{1,0:T(8,128)(2,1)} %exposure_hbm.1, s32[16,2048]{1,0:T(8,128)} %bits_hbm.1, s32[4,240]{1,0:T(4,128)} %bitcast.6, s32[1,240]{1,0:T(1,128)} %bitcast.9, f32[4,240]{1,0:T(4,128)} %bitcast.7), custom_call_target="tpu_custom_call" | custom-call | tf_op jit(solution)/shard_map/local/pallas_call | solution.py:229
  4.7 7.4 %all-to-all-start = ((bf16[16,40,128]{2,1,0:T(8,128)(2,1)}), bf16[16,40,128]{2,1,0:T(8,128)(2,1)S(1)}, u32[]{:S(2)}, u32[]{:S(2)}) async-start(bf16[16,40,128]{2,1,0:T(8,128)(2,1)} %get-tuple-element.10), calls=%async_computation | async-start | bytes 327680 | tf_op jit(solution)/shard_map/all_to_all | solution.py:253
  12.1 1.7 %carry.1 = (bf16[16,40,128]{2,1,0:T(8,128)(2,1)}, f32[40,128]{1,0:T(8,128)S(1)}) custom-call(f32[40,128]{1,0:T(8,128)} %fx_ref.3, f32[40,128]{1,0:T(8,128)} %rates_ref.1, f32[16,40]{1,0:T(8,128)} %bitcast.5), custom_call_target="tpu_custom_call" | custom-call | tf_op jit(solution)/shard_map/carry/pallas_call | solution.py:217
  13.7 6.8 %all-to-all-done.parts_ref = bf16[16,40,128]{2,1,0:T(8,128)(2,1)S(1)} async-done(((bf16[16,40,128]{2,1,0:T(8,128)(2,1)}), bf16[16,40,128]{2,1,0:T(8,128)(2,1)S(1)}, u32[]{:S(2)}, u32[]{:S(2)}) %all-to-all-start) | async-done | bytes 163872 | tf_op jit(solution)/shard_map/all_to_all | solution.py:253
  20.5 0.0 copy-start
  20.5 3.6 %all-to-all-start.1 = ((bf16[16,40,128]{2,1,0:T(8,128)(2,1)}), bf16[16,40,128]{2,1,0:T(8,128)(2,1)S(1)}, u32[]{:S(2)}, u32[]{:S(2)}) async-start(bf16[16,40,128]{2,1,0:T(8,128)(2,1)} %get-tuple-element.14), calls=%async_computation.1 | async-start | bytes 327680 | tf_op jit(solution)/shard_map/all_to_all | solution.py:228
  24.2 0.0 copy-done
  24.2 0.8 %final.1 = (f32[40,128]{1,0:T(8,128)}, f32[40,128]{1,0:T(8,128)}) custom-call(bf16[16,40,128]{2,1,0:T(8,128)(2,1)S(1)} %all-to-all-done.parts_ref, f32[40,128]{1,0:T(8,128)S(1)} %copy-done, f32[40,128]{1,0:T(8,128)S(1)} %get-tuple-element.11.discount_ref), custom_call_target="tpu_custom_call" | custom-call | tf_op jit(solution)/shard_map/final/pallas_call | solution.py:262
  25.0 7.6 %all-to-all-done.1.carried_ref = bf16[16,40,128]{2,1,0:T(8,128)(2,1)S(1)} async-done(((bf16[16,40,128]{2,1,0:T(8,128)(2,1)}), bf16[16,40,128]{2,1,0:T(8,128)(2,1)S(1)}, u32[]{:S(2)}, u32[]{:S(2)}) %all-to-all-start.1) | async-done | bytes 163872 | tf_op jit(solution)/shard_map/all_to_all | solution.py:228
  32.6 1.0 %projection.1 = f32[4,240]{1,0:T(4,128)} custom-call(bf16[16,40,128]{2,1,0:T(8,128)(2,1)S(1)} %all-to-all-done.1.carried_ref, bf16[240,2048]{1,0:T(8,128)(2,1)S(1)} %get-tuple-element.15.masked, s32[4,240]{1,0:T(4,128)S(1)} %get-tuple-element.16.used_ref), custom_call_target="tpu_custom_call" | custom-call | tf_op jit(solution)/shard_map/projection/pallas_call | solution.py:254
Async XLA Ops:
  4.7 15.8 %all-to-all-start = ((bf16[16,40,128]{2,1,0:T(8,128)(2,1)}), bf16[16,40,128]{2,1,0:T(8,128)(2,1)S(1)}, u32[]{:S(2)}, u32[]{:S(2)}) async-start(bf16[16,40,128]{2,1,0:T(8,128)(2,1)} %get-tuple-element.10), calls=%async_computation | async-start | bytes 327680 | tf_op jit(solution)/shard_map/all_to_all | solution.py:253
  20.5 3.7 %copy-start = (f32[40,128]{1,0:T(8,128)S(1)}, f32[40,128]{1,0:T(8,128)}, u32[]{:S(2)}) copy-start(f32[40,128]{1,0:T(8,128)} %fx_ref.3) | copy-start | bytes 61444
  20.5 12.1 %all-to-all-start.1 = ((bf16[16,40,128]{2,1,0:T(8,128)(2,1)}), bf16[16,40,128]{2,1,0:T(8,128)(2,1)S(1)}, u32[]{:S(2)}, u32[]{:S(2)}) async-start(bf16[16,40,128]{2,1,0:T(8,128)(2,1)} %get-tuple-element.14), calls=%async_computation.1 | async-start | bytes 327680 | tf_op jit(solution)/shard_map/all_to_all | solution.py:228

commit v6 on v3

v6 whole, which is shorter than its diff:
```python
import functools
import math

import jax
import jax.numpy as jnp
from jax import lax
from jax.experimental import pallas as pl
from jax.experimental.pallas import tpu as pltpu
from jax.sharding import PartitionSpec as P

step_years = 0.25
bits_per_row = 15
lanes = 128
chunks = 2


def spread_paths(values, dates):
    paths, columns = values.shape[0], values.shape[0] * dates
    path_of = lax.broadcasted_iota(jnp.int32, (paths, columns), 1) // dates
    own = lax.broadcasted_iota(jnp.int32, (paths, columns), 0)
    return lax.dot_general(
        values,
        (path_of == own).astype(jnp.float32),
        (((0,), (0,)), ((), ())),
        precision=lax.Precision.HIGHEST,
        preferred_element_type=jnp.float32,
    )


def sums_to_date(values, dates):
    width = values.shape[1]
    date = lax.broadcasted_iota(jnp.int32, values.shape, 1) % dates
    step = 1
    while step < dates:
        values = values + jnp.where(date >= step, pltpu.roll(values, step, 1), 0.0)
        step *= 2
    return values


def sums_from_date(values, dates):
    width = values.shape[1]
    date = lax.broadcasted_iota(jnp.int32, values.shape, 1) % dates
    step = 1
    while step < dates:
        values = values + jnp.where(date < dates - step, pltpu.roll(values, width - step, 1), 0.0)
        step *= 2
    return values


def used_currencies(currencies, counts):
    slot = lax.broadcasted_iota(jnp.int32, currencies.shape, 0)
    return jnp.where(slot < counts, currencies, -1)


def group_order(peers):
    first = max(peers - 2, 0)
    return [peer ^ first for peer in range(peers)]


def local_kernel(
    dates,
    exposure_hbm,
    bits_hbm,
    currencies_ref,
    counts_ref,
    notional_ref,
    fx_ref,
    rates_ref,
    start_ref,
    outgoing_ref,
    masked_ref,
    discount_ref,
    moved_ref,
    used_ref,
    exposure,
    bits,
    in_sems,
    bits_sems,
):
    sets, columns = exposure.shape
    currency_count, owned = fx_ref.shape
    peers = columns // owned
    width = columns // chunks
    place = group_order(peers)

    def exposure_copy(index):
        part = pl.ds(index * width, width)
        return pltpu.make_async_copy(
            exposure_hbm.at[:, part], exposure.at[:, part], in_sems.at[index]
        )

    def bits_copy(index):
        part = pl.ds(index * width, width)
        return pltpu.make_async_copy(bits_hbm.at[:, part], bits.at[:, part], bits_sems.at[index])

    for index in range(chunks):
        bits_copy(index).start()
        exposure_copy(index).start()

    used = used_currencies(currencies_ref[...], counts_ref[...])
    used_ref[...] = used
    notional = notional_ref[...]
    currency = lax.broadcasted_iota(jnp.int32, (currency_count, sets), 0)
    weights = jnp.zeros((currency_count, sets), jnp.float32)
    for slot in range(used.shape[0]):
        weights = weights + jnp.where(
            currency == used[slot : slot + 1], notional[slot : slot + 1], 0.0
        )
    weights = weights.astype(jnp.bfloat16)

    integral = spread_paths(start_ref[...], dates) + step_years * sums_to_date(rates_ref[...], dates)
    discount = jnp.exp(-integral)
    discount_ref[...] = discount
    moved = fx_ref[...] * discount
    moved_ref[...] = moved
    carried = moved.astype(jnp.bfloat16)
    for peer in range(peers):
        outgoing_ref[peer, 0:currency_count, :] = carried

    row = lax.broadcasted_iota(jnp.int32, (8, lanes), 0)

    def flag_of(tile):
        shift = row + (8 * tile) % bits_per_row
        shift = jnp.where(shift >= bits_per_row, shift - bits_per_row, shift)
        return jnp.left_shift(jnp.int32(1), shift)

    def masked_rows(pair, flags, part):
        values = exposure[16 * pair : 16 * pair + 16, part].astype(jnp.float32)
        kept = []
        for half in range(2):
            top = 16 * pair + 8 * half
            group = top // bits_per_row
            left = bits_per_row * (group + 1) - top
            packed = jnp.broadcast_to(bits[group : group + 1, part], (8, lanes))
            if left < 8:
                following = jnp.broadcast_to(bits[group + 1 : group + 2, part], (8, lanes))
                packed = jnp.where(row < left, packed, following)
            kept.append(
                jnp.where((packed & flags[half]) != 0, values[8 * half : 8 * half + 8], 0.0)
            )
        return jnp.concatenate(kept, axis=0).astype(jnp.bfloat16)

    group_width = min(width, 1024)
    dot_width = min(group_width, 256)

    for index in range(chunks):
        bits_copy(index).wait()
        exposure_copy(index).wait()

        def some_columns(step):
            first = index * width + step * group_width
            if not isinstance(first, int):
                first = pl.multiple_of(first, group_width)
            for pair in range(sets // 16):
                flags = [flag_of(2 * pair), flag_of(2 * pair + 1)]
                for block in range(group_width // lanes):
                    part = pl.ds(first + block * lanes, lanes)
                    masked_ref[16 * pair : 16 * pair + 16, part] = masked_rows(pair, flags, part)
            for dot in range(group_width // dot_width):
                terms = jnp.dot(
                    weights,
                    masked_ref[:, pl.ds(first + dot * dot_width, dot_width)],
                    preferred_element_type=jnp.float32,
                ).astype(jnp.bfloat16)
                for block in range(dot_width // owned):
                    peer = (first + dot * dot_width) // owned + block
                    where = place[peer] if isinstance(peer, int) else peer ^ place[0]
                    outgoing_ref[where, currency_count:, :] = terms[
                        :, block * owned : (block + 1) * owned
                    ]

        if width == group_width:
            some_columns(0)
        else:
            pl.loop(0, width // group_width)(some_columns)


def final_kernel(
    dates,
    arrived_ref,
    masked,
    used_ref,
    moved_ref,
    discount_ref,
    fx_adjoint_ref,
    rate_adjoint_ref,
    notional_adjoint_ref,
):
    sets, columns = masked.shape
    currency_count, owned = moved_ref.shape
    peers = columns // owned
    place = group_order(peers)

    aggregate = arrived_ref[0, currency_count:, :].astype(jnp.float32)
    for peer in range(1, peers):
        aggregate = aggregate + arrived_ref[peer, currency_count:, :].astype(jnp.float32)
    fx_adjoint_ref[...] = aggregate * discount_ref[...]
    rate_adjoint_ref[...] = -step_years * sums_from_date(aggregate * moved_ref[...], dates)

    width = min(columns, 2048)
    projected = jnp.zeros((sets, currency_count), jnp.float32)
    for index in range(columns // width):
        here = width // owned
        carried = jnp.concatenate(
            [
                arrived_ref[place[index * here + block], 0:currency_count, :]
                for block in range(here)
            ],
            axis=1,
        )
        projected = projected + lax.dot_general(
            masked[:, index * width : (index + 1) * width],
            carried,
            (((1,), (1,)), ((), ())),
            preferred_element_type=jnp.float32,
        )
    projected = projected.T
    used = used_ref[...]
    currency = lax.broadcasted_iota(jnp.int32, (currency_count, sets), 0)
    for slot in range(used.shape[0]):
        picked = jnp.sum(
            jnp.where(currency == used[slot : slot + 1], projected, 0.0), axis=0, keepdims=True
        )
        notional_adjoint_ref[slot : slot + 1, :] = picked * (1.0 / math.sqrt(columns))


def body(
    exposure_adjoint,
    positive_bits,
    currencies,
    mix_count,
    notional,
    fx_paths,
    short_rates,
    start_integral,
):
    sets, columns = exposure_adjoint.shape
    currency_count, owned = fx_paths.shape
    dates = owned // start_integral.shape[1]
    peers = columns // owned
    slots = currencies.shape[1]
    in_vmem = pl.BlockSpec(memory_space=pltpu.VMEM)
    anywhere = pl.BlockSpec(memory_space=pl.ANY)
    params = pltpu.CompilerParams(vmem_limit_bytes=32 * 2**20)
    block = (currency_count, owned)

    def in_hbm(value):
        return pltpu.with_memory_space_constraint(value, pltpu.HBM)

    outgoing, masked, discount, moved, used = pl.pallas_call(
        functools.partial(local_kernel, dates),
        out_shape=(
            pltpu.VMEM((peers, 2 * currency_count, owned), jnp.bfloat16),
            pltpu.VMEM((sets, columns), jnp.bfloat16),
            pltpu.VMEM(block, jnp.float32),
            pltpu.VMEM(block, jnp.float32),
            pltpu.VMEM((slots, sets), jnp.int32),
        ),
        in_specs=[anywhere] * 2 + [in_vmem] * 6,
        out_specs=(in_vmem,) * 5,
        scratch_shapes=[
            pltpu.VMEM((sets, columns), jnp.bfloat16),
            pltpu.VMEM(positive_bits.shape, jnp.int32),
            pltpu.SemaphoreType.DMA((chunks,)),
            pltpu.SemaphoreType.DMA((chunks,)),
        ],
        compiler_params=params,
        name="local",
    )(
        in_hbm(exposure_adjoint),
        in_hbm(positive_bits),
        in_hbm(currencies.T),
        in_hbm(mix_count.reshape(1, sets)),
        in_hbm(notional.T),
        in_hbm(fx_paths),
        in_hbm(short_rates),
        in_hbm(start_integral.T),
    )
    arrived = lax.all_to_all(
        outgoing, "sets", 0, 0, axis_index_groups=[group_order(peers)], tiled=True
    )
    fx_adjoint, rate_adjoint, notional_adjoint = pl.pallas_call(
        functools.partial(final_kernel, dates),
        out_shape=(
            jax.ShapeDtypeStruct(block, jnp.float32),
            jax.ShapeDtypeStruct(block, jnp.float32),
            jax.ShapeDtypeStruct((slots, sets), jnp.float32),
        ),
        in_specs=[in_vmem] * 5,
        out_specs=(in_vmem,) * 3,
        compiler_params=params,
        name="final",
    )(arrived, masked, used, moved, discount)
    return fx_adjoint, rate_adjoint, notional_adjoint.T


def solution(mesh):
    in_specs = (
        P(("grp", "sets"), None),
        P(("grp", "sets"), None),
        P(("grp", "sets"), None),
        P(("grp", "sets")),
        P(("grp", "sets"), None),
        P("grp", "sets"),
        P("grp", "sets"),
        P("grp", "sets"),
    )
    out_specs = (P("grp", "sets"), P("grp", "sets"), P(("grp", "sets"), None))
    return jax.shard_map(body, mesh=mesh, in_specs=in_specs, out_specs=out_specs, check_vma=False)
```

time: 24.4 us -> 21.5 us (0.88)
  blocking collectives: 18.3 us -> 16.8 us
  Pallas kernels: 4.52 us -> 3.76 us
  local copies, waits for them, and re-layouts: 0.69 us -> 0 us
    all_to_all x1, blocking collectives: 18.3 us -> 16.8 us  [body(): lax.all_to_all(outgoing, 'sets', 0, 0, axis_index_groups=[group_order(pee...]
    pallas_call x1, Pallas kernels: 3.47 us -> 2.71 us  [body(): pl.pallas_call(functools.partial(local_kernel, dates), out_shape=(pltpu.V...]
    unnamed x6 -> x0, local copies, waits for them, and re-layouts: 0.69 us -> none
where the time goes in v6:
time: 21.5 us; the launch traced here: 21.2 us
  blocking collectives  16.8 us (78%)
  Pallas kernels  3.76 us (17%)
  between operations  0.64 us (3%)
    all_to_all x1, blocking collectives, body(): lax.all_to_all(outgoing, 'sets', 0, 0, axis_index_groups=[group_order(pee...  16.8 us
    pallas_call x1, Pallas kernels, body(): pl.pallas_call(functools.partial(local_kernel, dates), out_shape=(pltpu.V...  2.71 us
    pallas_call x1, Pallas kernels, body(): pl.pallas_call(functools.partial(final_kernel, dates), out_shape=(jax.Sha...  1.05 us

profile of v6, /device:TPU:0, one launch (start us, length us, event | category | flops | bytes accessed | tf_op | source)
XLA Modules:
  0.0 21.2 jit_solution(9225280932093121152)
XLA Ops:
  0.6 2.7 %local.1 = (bf16[16,80,128]{2,1,0:T(8,128)(2,1)S(1)}, bf16[240,2048]{1,0:T(8,128)(2,1)S(1)}, f32[40,128]{1,0:T(8,128)S(1)}, f32[40,128]{1,0:T(8,128)S(1)}, s32[4,240]{1,0:T(4,128)S(1)}) custom-call(bf16[240,2048]{1,0:T(8,128)(2,1)} %exposure_hbm.1, s32[16,2048]{1,0:T(8,128)} %bits_hbm.1, s32[4,240]{1,0:T(4,128)} %bitcast.6, s32[1,240]{1,0:T(1,128)} %bitcast.8, ...), custom_call_target="tpu_custom_call" | custom-call | tf_op jit(solution)/shard_map/local/pallas_call | solution.py:250
  3.3 16.8 %all_to_all.5.arrived_ref = bf16[16,80,128]{2,1,0:T(8,128)(2,1)S(1)} all-to-all(bf16[16,80,128]{2,1,0:T(8,128)(2,1)S(1)} %get-tuple-element.11), channel_id=1, replica_groups={{14,15,12,13,10,11,8,9,6,7,4,5,2,3,0,1},{30,31,28,29,26,27,24,25,22,23,..., dimensions={0} | all-to-all | bytes 655360 | tf_op jit(solution)/shard_map/all_to_all | solution.py:279
  20.2 1.1 %final.1 = (f32[40,128]{1,0:T(8,128)}, f32[40,128]{1,0:T(8,128)}, f32[4,240]{1,0:T(4,128)}) custom-call(bf16[16,80,128]{2,1,0:T(8,128)(2,1)S(1)} %all_to_all.5.arrived_ref, bf16[240,2048]{1,0:T(8,128)(2,1)S(1)} %get-tuple-element.12.masked, s32[4,240]{1,0:T(4,128)S(1)} %get-tuple-element.13.used_ref, f32[40,128]{1,0:T(8,128)S(1)} %get-tuple-element.14.moved_ref, ...), custom_call_target="tpu_custom_call" | custom-call | tf_op jit(solution)/shard_map/final/pallas_call | solution.py:282

commit v7 on v6

--- a/solution.py
+++ b/solution.py
@@ -53,20 +53,25 @@
 
 
 def group_order(peers):
-    first = max(peers - 2, 0)
-    return [peer ^ first for peer in range(peers)]
+    near = min(4, peers)
+    far = peers // near
+    planes = []
+    for step in range((far + 1) // 2):
+        planes += [far - 1 - step, step]
+    planes = planes[:far]
+    return [plane * near + (index ^ (near // 2)) for index in range(near) for plane in planes]
 
 
 def local_kernel(
     dates,
     exposure_hbm,
     bits_hbm,
-    currencies_ref,
-    counts_ref,
-    notional_ref,
-    fx_ref,
-    rates_ref,
-    start_ref,
+    currencies_hbm,
+    counts_hbm,
+    notional_hbm,
+    fx_hbm,
+    rates_hbm,
+    start_hbm,
     outgoing_ref,
     masked_ref,
     discount_ref,
@@ -74,14 +79,22 @@
     used_ref,
     exposure,
     bits,
+    currencies_ref,
+    counts_ref,
+    notional_ref,
+    fx_ref,
+    rates_ref,
+    start_ref,
     in_sems,
     bits_sems,
+    small_sems,
 ):
     sets, columns = exposure.shape
     currency_count, owned = fx_ref.shape
     peers = columns // owned
     width = columns // chunks
-    place = group_order(peers)
+    order = group_order(peers)
+    place = [order.index(peer) for peer in range(peers)]
 
     def exposure_copy(index):
         part = pl.ds(index * width, width)
@@ -93,9 +106,26 @@
         part = pl.ds(index * width, width)
         return pltpu.make_async_copy(bits_hbm.at[:, part], bits.at[:, part], bits_sems.at[index])
 
+    small_copies = [
+        pltpu.make_async_copy(source, target, small_sems.at[index])
+        for index, (source, target) in enumerate(
+            [
+                (rates_hbm, rates_ref),
+                (start_hbm, start_ref),
+                (fx_hbm, fx_ref),
+                (currencies_hbm, currencies_ref),
+                (counts_hbm, counts_ref),
+                (notional_hbm, notional_ref),
+            ]
+        )
+    ]
+    for copy in small_copies:
+        copy.start()
     for index in range(chunks):
         bits_copy(index).start()
         exposure_copy(index).start()
+    for copy in small_copies:
+        copy.wait()
 
     used = used_currencies(currencies_ref[...], counts_ref[...])
     used_ref[...] = used
@@ -147,10 +177,7 @@
         bits_copy(index).wait()
         exposure_copy(index).wait()
 
-        def some_columns(step):
-            first = index * width + step * group_width
-            if not isinstance(first, int):
-                first = pl.multiple_of(first, group_width)
+        for first in range(index * width, (index + 1) * width, group_width):
             for pair in range(sets // 16):
                 flags = [flag_of(2 * pair), flag_of(2 * pair + 1)]
                 for block in range(group_width // lanes):
@@ -164,15 +191,9 @@
                 ).astype(jnp.bfloat16)
                 for block in range(dot_width // owned):
                     peer = (first + dot * dot_width) // owned + block
-                    where = place[peer] if isinstance(peer, int) else peer ^ place[0]
-                    outgoing_ref[where, currency_count:, :] = terms[
+                    outgoing_ref[place[peer], currency_count:, :] = terms[
                         :, block * owned : (block + 1) * owned
                     ]
-
-        if width == group_width:
-            some_columns(0)
-        else:
-            pl.loop(0, width // group_width)(some_columns)
 
 
 def final_kernel(
@@ -189,7 +210,8 @@
     sets, columns = masked.shape
     currency_count, owned = moved_ref.shape
     peers = columns // owned
-    place = group_order(peers)
+    order = group_order(peers)
+    place = [order.index(peer) for peer in range(peers)]
 
     aggregate = arrived_ref[0, currency_count:, :].astype(jnp.float32)
     for peer in range(1, peers):
@@ -256,13 +278,20 @@
             pltpu.VMEM(block, jnp.float32),
             pltpu.VMEM((slots, sets), jnp.int32),
         ),
-        in_specs=[anywhere] * 2 + [in_vmem] * 6,
+        in_specs=[anywhere] * 8,
         out_specs=(in_vmem,) * 5,
         scratch_shapes=[
             pltpu.VMEM((sets, columns), jnp.bfloat16),
             pltpu.VMEM(positive_bits.shape, jnp.int32),
+            pltpu.VMEM((slots, sets), jnp.int32),
+            pltpu.VMEM((1, sets), jnp.int32),
+            pltpu.VMEM((slots, sets), jnp.float32),
+            pltpu.VMEM(block, jnp.float32),
+            pltpu.VMEM(block, jnp.float32),
+            pltpu.VMEM((owned // dates, currency_count), jnp.float32),
             pltpu.SemaphoreType.DMA((chunks,)),
             pltpu.SemaphoreType.DMA((chunks,)),
+            pltpu.SemaphoreType.DMA((6,)),
         ],
         compiler_params=params,
         name="local",

time: 21.5 us -> 21.2 us (0.986)
  Pallas kernels: 3.76 us -> 3.16 us
  blocking collectives: 16.8 us -> 17.3 us
    pallas_call x1, Pallas kernels: 2.71 us -> 2.11 us  [body(): pl.pallas_call(functools.partial(local_kernel, dates), out_shape=(pltpu.V...]
    all_to_all x1, blocking collectives: 16.8 us -> 17.3 us  [body(): lax.all_to_all(outgoing, 'sets', 0, 0, axis_index_groups=[group_order(pee...]
where the time goes in v7:
time: 21.2 us; the launch traced here: 21.1 us
  blocking collectives  17.3 us (82%)
  Pallas kernels  3.16 us (15%)
  between operations  0.64 us (3%)
    all_to_all x1, blocking collectives, body(): lax.all_to_all(outgoing, 'sets', 0, 0, axis_index_groups=[group_order(pee...  17.3 us
    pallas_call x1, Pallas kernels, body(): pl.pallas_call(functools.partial(local_kernel, dates), out_shape=(pltpu.V...  2.11 us
    pallas_call x1, Pallas kernels, body(): pl.pallas_call(functools.partial(final_kernel, dates), out_shape=(jax.Sha...  1.06 us

profile of v7, /device:TPU:0, one launch (start us, length us, event | category | flops | bytes accessed | tf_op | source)
XLA Modules:
  0.0 21.1 jit_solution(12038463101161326701)
XLA Ops:
  0.6 2.1 %local.1 = (bf16[16,80,128]{2,1,0:T(8,128)(2,1)S(1)}, bf16[240,2048]{1,0:T(8,128)(2,1)S(1)}, f32[40,128]{1,0:T(8,128)S(1)}, f32[40,128]{1,0:T(8,128)S(1)}, s32[4,240]{1,0:T(4,128)S(1)}) custom-call(bf16[240,2048]{1,0:T(8,128)(2,1)} %exposure_hbm.1, s32[16,2048]{1,0:T(8,128)} %bits_hbm.1, s32[4,240]{1,0:T(4,128)} %bitcast.6, s32[1,240]{1,0:T(1,128)} %bitcast.8, ...), custom_call_target="tpu_custom_call" | custom-call | tf_op jit(solution)/shard_map/local/pallas_call | solution.py:272
  2.7 17.3 %all_to_all.5.arrived_ref = bf16[16,80,128]{2,1,0:T(8,128)(2,1)S(1)} all-to-all(bf16[16,80,128]{2,1,0:T(8,128)(2,1)S(1)} %get-tuple-element.11), channel_id=1, replica_groups={{14,2,10,6,15,3,11,7,12,0,8,4,13,1,9,5},{30,18,26,22,31,19,27,23,28,16,..., dimensions={0} | all-to-all | bytes 655360 | tf_op jit(solution)/shard_map/all_to_all | solution.py:308
  20.0 1.1 %final.1 = (f32[40,128]{1,0:T(8,128)}, f32[40,128]{1,0:T(8,128)}, f32[4,240]{1,0:T(4,128)}) custom-call(bf16[16,80,128]{2,1,0:T(8,128)(2,1)S(1)} %all_to_all.5.arrived_ref, bf16[240,2048]{1,0:T(8,128)(2,1)S(1)} %get-tuple-element.12.masked, s32[4,240]{1,0:T(4,128)S(1)} %get-tuple-element.13.used_ref, f32[40,128]{1,0:T(8,128)S(1)} %get-tuple-element.14.moved_ref, ...), custom_call_target="tpu_custom_call" | custom-call | tf_op jit(solution)/shard_map/final/pallas_call | solution.py:311

commit v8 on v7

v8 whole, which is shorter than its diff:
```python
import functools
import math

import jax
import jax.numpy as jnp
from jax import lax
from jax.experimental import pallas as pl
from jax.experimental.pallas import tpu as pltpu
from jax.sharding import PartitionSpec as P

step_years = 0.25
bits_per_row = 15
lanes = 128
chunks = 2


def spread_paths(values, dates):
    paths, columns = values.shape[0], values.shape[0] * dates
    path_of = lax.broadcasted_iota(jnp.int32, (paths, columns), 1) // dates
    own = lax.broadcasted_iota(jnp.int32, (paths, columns), 0)
    return lax.dot_general(
        values,
        (path_of == own).astype(jnp.float32),
        (((0,), (0,)), ((), ())),
        precision=lax.Precision.HIGHEST,
        preferred_element_type=jnp.float32,
    )


def sums_to_date(values, dates):
    width = values.shape[1]
    date = lax.broadcasted_iota(jnp.int32, values.shape, 1) % dates
    step = 1
    while step < dates:
        values = values + jnp.where(date >= step, pltpu.roll(values, step, 1), 0.0)
        step *= 2
    return values


def sums_from_date(values, dates):
    width = values.shape[1]
    date = lax.broadcasted_iota(jnp.int32, values.shape, 1) % dates
    step = 1
    while step < dates:
        values = values + jnp.where(date < dates - step, pltpu.roll(values, width - step, 1), 0.0)
        step *= 2
    return values


def used_currencies(currencies, counts):
    slot = lax.broadcasted_iota(jnp.int32, currencies.shape, 0)
    return jnp.where(slot < counts, currencies, -1)


def group_order(chips):
    first = chips - 1
    return [chip ^ first for chip in range(chips)]


def sibling_columns(chip, owned, core):
    return pl.ds(pl.multiple_of((2 * chip + core) * owned, owned), owned)


def row_flags(tile):
    shift = lax.broadcasted_iota(jnp.int32, (8, lanes), 0) + (8 * tile) % bits_per_row
    shift = jnp.where(shift >= bits_per_row, shift - bits_per_row, shift)
    return jnp.left_shift(jnp.int32(1), shift)


def masked_rows(exposure, bits, pair, flags, part):
    row = lax.broadcasted_iota(jnp.int32, (8, lanes), 0)
    values = exposure[16 * pair : 16 * pair + 16, part].astype(jnp.float32)
    kept = []
    for half in range(2):
        top = 16 * pair + 8 * half
        group = top // bits_per_row
        left = bits_per_row * (group + 1) - top
        packed = jnp.broadcast_to(bits[group : group + 1, part], (8, lanes))
        if left < 8:
            following = jnp.broadcast_to(bits[group + 1 : group + 2, part], (8, lanes))
            packed = jnp.where(row < left, packed, following)
        kept.append(jnp.where((packed & flags[half]) != 0, values[8 * half : 8 * half + 8], 0.0))
    return jnp.concatenate(kept, axis=0).astype(jnp.bfloat16)


def half_of_columns(exposure, bits, weights, masked_ref, terms_ref, core, first, last):
    sets = exposure.shape[0]
    owned = terms_ref.shape[2]
    for pair in range(sets // 16):
        flags = [row_flags(2 * pair), row_flags(2 * pair + 1)]
        for chip in range(first, last):
            masked_ref[16 * pair : 16 * pair + 16, chip * owned : (chip + 1) * owned] = masked_rows(
                exposure, bits, pair, flags, sibling_columns(chip, owned, core)
            )
    for chip in range(first, last, 2):
        terms = jnp.dot(
            weights,
            masked_ref[:, chip * owned : (chip + 2) * owned],
            preferred_element_type=jnp.float32,
        ).astype(terms_ref.dtype)
        terms_ref[chip] = terms[:, :owned]
        terms_ref[chip + 1] = terms[:, owned:]


def first_kernel(
    dates,
    exposure_hbm,
    bits_hbm,
    currencies_hbm,
    counts_hbm,
    notional_hbm,
    fx_hbm,
    rates_hbm,
    start_hbm,
    handed_ref,
    masked_ref,
    exposure,
    bits,
    weights_ref,
    carried_ref,
    discount_ref,
    moved_ref,
    used_ref,
    currencies_ref,
    counts_ref,
    notional_ref,
    fx_ref,
    rates_ref,
    start_ref,
    in_sems,
    bits_sems,
    small_sems,
):
    sets, columns = exposure.shape
    currency_count, owned = fx_ref.shape
    chips = columns // (2 * owned)
    width = columns // chunks

    def exposure_copy(index):
        part = pl.ds(index * width, width)
        return pltpu.make_async_copy(
            exposure_hbm.at[:, part], exposure.at[:, part], in_sems.at[index]
        )

    def bits_copy(index):
        part = pl.ds(index * width, width)
        return pltpu.make_async_copy(bits_hbm.at[:, part], bits.at[:, part], bits_sems.at[index])

    small_copies = [
        pltpu.make_async_copy(source, target, small_sems.at[index])
        for index, (source, target) in enumerate(
            [
                (rates_hbm, rates_ref),
                (start_hbm, start_ref),
                (fx_hbm, fx_ref),
                (currencies_hbm, currencies_ref),
                (counts_hbm, counts_ref),
                (notional_hbm, notional_ref),
            ]
        )
    ]
    for copy in small_copies:
        copy.start()
    for index in range(chunks):
        bits_copy(index).start()
        exposure_copy(index).start()
    for copy in small_copies:
        copy.wait()

    used = used_currencies(currencies_ref[...], counts_ref[...])
    used_ref[...] = used
    notional = notional_ref[...]
    currency = lax.broadcasted_iota(jnp.int32, (currency_count, sets), 0)
    weights = jnp.zeros((currency_count, sets), jnp.float32)
    for slot in range(used.shape[0]):
        weights = weights + jnp.where(
            currency == used[slot : slot + 1], notional[slot : slot + 1], 0.0
        )
    weights = weights.astype(jnp.bfloat16)
    weights_ref[...] = weights

    integral = spread_paths(start_ref[...], dates) + step_years * sums_to_date(rates_ref[...], dates)
    discount = jnp.exp(-integral)
    discount_ref[...] = discount
    moved = fx_ref[...] * discount
    moved_ref[...] = moved
    carried = moved.astype(jnp.bfloat16)
    carried_ref[...] = carried
    handed_ref[chips] = carried

    other = 1 - lax.axis_index("sets") % 2
    for index in range(chunks):
        bits_copy(index).wait()
        exposure_copy(index).wait()
        here = chips // chunks
        half_of_columns(
            exposure,
            bits,
            weights,
            masked_ref,
            handed_ref,
            other,
            index * here,
            (index + 1) * here,
        )


def second_kernel(exposure, bits, weights_ref, masked_ref, terms_ref):
    half_of_columns(
        exposure,
        bits,
        weights_ref[...],
        masked_ref,
        terms_ref,
        lax.axis_index("sets") % 2,
        0,
        terms_ref.shape[0],
    )


def merging_kernel(given_ref, terms_ref, carried_ref, outgoing_ref):
    chips, currency_count, owned = terms_ref.shape
    order = group_order(chips)
    carried = carried_ref[...]
    sibling = given_ref[chips]
    for place in range(chips):
        outgoing_ref[place, 0:currency_count, :] = carried
        outgoing_ref[place, currency_count : 2 * currency_count, :] = sibling
        outgoing_ref[place, 2 * currency_count :, :] = (
            terms_ref[order[place]] + given_ref[order[place]].astype(jnp.float32)
        ).astype(jnp.bfloat16)


def final_kernel(
    dates,
    arrived_ref,
    masked_other,
    masked_own,
    used_ref,
    moved_ref,
    discount_ref,
    fx_adjoint_ref,
    rate_adjoint_ref,
    notional_adjoint_ref,
):
    sets, half = masked_own.shape
    currency_count, owned = moved_ref.shape
    chips = half // owned
    order = group_order(chips)
    place = [order.index(chip) for chip in range(chips)]

    aggregate = arrived_ref[0, 2 * currency_count :, :].astype(jnp.float32)
    for chip in range(1, chips):
        aggregate = aggregate + arrived_ref[chip, 2 * currency_count :, :].astype(jnp.float32)
    fx_adjoint_ref[...] = aggregate * discount_ref[...]
    rate_adjoint_ref[...] = -step_years * sums_from_date(aggregate * moved_ref[...], dates)

    width = min(half, 1024)
    projected = jnp.zeros((sets, currency_count), jnp.float32)
    for index in range(half // width):
        here = width // owned
        for masked, top in ((masked_own, 0), (masked_other, currency_count)):
            carried = jnp.concatenate(
                [
                    arrived_ref[place[index * here + block], top : top + currency_count, :]
                    for block in range(here)
                ],
                axis=1,
            )
            projected = projected + lax.dot_general(
                masked[:, index * width : (index + 1) * width],
                carried,
                (((1,), (1,)), ((), ())),
                preferred_element_type=jnp.float32,
            )
    projected = projected.T
    used = used_ref[...]
    currency = lax.broadcasted_iota(jnp.int32, (currency_count, sets), 0)
    for slot in range(used.shape[0]):
        picked = jnp.sum(
            jnp.where(currency == used[slot : slot + 1], projected, 0.0), axis=0, keepdims=True
        )
        notional_adjoint_ref[slot : slot + 1, :] = picked * (1.0 / math.sqrt(2 * half))


def body(
    exposure_adjoint,
    positive_bits,
    currencies,
    mix_count,
    notional,
    fx_paths,
    short_rates,
    start_integral,
):
    sets, columns = exposure_adjoint.shape
    currency_count, owned = fx_paths.shape
    dates = owned // start_integral.shape[1]
    peers = columns // owned
    chips = peers // 2
    slots = currencies.shape[1]
    in_vmem = pl.BlockSpec(memory_space=pltpu.VMEM)
    anywhere = pl.BlockSpec(memory_space=pl.ANY)
    params = pltpu.CompilerParams(vmem_limit_bytes=32 * 2**20)
    block = (currency_count, owned)

    def in_hbm(value):
        return pltpu.with_memory_space_constraint(value, pltpu.HBM)

    handed, masked_other, exposure, bits, weights, carried, discount, moved, used = pl.pallas_call(
        functools.partial(first_kernel, dates),
        out_shape=(
            pltpu.VMEM((chips + 1,) + block, jnp.bfloat16),
            pltpu.VMEM((sets, columns // 2), jnp.bfloat16),
            pltpu.VMEM((sets, columns), jnp.bfloat16),
            pltpu.VMEM(positive_bits.shape, jnp.int32),
            pltpu.VMEM((currency_count, sets), jnp.bfloat16),
            pltpu.VMEM(block, jnp.bfloat16),
            pltpu.VMEM(block, jnp.float32),
            pltpu.VMEM(block, jnp.float32),
            pltpu.VMEM((slots, sets), jnp.int32),
        ),
        in_specs=[anywhere] * 8,
        out_specs=(in_vmem,) * 9,
        scratch_shapes=[
            pltpu.VMEM((slots, sets), jnp.int32),
            pltpu.VMEM((1, sets), jnp.int32),
            pltpu.VMEM((slots, sets), jnp.float32),
            pltpu.VMEM(block, jnp.float32),
            pltpu.VMEM(block, jnp.float32),
            pltpu.VMEM((owned // dates, currency_count), jnp.float32),
            pltpu.SemaphoreType.DMA((chunks,)),
            pltpu.SemaphoreType.DMA((chunks,)),
            pltpu.SemaphoreType.DMA((6,)),
        ],
        compiler_params=params,
        name="first",
    )(
        in_hbm(exposure_adjoint),
        in_hbm(positive_bits),
        in_hbm(currencies.T),
        in_hbm(mix_count.reshape(1, sets)),
        in_hbm(notional.T),
        in_hbm(fx_paths),
        in_hbm(short_rates),
        in_hbm(start_integral.T),
    )
    given = lax.ppermute(handed, "sets", [(peer, peer ^ 1) for peer in range(peers)])
    masked_own, terms = pl.pallas_call(
        second_kernel,
        out_shape=(
            pltpu.VMEM((sets, columns // 2), jnp.bfloat16),
            pltpu.VMEM((chips,) + block, jnp.float32),
        ),
        in_specs=[in_vmem] * 3,
        out_specs=(in_vmem,) * 2,
        compiler_params=params,
        name="second",
    )(exposure, bits, weights)
    outgoing = pl.pallas_call(
        merging_kernel,
        out_shape=pltpu.VMEM((chips, 3 * currency_count, owned), jnp.bfloat16),
        in_specs=[in_vmem] * 3,
        out_specs=in_vmem,
        compiler_params=params,
        name="merging",
    )(given, terms, carried)
    arrived = lax.all_to_all(
        outgoing,
        "sets",
        0,
        0,
        axis_index_groups=[[2 * chip + core for chip in group_order(chips)] for core in range(2)],
        tiled=True,
    )
    fx_adjoint, rate_adjoint, notional_adjoint = pl.pallas_call(
        functools.partial(final_kernel, dates),
        out_shape=(
            jax.ShapeDtypeStruct(block, jnp.float32),
            jax.ShapeDtypeStruct(block, jnp.float32),
            jax.ShapeDtypeStruct((slots, sets), jnp.float32),
        ),
        in_specs=[in_vmem] * 6,
        out_specs=(in_vmem,) * 3,
        compiler_params=params,
        name="final",
    )(arrived, masked_other, masked_own, used, moved, discount)
    return fx_adjoint, rate_adjoint, notional_adjoint.T


def solution(mesh):
    in_specs = (
        P(("grp", "sets"), None),
        P(("grp", "sets"), None),
        P(("grp", "sets"), None),
        P(("grp", "sets")),
        P(("grp", "sets"), None),
        P("grp", "sets"),
        P("grp", "sets"),
        P("grp", "sets"),
    )
    out_specs = (P("grp", "sets"), P("grp", "sets"), P(("grp", "sets"), None))
    return jax.shard_map(body, mesh=mesh, in_specs=in_specs, out_specs=out_specs, check_vma=False)
```

time: 21.2 us -> 20.2 us (0.953)
  blocking collectives: 17.3 us -> 15 us
  waiting for transfers between devices: 0 us -> 0.53 us
  starting transfers between devices: 0 us -> 0.51 us
    all_to_all x1, blocking collectives: 17.3 us -> 15 us  [body(): lax.all_to_all(outgoing, 'sets', 0, 0, axis_index_groups=[[2 * chip + cor...]
    ppermute x0 -> x1, waiting for transfers between devices: none -> 0.53 us  [body(): lax.ppermute(handed, 'sets', [(peer, peer ^ 1) for peer in range(peers)])]
    ppermute x0 -> x1, starting transfers between devices: none -> 0.51 us  [body(): lax.ppermute(handed, 'sets', [(peer, peer ^ 1) for peer in range(peers)])]
    pallas_call x1 -> x3, Pallas kernels: 2.11 us -> 2.27 us  [the longest x1 1.84 us: body(): pl.pallas_call(functools.partial(first_kernel, dates), out_shape=(pltpu.V...]
  transfers between devices with their start and end apart: 0 -> 1, of which waited for: 0 -> 1; matrix products, arithmetic and copies ran while one was open for 0% -> 0% of each run, Pallas kernels for 0% -> 2%
where the time goes in v8:
time: 20.2 us; the launch traced here: 20.1 us
  blocking collectives  15 us (74%)
  Pallas kernels  3.34 us (17%)
  between operations  0.65 us (3%)
  waiting for transfers between devices  0.53 us (3%)
  starting transfers between devices  0.51 us (3%)
    all_to_all x1, blocking collectives, body(): lax.all_to_all(outgoing, 'sets', 0, 0, axis_index_groups=[[2 * chip + cor...  15 us
    pallas_call x1, Pallas kernels, body(): pl.pallas_call(functools.partial(first_kernel, dates), out_shape=(pltpu.V...  1.84 us
    pallas_call x1, Pallas kernels, body(): pl.pallas_call(functools.partial(final_kernel, dates), out_shape=(jax.Sha...  1.07 us
    ppermute x1, waiting for transfers between devices, body(): lax.ppermute(handed, 'sets', [(peer, peer ^ 1) for peer in range(peers)])  0.53 us
    ppermute x1, starting transfers between devices, body(): lax.ppermute(handed, 'sets', [(peer, peer ^ 1) for peer in range(peers)])  0.51 us
  transfers between devices with their start and end apart: 1, of which 1 were waited for; matrix products, arithmetic and copies ran while one was open for 0% of the time, Pallas kernels for 2%

profile of v8, /device:TPU:0, one launch (start us, length us, event | category | flops | bytes accessed | tf_op | source)
XLA Modules:
  0.0 20.1 jit_solution(7431223125165507314)
XLA Ops:
  0.6 1.8 %first.1 = (bf16[9,40,128]{2,1,0:T(8,128)(2,1)S(1)}, bf16[240,1024]{1,0:T(8,128)(2,1)S(1)}, bf16[240,2048]{1,0:T(8,128)(2,1)S(1)}, s32[16,2048]{1,0:T(8,128)S(1)...) custom-call(bf16[240,2048]{1,0:T(8,128)(2,1)} %exposure_hbm.1, ...), custom_call_target="tpu_custom_call" | custom-call | tf_op jit(solution)/shard_map/first/pallas_call | solution.py:310
  2.5 0.5 %collective-permute-start = (bf16[9,40,128]{2,1,0:T(8,128)(2,1)S(1)}, bf16[9,40,128]{2,1,0:T(8,128)(2,1)S(1)}, u32[]{:S(2)}, u32[]{:S(2)}) collective-permute-start(bf16[9,40,128]{2,1,0:T(8,128)(2,1)S(1)} %get-tuple-element.17), channel_id=1, source_target_pairs={{0,1},{1,0},{2,3},{3,2},{4,5},{5,4},{6,7},{7,6},{8,9},{9,8},{10,11... | collective-permute-start | bytes 276488 | tf_op jit(solution)/shard_map/ppermute | solution.py:348
  3.0 0.4 %second.1 = (bf16[240,1024]{1,0:T(8,128)(2,1)S(1)}, f32[8,40,128]{2,1,0:T(8,128)S(1)}) custom-call(bf16[240,2048]{1,0:T(8,128)(2,1)S(1)} %get-tuple-element.18.exposure, s32[16,2048]{1,0:T(8,128)S(1)} %get-tuple-element.19.bits, bf16[40,240]{1,0:T(8,128)(2,1)S(1)} %get-tuple-element.20.weights_ref), custom_call_target="tpu_custom_call" | custom-call | tf_op jit(solution)/shard_map/second/pallas_call | solution.py:349
  3.4 0.5 %collective-permute-done.given_ref = bf16[9,40,128]{2,1,0:T(8,128)(2,1)S(1)} collective-permute-done((bf16[9,40,128]{2,1,0:T(8,128)(2,1)S(1)}, bf16[9,40,128]{2,1,0:T(8,128)(2,1)S(1)}, u32[]{:S(2)}, u32[]{:S(2)}) %collective-permute-start) | collective-permute-done | bytes 92192 | tf_op jit(solution)/shard_map/ppermute | solution.py:348
  4.0 15.0 %all_to_all.5.arrived_ref = bf16[8,120,128]{2,1,0:T(8,128)(2,1)S(1)} all-to-all(bf16[8,120,128]{2,1,0:T(8,128)(2,1)S(1)} %merging.1), channel_id=1, replica_groups={{14,12,10,8,6,4,2,0},{15,13,11,9,7,5,3,1},{30,28,26,24,22,20,18,16},{31..., dimensions={0} | all-to-all | bytes 491520 | tf_op jit(solution)/shard_map/all_to_all | solution.py:368
  19.0 1.1 %final.1 = (f32[40,128]{1,0:T(8,128)}, f32[40,128]{1,0:T(8,128)}, f32[4,240]{1,0:T(4,128)}) custom-call(bf16[8,120,128]{2,1,0:T(8,128)(2,1)S(1)} %all_to_all.5.arrived_ref, bf16[240,1024]{1,0:T(8,128)(2,1)S(1)} %get-tuple-element.23.masked_other, bf16[240,1024]{1,0:T(8,128)(2,1)S(1)} %get-tuple-element.24.masked_own, ...), custom_call_target="tpu_custom_call" | custom-call | tf_op jit(solution)/shard_map/final/pallas_call | solution.py:376
  (1 shorter events, 0.0 us)
Async XLA Ops:
  2.5 1.4 %collective-permute-start = (bf16[9,40,128]{2,1,0:T(8,128)(2,1)S(1)}, bf16[9,40,128]{2,1,0:T(8,128)(2,1)S(1)}, u32[]{:S(2)}, u32[]{:S(2)}) collective-permute-start(bf16[9,40,128]{2,1,0:T(8,128)(2,1)S(1)} %get-tuple-element.17), channel_id=1, source_target_pairs={{0,1},{1,0},{2,3},{3,2},{4,5},{5,4},{6,7},{7,6},{8,9},{9,8},{10,11... | collective-permute-start | bytes 276488 | tf_op jit(solution)/shard_map/ppermute | solution.py:348

commit v9 on v8

--- a/solution.py
+++ b/solution.py
@@ -11,7 +11,6 @@
 step_years = 0.25
 bits_per_row = 15
 lanes = 128
-chunks = 2
 
 
 def spread_paths(values, dates):
@@ -103,7 +102,6 @@
 
 
 def first_kernel(
-    dates,
     exposure_hbm,
     bits_hbm,
     currencies_hbm,
@@ -117,54 +115,35 @@
     exposure,
     bits,
     weights_ref,
-    carried_ref,
-    discount_ref,
-    moved_ref,
     used_ref,
+    fx_ref,
+    rates_ref,
+    start_ref,
     currencies_ref,
     counts_ref,
     notional_ref,
-    fx_ref,
-    rates_ref,
-    start_ref,
-    in_sems,
-    bits_sems,
-    small_sems,
+    sems,
 ):
-    sets, columns = exposure.shape
-    currency_count, owned = fx_ref.shape
-    chips = columns // (2 * owned)
-    width = columns // chunks
-
-    def exposure_copy(index):
-        part = pl.ds(index * width, width)
-        return pltpu.make_async_copy(
-            exposure_hbm.at[:, part], exposure.at[:, part], in_sems.at[index]
-        )
-
-    def bits_copy(index):
-        part = pl.ds(index * width, width)
-        return pltpu.make_async_copy(bits_hbm.at[:, part], bits.at[:, part], bits_sems.at[index])
-
-    small_copies = [
-        pltpu.make_async_copy(source, target, small_sems.at[index])
+    sets = exposure.shape[0]
+    chips, currency_count = handed_ref.shape[:2]
+    copies = [
+        pltpu.make_async_copy(source, target, sems.at[index])
         for index, (source, target) in enumerate(
             [
+                (currencies_hbm, currencies_ref),
+                (counts_hbm, counts_ref),
+                (notional_hbm, notional_ref),
+                (bits_hbm, bits),
+                (exposure_hbm, exposure),
                 (rates_hbm, rates_ref),
                 (start_hbm, start_ref),
                 (fx_hbm, fx_ref),
-                (currencies_hbm, currencies_ref),
-                (counts_hbm, counts_ref),
-                (notional_hbm, notional_ref),
             ]
         )
     ]
-    for copy in small_copies:
+    for copy in copies:
         copy.start()
-    for index in range(chunks):
-        bits_copy(index).start()
-        exposure_copy(index).start()
-    for copy in small_copies:
+    for copy in copies:
         copy.wait()
 
     used = used_currencies(currencies_ref[...], counts_ref[...])
@@ -178,34 +157,30 @@
         )
     weights = weights.astype(jnp.bfloat16)
     weights_ref[...] = weights
-
+    other = 1 - lax.axis_index("sets") % 2
+    half_of_columns(exposure, bits, weights, masked_ref, handed_ref, other, 0, chips)
+
+
+def second_kernel(
+    dates,
+    exposure,
+    bits,
+    weights_ref,
+    fx_ref,
+    rates_ref,
+    start_ref,
+    masked_ref,
+    terms_ref,
+    carried_ref,
+    discount_ref,
+    moved_ref,
+):
     integral = spread_paths(start_ref[...], dates) + step_years * sums_to_date(rates_ref[...], dates)
     discount = jnp.exp(-integral)
     discount_ref[...] = discount
     moved = fx_ref[...] * discount
     moved_ref[...] = moved
-    carried = moved.astype(jnp.bfloat16)
-    carried_ref[...] = carried
-    handed_ref[chips] = carried
-
-    other = 1 - lax.axis_index("sets") % 2
-    for index in range(chunks):
-        bits_copy(index).wait()
-        exposure_copy(index).wait()
-        here = chips // chunks
-        half_of_columns(
-            exposure,
-            bits,
-            weights,
-            masked_ref,
-            handed_ref,
-            other,
-            index * here,
-            (index + 1) * here,
-        )
-
-
-def second_kernel(exposure, bits, weights_ref, masked_ref, terms_ref):
+    carried_ref[...] = moved.astype(jnp.bfloat16)
     half_of_columns(
         exposure,
         bits,
@@ -222,58 +197,60 @@
     chips, currency_count, owned = terms_ref.shape
     order = group_order(chips)
     carried = carried_ref[...]
-    sibling = given_ref[chips]
     for place in range(chips):
         outgoing_ref[place, 0:currency_count, :] = carried
-        outgoing_ref[place, currency_count : 2 * currency_count, :] = sibling
-        outgoing_ref[place, 2 * currency_count :, :] = (
+        outgoing_ref[place, currency_count:, :] = (
             terms_ref[order[place]] + given_ref[order[place]].astype(jnp.float32)
         ).astype(jnp.bfloat16)
 
 
-def final_kernel(
+def unpacking_kernel(arrived_ref, carried_ref):
+    chips, currency_count, owned = carried_ref.shape
+    order = group_order(chips)
+    for place in range(chips):
+        carried_ref[order[place]] = arrived_ref[place, 0:currency_count, :]
+
+
+def projection(masked, carried_ref):
+    sets, half = masked.shape
+    chips, currency_count, owned = carried_ref.shape
+    here = min(chips, 8)
+    projected = jnp.zeros((sets, currency_count), jnp.float32)
+    for first in range(0, chips, here):
+        carried = jnp.concatenate([carried_ref[first + chip] for chip in range(here)], axis=1)
+        projected = projected + lax.dot_general(
+            masked[:, first * owned : (first + here) * owned],
+            carried,
+            (((1,), (1,)), ((), ())),
+            preferred_element_type=jnp.float32,
+        )
+    return projected
+
+
+def adjoint_kernel(
     dates,
     arrived_ref,
-    masked_other,
+    carried_ref,
     masked_own,
-    used_ref,
     moved_ref,
     discount_ref,
     fx_adjoint_ref,
     rate_adjoint_ref,
-    notional_adjoint_ref,
+    projected_ref,
 ):
-    sets, half = masked_own.shape
-    currency_count, owned = moved_ref.shape
-    chips = half // owned
-    order = group_order(chips)
-    place = [order.index(chip) for chip in range(chips)]
-
-    aggregate = arrived_ref[0, 2 * currency_count :, :].astype(jnp.float32)
+    chips, currency_count, owned = carried_ref.shape
+    aggregate = arrived_ref[0, currency_count:, :].astype(jnp.float32)
     for chip in range(1, chips):
-        aggregate = aggregate + arrived_ref[chip, 2 * currency_count :, :].astype(jnp.float32)
+        aggregate = aggregate + arrived_ref[chip, currency_count:, :].astype(jnp.float32)
     fx_adjoint_ref[...] = aggregate * discount_ref[...]
     rate_adjoint_ref[...] = -step_years * sums_from_date(aggregate * moved_ref[...], dates)
-
-    width = min(half, 1024)
-    projected = jnp.zeros((sets, currency_count), jnp.float32)
-    for index in range(half // width):
-        here = width // owned
-        for masked, top in ((masked_own, 0), (masked_other, currency_count)):
-            carried = jnp.concatenate(
-                [
-                    arrived_ref[place[index * here + block], top : top + currency_count, :]
-                    for block in range(here)
-                ],
-                axis=1,
-            )
-            projected = projected + lax.dot_general(
-                masked[:, index * width : (index + 1) * width],
-                carried,
-                (((1,), (1,)), ((), ())),
-                preferred_element_type=jnp.float32,
-            )
-    projected = projected.T
+    projected_ref[...] = projection(masked_own, carried_ref)
+
+
+def picking_kernel(carried_ref, masked_other, projected_ref, used_ref, notional_adjoint_ref):
+    sets, half = masked_other.shape
+    currency_count = carried_ref.shape[1]
+    projected = (projected_ref[...] + projection(masked_other, carried_ref)).T
     used = used_ref[...]
     currency = lax.broadcasted_iota(jnp.int32, (currency_count, sets), 0)
     for slot in range(used.shape[0]):
@@ -307,18 +284,21 @@
     def in_hbm(value):
         return pltpu.with_memory_space_constraint(value, pltpu.HBM)
 
-    handed, masked_other, exposure, bits, weights, carried, discount, moved, used = pl.pallas_call(
-        functools.partial(first_kernel, dates),
+    def swapped(value):
+        return lax.ppermute(value, "sets", [(peer, peer ^ 1) for peer in range(peers)])
+
+    handed, masked_other, exposure, bits, weights, used, fx, rates, start = pl.pallas_call(
+        first_kernel,
         out_shape=(
-            pltpu.VMEM((chips + 1,) + block, jnp.bfloat16),
+            pltpu.VMEM((chips,) + block, jnp.bfloat16),
             pltpu.VMEM((sets, columns // 2), jnp.bfloat16),
             pltpu.VMEM((sets, columns), jnp.bfloat16),
             pltpu.VMEM(positive_bits.shape, jnp.int32),
             pltpu.VMEM((currency_count, sets), jnp.bfloat16),
-            pltpu.VMEM(block, jnp.bfloat16),
+            pltpu.VMEM((slots, sets), jnp.int32),
             pltpu.VMEM(block, jnp.float32),
             pltpu.VMEM(block, jnp.float32),
-            pltpu.VMEM((slots, sets), jnp.int32),
+            pltpu.VMEM((owned // dates, currency_count), jnp.float32),
         ),
         in_specs=[anywhere] * 8,
         out_specs=(in_vmem,) * 9,
@@ -326,12 +306,7 @@
             pltpu.VMEM((slots, sets), jnp.int32),
             pltpu.VMEM((1, sets), jnp.int32),
             pltpu.VMEM((slots, sets), jnp.float32),
-            pltpu.VMEM(block, jnp.float32),
-            pltpu.VMEM(block, jnp.float32),
-            pltpu.VMEM((owned // dates, currency_count), jnp.float32),
-            pltpu.SemaphoreType.DMA((chunks,)),
-            pltpu.SemaphoreType.DMA((chunks,)),
-            pltpu.SemaphoreType.DMA((6,)),
+            pltpu.SemaphoreType.DMA((8,)),
         ],
         compiler_params=params,
         name="first",
@@ -345,21 +320,24 @@
         in_hbm(short_rates),
         in_hbm(start_integral.T),
     )
-    given = lax.ppermute(handed, "sets", [(peer, peer ^ 1) for peer in range(peers)])
-    masked_own, terms = pl.pallas_call(
-        second_kernel,
+    given = swapped(handed)
+    masked_own, terms, carried, discount, moved = pl.pallas_call(
+        functools.partial(second_kernel, dates),
         out_shape=(
             pltpu.VMEM((sets, columns // 2), jnp.bfloat16),
             pltpu.VMEM((chips,) + block, jnp.float32),
+            pltpu.VMEM(block, jnp.bfloat16),
+            pltpu.VMEM(block, jnp.float32),
+            pltpu.VMEM(block, jnp.float32),
         ),
-        in_specs=[in_vmem] * 3,
-        out_specs=(in_vmem,) * 2,
+        in_specs=[in_vmem] * 6,
+        out_specs=(in_vmem,) * 5,
         compiler_params=params,
         name="second",
-    )(exposure, bits, weights)
+    )(exposure, bits, weights, fx, rates, start)
     outgoing = pl.pallas_call(
         merging_kernel,
-        out_shape=pltpu.VMEM((chips, 3 * currency_count, owned), jnp.bfloat16),
+        out_shape=pltpu.VMEM((chips, 2 * currency_count, owned), jnp.bfloat16),
         in_specs=[in_vmem] * 3,
         out_specs=in_vmem,
         compiler_params=params,
@@ -373,18 +351,35 @@
         axis_index_groups=[[2 * chip + core for chip in group_order(chips)] for core in range(2)],
         tiled=True,
     )
-    fx_adjoint, rate_adjoint, notional_adjoint = pl.pallas_call(
-        functools.partial(final_kernel, dates),
+    carried_own = pl.pallas_call(
+        unpacking_kernel,
+        out_shape=pltpu.VMEM((chips,) + block, jnp.bfloat16),
+        in_specs=[in_vmem],
+        out_specs=in_vmem,
+        compiler_params=params,
+        name="unpacking",
+    )(arrived)
+    carried_other = swapped(carried_own)
+    fx_adjoint, rate_adjoint, projected = pl.pallas_call(
+        functools.partial(adjoint_kernel, dates),
         out_shape=(
             jax.ShapeDtypeStruct(block, jnp.float32),
             jax.ShapeDtypeStruct(block, jnp.float32),
-            jax.ShapeDtypeStruct((slots, sets), jnp.float32),
+            pltpu.VMEM((sets, currency_count), jnp.float32),
         ),
-        in_specs=[in_vmem] * 6,
+        in_specs=[in_vmem] * 5,
         out_specs=(in_vmem,) * 3,
         compiler_params=params,
-        name="final",
-    )(arrived, masked_other, masked_own, used, moved, discount)
+        name="adjoint",
+    )(arrived, carried_own, masked_own, moved, discount)
+    notional_adjoint = pl.pallas_call(
+        picking_kernel,
+        out_shape=jax.ShapeDtypeStruct((slots, sets), jnp.float32),
+        in_specs=[in_vmem] * 4,
+        out_specs=in_vmem,
+        compiler_params=params,
+        name="picking",
+    )(carried_other, masked_other, projected, used)
     return fx_adjoint, rate_adjoint, notional_adjoint.T
 
 

time: 20.2 us -> 19.7 us (0.975)
  blocking collectives: 15 us -> 13.3 us
  Pallas kernels: 3.34 us -> 4.04 us
  waiting for transfers between devices: 0.53 us -> 0.92 us
    all_to_all x1, blocking collectives: 15 us -> 13.3 us  [body(): lax.all_to_all(outgoing, 'sets', 0, 0, axis_index_groups=[[2 * chip + cor...]
    pallas_call x4 -> x6, Pallas kernels: 3.34 us -> 4.04 us  [the longest x1 1.83 us: body(): pl.pallas_call(first_kernel, out_shape=(pltpu.VMEM((chips,) + block, jnp....]
    ppermute x1 -> x2, waiting for transfers between devices: 0.53 us -> 0.92 us  [swapped(): lax.ppermute(value, 'sets', [(peer, peer ^ 1) for peer in range(peers)])]
    ppermute x1 -> x2, starting transfers between devices: 0.51 us -> 0.58 us  [swapped(): lax.ppermute(value, 'sets', [(peer, peer ^ 1) for peer in range(peers)])]
  transfers between devices with their start and end apart: 1 -> 2, of which waited for: 1 -> 2; matrix products, arithmetic and copies ran while one was open for 0% -> 0% of each run, Pallas kernels for 2% -> 6%
where the time goes in v9:
time: 19.7 us; the launch traced here: 19.5 us
  blocking collectives  13.3 us (68%)
  Pallas kernels  4.04 us (21%)
  waiting for transfers between devices  0.92 us (5%)
  between operations  0.66 us (3%)
  starting transfers between devices  0.58 us (3%)
    all_to_all x1, blocking collectives, body(): lax.all_to_all(outgoing, 'sets', 0, 0, axis_index_groups=[[2 * chip + cor...  13.3 us
    pallas_call x1, Pallas kernels, body(): pl.pallas_call(first_kernel, out_shape=(pltpu.VMEM((chips,) + block, jnp....  1.83 us
    pallas_call x1, Pallas kernels, body(): pl.pallas_call(picking_kernel, out_shape=jax.ShapeDtypeStruct((slots, set...  0.93 us
    ppermute x2, waiting for transfers between devices, swapped(): lax.ppermute(value, 'sets', [(peer, peer ^ 1) for peer in range(peers)])  0.92 us
    pallas_call x1, Pallas kernels, body(): pl.pallas_call(functools.partial(adjoint_kernel, dates), out_shape=(jax.S...  0.85 us
    ppermute x2, starting transfers between devices, swapped(): lax.ppermute(value, 'sets', [(peer, peer ^ 1) for peer in range(peers)])  0.58 us
    pallas_call x1, Pallas kernels, body(): pl.pallas_call(functools.partial(second_kernel, dates), out_shape=(pltpu....  0.4 us
  transfers between devices with their start and end apart: 2, of which 2 were waited for; matrix products, arithmetic and copies ran while one was open for 0% of the time, Pallas kernels for 6%

profile of v9, /device:TPU:0, one launch (start us, length us, event | category | flops | bytes accessed | tf_op | source)
XLA Modules:
  0.0 19.5 jit_solution(3401192530405517094)
XLA Ops:
  0.6 1.8 %first.1 = (bf16[8,40,128]{2,1,0:T(8,128)(2,1)S(1)}, bf16[240,1024]{1,0:T(8,128)(2,1)S(1)}, bf16[240,2048]{1,0:T(8,128)(2,1)S(1)}, s32[16,2048]{1,0:T(8,128)S(1)...) custom-call(bf16[240,2048]{1,0:T(8,128)(2,1)} %exposure_hbm.1, ...), custom_call_target="tpu_custom_call" | custom-call | tf_op jit(solution)/shard_map/first/pallas_call | solution.py:290
  2.5 0.5 %collective-permute-start = (bf16[8,40,128]{2,1,0:T(8,128)(2,1)S(1)}, bf16[8,40,128]{2,1,0:T(8,128)(2,1)S(1)}, u32[]{:S(2)}, u32[]{:S(2)}) collective-permute-start(bf16[8,40,128]{2,1,0:T(8,128)(2,1)S(1)} %get-tuple-element.20), channel_id=1, source_target_pairs={{0,1},{1,0},{2,3},{3,2},{4,5},{5,4},{6,7},{7,6},{8,9},{9,8},{10,11... | collective-permute-start | bytes 245768 | tf_op jit(solution)/shard_map/ppermute | solution.py:288
  3.0 0.4 %second.1 = (bf16[240,1024]{1,0:T(8,128)(2,1)S(1)}, f32[8,40,128]{2,1,0:T(8,128)S(1)}, bf16[40,128]{1,0:T(8,128)(2,1)S(1)}, f32[40,128]{1,0:T(8,128)S(1)}, f32[40,128]{1,0:T(8,128)S(1)}) custom-call(bf16[240,2048]{1,0:T(8,128)(2,1)S(1)} %get-tuple-element.21.exposure, s32[16,2048]{1,0:T(8,128)S(1)} %get-tuple-element.22.bits, ...), custom_call_target="tpu_custom_call" | custom-call | tf_op jit(solution)/shard_map/second/pallas_call | solution.py:324
  3.4 0.5 %collective-permute-done.given_ref = bf16[8,40,128]{2,1,0:T(8,128)(2,1)S(1)} collective-permute-done((bf16[8,40,128]{2,1,0:T(8,128)(2,1)S(1)}, bf16[8,40,128]{2,1,0:T(8,128)(2,1)S(1)}, u32[]{:S(2)}, u32[]{:S(2)}) %collective-permute-start) | collective-permute-done | bytes 81952 | tf_op jit(solution)/shard_map/ppermute | solution.py:288
  3.9 13.3 %all_to_all.5.arrived_ref = bf16[8,80,128]{2,1,0:T(8,128)(2,1)S(1)} all-to-all(bf16[8,80,128]{2,1,0:T(8,128)(2,1)S(1)} %merging.1), channel_id=1, replica_groups={{14,12,10,8,6,4,2,0},{15,13,11,9,7,5,3,1},{30,28,26,24,22,20,18,16},{31..., dimensions={0} | all-to-all | bytes 327680 | tf_op jit(solution)/shard_map/all_to_all | solution.py:346
  17.2 0.1 collective-permute-start.1
  17.3 0.9 %adjoint.1 = (f32[40,128]{1,0:T(8,128)}, f32[40,128]{1,0:T(8,128)}, f32[240,40]{1,0:T(8,128)S(1)}) custom-call(bf16[8,80,128]{2,1,0:T(8,128)(2,1)S(1)} %all_to_all.5.arrived_ref, bf16[8,40,128]{2,1,0:T(8,128)(2,1)S(1)} %unpacking.1.carried_ref, bf16[240,1024]{1,0:T(8,128)(2,1)S(1)} %get-tuple-element.29.masked_own, ...), custom_call_target="tpu_custom_call" | custom-call | tf_op jit(solution)/shard_map/adjoint/pallas_call | solution.py:363
  18.1 0.4 %collective-permute-done.1.carried_ref = bf16[8,40,128]{2,1,0:T(8,128)(2,1)S(1)} collective-permute-done((bf16[8,40,128]{2,1,0:T(8,128)(2,1)S(1)}, bf16[8,40,128]{2,1,0:T(8,128)(2,1)S(1)}, u32[]{:S(2)}, u32[]{:S(2)}) %collective-permute-start.1) | collective-permute-done | bytes 81952 | tf_op jit(solution)/shard_map/ppermute | solution.py:288
  18.6 0.9 %picking.1 = f32[4,240]{1,0:T(4,128)} custom-call(bf16[8,40,128]{2,1,0:T(8,128)(2,1)S(1)} %collective-permute-done.1.carried_ref, bf16[240,1024]{1,0:T(8,128)(2,1)S(1)} %get-tuple-element.34.masked_other, f32[240,40]{1,0:T(8,128)S(1)} %get-tuple-element.35.projected_ref, s32[4,240]{1,0:T(4,128)S(1)} %get-tuple-element.36.used_ref), custom_call_target="tpu_custom_call" | custom-call | tf_op jit(solution)/shard_map/picking/pallas_call | solution.py:375
  (2 shorter events, 0.0 us)
Async XLA Ops:
  2.5 1.4 %collective-permute-start = (bf16[8,40,128]{2,1,0:T(8,128)(2,1)S(1)}, bf16[8,40,128]{2,1,0:T(8,128)(2,1)S(1)}, u32[]{:S(2)}, u32[]{:S(2)}) collective-permute-start(bf16[8,40,128]{2,1,0:T(8,128)(2,1)S(1)} %get-tuple-element.20), channel_id=1, source_target_pairs={{0,1},{1,0},{2,3},{3,2},{4,5},{5,4},{6,7},{7,6},{8,9},{9,8},{10,11... | collective-permute-start | bytes 245768 | tf_op jit(solution)/shard_map/ppermute | solution.py:288
  17.2 1.3 %collective-permute-start.1 = (bf16[8,40,128]{2,1,0:T(8,128)(2,1)S(1)}, bf16[8,40,128]{2,1,0:T(8,128)(2,1)S(1)}, u32[]{:S(2)}, u32[]{:S(2)}) collective-permute-start(bf16[8,40,128]{2,1,0:T(8,128)(2,1)S(1)} %unpacking.1.carried_ref), channel_id=1, source_target_pairs={{0,1},{1,0},{2,3},{3,2},{4,5},{5,4},{6,7},{7,6},{8,9},{9,8},{10,11... | collective-permute-start | bytes 245768 | tf_op jit(solution)/shard_map/ppermute | solution.py:288

commit v10 on v9

--- a/solution.py
+++ b/solution.py
@@ -52,8 +52,8 @@
 
 
 def group_order(chips):
-    first = chips - 1
-    return [chip ^ first for chip in range(chips)]
+    middle = chips // 2
+    return list(range(chips - 1, middle - 1, -1)) + list(range(middle))
 
 
 def sibling_columns(chip, owned, core):
@@ -82,16 +82,18 @@
     return jnp.concatenate(kept, axis=0).astype(jnp.bfloat16)
 
 
-def half_of_columns(exposure, bits, weights, masked_ref, terms_ref, core, first, last):
-    sets = exposure.shape[0]
-    owned = terms_ref.shape[2]
-    for pair in range(sets // 16):
+def mask_rows(exposure, bits, masked_ref, core, owned, first, last):
+    for pair in range(first // 16, last // 16):
         flags = [row_flags(2 * pair), row_flags(2 * pair + 1)]
-        for chip in range(first, last):
+        for chip in range(masked_ref.shape[1] // owned):
             masked_ref[16 * pair : 16 * pair + 16, chip * owned : (chip + 1) * owned] = masked_rows(
                 exposure, bits, pair, flags, sibling_columns(chip, owned, core)
             )
-    for chip in range(first, last, 2):
+
+
+def sum_sets(weights, masked_ref, terms_ref):
+    owned = terms_ref.shape[2]
+    for chip in range(0, terms_ref.shape[0], 2):
         terms = jnp.dot(
             weights,
             masked_ref[:, chip * owned : (chip + 2) * owned],
@@ -123,9 +125,19 @@
     counts_ref,
     notional_ref,
     sems,
+    exposure_sems,
 ):
     sets = exposure.shape[0]
     chips, currency_count = handed_ref.shape[:2]
+    parts = exposure_sems.shape[0]
+    rows = sets // parts
+
+    def exposure_copy(index):
+        part = pl.ds(index * rows, rows)
+        return pltpu.make_async_copy(
+            exposure_hbm.at[part], exposure.at[part], exposure_sems.at[index]
+        )
+
     copies = [
         pltpu.make_async_copy(source, target, sems.at[index])
         for index, (source, target) in enumerate(
@@ -134,14 +146,17 @@
                 (counts_hbm, counts_ref),
                 (notional_hbm, notional_ref),
                 (bits_hbm, bits),
-                (exposure_hbm, exposure),
                 (rates_hbm, rates_ref),
                 (start_hbm, start_ref),
                 (fx_hbm, fx_ref),
             ]
         )
     ]
-    for copy in copies:
+    for copy in copies[:4]:
+        copy.start()
+    for index in range(parts):
+        exposure_copy(index).start()
+    for copy in copies[4:]:
         copy.start()
     for copy in copies:
         copy.wait()
@@ -158,7 +173,12 @@
     weights = weights.astype(jnp.bfloat16)
     weights_ref[...] = weights
     other = 1 - lax.axis_index("sets") % 2
-    half_of_columns(exposure, bits, weights, masked_ref, handed_ref, other, 0, chips)
+    for index in range(parts):
+        exposure_copy(index).wait()
+        mask_rows(
+            exposure, bits, masked_ref, other, handed_ref.shape[2], index * rows, (index + 1) * rows
+        )
+    sum_sets(weights, masked_ref, handed_ref)
 
 
 def second_kernel(
@@ -181,16 +201,9 @@
     moved = fx_ref[...] * discount
     moved_ref[...] = moved
     carried_ref[...] = moved.astype(jnp.bfloat16)
-    half_of_columns(
-        exposure,
-        bits,
-        weights_ref[...],
-        masked_ref,
-        terms_ref,
-        lax.axis_index("sets") % 2,
-        0,
-        terms_ref.shape[0],
-    )
+    own = lax.axis_index("sets") % 2
+    mask_rows(exposure, bits, masked_ref, own, terms_ref.shape[2], 0, exposure.shape[0])
+    sum_sets(weights_ref[...], masked_ref, terms_ref)
 
 
 def merging_kernel(given_ref, terms_ref, carried_ref, outgoing_ref):
@@ -215,12 +228,12 @@
     sets, half = masked.shape
     chips, currency_count, owned = carried_ref.shape
     here = min(chips, 8)
-    projected = jnp.zeros((sets, currency_count), jnp.float32)
+    projected = jnp.zeros((currency_count, sets), jnp.float32)
     for first in range(0, chips, here):
         carried = jnp.concatenate([carried_ref[first + chip] for chip in range(here)], axis=1)
         projected = projected + lax.dot_general(
+            carried,
             masked[:, first * owned : (first + here) * owned],
-            carried,
             (((1,), (1,)), ((), ())),
             preferred_element_type=jnp.float32,
         )
@@ -250,7 +263,7 @@
 def picking_kernel(carried_ref, masked_other, projected_ref, used_ref, notional_adjoint_ref):
     sets, half = masked_other.shape
     currency_count = carried_ref.shape[1]
-    projected = (projected_ref[...] + projection(masked_other, carried_ref)).T
+    projected = projected_ref[...] + projection(masked_other, carried_ref)
     used = used_ref[...]
     currency = lax.broadcasted_iota(jnp.int32, (currency_count, sets), 0)
     for slot in range(used.shape[0]):
@@ -306,7 +319,8 @@
             pltpu.VMEM((slots, sets), jnp.int32),
             pltpu.VMEM((1, sets), jnp.int32),
             pltpu.VMEM((slots, sets), jnp.float32),
-            pltpu.SemaphoreType.DMA((8,)),
+            pltpu.SemaphoreType.DMA((7,)),
+            pltpu.SemaphoreType.DMA((math.gcd(sets // 16, 5),)),
         ],
         compiler_params=params,
         name="first",
@@ -365,7 +379,7 @@
         out_shape=(
             jax.ShapeDtypeStruct(block, jnp.float32),
             jax.ShapeDtypeStruct(block, jnp.float32),
-            pltpu.VMEM((sets, currency_count), jnp.float32),
+            pltpu.VMEM((currency_count, sets), jnp.float32),
         ),
         in_specs=[in_vmem] * 5,
         out_specs=(in_vmem,) * 3,

time: 19.7 us -> 19.3 us (0.980)
  blocking collectives: 13.3 us -> 13 us
    all_to_all x1, blocking collectives: 13.3 us -> 13 us  [body(): lax.all_to_all(outgoing, 'sets', 0, 0, axis_index_groups=[[2 * chip + cor...]
  transfers between devices with their start and end apart: 2 -> 2, of which waited for: 2 -> 2; matrix products, arithmetic and copies ran while one was open for 0% -> 0% of each run, Pallas kernels for 6% -> 7%
where the time goes in v10:
time: 19.3 us; the launch traced here: 19.1 us
  blocking collectives  13 us (67%)
  Pallas kernels  3.93 us (20%)
  waiting for transfers between devices  0.92 us (5%)
  between operations  0.66 us (3%)
  starting transfers between devices  0.58 us (3%)
    all_to_all x1, blocking collectives, body(): lax.all_to_all(outgoing, 'sets', 0, 0, axis_index_groups=[[2 * chip + cor...  13 us
    pallas_call x1, Pallas kernels, body(): pl.pallas_call(first_kernel, out_shape=(pltpu.VMEM((chips,) + block, jnp....  1.76 us
    ppermute x2, waiting for transfers between devices, swapped(): lax.ppermute(value, 'sets', [(peer, peer ^ 1) for peer in range(peers)])  0.92 us
    pallas_call x1, Pallas kernels, body(): pl.pallas_call(picking_kernel, out_shape=jax.ShapeDtypeStruct((slots, set...  0.88 us
    pallas_call x1, Pallas kernels, body(): pl.pallas_call(functools.partial(adjoint_kernel, dates), out_shape=(jax.S...  0.85 us
    ppermute x2, starting transfers between devices, swapped(): lax.ppermute(value, 'sets', [(peer, peer ^ 1) for peer in range(peers)])  0.58 us
    pallas_call x1, Pallas kernels, body(): pl.pallas_call(functools.partial(second_kernel, dates), out_shape=(pltpu....  0.4 us
  transfers between devices with their start and end apart: 2, of which 2 were waited for; matrix products, arithmetic and copies ran while one was open for 0% of the time, Pallas kernels for 7%

profile of v10, /device:TPU:0, one launch (start us, length us, event | category | flops | bytes accessed | tf_op | source)
XLA Modules:
  0.0 19.1 jit_solution(632981584080476898)
XLA Ops:
  0.6 1.8 %first.1 = (bf16[8,40,128]{2,1,0:T(8,128)(2,1)S(1)}, bf16[240,1024]{1,0:T(8,128)(2,1)S(1)}, bf16[240,2048]{1,0:T(8,128)(2,1)S(1)}, s32[16,2048]{1,0:T(8,128)S(1)...) custom-call(bf16[240,2048]{1,0:T(8,128)(2,1)} %exposure_hbm.1, ...), custom_call_target="tpu_custom_call" | custom-call | tf_op jit(solution)/shard_map/first/pallas_call | solution.py:303
  2.4 0.5 %collective-permute-start = (bf16[8,40,128]{2,1,0:T(8,128)(2,1)S(1)}, bf16[8,40,128]{2,1,0:T(8,128)(2,1)S(1)}, u32[]{:S(2)}, u32[]{:S(2)}) collective-permute-start(bf16[8,40,128]{2,1,0:T(8,128)(2,1)S(1)} %get-tuple-element.20), channel_id=1, source_target_pairs={{0,1},{1,0},{2,3},{3,2},{4,5},{5,4},{6,7},{7,6},{8,9},{9,8},{10,11... | collective-permute-start | bytes 245768 | tf_op jit(solution)/shard_map/ppermute | solution.py:301
  2.9 0.4 %second.1 = (bf16[240,1024]{1,0:T(8,128)(2,1)S(1)}, f32[8,40,128]{2,1,0:T(8,128)S(1)}, bf16[40,128]{1,0:T(8,128)(2,1)S(1)}, f32[40,128]{1,0:T(8,128)S(1)}, f32[40,128]{1,0:T(8,128)S(1)}) custom-call(bf16[240,2048]{1,0:T(8,128)(2,1)S(1)} %get-tuple-element.21.exposure, s32[16,2048]{1,0:T(8,128)S(1)} %get-tuple-element.22.bits, ...), custom_call_target="tpu_custom_call" | custom-call | tf_op jit(solution)/shard_map/second/pallas_call | solution.py:338
  3.3 0.5 %collective-permute-done.given_ref = bf16[8,40,128]{2,1,0:T(8,128)(2,1)S(1)} collective-permute-done((bf16[8,40,128]{2,1,0:T(8,128)(2,1)S(1)}, bf16[8,40,128]{2,1,0:T(8,128)(2,1)S(1)}, u32[]{:S(2)}, u32[]{:S(2)}) %collective-permute-start) | collective-permute-done | bytes 81952 | tf_op jit(solution)/shard_map/ppermute | solution.py:301
  3.9 13.0 %all_to_all.5.arrived_ref = bf16[8,80,128]{2,1,0:T(8,128)(2,1)S(1)} all-to-all(bf16[8,80,128]{2,1,0:T(8,128)(2,1)S(1)} %merging.1), channel_id=1, replica_groups={{14,12,10,8,0,2,4,6},{15,13,11,9,1,3,5,7},{30,28,26,24,16,18,20,22},{31..., dimensions={0} | all-to-all | bytes 327680 | tf_op jit(solution)/shard_map/all_to_all | solution.py:360
  16.9 0.1 collective-permute-start.1
  17.0 0.9 %adjoint.1 = (f32[40,128]{1,0:T(8,128)}, f32[40,128]{1,0:T(8,128)}, f32[40,240]{1,0:T(8,128)S(1)}) custom-call(bf16[8,80,128]{2,1,0:T(8,128)(2,1)S(1)} %all_to_all.5.arrived_ref, bf16[8,40,128]{2,1,0:T(8,128)(2,1)S(1)} %unpacking.1.carried_ref, bf16[240,1024]{1,0:T(8,128)(2,1)S(1)} %get-tuple-element.29.masked_own, ...), custom_call_target="tpu_custom_call" | custom-call | tf_op jit(solution)/shard_map/adjoint/pallas_call | solution.py:377
  17.9 0.4 %collective-permute-done.1.carried_ref = bf16[8,40,128]{2,1,0:T(8,128)(2,1)S(1)} collective-permute-done((bf16[8,40,128]{2,1,0:T(8,128)(2,1)S(1)}, bf16[8,40,128]{2,1,0:T(8,128)(2,1)S(1)}, u32[]{:S(2)}, u32[]{:S(2)}) %collective-permute-start.1) | collective-permute-done | bytes 81952 | tf_op jit(solution)/shard_map/ppermute | solution.py:301
  18.3 0.9 %picking.1 = f32[4,240]{1,0:T(4,128)} custom-call(bf16[8,40,128]{2,1,0:T(8,128)(2,1)S(1)} %collective-permute-done.1.carried_ref, bf16[240,1024]{1,0:T(8,128)(2,1)S(1)} %get-tuple-element.34.masked_other, f32[40,240]{1,0:T(8,128)S(1)} %get-tuple-element.35.projected_ref, s32[4,240]{1,0:T(4,128)S(1)} %get-tuple-element.36.used_ref), custom_call_target="tpu_custom_call" | custom-call | tf_op jit(solution)/shard_map/picking/pallas_call | solution.py:389
  (2 shorter events, 0.0 us)
Async XLA Ops:
  2.4 1.4 %collective-permute-start = (bf16[8,40,128]{2,1,0:T(8,128)(2,1)S(1)}, bf16[8,40,128]{2,1,0:T(8,128)(2,1)S(1)}, u32[]{:S(2)}, u32[]{:S(2)}) collective-permute-start(bf16[8,40,128]{2,1,0:T(8,128)(2,1)S(1)} %get-tuple-element.20), channel_id=1, source_target_pairs={{0,1},{1,0},{2,3},{3,2},{4,5},{5,4},{6,7},{7,6},{8,9},{9,8},{10,11... | collective-permute-start | bytes 245768 | tf_op jit(solution)/shard_map/ppermute | solution.py:301
  16.9 1.3 %collective-permute-start.1 = (bf16[8,40,128]{2,1,0:T(8,128)(2,1)S(1)}, bf16[8,40,128]{2,1,0:T(8,128)(2,1)S(1)}, u32[]{:S(2)}, u32[]{:S(2)}) collective-permute-start(bf16[8,40,128]{2,1,0:T(8,128)(2,1)S(1)} %unpacking.1.carried_ref), channel_id=1, source_target_pairs={{0,1},{1,0},{2,3},{3,2},{4,5},{5,4},{6,7},{7,6},{8,9},{9,8},{10,11... | collective-permute-start | bytes 245768 | tf_op jit(solution)/shard_map/ppermute | solution.py:301

commit v11 on v10

--- a/solution.py
+++ b/solution.py
@@ -66,28 +66,28 @@
     return jnp.left_shift(jnp.int32(1), shift)
 
 
-def masked_rows(exposure, bits, pair, flags, part):
+def masked_rows(exposure, bits, pair, flags, column, packed_columns):
     row = lax.broadcasted_iota(jnp.int32, (8, lanes), 0)
-    values = exposure[16 * pair : 16 * pair + 16, part].astype(jnp.float32)
+    values = exposure[16 * pair : 16 * pair + 16, column : column + lanes].astype(jnp.float32)
     kept = []
     for half in range(2):
         top = 16 * pair + 8 * half
         group = top // bits_per_row
         left = bits_per_row * (group + 1) - top
-        packed = jnp.broadcast_to(bits[group : group + 1, part], (8, lanes))
+        packed = jnp.broadcast_to(bits[group : group + 1, packed_columns], (8, lanes))
         if left < 8:
-            following = jnp.broadcast_to(bits[group + 1 : group + 2, part], (8, lanes))
+            following = jnp.broadcast_to(bits[group + 1 : group + 2, packed_columns], (8, lanes))
             packed = jnp.where(row < left, packed, following)
         kept.append(jnp.where((packed & flags[half]) != 0, values[8 * half : 8 * half + 8], 0.0))
     return jnp.concatenate(kept, axis=0).astype(jnp.bfloat16)
 
 
-def mask_rows(exposure, bits, masked_ref, core, owned, first, last):
-    for pair in range(first // 16, last // 16):
+def mask_blocks(exposure, bits, masked_ref, core, owned, blocks):
+    for pair in range(masked_ref.shape[0] // 16):
         flags = [row_flags(2 * pair), row_flags(2 * pair + 1)]
-        for chip in range(masked_ref.shape[1] // owned):
+        for chip in blocks:
             masked_ref[16 * pair : 16 * pair + 16, chip * owned : (chip + 1) * owned] = masked_rows(
-                exposure, bits, pair, flags, sibling_columns(chip, owned, core)
+                exposure, bits, pair, flags, chip * owned, sibling_columns(chip, owned, core)
             )
 
 
@@ -114,28 +114,31 @@
     start_hbm,
     handed_ref,
     masked_ref,
-    exposure,
+    exposure_own,
     bits,
     weights_ref,
     used_ref,
     fx_ref,
     rates_ref,
     start_ref,
+    exposure_other,
     currencies_ref,
     counts_ref,
     notional_ref,
     sems,
-    exposure_sems,
+    own_sems,
+    other_sems,
 ):
-    sets = exposure.shape[0]
-    chips, currency_count = handed_ref.shape[:2]
-    parts = exposure_sems.shape[0]
-    rows = sets // parts
-
-    def exposure_copy(index):
-        part = pl.ds(index * rows, rows)
+    sets = exposure_own.shape[0]
+    chips, currency_count, owned = handed_ref.shape
+    own = lax.axis_index("sets") % 2
+    other = 1 - own
+
+    def block_copy(chip, core, target, block_sems):
         return pltpu.make_async_copy(
-            exposure_hbm.at[part], exposure.at[part], exposure_sems.at[index]
+            exposure_hbm.at[:, sibling_columns(chip, owned, core)],
+            target.at[:, pl.ds(chip * owned, owned)],
+            block_sems.at[chip],
         )
 
     copies = [
@@ -154,11 +157,13 @@
     ]
     for copy in copies[:4]:
         copy.start()
-    for index in range(parts):
-        exposure_copy(index).start()
+    for chip in range(chips):
+        block_copy(chip, other, exposure_other, other_sems).start()
+    for chip in range(chips):
+        block_copy(chip, own, exposure_own, own_sems).start()
     for copy in copies[4:]:
         copy.start()
-    for copy in copies:
+    for copy in copies[:4]:
         copy.wait()
 
     used = used_currencies(currencies_ref[...], counts_ref[...])
@@ -172,13 +177,18 @@
         )
     weights = weights.astype(jnp.bfloat16)
     weights_ref[...] = weights
-    other = 1 - lax.axis_index("sets") % 2
-    for index in range(parts):
-        exposure_copy(index).wait()
-        mask_rows(
-            exposure, bits, masked_ref, other, handed_ref.shape[2], index * rows, (index + 1) * rows
+    step = 2
+    for first in range(0, chips, step):
+        for chip in range(first, first + step):
+            block_copy(chip, other, exposure_other, other_sems).wait()
+        mask_blocks(
+            exposure_other, bits, masked_ref, other, owned, range(first, first + step)
         )
     sum_sets(weights, masked_ref, handed_ref)
+    for chip in range(chips):
+        block_copy(chip, own, exposure_own, own_sems).wait()
+    for copy in copies[4:]:
+        copy.wait()
 
 
 def second_kernel(
@@ -202,7 +212,8 @@
     moved_ref[...] = moved
     carried_ref[...] = moved.astype(jnp.bfloat16)
     own = lax.axis_index("sets") % 2
-    mask_rows(exposure, bits, masked_ref, own, terms_ref.shape[2], 0, exposure.shape[0])
+    chips, currency_count, owned = terms_ref.shape
+    mask_blocks(exposure, bits, masked_ref, own, owned, range(chips))
     sum_sets(weights_ref[...], masked_ref, terms_ref)
 
 
@@ -305,7 +316,7 @@
         out_shape=(
             pltpu.VMEM((chips,) + block, jnp.bfloat16),
             pltpu.VMEM((sets, columns // 2), jnp.bfloat16),
-            pltpu.VMEM((sets, columns), jnp.bfloat16),
+            pltpu.VMEM((sets, columns // 2), jnp.bfloat16),
             pltpu.VMEM(positive_bits.shape, jnp.int32),
             pltpu.VMEM((currency_count, sets), jnp.bfloat16),
             pltpu.VMEM((slots, sets), jnp.int32),
@@ -316,11 +327,13 @@
         in_specs=[anywhere] * 8,
         out_specs=(in_vmem,) * 9,
         scratch_shapes=[
+            pltpu.VMEM((sets, columns // 2), jnp.bfloat16),
             pltpu.VMEM((slots, sets), jnp.int32),
             pltpu.VMEM((1, sets), jnp.int32),
             pltpu.VMEM((slots, sets), jnp.float32),
             pltpu.SemaphoreType.DMA((7,)),
-            pltpu.SemaphoreType.DMA((math.gcd(sets // 16, 5),)),
+            pltpu.SemaphoreType.DMA((chips,)),
+            pltpu.SemaphoreType.DMA((chips,)),
         ],
         compiler_params=params,
         name="first",

time: 19.3 us -> 19.5 us (1.010)
  no operation moved by 1% of the time
where the time goes in v11:
time: 19.5 us; the launch traced here: 19.2 us
  blocking collectives  13 us (67%)
  Pallas kernels  4.02 us (21%)
  waiting for transfers between devices  0.93 us (5%)
  between operations  0.66 us (3%)
  starting transfers between devices  0.59 us (3%)
    all_to_all x1, blocking collectives, body(): lax.all_to_all(outgoing, 'sets', 0, 0, axis_index_groups=[[2 * chip + cor...  13 us
    pallas_call x1, Pallas kernels, body(): pl.pallas_call(first_kernel, out_shape=(pltpu.VMEM((chips,) + block, jnp....  1.86 us
    ppermute x2, waiting for transfers between devices, swapped(): lax.ppermute(value, 'sets', [(peer, peer ^ 1) for peer in range(peers)])  0.93 us
    pallas_call x1, Pallas kernels, body(): pl.pallas_call(picking_kernel, out_shape=jax.ShapeDtypeStruct((slots, set...  0.88 us
    pallas_call x1, Pallas kernels, body(): pl.pallas_call(functools.partial(adjoint_kernel, dates), out_shape=(jax.S...  0.85 us
    ppermute x2, starting transfers between devices, swapped(): lax.ppermute(value, 'sets', [(peer, peer ^ 1) for peer in range(peers)])  0.59 us
    pallas_call x1, Pallas kernels, body(): pl.pallas_call(functools.partial(second_kernel, dates), out_shape=(pltpu....  0.4 us
  transfers between devices with their start and end apart: 2, of which 2 were waited for; matrix products, arithmetic and copies ran while one was open for 0% of the time, Pallas kernels for 7%

profile of v11, /device:TPU:0, one launch (start us, length us, event | category | flops | bytes accessed | tf_op | source)
XLA Modules:
  0.0 19.2 jit_solution(2255072452068235769)
XLA Ops:
  0.6 1.9 %first.1 = (bf16[8,40,128]{2,1,0:T(8,128)(2,1)S(1)}, bf16[240,1024]{1,0:T(8,128)(2,1)S(1)}, bf16[240,1024]{1,0:T(8,128)(2,1)S(1)}, s32[16,2048]{1,0:T(8,128)S(1)...) custom-call(bf16[240,2048]{1,0:T(8,128)(2,1)} %exposure_hbm.1, ...), custom_call_target="tpu_custom_call" | custom-call | tf_op jit(solution)/shard_map/first/pallas_call | solution.py:314
  2.5 0.5 %collective-permute-start = (bf16[8,40,128]{2,1,0:T(8,128)(2,1)S(1)}, bf16[8,40,128]{2,1,0:T(8,128)(2,1)S(1)}, u32[]{:S(2)}, u32[]{:S(2)}) collective-permute-start(bf16[8,40,128]{2,1,0:T(8,128)(2,1)S(1)} %get-tuple-element.20), channel_id=1, source_target_pairs={{0,1},{1,0},{2,3},{3,2},{4,5},{5,4},{6,7},{7,6},{8,9},{9,8},{10,11... | collective-permute-start | bytes 245768 | tf_op jit(solution)/shard_map/ppermute | solution.py:312
  3.0 0.4 %second.1 = (bf16[240,1024]{1,0:T(8,128)(2,1)S(1)}, f32[8,40,128]{2,1,0:T(8,128)S(1)}, bf16[40,128]{1,0:T(8,128)(2,1)S(1)}, f32[40,128]{1,0:T(8,128)S(1)}, f32[40,128]{1,0:T(8,128)S(1)}) custom-call(bf16[240,1024]{1,0:T(8,128)(2,1)S(1)} %get-tuple-element.21.exposure, s32[16,2048]{1,0:T(8,128)S(1)} %get-tuple-element.22.bits, ...), custom_call_target="tpu_custom_call" | custom-call | tf_op jit(solution)/shard_map/second/pallas_call | solution.py:351
  3.4 0.5 %collective-permute-done.given_ref = bf16[8,40,128]{2,1,0:T(8,128)(2,1)S(1)} collective-permute-done((bf16[8,40,128]{2,1,0:T(8,128)(2,1)S(1)}, bf16[8,40,128]{2,1,0:T(8,128)(2,1)S(1)}, u32[]{:S(2)}, u32[]{:S(2)}) %collective-permute-start) | collective-permute-done | bytes 81952 | tf_op jit(solution)/shard_map/ppermute | solution.py:312
  4.0 13.0 %all_to_all.5.arrived_ref = bf16[8,80,128]{2,1,0:T(8,128)(2,1)S(1)} all-to-all(bf16[8,80,128]{2,1,0:T(8,128)(2,1)S(1)} %merging.1), channel_id=1, replica_groups={{14,12,10,8,0,2,4,6},{15,13,11,9,1,3,5,7},{30,28,26,24,16,18,20,22},{31..., dimensions={0} | all-to-all | bytes 327680 | tf_op jit(solution)/shard_map/all_to_all | solution.py:373
  17.0 0.1 collective-permute-start.1
  17.1 0.9 %adjoint.1 = (f32[40,128]{1,0:T(8,128)}, f32[40,128]{1,0:T(8,128)}, f32[40,240]{1,0:T(8,128)S(1)}) custom-call(bf16[8,80,128]{2,1,0:T(8,128)(2,1)S(1)} %all_to_all.5.arrived_ref, bf16[8,40,128]{2,1,0:T(8,128)(2,1)S(1)} %unpacking.1.carried_ref, bf16[240,1024]{1,0:T(8,128)(2,1)S(1)} %get-tuple-element.29.masked_own, ...), custom_call_target="tpu_custom_call" | custom-call | tf_op jit(solution)/shard_map/adjoint/pallas_call | solution.py:390
  17.9 0.4 %collective-permute-done.1.carried_ref = bf16[8,40,128]{2,1,0:T(8,128)(2,1)S(1)} collective-permute-done((bf16[8,40,128]{2,1,0:T(8,128)(2,1)S(1)}, bf16[8,40,128]{2,1,0:T(8,128)(2,1)S(1)}, u32[]{:S(2)}, u32[]{:S(2)}) %collective-permute-start.1) | collective-permute-done | bytes 81952 | tf_op jit(solution)/shard_map/ppermute | solution.py:312
  18.4 0.9 %picking.1 = f32[4,240]{1,0:T(4,128)} custom-call(bf16[8,40,128]{2,1,0:T(8,128)(2,1)S(1)} %collective-permute-done.1.carried_ref, bf16[240,1024]{1,0:T(8,128)(2,1)S(1)} %get-tuple-element.34.masked_other, f32[40,240]{1,0:T(8,128)S(1)} %get-tuple-element.35.projected_ref, s32[4,240]{1,0:T(4,128)S(1)} %get-tuple-element.36.used_ref), custom_call_target="tpu_custom_call" | custom-call | tf_op jit(solution)/shard_map/picking/pallas_call | solution.py:402
  (2 shorter events, 0.0 us)
Async XLA Ops:
  2.5 1.4 %collective-permute-start = (bf16[8,40,128]{2,1,0:T(8,128)(2,1)S(1)}, bf16[8,40,128]{2,1,0:T(8,128)(2,1)S(1)}, u32[]{:S(2)}, u32[]{:S(2)}) collective-permute-start(bf16[8,40,128]{2,1,0:T(8,128)(2,1)S(1)} %get-tuple-element.20), channel_id=1, source_target_pairs={{0,1},{1,0},{2,3},{3,2},{4,5},{5,4},{6,7},{7,6},{8,9},{9,8},{10,11... | collective-permute-start | bytes 245768 | tf_op jit(solution)/shard_map/ppermute | solution.py:312
  17.0 1.3 %collective-permute-start.1 = (bf16[8,40,128]{2,1,0:T(8,128)(2,1)S(1)}, bf16[8,40,128]{2,1,0:T(8,128)(2,1)S(1)}, u32[]{:S(2)}, u32[]{:S(2)}) collective-permute-start(bf16[8,40,128]{2,1,0:T(8,128)(2,1)S(1)} %unpacking.1.carried_ref), channel_id=1, source_target_pairs={{0,1},{1,0},{2,3},{3,2},{4,5},{5,4},{6,7},{7,6},{8,9},{9,8},{10,11... | collective-permute-start | bytes 245768 | tf_op jit(solution)/shard_map/ppermute | solution.py:312

commit v12 on v11

--- a/solution.py
+++ b/solution.py
@@ -103,44 +103,38 @@
         terms_ref[chip + 1] = terms[:, owned:]
 
 
+def block_copies(exposure_hbm, exposure, sems, core, owned):
+    return [
+        pltpu.make_async_copy(
+            exposure_hbm.at[:, sibling_columns(chip, owned, core)],
+            exposure.at[:, pl.ds(chip * owned, owned)],
+            sems.at[chip],
+        )
+        for chip in range(exposure.shape[1] // owned)
+    ]
+
+
 def first_kernel(
     exposure_hbm,
     bits_hbm,
     currencies_hbm,
     counts_hbm,
     notional_hbm,
-    fx_hbm,
-    rates_hbm,
-    start_hbm,
     handed_ref,
     masked_ref,
-    exposure_own,
     bits,
     weights_ref,
     used_ref,
-    fx_ref,
-    rates_ref,
-    start_ref,
-    exposure_other,
+    exposure,
     currencies_ref,
     counts_ref,
     notional_ref,
     sems,
-    own_sems,
-    other_sems,
+    exposure_sems,
 ):
-    sets = exposure_own.shape[0]
+    sets = exposure.shape[0]
     chips, currency_count, owned = handed_ref.shape
-    own = lax.axis_index("sets") % 2
-    other = 1 - own
-
-    def block_copy(chip, core, target, block_sems):
-        return pltpu.make_async_copy(
-            exposure_hbm.at[:, sibling_columns(chip, owned, core)],
-            target.at[:, pl.ds(chip * owned, owned)],
-            block_sems.at[chip],
-        )
-
+    other = 1 - lax.axis_index("sets") % 2
     copies = [
         pltpu.make_async_copy(source, target, sems.at[index])
         for index, (source, target) in enumerate(
@@ -149,21 +143,15 @@
                 (counts_hbm, counts_ref),
                 (notional_hbm, notional_ref),
                 (bits_hbm, bits),
-                (rates_hbm, rates_ref),
-                (start_hbm, start_ref),
-                (fx_hbm, fx_ref),
             ]
         )
     ]
-    for copy in copies[:4]:
+    exposure_copies = block_copies(exposure_hbm, exposure, exposure_sems, other, owned)
+    for copy in copies:
         copy.start()
-    for chip in range(chips):
-        block_copy(chip, other, exposure_other, other_sems).start()
-    for chip in range(chips):
-        block_copy(chip, own, exposure_own, own_sems).start()
-    for copy in copies[4:]:
+    for copy in exposure_copies:
         copy.start()
-    for copy in copies[:4]:
+    for copy in copies:
         copy.wait()
 
     used = used_currencies(currencies_ref[...], counts_ref[...])
@@ -179,40 +167,53 @@
     weights_ref[...] = weights
     step = 2
     for first in range(0, chips, step):
-        for chip in range(first, first + step):
-            block_copy(chip, other, exposure_other, other_sems).wait()
-        mask_blocks(
-            exposure_other, bits, masked_ref, other, owned, range(first, first + step)
-        )
+        for copy in exposure_copies[first : first + step]:
+            copy.wait()
+        mask_blocks(exposure, bits, masked_ref, other, owned, range(first, first + step))
     sum_sets(weights, masked_ref, handed_ref)
-    for chip in range(chips):
-        block_copy(chip, own, exposure_own, own_sems).wait()
-    for copy in copies[4:]:
-        copy.wait()
 
 
 def second_kernel(
     dates,
-    exposure,
+    exposure_hbm,
+    fx_hbm,
+    rates_hbm,
+    start_hbm,
     bits,
     weights_ref,
-    fx_ref,
-    rates_ref,
-    start_ref,
     masked_ref,
     terms_ref,
     carried_ref,
     discount_ref,
     moved_ref,
+    exposure,
+    fx_ref,
+    rates_ref,
+    start_ref,
+    sems,
+    exposure_sems,
 ):
+    chips, currency_count, owned = terms_ref.shape
+    own = lax.axis_index("sets") % 2
+    copies = [
+        pltpu.make_async_copy(source, target, sems.at[index])
+        for index, (source, target) in enumerate(
+            [(rates_hbm, rates_ref), (start_hbm, start_ref), (fx_hbm, fx_ref)]
+        )
+    ]
+    exposure_copies = block_copies(exposure_hbm, exposure, exposure_sems, own, owned)
+    for copy in copies + exposure_copies:
+        copy.start()
+    for copy in copies:
+        copy.wait()
     integral = spread_paths(start_ref[...], dates) + step_years * sums_to_date(rates_ref[...], dates)
     discount = jnp.exp(-integral)
     discount_ref[...] = discount
     moved = fx_ref[...] * discount
     moved_ref[...] = moved
     carried_ref[...] = moved.astype(jnp.bfloat16)
-    own = lax.axis_index("sets") % 2
-    chips, currency_count, owned = terms_ref.shape
+    for copy in exposure_copies:
+        copy.wait()
     mask_blocks(exposure, bits, masked_ref, own, owned, range(chips))
     sum_sets(weights_ref[...], masked_ref, terms_ref)
 
@@ -311,41 +312,34 @@
     def swapped(value):
         return lax.ppermute(value, "sets", [(peer, peer ^ 1) for peer in range(peers)])
 
-    handed, masked_other, exposure, bits, weights, used, fx, rates, start = pl.pallas_call(
+    exposure_adjoint = in_hbm(exposure_adjoint)
+    handed, masked_other, bits, weights, used = pl.pallas_call(
         first_kernel,
         out_shape=(
             pltpu.VMEM((chips,) + block, jnp.bfloat16),
             pltpu.VMEM((sets, columns // 2), jnp.bfloat16),
-            pltpu.VMEM((sets, columns // 2), jnp.bfloat16),
             pltpu.VMEM(positive_bits.shape, jnp.int32),
             pltpu.VMEM((currency_count, sets), jnp.bfloat16),
             pltpu.VMEM((slots, sets), jnp.int32),
-            pltpu.VMEM(block, jnp.float32),
-            pltpu.VMEM(block, jnp.float32),
-            pltpu.VMEM((owned // dates, currency_count), jnp.float32),
         ),
-        in_specs=[anywhere] * 8,
-        out_specs=(in_vmem,) * 9,
+        in_specs=[anywhere] * 5,
+        out_specs=(in_vmem,) * 5,
         scratch_shapes=[
             pltpu.VMEM((sets, columns // 2), jnp.bfloat16),
             pltpu.VMEM((slots, sets), jnp.int32),
             pltpu.VMEM((1, sets), jnp.int32),
             pltpu.VMEM((slots, sets), jnp.float32),
-            pltpu.SemaphoreType.DMA((7,)),
-            pltpu.SemaphoreType.DMA((chips,)),
+            pltpu.SemaphoreType.DMA((4,)),
             pltpu.SemaphoreType.DMA((chips,)),
         ],
         compiler_params=params,
         name="first",
     )(
-        in_hbm(exposure_adjoint),
+        exposure_adjoint,
         in_hbm(positive_bits),
         in_hbm(currencies.T),
         in_hbm(mix_count.reshape(1, sets)),
         in_hbm(notional.T),
-        in_hbm(fx_paths),
-        in_hbm(short_rates),
-        in_hbm(start_integral.T),
     )
     given = swapped(handed)
     masked_own, terms, carried, discount, moved = pl.pallas_call(
@@ -357,11 +351,26 @@
             pltpu.VMEM(block, jnp.float32),
             pltpu.VMEM(block, jnp.float32),
         ),
-        in_specs=[in_vmem] * 6,
+        in_specs=[anywhere] * 4 + [in_vmem] * 2,
         out_specs=(in_vmem,) * 5,
+        scratch_shapes=[
+            pltpu.VMEM((sets, columns // 2), jnp.bfloat16),
+            pltpu.VMEM(block, jnp.float32),
+            pltpu.VMEM(block, jnp.float32),
+            pltpu.VMEM((owned // dates, currency_count), jnp.float32),
+            pltpu.SemaphoreType.DMA((3,)),
+            pltpu.SemaphoreType.DMA((chips,)),
+        ],
         compiler_params=params,
         name="second",
-    )(exposure, bits, weights, fx, rates, start)
+    )(
+        exposure_adjoint,
+        in_hbm(fx_paths),
+        in_hbm(short_rates),
+        in_hbm(start_integral.T),
+        bits,
+        weights,
+    )
     outgoing = pl.pallas_call(
         merging_kernel,
         out_shape=pltpu.VMEM((chips, 2 * currency_count, owned), jnp.bfloat16),

time: 19.5 us -> 20 us (1.026)
  Pallas kernels: 4.02 us -> 5.21 us
  waiting for transfers between devices: 0.93 us -> 0.41 us
    pallas_call x1, Pallas kernels: 0.4 us -> 1.74 us  [body(): pl.pallas_call(functools.partial(second_kernel, dates), out_shape=(pltpu....]
    ppermute x2, waiting for transfers between devices: 0.93 us -> 0.41 us  [swapped(): lax.ppermute(value, 'sets', [(peer, peer ^ 1) for peer in range(peers)])]
  transfers between devices with their start and end apart: 2 -> 2, of which waited for: 2 -> 1; matrix products, arithmetic and copies ran while one was open for 0% -> 0% of each run, Pallas kernels for 7% -> 13%
where the time goes in v12:
time: 20 us; the launch traced here: 19.8 us
  blocking collectives  12.9 us (64%)
  Pallas kernels  5.21 us (26%)
  between operations  0.67 us (3%)
  starting transfers between devices  0.61 us (3%)
  waiting for transfers between devices  0.41 us (2%)
    all_to_all x1, blocking collectives, body(): lax.all_to_all(outgoing, 'sets', 0, 0, axis_index_groups=[[2 * chip + cor...  12.9 us
    pallas_call x1, Pallas kernels, body(): pl.pallas_call(functools.partial(second_kernel, dates), out_shape=(pltpu....  1.74 us
    pallas_call x1, Pallas kernels, body(): pl.pallas_call(first_kernel, out_shape=(pltpu.VMEM((chips,) + block, jnp....  1.71 us
    pallas_call x1, Pallas kernels, body(): pl.pallas_call(picking_kernel, out_shape=jax.ShapeDtypeStruct((slots, set...  0.88 us
    pallas_call x1, Pallas kernels, body(): pl.pallas_call(functools.partial(adjoint_kernel, dates), out_shape=(jax.S...  0.85 us
    ppermute x2, starting transfers between devices, swapped(): lax.ppermute(value, 'sets', [(peer, peer ^ 1) for peer in range(peers)])  0.61 us
    ppermute x2, waiting for transfers between devices, swapped(): lax.ppermute(value, 'sets', [(peer, peer ^ 1) for peer in range(peers)])  0.41 us
  transfers between devices with their start and end apart: 2, of which 1 were waited for; matrix products, arithmetic and copies ran while one was open for 0% of the time, Pallas kernels for 13%

profile of v12, /device:TPU:0, one launch (start us, length us, event | category | flops | bytes accessed | tf_op | source)
XLA Modules:
  0.0 19.8 jit_solution(6497450247821122351)
XLA Ops:
  0.6 1.7 %first.1 = (bf16[8,40,128]{2,1,0:T(8,128)(2,1)S(1)}, bf16[240,1024]{1,0:T(8,128)(2,1)S(1)}, s32[16,2048]{1,0:T(8,128)S(1)}, bf16[40,240]{1,0:T(8,128)(2,1)S(1)}, s32[4,240]{1,0:T(4,128)S(1)}) custom-call(bf16[240,2048]{1,0:T(8,128)(2,1)} %exposure_hbm.3, s32[16,2048]{1,0:T(8,128)} %bits_hbm.1, s32[4,240]{1,0:T(4,128)} %bitcast.6, s32[1,240]{1,0:T(1,128)} %bitcast.9, ...), custom_call_target="tpu_custom_call" | custom-call | tf_op jit(solution)/shard_map/first/pallas_call | solution.py:316
  2.3 0.5 %collective-permute-start = (bf16[8,40,128]{2,1,0:T(8,128)(2,1)S(1)}, bf16[8,40,128]{2,1,0:T(8,128)(2,1)S(1)}, u32[]{:S(2)}, u32[]{:S(2)}) collective-permute-start(bf16[8,40,128]{2,1,0:T(8,128)(2,1)S(1)} %get-tuple-element.16), channel_id=1, source_target_pairs={{0,1},{1,0},{2,3},{3,2},{4,5},{5,4},{6,7},{7,6},{8,9},{9,8},{10,11... | collective-permute-start | bytes 245768 | tf_op jit(solution)/shard_map/ppermute | solution.py:313
  2.9 1.7 %second.1 = (bf16[240,1024]{1,0:T(8,128)(2,1)S(1)}, f32[8,40,128]{2,1,0:T(8,128)S(1)}, bf16[40,128]{1,0:T(8,128)(2,1)S(1)}, f32[40,128]{1,0:T(8,128)S(1)}, f32[40,128]{1,0:T(8,128)S(1)}) custom-call(bf16[240,2048]{1,0:T(8,128)(2,1)} %exposure_hbm.3, f32[40,128]{1,0:T(8,128)} %fx_hbm.1, f32[40,128]{1,0:T(8,128)} %rates_hbm.1, f32[16,40]{1,0:T(8,128)} %bitcast.5, ...), custom_call_target="tpu_custom_call" | custom-call | tf_op jit(solution)/shard_map/second/pallas_call | solution.py:345
  4.6 0.0 collective-permute-done.given_ref
  4.7 12.9 %all_to_all.5.arrived_ref = bf16[8,80,128]{2,1,0:T(8,128)(2,1)S(1)} all-to-all(bf16[8,80,128]{2,1,0:T(8,128)(2,1)S(1)} %merging.1), channel_id=1, replica_groups={{14,12,10,8,0,2,4,6},{15,13,11,9,1,3,5,7},{30,28,26,24,16,18,20,22},{31..., dimensions={0} | all-to-all | bytes 327680 | tf_op jit(solution)/shard_map/all_to_all | solution.py:382
  17.5 0.1 collective-permute-start.1
  17.6 0.8 %adjoint.1 = (f32[40,128]{1,0:T(8,128)}, f32[40,128]{1,0:T(8,128)}, f32[40,240]{1,0:T(8,128)S(1)}) custom-call(bf16[8,80,128]{2,1,0:T(8,128)(2,1)S(1)} %all_to_all.5.arrived_ref, bf16[8,40,128]{2,1,0:T(8,128)(2,1)S(1)} %unpacking.1.carried_ref, bf16[240,1024]{1,0:T(8,128)(2,1)S(1)} %get-tuple-element.21.masked_own, ...), custom_call_target="tpu_custom_call" | custom-call | tf_op jit(solution)/shard_map/adjoint/pallas_call | solution.py:399
  18.5 0.4 %collective-permute-done.1.carried_ref = bf16[8,40,128]{2,1,0:T(8,128)(2,1)S(1)} collective-permute-done((bf16[8,40,128]{2,1,0:T(8,128)(2,1)S(1)}, bf16[8,40,128]{2,1,0:T(8,128)(2,1)S(1)}, u32[]{:S(2)}, u32[]{:S(2)}) %collective-permute-start.1) | collective-permute-done | bytes 81952 | tf_op jit(solution)/shard_map/ppermute | solution.py:313
  18.9 0.9 %picking.1 = f32[4,240]{1,0:T(4,128)} custom-call(bf16[8,40,128]{2,1,0:T(8,128)(2,1)S(1)} %collective-permute-done.1.carried_ref, bf16[240,1024]{1,0:T(8,128)(2,1)S(1)} %get-tuple-element.26.masked_other, f32[40,240]{1,0:T(8,128)S(1)} %get-tuple-element.27.projected_ref, s32[4,240]{1,0:T(4,128)S(1)} %get-tuple-element.28.used_ref), custom_call_target="tpu_custom_call" | custom-call | tf_op jit(solution)/shard_map/picking/pallas_call | solution.py:411
  (2 shorter events, 0.0 us)
Async XLA Ops:
  2.3 2.3 %collective-permute-start = (bf16[8,40,128]{2,1,0:T(8,128)(2,1)S(1)}, bf16[8,40,128]{2,1,0:T(8,128)(2,1)S(1)}, u32[]{:S(2)}, u32[]{:S(2)}) collective-permute-start(bf16[8,40,128]{2,1,0:T(8,128)(2,1)S(1)} %get-tuple-element.16), channel_id=1, source_target_pairs={{0,1},{1,0},{2,3},{3,2},{4,5},{5,4},{6,7},{7,6},{8,9},{9,8},{10,11... | collective-permute-start | bytes 245768 | tf_op jit(solution)/shard_map/ppermute | solution.py:313
  17.5 1.3 %collective-permute-start.1 = (bf16[8,40,128]{2,1,0:T(8,128)(2,1)S(1)}, bf16[8,40,128]{2,1,0:T(8,128)(2,1)S(1)}, u32[]{:S(2)}, u32[]{:S(2)}) collective-permute-start(bf16[8,40,128]{2,1,0:T(8,128)(2,1)S(1)} %unpacking.1.carried_ref), channel_id=1, source_target_pairs={{0,1},{1,0},{2,3},{3,2},{4,5},{5,4},{6,7},{7,6},{8,9},{9,8},{10,11... | collective-permute-start | bytes 245768 | tf_op jit(solution)/shard_map/ppermute | solution.py:313

commit v13 on v10

--- a/solution.py
+++ b/solution.py
@@ -155,7 +155,7 @@
     for copy in copies[:4]:
         copy.start()
     for index in range(parts):
-        exposure_copy(index).start()
+        exposure_copy(index).start(priority=index % 2)
     for copy in copies[4:]:
         copy.start()
     for copy in copies:
@@ -217,24 +217,29 @@
         ).astype(jnp.bfloat16)
 
 
-def unpacking_kernel(arrived_ref, carried_ref):
+def unpacking_kernel(arrived_ref, turned_own, turned_other, carried_ref):
     chips, currency_count, owned = carried_ref.shape
     order = group_order(chips)
     for place in range(chips):
         carried_ref[order[place]] = arrived_ref[place, 0:currency_count, :]
 
 
-def projection(masked, carried_ref):
-    sets, half = masked.shape
+def turning_kernel(masked_own, masked_other, turned_own, turned_other):
+    for masked, turned in ((masked_own, turned_own), (masked_other, turned_other)):
+        for column in range(0, masked.shape[1], lanes):
+            turned[column : column + lanes, :] = masked[:, column : column + lanes].T
+
+
+def projection(turned, carried_ref):
+    half, sets = turned.shape
     chips, currency_count, owned = carried_ref.shape
     here = min(chips, 8)
     projected = jnp.zeros((currency_count, sets), jnp.float32)
     for first in range(0, chips, here):
         carried = jnp.concatenate([carried_ref[first + chip] for chip in range(here)], axis=1)
-        projected = projected + lax.dot_general(
+        projected = projected + jnp.dot(
             carried,
-            masked[:, first * owned : (first + here) * owned],
-            (((1,), (1,)), ((), ())),
+            turned[first * owned : (first + here) * owned, :],
             preferred_element_type=jnp.float32,
         )
     return projected
@@ -244,7 +249,7 @@
     dates,
     arrived_ref,
     carried_ref,
-    masked_own,
+    turned_own,
     moved_ref,
     discount_ref,
     fx_adjoint_ref,
@@ -257,13 +262,13 @@
         aggregate = aggregate + arrived_ref[chip, currency_count:, :].astype(jnp.float32)
     fx_adjoint_ref[...] = aggregate * discount_ref[...]
     rate_adjoint_ref[...] = -step_years * sums_from_date(aggregate * moved_ref[...], dates)
-    projected_ref[...] = projection(masked_own, carried_ref)
-
-
-def picking_kernel(carried_ref, masked_other, projected_ref, used_ref, notional_adjoint_ref):
-    sets, half = masked_other.shape
+    projected_ref[...] = projection(turned_own, carried_ref)
+
+
+def picking_kernel(carried_ref, turned_other, projected_ref, used_ref, notional_adjoint_ref):
+    half, sets = turned_other.shape
     currency_count = carried_ref.shape[1]
-    projected = projected_ref[...] + projection(masked_other, carried_ref)
+    projected = projected_ref[...] + projection(turned_other, carried_ref)
     used = used_ref[...]
     currency = lax.broadcasted_iota(jnp.int32, (currency_count, sets), 0)
     for slot in range(used.shape[0]):
@@ -365,14 +370,22 @@
         axis_index_groups=[[2 * chip + core for chip in group_order(chips)] for core in range(2)],
         tiled=True,
     )
+    turned_own, turned_other = pl.pallas_call(
+        turning_kernel,
+        out_shape=(pltpu.VMEM((columns // 2, sets), jnp.bfloat16),) * 2,
+        in_specs=[in_vmem] * 2,
+        out_specs=(in_vmem,) * 2,
+        compiler_params=params,
+        name="turning",
+    )(masked_own, masked_other)
     carried_own = pl.pallas_call(
         unpacking_kernel,
         out_shape=pltpu.VMEM((chips,) + block, jnp.bfloat16),
-        in_specs=[in_vmem],
+        in_specs=[in_vmem, anywhere, anywhere],
         out_specs=in_vmem,
         compiler_params=params,
         name="unpacking",
-    )(arrived)
+    )(arrived, turned_own, turned_other)
     carried_other = swapped(carried_own)
     fx_adjoint, rate_adjoint, projected = pl.pallas_call(
         functools.partial(adjoint_kernel, dates),
@@ -385,7 +398,7 @@
         out_specs=(in_vmem,) * 3,
         compiler_params=params,
         name="adjoint",
-    )(arrived, carried_own, masked_own, moved, discount)
+    )(arrived, carried_own, turned_own, moved, discount)
     notional_adjoint = pl.pallas_call(
         picking_kernel,
         out_shape=jax.ShapeDtypeStruct((slots, sets), jnp.float32),
@@ -393,7 +406,7 @@
         out_specs=in_vmem,
         compiler_params=params,
         name="picking",
-    )(carried_other, masked_other, projected, used)
+    )(carried_other, turned_other, projected, used)
     return fx_adjoint, rate_adjoint, notional_adjoint.T
 
 

time: 19.3 us -> 20.9 us (1.083)
  blocking collectives: 13 us -> 0 us
  starting transfers between devices: 0.58 us -> 9.77 us
  waiting for transfers between devices: 0.92 us -> 5.32 us
  Pallas kernels: 3.93 us -> 4.91 us
    all_to_all x1 -> x0, blocking collectives: 13 us -> none  [body(): lax.all_to_all(outgoing, 'sets', 0, 0, axis_index_groups=[[2 * chip + cor...]
    all_to_all x0 -> x1, starting transfers between devices: none -> 9.18 us  [body(): lax.all_to_all(outgoing, 'sets', 0, 0, axis_index_groups=[[2 * chip + cor...]
    all_to_all x0 -> x1, waiting for transfers between devices: none -> 4.41 us  [body(): lax.all_to_all(outgoing, 'sets', 0, 0, axis_index_groups=[[2 * chip + cor...]
    pallas_call x1, Pallas kernels: 0.02 us -> 0.68 us  [body(): pl.pallas_call(merging_kernel, out_shape=pltpu.VMEM((chips, 2 * currency_...]
    pallas_call x0 -> x1, Pallas kernels: none -> 0.35 us  [body(): pl.pallas_call(turning_kernel, out_shape=(pltpu.VMEM((columns // 2, sets)...]
  transfers between devices with their start and end apart: 2 -> 3, of which waited for: 2 -> 3; matrix products, arithmetic and copies ran while one was open for 0% -> 0% of each run, Pallas kernels for 7% -> 8%
where the time goes in v13:
time: 20.9 us; the launch traced here: 20.7 us
  starting transfers between devices  9.77 us (47%)
  waiting for transfers between devices  5.32 us (25%)
  Pallas kernels  4.91 us (23%)
  between operations  0.67 us (3%)
    all_to_all x1, starting transfers between devices, body(): lax.all_to_all(outgoing, 'sets', 0, 0, axis_index_groups=[[2 * chip + cor...  9.18 us
    all_to_all x1, waiting for transfers between devices, body(): lax.all_to_all(outgoing, 'sets', 0, 0, axis_index_groups=[[2 * chip + cor...  4.41 us
    pallas_call x1, Pallas kernels, body(): pl.pallas_call(first_kernel, out_shape=(pltpu.VMEM((chips,) + block, jnp....  1.78 us
    ppermute x2, waiting for transfers between devices, swapped(): lax.ppermute(value, 'sets', [(peer, peer ^ 1) for peer in range(peers)])  0.91 us
    pallas_call x1, Pallas kernels, body(): pl.pallas_call(functools.partial(adjoint_kernel, dates), out_shape=(jax.S...  0.86 us
    pallas_call x1, Pallas kernels, body(): pl.pallas_call(picking_kernel, out_shape=jax.ShapeDtypeStruct((slots, set...  0.82 us
    pallas_call x1, Pallas kernels, body(): pl.pallas_call(merging_kernel, out_shape=pltpu.VMEM((chips, 2 * currency_...  0.68 us
    ppermute x2, starting transfers between devices, swapped(): lax.ppermute(value, 'sets', [(peer, peer ^ 1) for peer in range(peers)])  0.59 us
  transfers between devices with their start and end apart: 3, of which 3 were waited for; matrix products, arithmetic and copies ran while one was open for 0% of the time, Pallas kernels for 8%

profile of v13, /device:TPU:0, one launch (start us, length us, event | category | flops | bytes accessed | tf_op | source)
XLA Modules:
  0.0 20.7 jit_solution(18352620894483868925)
XLA Ops:
  0.6 1.8 %first.1 = (bf16[8,40,128]{2,1,0:T(8,128)(2,1)S(1)}, bf16[240,1024]{1,0:T(8,128)(2,1)S(1)}, bf16[240,2048]{1,0:T(8,128)(2,1)S(1)}, s32[16,2048]{1,0:T(8,128)S(1)...) custom-call(bf16[240,2048]{1,0:T(8,128)(2,1)} %exposure_hbm.1, ...), custom_call_target="tpu_custom_call" | custom-call | tf_op jit(solution)/shard_map/first/pallas_call | solution.py:308
  2.4 0.5 %collective-permute-start = (bf16[8,40,128]{2,1,0:T(8,128)(2,1)S(1)}, bf16[8,40,128]{2,1,0:T(8,128)(2,1)S(1)}, u32[]{:S(2)}, u32[]{:S(2)}) collective-permute-start(bf16[8,40,128]{2,1,0:T(8,128)(2,1)S(1)} %get-tuple-element.22), channel_id=1, source_target_pairs={{0,1},{1,0},{2,3},{3,2},{4,5},{5,4},{6,7},{7,6},{8,9},{9,8},{10,11... | collective-permute-start | bytes 245768 | tf_op jit(solution)/shard_map/ppermute | solution.py:306
  2.9 0.4 %second.1 = (bf16[240,1024]{1,0:T(8,128)(2,1)S(1)}, f32[8,40,128]{2,1,0:T(8,128)S(1)}, bf16[40,128]{1,0:T(8,128)(2,1)S(1)}, f32[40,128]{1,0:T(8,128)S(1)}, f32[40,128]{1,0:T(8,128)S(1)}) custom-call(bf16[240,2048]{1,0:T(8,128)(2,1)S(1)} %get-tuple-element.23.exposure, s32[16,2048]{1,0:T(8,128)S(1)} %get-tuple-element.24.bits, ...), custom_call_target="tpu_custom_call" | custom-call | tf_op jit(solution)/shard_map/second/pallas_call | solution.py:343
  3.4 0.5 %collective-permute-done.given_ref = bf16[8,40,128]{2,1,0:T(8,128)(2,1)S(1)} collective-permute-done((bf16[8,40,128]{2,1,0:T(8,128)(2,1)S(1)}, bf16[8,40,128]{2,1,0:T(8,128)(2,1)S(1)}, u32[]{:S(2)}, u32[]{:S(2)}) %collective-permute-start) | collective-permute-done | bytes 81952 | tf_op jit(solution)/shard_map/ppermute | solution.py:306
  3.9 0.7 %merging.1 = bf16[8,80,128]{2,1,0:T(8,128)(2,1)} custom-call(bf16[8,40,128]{2,1,0:T(8,128)(2,1)S(1)} %collective-permute-done.given_ref, f32[8,40,128]{2,1,0:T(8,128)S(1)} %get-tuple-element.29.terms_ref, bf16[40,128]{1,0:T(8,128)(2,1)S(1)} %get-tuple-element.30.carried_ref), custom_call_target="tpu_custom_call" | custom-call | tf_op jit(solution)/shard_map/merging/pallas_call | solution.py:357
  4.5 9.2 %all-to-all-start = ((bf16[8,80,128]{2,1,0:T(8,128)(2,1)}), bf16[8,80,128]{2,1,0:T(8,128)(2,1)S(1)}, u32[]{:S(2)}, u32[]{:S(2)}) async-start(bf16[8,80,128]{2,1,0:T(8,128)(2,1)} %merging.1), calls=%async_computation | async-start | bytes 327680 | tf_op jit(solution)/shard_map/all_to_all | solution.py:365
  13.7 0.3 %turning.1 = (bf16[1024,240]{1,0:T(8,128)(2,1)S(1)}, bf16[1024,240]{1,0:T(8,128)(2,1)S(1)}) custom-call(bf16[240,1024]{1,0:T(8,128)(2,1)S(1)} %get-tuple-element.31.masked_own, bf16[240,1024]{1,0:T(8,128)(2,1)S(1)} %get-tuple-element.32.masked_other), custom_call_target="tpu_custom_call" | custom-call | tf_op jit(solution)/shard_map/turning/pallas_call | solution.py:373
  14.1 4.4 %all-to-all-done.arrived_ref = bf16[8,80,128]{2,1,0:T(8,128)(2,1)S(1)} async-done(((bf16[8,80,128]{2,1,0:T(8,128)(2,1)}), bf16[8,80,128]{2,1,0:T(8,128)(2,1)S(1)}, u32[]{:S(2)}, u32[]{:S(2)}) %all-to-all-start) | async-done | bytes 163872 | tf_op jit(solution)/shard_map/all_to_all | solution.py:365
  18.5 0.1 collective-permute-start.1
  18.6 0.9 %adjoint.1 = (f32[40,128]{1,0:T(8,128)}, f32[40,128]{1,0:T(8,128)}, f32[40,240]{1,0:T(8,128)S(1)}) custom-call(bf16[8,80,128]{2,1,0:T(8,128)(2,1)S(1)} %all-to-all-done.arrived_ref, bf16[8,40,128]{2,1,0:T(8,128)(2,1)S(1)} %unpacking.1.carried_ref, bf16[1024,240]{1,0:T(8,128)(2,1)S(1)} %get-tuple-element.33.turned_own, ...), custom_call_target="tpu_custom_call" | custom-call | tf_op jit(solution)/shard_map/adjoint/pallas_call | solution.py:390
  19.4 0.4 %collective-permute-done.1.carried_ref = bf16[8,40,128]{2,1,0:T(8,128)(2,1)S(1)} collective-permute-done((bf16[8,40,128]{2,1,0:T(8,128)(2,1)S(1)}, bf16[8,40,128]{2,1,0:T(8,128)(2,1)S(1)}, u32[]{:S(2)}, u32[]{:S(2)}) %collective-permute-start.1) | collective-permute-done | bytes 81952 | tf_op jit(solution)/shard_map/ppermute | solution.py:306
  19.8 0.8 %picking.1 = f32[4,240]{1,0:T(4,128)} custom-call(bf16[8,40,128]{2,1,0:T(8,128)(2,1)S(1)} %collective-permute-done.1.carried_ref, bf16[1024,240]{1,0:T(8,128)(2,1)S(1)} %get-tuple-element.34.turned_other, f32[40,240]{1,0:T(8,128)S(1)} %get-tuple-element.39.projected_ref, s32[4,240]{1,0:T(4,128)S(1)} %get-tuple-element.40.used_ref), custom_call_target="tpu_custom_call" | custom-call | tf_op jit(solution)/shard_map/picking/pallas_call | solution.py:402
  (1 shorter events, 0.0 us)
Async XLA Ops:
  2.4 1.4 %collective-permute-start = (bf16[8,40,128]{2,1,0:T(8,128)(2,1)S(1)}, bf16[8,40,128]{2,1,0:T(8,128)(2,1)S(1)}, u32[]{:S(2)}, u32[]{:S(2)}) collective-permute-start(bf16[8,40,128]{2,1,0:T(8,128)(2,1)S(1)} %get-tuple-element.22), channel_id=1, source_target_pairs={{0,1},{1,0},{2,3},{3,2},{4,5},{5,4},{6,7},{7,6},{8,9},{9,8},{10,11... | collective-permute-start | bytes 245768 | tf_op jit(solution)/shard_map/ppermute | solution.py:306
  4.5 13.9 %all-to-all-start = ((bf16[8,80,128]{2,1,0:T(8,128)(2,1)}), bf16[8,80,128]{2,1,0:T(8,128)(2,1)S(1)}, u32[]{:S(2)}, u32[]{:S(2)}) async-start(bf16[8,80,128]{2,1,0:T(8,128)(2,1)} %merging.1), calls=%async_computation | async-start | bytes 327680 | tf_op jit(solution)/shard_map/all_to_all | solution.py:365
  18.5 1.3 %collective-permute-start.1 = (bf16[8,40,128]{2,1,0:T(8,128)(2,1)S(1)}, bf16[8,40,128]{2,1,0:T(8,128)(2,1)S(1)}, u32[]{:S(2)}, u32[]{:S(2)}) collective-permute-start(bf16[8,40,128]{2,1,0:T(8,128)(2,1)S(1)} %unpacking.1.carried_ref), channel_id=1, source_target_pairs={{0,1},{1,0},{2,3},{3,2},{4,5},{5,4},{6,7},{7,6},{8,9},{9,8},{10,11... | collective-permute-start | bytes 245768 | tf_op jit(solution)/shard_map/ppermute | solution.py:306

commit v14 on v10

--- a/solution.py
+++ b/solution.py
@@ -53,7 +53,7 @@
 
 def group_order(chips):
     middle = chips // 2
-    return list(range(chips - 1, middle - 1, -1)) + list(range(middle))
+    return list(range(middle, chips)) + list(range(middle))
 
 
 def sibling_columns(chip, owned, core):
@@ -126,6 +126,7 @@
     notional_ref,
     sems,
     exposure_sems,
+    bits_sems,
 ):
     sets = exposure.shape[0]
     chips, currency_count = handed_ref.shape[:2]
@@ -137,6 +138,13 @@
         return pltpu.make_async_copy(
             exposure_hbm.at[part], exposure.at[part], exposure_sems.at[index]
         )
+
+    bits_parts = bits_sems.shape[0]
+    bits_width = bits.shape[1] // bits_parts
+
+    def bits_copy(index):
+        part = pl.ds(index * bits_width, bits_width)
+        return pltpu.make_async_copy(bits_hbm.at[:, part], bits.at[:, part], bits_sems.at[index])
 
     copies = [
         pltpu.make_async_copy(source, target, sems.at[index])
@@ -145,22 +153,30 @@
                 (currencies_hbm, currencies_ref),
                 (counts_hbm, counts_ref),
                 (notional_hbm, notional_ref),
-                (bits_hbm, bits),
                 (rates_hbm, rates_ref),
                 (start_hbm, start_ref),
                 (fx_hbm, fx_ref),
             ]
         )
     ]
-    for copy in copies[:4]:
-        copy.start()
+    for index in range(bits_parts):
+        bits_copy(index).start()
     for index in range(parts):
         exposure_copy(index).start()
-    for copy in copies[4:]:
+    for copy in copies:
         copy.start()
+    for index in range(bits_parts):
+        bits_copy(index).wait()
+
+    other = 1 - lax.axis_index("sets") % 2
+    for index in range(parts):
+        exposure_copy(index).wait()
+        mask_rows(
+            exposure, bits, masked_ref, other, handed_ref.shape[2], index * rows, (index + 1) * rows
+        )
+
     for copy in copies:
         copy.wait()
-
     used = used_currencies(currencies_ref[...], counts_ref[...])
     used_ref[...] = used
     notional = notional_ref[...]
@@ -172,12 +188,6 @@
         )
     weights = weights.astype(jnp.bfloat16)
     weights_ref[...] = weights
-    other = 1 - lax.axis_index("sets") % 2
-    for index in range(parts):
-        exposure_copy(index).wait()
-        mask_rows(
-            exposure, bits, masked_ref, other, handed_ref.shape[2], index * rows, (index + 1) * rows
-        )
     sum_sets(weights, masked_ref, handed_ref)
 
 
@@ -319,8 +329,9 @@
             pltpu.VMEM((slots, sets), jnp.int32),
             pltpu.VMEM((1, sets), jnp.int32),
             pltpu.VMEM((slots, sets), jnp.float32),
-            pltpu.SemaphoreType.DMA((7,)),
+            pltpu.SemaphoreType.DMA((6,)),
             pltpu.SemaphoreType.DMA((math.gcd(sets // 16, 5),)),
+            pltpu.SemaphoreType.DMA((4,)),
         ],
         compiler_params=params,
         name="first",

time: 19.3 us -> 19.2 us (level)
  no operation moved by 1% of the time
where the time goes in v14:
time: 19.2 us; the launch traced here: 19.1 us
  blocking collectives  12.9 us (67%)
  Pallas kernels  3.95 us (21%)
  waiting for transfers between devices  0.92 us (5%)
  between operations  0.66 us (3%)
  starting transfers between devices  0.58 us (3%)
    all_to_all x1, blocking collectives, body(): lax.all_to_all(outgoing, 'sets', 0, 0, axis_index_groups=[[2 * chip + cor...  12.9 us
    pallas_call x1, Pallas kernels, body(): pl.pallas_call(first_kernel, out_shape=(pltpu.VMEM((chips,) + block, jnp....  1.78 us
    ppermute x2, waiting for transfers between devices, swapped(): lax.ppermute(value, 'sets', [(peer, peer ^ 1) for peer in range(peers)])  0.92 us
    pallas_call x1, Pallas kernels, body(): pl.pallas_call(picking_kernel, out_shape=jax.ShapeDtypeStruct((slots, set...  0.88 us
    pallas_call x1, Pallas kernels, body(): pl.pallas_call(functools.partial(adjoint_kernel, dates), out_shape=(jax.S...  0.85 us
    ppermute x2, starting transfers between devices, swapped(): lax.ppermute(value, 'sets', [(peer, peer ^ 1) for peer in range(peers)])  0.58 us
    pallas_call x1, Pallas kernels, body(): pl.pallas_call(functools.partial(second_kernel, dates), out_shape=(pltpu....  0.4 us
  transfers between devices with their start and end apart: 2, of which 2 were waited for; matrix products, arithmetic and copies ran while one was open for 0% of the time, Pallas kernels for 7%

profile of v14, /device:TPU:0, one launch (start us, length us, event | category | flops | bytes accessed | tf_op | source)
XLA Modules:
  0.0 19.1 jit_solution(9680431987510312662)
XLA Ops:
  0.6 1.8 %first.1 = (bf16[8,40,128]{2,1,0:T(8,128)(2,1)S(1)}, bf16[240,1024]{1,0:T(8,128)(2,1)S(1)}, bf16[240,2048]{1,0:T(8,128)(2,1)S(1)}, s32[16,2048]{1,0:T(8,128)S(1)...) custom-call(bf16[240,2048]{1,0:T(8,128)(2,1)} %exposure_hbm.1, ...), custom_call_target="tpu_custom_call" | custom-call | tf_op jit(solution)/shard_map/first/pallas_call | solution.py:313
  2.4 0.5 %collective-permute-start = (bf16[8,40,128]{2,1,0:T(8,128)(2,1)S(1)}, bf16[8,40,128]{2,1,0:T(8,128)(2,1)S(1)}, u32[]{:S(2)}, u32[]{:S(2)}) collective-permute-start(bf16[8,40,128]{2,1,0:T(8,128)(2,1)S(1)} %get-tuple-element.20), channel_id=1, source_target_pairs={{0,1},{1,0},{2,3},{3,2},{4,5},{5,4},{6,7},{7,6},{8,9},{9,8},{10,11... | collective-permute-start | bytes 245768 | tf_op jit(solution)/shard_map/ppermute | solution.py:311
  2.9 0.4 %second.1 = (bf16[240,1024]{1,0:T(8,128)(2,1)S(1)}, f32[8,40,128]{2,1,0:T(8,128)S(1)}, bf16[40,128]{1,0:T(8,128)(2,1)S(1)}, f32[40,128]{1,0:T(8,128)S(1)}, f32[40,128]{1,0:T(8,128)S(1)}) custom-call(bf16[240,2048]{1,0:T(8,128)(2,1)S(1)} %get-tuple-element.21.exposure, s32[16,2048]{1,0:T(8,128)S(1)} %get-tuple-element.22.bits, ...), custom_call_target="tpu_custom_call" | custom-call | tf_op jit(solution)/shard_map/second/pallas_call | solution.py:349
  3.4 0.5 %collective-permute-done.given_ref = bf16[8,40,128]{2,1,0:T(8,128)(2,1)S(1)} collective-permute-done((bf16[8,40,128]{2,1,0:T(8,128)(2,1)S(1)}, bf16[8,40,128]{2,1,0:T(8,128)(2,1)S(1)}, u32[]{:S(2)}, u32[]{:S(2)}) %collective-permute-start) | collective-permute-done | bytes 81952 | tf_op jit(solution)/shard_map/ppermute | solution.py:311
  3.9 12.9 %all_to_all.5.arrived_ref = bf16[8,80,128]{2,1,0:T(8,128)(2,1)S(1)} all-to-all(bf16[8,80,128]{2,1,0:T(8,128)(2,1)S(1)} %merging.1), channel_id=1, replica_groups={{8,10,12,14,0,2,4,6},{9,11,13,15,1,3,5,7},{24,26,28,30,16,18,20,22},{25..., dimensions={0} | all-to-all | bytes 327680 | tf_op jit(solution)/shard_map/all_to_all | solution.py:371
  16.8 0.1 collective-permute-start.1
  16.9 0.9 %adjoint.1 = (f32[40,128]{1,0:T(8,128)}, f32[40,128]{1,0:T(8,128)}, f32[40,240]{1,0:T(8,128)S(1)}) custom-call(bf16[8,80,128]{2,1,0:T(8,128)(2,1)S(1)} %all_to_all.5.arrived_ref, bf16[8,40,128]{2,1,0:T(8,128)(2,1)S(1)} %unpacking.1.carried_ref, bf16[240,1024]{1,0:T(8,128)(2,1)S(1)} %get-tuple-element.29.masked_own, ...), custom_call_target="tpu_custom_call" | custom-call | tf_op jit(solution)/shard_map/adjoint/pallas_call | solution.py:388
  17.8 0.4 %collective-permute-done.1.carried_ref = bf16[8,40,128]{2,1,0:T(8,128)(2,1)S(1)} collective-permute-done((bf16[8,40,128]{2,1,0:T(8,128)(2,1)S(1)}, bf16[8,40,128]{2,1,0:T(8,128)(2,1)S(1)}, u32[]{:S(2)}, u32[]{:S(2)}) %collective-permute-start.1) | collective-permute-done | bytes 81952 | tf_op jit(solution)/shard_map/ppermute | solution.py:311
  18.2 0.9 %picking.1 = f32[4,240]{1,0:T(4,128)} custom-call(bf16[8,40,128]{2,1,0:T(8,128)(2,1)S(1)} %collective-permute-done.1.carried_ref, bf16[240,1024]{1,0:T(8,128)(2,1)S(1)} %get-tuple-element.34.masked_other, f32[40,240]{1,0:T(8,128)S(1)} %get-tuple-element.35.projected_ref, s32[4,240]{1,0:T(4,128)S(1)} %get-tuple-element.36.used_ref), custom_call_target="tpu_custom_call" | custom-call | tf_op jit(solution)/shard_map/picking/pallas_call | solution.py:400
  (2 shorter events, 0.0 us)
Async XLA Ops:
  2.4 1.4 %collective-permute-start = (bf16[8,40,128]{2,1,0:T(8,128)(2,1)S(1)}, bf16[8,40,128]{2,1,0:T(8,128)(2,1)S(1)}, u32[]{:S(2)}, u32[]{:S(2)}) collective-permute-start(bf16[8,40,128]{2,1,0:T(8,128)(2,1)S(1)} %get-tuple-element.20), channel_id=1, source_target_pairs={{0,1},{1,0},{2,3},{3,2},{4,5},{5,4},{6,7},{7,6},{8,9},{9,8},{10,11... | collective-permute-start | bytes 245768 | tf_op jit(solution)/shard_map/ppermute | solution.py:311
  16.8 1.3 %collective-permute-start.1 = (bf16[8,40,128]{2,1,0:T(8,128)(2,1)S(1)}, bf16[8,40,128]{2,1,0:T(8,128)(2,1)S(1)}, u32[]{:S(2)}, u32[]{:S(2)}) collective-permute-start(bf16[8,40,128]{2,1,0:T(8,128)(2,1)S(1)} %unpacking.1.carried_ref), channel_id=1, source_target_pairs={{0,1},{1,0},{2,3},{3,2},{4,5},{5,4},{6,7},{7,6},{8,9},{9,8},{10,11... | collective-permute-start | bytes 245768 | tf_op jit(solution)/shard_map/ppermute | solution.py:311

commit v15 on v14

--- a/solution.py
+++ b/solution.py
@@ -52,8 +52,7 @@
 
 
 def group_order(chips):
-    middle = chips // 2
-    return list(range(middle, chips)) + list(range(middle))
+    return list(range(chips - 1, -1, -1))
 
 
 def sibling_columns(chip, owned, core):
@@ -218,20 +217,41 @@
 
 def merging_kernel(given_ref, terms_ref, carried_ref, outgoing_ref):
     chips, currency_count, owned = terms_ref.shape
-    order = group_order(chips)
+    near = chips // 2
+    half = lax.axis_index("sets") // (2 * near)
     carried = carried_ref[...]
-    for place in range(chips):
+    for place, chip in enumerate(group_order(near)):
         outgoing_ref[place, 0:currency_count, :] = carried
-        outgoing_ref[place, currency_count:, :] = (
-            terms_ref[order[place]] + given_ref[order[place]].astype(jnp.float32)
-        ).astype(jnp.bfloat16)
-
-
-def unpacking_kernel(arrived_ref, carried_ref):
-    chips, currency_count, owned = carried_ref.shape
-    order = group_order(chips)
-    for place in range(chips):
-        carried_ref[order[place]] = arrived_ref[place, 0:currency_count, :]
+        for part, chosen in enumerate((half, 1 - half)):
+            index = chosen * near + chip
+            rows = pl.ds((1 + part) * currency_count, currency_count)
+            outgoing_ref[place, rows, :] = (
+                terms_ref[index] + given_ref[index].astype(jnp.float32)
+            ).astype(jnp.bfloat16)
+
+
+def halfway_kernel(arrived_ref, crossing_ref, summed_ref):
+    near = arrived_ref.shape[0]
+    currency_count = summed_ref.shape[0]
+    for place, chip in enumerate(group_order(near)):
+        crossing_ref[chip] = arrived_ref[place, 0:currency_count, :]
+    sums = []
+    for part in range(2):
+        rows = pl.ds((1 + part) * currency_count, currency_count)
+        total = arrived_ref[0, rows, :].astype(jnp.float32)
+        for place in range(1, near):
+            total = total + arrived_ref[place, rows, :].astype(jnp.float32)
+        sums.append(total)
+    summed_ref[...] = sums[0]
+    crossing_ref[near] = sums[1].astype(jnp.bfloat16)
+
+
+def unpacking_kernel(crossing_ref, crossed_ref, carried_ref):
+    near = crossing_ref.shape[0] - 1
+    half = lax.axis_index("sets") // (2 * near)
+    for chip in range(near):
+        carried_ref[half * near + chip] = crossing_ref[chip]
+        carried_ref[(1 - half) * near + chip] = crossed_ref[chip]
 
 
 def projection(masked, carried_ref):
@@ -252,7 +272,8 @@
 
 def adjoint_kernel(
     dates,
-    arrived_ref,
+    summed_ref,
+    crossed_ref,
     carried_ref,
     masked_own,
     moved_ref,
@@ -261,10 +282,8 @@
     rate_adjoint_ref,
     projected_ref,
 ):
-    chips, currency_count, owned = carried_ref.shape
-    aggregate = arrived_ref[0, currency_count:, :].astype(jnp.float32)
-    for chip in range(1, chips):
-        aggregate = aggregate + arrived_ref[chip, currency_count:, :].astype(jnp.float32)
+    near = crossed_ref.shape[0] - 1
+    aggregate = summed_ref[...] + crossed_ref[near].astype(jnp.float32)
     fx_adjoint_ref[...] = aggregate * discount_ref[...]
     rate_adjoint_ref[...] = -step_years * sums_from_date(aggregate * moved_ref[...], dates)
     projected_ref[...] = projection(masked_own, carried_ref)
@@ -298,6 +317,7 @@
     dates = owned // start_integral.shape[1]
     peers = columns // owned
     chips = peers // 2
+    near = chips // 2
     slots = currencies.shape[1]
     in_vmem = pl.BlockSpec(memory_space=pltpu.VMEM)
     anywhere = pl.BlockSpec(memory_space=pl.ANY)
@@ -307,8 +327,8 @@
     def in_hbm(value):
         return pltpu.with_memory_space_constraint(value, pltpu.HBM)
 
-    def swapped(value):
-        return lax.ppermute(value, "sets", [(peer, peer ^ 1) for peer in range(peers)])
+    def swapped(value, offset=1):
+        return lax.ppermute(value, "sets", [(peer, peer ^ offset) for peer in range(peers)])
 
     handed, masked_other, exposure, bits, weights, used, fx, rates, start = pl.pallas_call(
         first_kernel,
@@ -362,7 +382,7 @@
     )(exposure, bits, weights, fx, rates, start)
     outgoing = pl.pallas_call(
         merging_kernel,
-        out_shape=pltpu.VMEM((chips, 2 * currency_count, owned), jnp.bfloat16),
+        out_shape=pltpu.VMEM((near, 3 * currency_count, owned), jnp.bfloat16),
         in_specs=[in_vmem] * 3,
         out_specs=in_vmem,
         compiler_params=params,
@@ -373,17 +393,33 @@
         "sets",
         0,
         0,
-        axis_index_groups=[[2 * chip + core for chip in group_order(chips)] for core in range(2)],
+        axis_index_groups=[
+            [2 * (half * near + chip) + core for chip in group_order(near)]
+            for half in range(2)
+            for core in range(2)
+        ],
         tiled=True,
     )
+    crossing, summed = pl.pallas_call(
+        halfway_kernel,
+        out_shape=(
+            pltpu.VMEM((near + 1,) + block, jnp.bfloat16),
+            pltpu.VMEM(block, jnp.float32),
+        ),
+        in_specs=[in_vmem],
+        out_specs=(in_vmem,) * 2,
+        compiler_params=params,
+        name="halfway",
+    )(arrived)
+    crossed = swapped(crossing, 2 * near)
     carried_own = pl.pallas_call(
         unpacking_kernel,
         out_shape=pltpu.VMEM((chips,) + block, jnp.bfloat16),
-        in_specs=[in_vmem],
+        in_specs=[in_vmem] * 2,
         out_specs=in_vmem,
         compiler_params=params,
         name="unpacking",
-    )(arrived)
+    )(crossing, crossed)
     carried_other = swapped(carried_own)
     fx_adjoint, rate_adjoint, projected = pl.pallas_call(
         functools.partial(adjoint_kernel, dates),
@@ -392,11 +428,11 @@
             jax.ShapeDtypeStruct(block, jnp.float32),
             pltpu.VMEM((currency_count, sets), jnp.float32),
         ),
-        in_specs=[in_vmem] * 5,
+        in_specs=[in_vmem] * 6,
         out_specs=(in_vmem,) * 3,
         compiler_params=params,
         name="adjoint",
-    )(arrived, carried_own, masked_own, moved, discount)
+    )(summed, crossed, carried_own, masked_own, moved, discount)
     notional_adjoint = pl.pallas_call(
         picking_kernel,
         out_shape=jax.ShapeDtypeStruct((slots, sets), jnp.float32),

time: 19.2 us -> 20.6 us (1.073)
  blocking collectives: 12.9 us -> 9.2 us
  starting transfers between devices: 0.58 us -> 3.24 us
  waiting for transfers between devices: 0.92 us -> 3.34 us
    all_to_all x1, blocking collectives: 12.9 us -> 9.2 us  [body(): lax.all_to_all(outgoing, 'sets', 0, 0, axis_index_groups=[[2 * (half * ne...]
    ppermute x2 -> x3, starting transfers between devices: 0.58 us -> 3.24 us  [swapped(): lax.ppermute(value, 'sets', [(peer, peer ^ offset) for peer in range(peer...]
    ppermute x2 -> x3, waiting for transfers between devices: 0.92 us -> 3.34 us  [swapped(): lax.ppermute(value, 'sets', [(peer, peer ^ offset) for peer in range(peer...]
  transfers between devices with their start and end apart: 2 -> 3, of which waited for: 2 -> 3; matrix products, arithmetic and copies ran while one was open for 0% -> 0% of each run, Pallas kernels for 7% -> 6%
where the time goes in v15:
time: 20.6 us; the launch traced here: 20.4 us
  blocking collectives  9.2 us (45%)
  Pallas kernels  3.98 us (19%)
  waiting for transfers between devices  3.34 us (16%)
  starting transfers between devices  3.24 us (16%)
  between operations  0.67 us (3%)
    all_to_all x1, blocking collectives, body(): lax.all_to_all(outgoing, 'sets', 0, 0, axis_index_groups=[[2 * (half * ne...  9.2 us
    ppermute x3, waiting for transfers between devices, swapped(): lax.ppermute(value, 'sets', [(peer, peer ^ offset) for peer in range(peer...  3.34 us
    ppermute x3, starting transfers between devices, swapped(): lax.ppermute(value, 'sets', [(peer, peer ^ offset) for peer in range(peer...  3.24 us
    pallas_call x1, Pallas kernels, body(): pl.pallas_call(first_kernel, out_shape=(pltpu.VMEM((chips,) + block, jnp....  1.78 us
    pallas_call x1, Pallas kernels, body(): pl.pallas_call(picking_kernel, out_shape=jax.ShapeDtypeStruct((slots, set...  0.88 us
    pallas_call x1, Pallas kernels, body(): pl.pallas_call(functools.partial(adjoint_kernel, dates), out_shape=(jax.S...  0.85 us
  transfers between devices with their start and end apart: 3, of which 3 were waited for; matrix products, arithmetic and copies ran while one was open for 0% of the time, Pallas kernels for 6%

profile of v15, /device:TPU:0, one launch (start us, length us, event | category | flops | bytes accessed | tf_op | source)
XLA Modules:
  0.0 20.4 jit_solution(7800484303081046611)
XLA Ops:
  0.6 1.8 %first.1 = (bf16[8,40,128]{2,1,0:T(8,128)(2,1)S(1)}, bf16[240,1024]{1,0:T(8,128)(2,1)S(1)}, bf16[240,2048]{1,0:T(8,128)(2,1)S(1)}, s32[16,2048]{1,0:T(8,128)S(1)...) custom-call(bf16[240,2048]{1,0:T(8,128)(2,1)} %exposure_hbm.1, ...), custom_call_target="tpu_custom_call" | custom-call | tf_op jit(solution)/shard_map/first/pallas_call | solution.py:333
  2.4 0.5 %collective-permute-start = (bf16[8,40,128]{2,1,0:T(8,128)(2,1)S(1)}, bf16[8,40,128]{2,1,0:T(8,128)(2,1)S(1)}, u32[]{:S(2)}, u32[]{:S(2)}) collective-permute-start(bf16[8,40,128]{2,1,0:T(8,128)(2,1)S(1)} %get-tuple-element.22), channel_id=1, source_target_pairs={{0,1},{1,0},{2,3},{3,2},{4,5},{5,4},{6,7},{7,6},{8,9},{9,8},{10,11... | collective-permute-start | bytes 245768 | tf_op jit(solution)/shard_map/ppermute | solution.py:331
  2.9 0.4 %second.1 = (bf16[240,1024]{1,0:T(8,128)(2,1)S(1)}, f32[8,40,128]{2,1,0:T(8,128)S(1)}, bf16[40,128]{1,0:T(8,128)(2,1)S(1)}, f32[40,128]{1,0:T(8,128)S(1)}, f32[40,128]{1,0:T(8,128)S(1)}) custom-call(bf16[240,2048]{1,0:T(8,128)(2,1)S(1)} %get-tuple-element.23.exposure, s32[16,2048]{1,0:T(8,128)S(1)} %get-tuple-element.24.bits, ...), custom_call_target="tpu_custom_call" | custom-call | tf_op jit(solution)/shard_map/second/pallas_call | solution.py:369
  3.4 0.5 %collective-permute-done.given_ref = bf16[8,40,128]{2,1,0:T(8,128)(2,1)S(1)} collective-permute-done((bf16[8,40,128]{2,1,0:T(8,128)(2,1)S(1)}, bf16[8,40,128]{2,1,0:T(8,128)(2,1)S(1)}, u32[]{:S(2)}, u32[]{:S(2)}) %collective-permute-start) | collective-permute-done | bytes 81952 | tf_op jit(solution)/shard_map/ppermute | solution.py:331
  3.9 9.2 %all_to_all.5.arrived_ref = bf16[4,120,128]{2,1,0:T(8,128)(2,1)S(1)} all-to-all(bf16[4,120,128]{2,1,0:T(8,128)(2,1)S(1)} %merging.1), channel_id=1, replica_groups={{6,4,2,0},{7,5,3,1},{14,12,10,8},{15,13,11,9},{22,20,18,16},{23,21,19,1..., dimensions={0} | all-to-all | bytes 245760 | tf_op jit(solution)/shard_map/all_to_all | solution.py:391
  13.1 2.7 %collective-permute-start.1 = (bf16[5,40,128]{2,1,0:T(8,128)(2,1)S(1)}, bf16[5,40,128]{2,1,0:T(8,128)(2,1)S(1)}, u32[]{:S(2)}, u32[]{:S(2)}) collective-permute-start(bf16[5,40,128]{2,1,0:T(8,128)(2,1)S(1)} %get-tuple-element.32.crossing_ref), channel_id=1, source_target_pairs={{0,8},{1,9},{2,10},{3,11},{4,12},{5,13},{6,14},{7,15},{8,0},{9,1},... | collective-permute-start | bytes 153608 | tf_op jit(solution)/shard_map/ppermute | solution.py:331
  15.8 2.4 %collective-permute-done.1.crossed_ref = bf16[5,40,128]{2,1,0:T(8,128)(2,1)S(1)} collective-permute-done((bf16[5,40,128]{2,1,0:T(8,128)(2,1)S(1)}, bf16[5,40,128]{2,1,0:T(8,128)(2,1)S(1)}, u32[]{:S(2)}, u32[]{:S(2)}) %collective-permute-start.1) | collective-permute-done | bytes 51232 | tf_op jit(solution)/shard_map/ppermute | solution.py:331
  18.2 0.1 collective-permute-start.2
  18.3 0.9 %adjoint.1 = (f32[40,128]{1,0:T(8,128)}, f32[40,128]{1,0:T(8,128)}, f32[40,240]{1,0:T(8,128)S(1)}) custom-call(f32[40,128]{1,0:T(8,128)S(1)} %get-tuple-element.31.summed_ref, bf16[5,40,128]{2,1,0:T(8,128)(2,1)S(1)} %collective-permute-done.1.crossed_ref, bf16[8,40,128]{2,1,0:T(8,128)(2,1)S(1)} %unpacking.1.carried_ref, ...), custom_call_target="tpu_custom_call" | custom-call | tf_op jit(solution)/shard_map/adjoint/pallas_call | solution.py:424
  19.1 0.4 %collective-permute-done.2.carried_ref = bf16[8,40,128]{2,1,0:T(8,128)(2,1)S(1)} collective-permute-done((bf16[8,40,128]{2,1,0:T(8,128)(2,1)S(1)}, bf16[8,40,128]{2,1,0:T(8,128)(2,1)S(1)}, u32[]{:S(2)}, u32[]{:S(2)}) %collective-permute-start.2) | collective-permute-done | bytes 81952 | tf_op jit(solution)/shard_map/ppermute | solution.py:331
  19.6 0.9 %picking.1 = f32[4,240]{1,0:T(4,128)} custom-call(bf16[8,40,128]{2,1,0:T(8,128)(2,1)S(1)} %collective-permute-done.2.carried_ref, bf16[240,1024]{1,0:T(8,128)(2,1)S(1)} %get-tuple-element.38.masked_other, f32[40,240]{1,0:T(8,128)S(1)} %get-tuple-element.39.projected_ref, s32[4,240]{1,0:T(4,128)S(1)} %get-tuple-element.40.used_ref), custom_call_target="tpu_custom_call" | custom-call | tf_op jit(solution)/shard_map/picking/pallas_call | solution.py:436
  (3 shorter events, 0.1 us)
Async XLA Ops:
  2.4 1.4 %collective-permute-start = (bf16[8,40,128]{2,1,0:T(8,128)(2,1)S(1)}, bf16[8,40,128]{2,1,0:T(8,128)(2,1)S(1)}, u32[]{:S(2)}, u32[]{:S(2)}) collective-permute-start(bf16[8,40,128]{2,1,0:T(8,128)(2,1)S(1)} %get-tuple-element.22), channel_id=1, source_target_pairs={{0,1},{1,0},{2,3},{3,2},{4,5},{5,4},{6,7},{7,6},{8,9},{9,8},{10,11... | collective-permute-start | bytes 245768 | tf_op jit(solution)/shard_map/ppermute | solution.py:331
  13.1 5.1 %collective-permute-start.1 = (bf16[5,40,128]{2,1,0:T(8,128)(2,1)S(1)}, bf16[5,40,128]{2,1,0:T(8,128)(2,1)S(1)}, u32[]{:S(2)}, u32[]{:S(2)}) collective-permute-start(bf16[5,40,128]{2,1,0:T(8,128)(2,1)S(1)} %get-tuple-element.32.crossing_ref), channel_id=1, source_target_pairs={{0,8},{1,9},{2,10},{3,11},{4,12},{5,13},{6,14},{7,15},{8,0},{9,1},... | collective-permute-start | bytes 153608 | tf_op jit(solution)/shard_map/ppermute | solution.py:331
  18.2 1.3 %collective-permute-start.2 = (bf16[8,40,128]{2,1,0:T(8,128)(2,1)S(1)}, bf16[8,40,128]{2,1,0:T(8,128)(2,1)S(1)}, u32[]{:S(2)}, u32[]{:S(2)}) collective-permute-start(bf16[8,40,128]{2,1,0:T(8,128)(2,1)S(1)} %unpacking.1.carried_ref), channel_id=1, source_target_pairs={{0,1},{1,0},{2,3},{3,2},{4,5},{5,4},{6,7},{7,6},{8,9},{9,8},{10,11... | collective-permute-start | bytes 245768 | tf_op jit(solution)/shard_map/ppermute | solution.py:331

commit v16 on v14

--- a/solution.py
+++ b/solution.py
@@ -96,7 +96,7 @@
     for chip in range(0, terms_ref.shape[0], 2):
         terms = jnp.dot(
             weights,
-            masked_ref[:, chip * owned : (chip + 2) * owned],
+            masked_ref[0 : weights.shape[1], chip * owned : (chip + 2) * owned],
             preferred_element_type=jnp.float32,
         ).astype(terms_ref.dtype)
         terms_ref[chip] = terms[:, :owned]
@@ -113,7 +113,7 @@
     rates_hbm,
     start_hbm,
     handed_ref,
-    masked_ref,
+    lent_ref,
     exposure,
     bits,
     weights_ref,
@@ -165,20 +165,11 @@
         exposure_copy(index).start()
     for copy in copies:
         copy.start()
-    for index in range(bits_parts):
-        bits_copy(index).wait()
-
-    other = 1 - lax.axis_index("sets") % 2
-    for index in range(parts):
-        exposure_copy(index).wait()
-        mask_rows(
-            exposure, bits, masked_ref, other, handed_ref.shape[2], index * rows, (index + 1) * rows
-        )
-
     for copy in copies:
         copy.wait()
     used = used_currencies(currencies_ref[...], counts_ref[...])
     used_ref[...] = used
+    lent_ref[sets : sets + used.shape[0], 0:sets] = used.astype(jnp.float32).astype(jnp.bfloat16)
     notional = notional_ref[...]
     currency = lax.broadcasted_iota(jnp.int32, (currency_count, sets), 0)
     weights = jnp.zeros((currency_count, sets), jnp.float32)
@@ -188,7 +179,16 @@
         )
     weights = weights.astype(jnp.bfloat16)
     weights_ref[...] = weights
-    sum_sets(weights, masked_ref, handed_ref)
+    for index in range(bits_parts):
+        bits_copy(index).wait()
+
+    other = 1 - lax.axis_index("sets") % 2
+    for index in range(parts):
+        exposure_copy(index).wait()
+        mask_rows(
+            exposure, bits, lent_ref, other, handed_ref.shape[2], index * rows, (index + 1) * rows
+        )
+    sum_sets(weights, lent_ref, handed_ref)
 
 
 def second_kernel(
@@ -227,60 +227,52 @@
         ).astype(jnp.bfloat16)
 
 
-def unpacking_kernel(arrived_ref, carried_ref):
-    chips, currency_count, owned = carried_ref.shape
+def projecting_kernel(arrived_ref, masked_own, lent_ref, used_ref, own_ref, others_ref):
+    sets, half = masked_own.shape
+    chips, owned = arrived_ref.shape[0], arrived_ref.shape[2]
+    currency_count = arrived_ref.shape[1] // 2
+    slots = used_ref.shape[0]
     order = group_order(chips)
-    for place in range(chips):
-        carried_ref[order[place]] = arrived_ref[place, 0:currency_count, :]
-
-
-def projection(masked, carried_ref):
-    sets, half = masked.shape
-    chips, currency_count, owned = carried_ref.shape
+    place = [order.index(chip) for chip in range(chips)]
     here = min(chips, 8)
-    projected = jnp.zeros((currency_count, sets), jnp.float32)
-    for first in range(0, chips, here):
-        carried = jnp.concatenate([carried_ref[first + chip] for chip in range(here)], axis=1)
-        projected = projected + lax.dot_general(
-            carried,
-            masked[:, first * owned : (first + here) * owned],
-            (((1,), (1,)), ((), ())),
-            preferred_element_type=jnp.float32,
-        )
-    return projected
+    currency = lax.broadcasted_iota(jnp.int32, (currency_count, sets), 0).astype(jnp.float32)
+    used_own = used_ref[...].astype(jnp.float32)
+    used_others = lent_ref[sets : sets + slots, 0:sets].astype(jnp.float32)
+    for masked, used, picked_ref in (
+        (lent_ref, used_others, others_ref),
+        (masked_own, used_own, own_ref),
+    ):
+        projected = jnp.zeros((currency_count, sets), jnp.float32)
+        for first in range(0, chips, here):
+            carried = jnp.concatenate(
+                [arrived_ref[place[first + chip], 0:currency_count, :] for chip in range(here)],
+                axis=1,
+            )
+            projected = projected + lax.dot_general(
+                carried,
+                masked[0:sets, first * owned : (first + here) * owned],
+                (((1,), (1,)), ((), ())),
+                preferred_element_type=jnp.float32,
+            )
+        for slot in range(slots):
+            picked_ref[slot : slot + 1, :] = jnp.sum(
+                jnp.where(currency == used[slot : slot + 1], projected, 0.0), axis=0, keepdims=True
+            )
 
 
 def adjoint_kernel(
-    dates,
-    arrived_ref,
-    carried_ref,
-    masked_own,
-    moved_ref,
-    discount_ref,
-    fx_adjoint_ref,
-    rate_adjoint_ref,
-    projected_ref,
+    dates, arrived_ref, moved_ref, discount_ref, fx_adjoint_ref, rate_adjoint_ref
 ):
-    chips, currency_count, owned = carried_ref.shape
+    currency_count = moved_ref.shape[0]
     aggregate = arrived_ref[0, currency_count:, :].astype(jnp.float32)
-    for chip in range(1, chips):
+    for chip in range(1, arrived_ref.shape[0]):
         aggregate = aggregate + arrived_ref[chip, currency_count:, :].astype(jnp.float32)
     fx_adjoint_ref[...] = aggregate * discount_ref[...]
     rate_adjoint_ref[...] = -step_years * sums_from_date(aggregate * moved_ref[...], dates)
-    projected_ref[...] = projection(masked_own, carried_ref)
-
-
-def picking_kernel(carried_ref, masked_other, projected_ref, used_ref, notional_adjoint_ref):
-    sets, half = masked_other.shape
-    currency_count = carried_ref.shape[1]
-    projected = projected_ref[...] + projection(masked_other, carried_ref)
-    used = used_ref[...]
-    currency = lax.broadcasted_iota(jnp.int32, (currency_count, sets), 0)
-    for slot in range(used.shape[0]):
-        picked = jnp.sum(
-            jnp.where(currency == used[slot : slot + 1], projected, 0.0), axis=0, keepdims=True
-        )
-        notional_adjoint_ref[slot : slot + 1, :] = picked * (1.0 / math.sqrt(2 * half))
+
+
+def adding_kernel(columns, own_ref, given_ref, notional_adjoint_ref):
+    notional_adjoint_ref[...] = (own_ref[...] + given_ref[...]) * (1.0 / math.sqrt(columns))
 
 
 def body(
@@ -310,11 +302,11 @@
     def swapped(value):
         return lax.ppermute(value, "sets", [(peer, peer ^ 1) for peer in range(peers)])
 
-    handed, masked_other, exposure, bits, weights, used, fx, rates, start = pl.pallas_call(
+    handed, lent, exposure, bits, weights, used, fx, rates, start = pl.pallas_call(
         first_kernel,
         out_shape=(
             pltpu.VMEM((chips,) + block, jnp.bfloat16),
-            pltpu.VMEM((sets, columns // 2), jnp.bfloat16),
+            pltpu.VMEM((sets + 16, columns // 2), jnp.bfloat16),
             pltpu.VMEM((sets, columns), jnp.bfloat16),
             pltpu.VMEM(positive_bits.shape, jnp.int32),
             pltpu.VMEM((currency_count, sets), jnp.bfloat16),
@@ -346,6 +338,7 @@
         in_hbm(start_integral.T),
     )
     given = swapped(handed)
+    borrowed = swapped(lent)
     masked_own, terms, carried, discount, moved = pl.pallas_call(
         functools.partial(second_kernel, dates),
         out_shape=(
@@ -376,35 +369,31 @@
         axis_index_groups=[[2 * chip + core for chip in group_order(chips)] for core in range(2)],
         tiled=True,
     )
-    carried_own = pl.pallas_call(
-        unpacking_kernel,
-        out_shape=pltpu.VMEM((chips,) + block, jnp.bfloat16),
-        in_specs=[in_vmem],
+    own_part, others_part = pl.pallas_call(
+        projecting_kernel,
+        out_shape=(pltpu.VMEM((slots, sets), jnp.float32),) * 2,
+        in_specs=[in_vmem] * 4,
+        out_specs=(in_vmem,) * 2,
+        compiler_params=params,
+        name="projecting",
+    )(arrived, masked_own, borrowed, used)
+    given_part = swapped(others_part)
+    fx_adjoint, rate_adjoint = pl.pallas_call(
+        functools.partial(adjoint_kernel, dates),
+        out_shape=(jax.ShapeDtypeStruct(block, jnp.float32),) * 2,
+        in_specs=[in_vmem] * 3,
+        out_specs=(in_vmem,) * 2,
+        compiler_params=params,
+        name="adjoint",
+    )(arrived, moved, discount)
+    notional_adjoint = pl.pallas_call(
+        functools.partial(adding_kernel, columns),
+        out_shape=jax.ShapeDtypeStruct((slots, sets), jnp.float32),
+        in_specs=[in_vmem] * 2,
         out_specs=in_vmem,
         compiler_params=params,
-        name="unpacking",
-    )(arrived)
-    carried_other = swapped(carried_own)
-    fx_adjoint, rate_adjoint, projected = pl.pallas_call(
-        functools.partial(adjoint_kernel, dates),
-        out_shape=(
-            jax.ShapeDtypeStruct(block, jnp.float32),
-            jax.ShapeDtypeStruct(block, jnp.float32),
-            pltpu.VMEM((currency_count, sets), jnp.float32),
-        ),
-        in_specs=[in_vmem] * 5,
-        out_specs=(in_vmem,) * 3,
-        compiler_params=params,
-        name="adjoint",
-    )(arrived, carried_own, masked_own, moved, discount)
-    notional_adjoint = pl.pallas_call(
-        picking_kernel,
-        out_shape=jax.ShapeDtypeStruct((slots, sets), jnp.float32),
-        in_specs=[in_vmem] * 4,
-        out_specs=in_vmem,
-        compiler_params=params,
-        name="picking",
-    )(carried_other, masked_other, projected, used)
+        name="adding",
+    )(own_part, given_part)
     return fx_adjoint, rate_adjoint, notional_adjoint.T
 
 

time: 19.2 us -> 20.1 us (1.047)
  waiting for transfers between devices: 0.92 us -> 1.49 us
    ppermute x2 -> x3, waiting for transfers between devices: 0.92 us -> 1.49 us  [swapped(): lax.ppermute(value, 'sets', [(peer, peer ^ 1) for peer in range(peers)])]
    ppermute x2 -> x3, starting transfers between devices: 0.58 us -> 0.66 us  [swapped(): lax.ppermute(value, 'sets', [(peer, peer ^ 1) for peer in range(peers)])]
  transfers between devices with their start and end apart: 2 -> 3, of which waited for: 2 -> 2; matrix products, arithmetic and copies ran while one was open for 0% -> 0% of each run, Pallas kernels for 7% -> 6%
where the time goes in v16:
time: 20.1 us; the launch traced here: 19.9 us
  blocking collectives  12.9 us (64%)
  Pallas kernels  4.12 us (20%)
  waiting for transfers between devices  1.49 us (7%)
  between operations  0.67 us (3%)
  starting transfers between devices  0.66 us (3%)
    all_to_all x1, blocking collectives, body(): lax.all_to_all(outgoing, 'sets', 0, 0, axis_index_groups=[[2 * chip + cor...  12.9 us
    pallas_call x1, Pallas kernels, body(): pl.pallas_call(first_kernel, out_shape=(pltpu.VMEM((chips,) + block, jnp....  1.81 us
    ppermute x3, waiting for transfers between devices, swapped(): lax.ppermute(value, 'sets', [(peer, peer ^ 1) for peer in range(peers)])  1.49 us
    pallas_call x1, Pallas kernels, body(): pl.pallas_call(functools.partial(adjoint_kernel, dates), out_shape=(jax.S...  0.83 us
    ppermute x3, starting transfers between devices, swapped(): lax.ppermute(value, 'sets', [(peer, peer ^ 1) for peer in range(peers)])  0.66 us
    pallas_call x1, Pallas kernels, body(): pl.pallas_call(functools.partial(adding_kernel, columns), out_shape=jax.S...  0.6 us
    pallas_call x1, Pallas kernels, body(): pl.pallas_call(projecting_kernel, out_shape=(pltpu.VMEM((slots, sets), jn...  0.45 us
  transfers between devices with their start and end apart: 3, of which 2 were waited for; matrix products, arithmetic and copies ran while one was open for 0% of the time, Pallas kernels for 6%

profile of v16, /device:TPU:0, one launch (start us, length us, event | category | flops | bytes accessed | tf_op | source)
XLA Modules:
  0.0 19.9 jit_solution(4193915085206494559)
XLA Ops:
  0.6 1.8 %first.1 = (bf16[8,40,128]{2,1,0:T(8,128)(2,1)S(1)}, bf16[256,1024]{1,0:T(8,128)(2,1)S(1)}, bf16[240,2048]{1,0:T(8,128)(2,1)S(1)}, s32[16,2048]{1,0:T(8,128)S(1)...) custom-call(bf16[240,2048]{1,0:T(8,128)(2,1)} %exposure_hbm.1, ...), custom_call_target="tpu_custom_call" | custom-call | tf_op jit(solution)/shard_map/first/pallas_call | solution.py:305
  2.5 0.5 %collective-permute-start.1 = (bf16[256,1024]{1,0:T(8,128)(2,1)S(1)}, bf16[256,1024]{1,0:T(8,128)(2,1)S(1)}, u32[]{:S(2)}, u32[]{:S(2)}) collective-permute-start(bf16[256,1024]{1,0:T(8,128)(2,1)S(1)} %get-tuple-element.35), channel_id=1, source_target_pairs={{0,1},{1,0},{2,3},{3,2},{4,5},{5,4},{6,7},{7,6},{8,9},{9,8},{10,11... | collective-permute-start | bytes 1572872 | tf_op jit(solution)/shard_map/ppermute | solution.py:303
  3.0 0.1 collective-permute-start
  3.0 0.4 %second.1 = (bf16[240,1024]{1,0:T(8,128)(2,1)S(1)}, f32[8,40,128]{2,1,0:T(8,128)S(1)}, bf16[40,128]{1,0:T(8,128)(2,1)S(1)}, f32[40,128]{1,0:T(8,128)S(1)}, f32[40,128]{1,0:T(8,128)S(1)}) custom-call(bf16[240,2048]{1,0:T(8,128)(2,1)S(1)} %get-tuple-element.22.exposure, s32[16,2048]{1,0:T(8,128)S(1)} %get-tuple-element.23.bits, ...), custom_call_target="tpu_custom_call" | custom-call | tf_op jit(solution)/shard_map/second/pallas_call | solution.py:342
  3.5 1.2 %collective-permute-done.given_ref = bf16[8,40,128]{2,1,0:T(8,128)(2,1)S(1)} collective-permute-done((bf16[8,40,128]{2,1,0:T(8,128)(2,1)S(1)}, bf16[8,40,128]{2,1,0:T(8,128)(2,1)S(1)}, u32[]{:S(2)}, u32[]{:S(2)}) %collective-permute-start) | collective-permute-done | bytes 81952 | tf_op jit(solution)/shard_map/ppermute | solution.py:303
  4.6 12.9 %all_to_all.5.arrived_ref = bf16[8,80,128]{2,1,0:T(8,128)(2,1)S(1)} all-to-all(bf16[8,80,128]{2,1,0:T(8,128)(2,1)S(1)} %merging.1), channel_id=1, replica_groups={{8,10,12,14,0,2,4,6},{9,11,13,15,1,3,5,7},{24,26,28,30,16,18,20,22},{25..., dimensions={0} | all-to-all | bytes 327680 | tf_op jit(solution)/shard_map/all_to_all | solution.py:364
  17.6 0.0 collective-permute-done.1.lent_ref
  17.6 0.5 %projecting.1 = (f32[4,240]{1,0:T(4,128)S(1)}, f32[4,240]{1,0:T(4,128)S(1)}) custom-call(bf16[8,80,128]{2,1,0:T(8,128)(2,1)S(1)} %all_to_all.5.arrived_ref, bf16[240,1024]{1,0:T(8,128)(2,1)S(1)} %get-tuple-element.34.masked_own, bf16[256,1024]{1,0:T(8,128)(2,1)S(1)} %collective-permute-done.1.lent_ref, s32[4,240]{1,0:T(4,128)S(1)} %get-tuple-element.36.used_ref), custom_call_target="tpu_custom_call" | custom-call | tf_op jit(solution)/shard_map/projecting/pallas_call | solution.py:372
  18.1 0.1 collective-permute-start.2
  18.1 0.8 %adjoint.1 = (f32[40,128]{1,0:T(8,128)}, f32[40,128]{1,0:T(8,128)}) custom-call(bf16[8,80,128]{2,1,0:T(8,128)(2,1)S(1)} %all_to_all.5.arrived_ref, f32[40,128]{1,0:T(8,128)S(1)} %get-tuple-element.30.moved_ref, f32[40,128]{1,0:T(8,128)S(1)} %get-tuple-element.31.discount_ref), custom_call_target="tpu_custom_call" | custom-call | tf_op jit(solution)/shard_map/adjoint/pallas_call | solution.py:381
  19.0 0.3 %collective-permute-done.2.given_ref = f32[4,240]{1,0:T(4,128)S(1)} collective-permute-done((f32[4,240]{1,0:T(4,128)S(1)}, f32[4,240]{1,0:T(4,128)S(1)}, u32[]{:S(2)}, u32[]{:S(2)}) %collective-permute-start.2) | collective-permute-done | bytes 3872 | tf_op jit(solution)/shard_map/ppermute | solution.py:303
  19.3 0.6 %adding.1 = f32[4,240]{1,0:T(4,128)} custom-call(f32[4,240]{1,0:T(4,128)S(1)} %get-tuple-element.37.own_ref, f32[4,240]{1,0:T(4,128)S(1)} %collective-permute-done.2.given_ref), custom_call_target="tpu_custom_call" | custom-call | tf_op jit(solution)/shard_map/adding/pallas_call | solution.py:389
  (1 shorter events, 0.0 us)
Async XLA Ops:
  2.5 15.1 %collective-permute-start.1 = (bf16[256,1024]{1,0:T(8,128)(2,1)S(1)}, bf16[256,1024]{1,0:T(8,128)(2,1)S(1)}, u32[]{:S(2)}, u32[]{:S(2)}) collective-permute-start(bf16[256,1024]{1,0:T(8,128)(2,1)S(1)} %get-tuple-element.35), channel_id=1, source_target_pairs={{0,1},{1,0},{2,3},{3,2},{4,5},{5,4},{6,7},{7,6},{8,9},{9,8},{10,11... | collective-permute-start | bytes 1572872 | tf_op jit(solution)/shard_map/ppermute | solution.py:303
  3.0 1.7 %collective-permute-start = (bf16[8,40,128]{2,1,0:T(8,128)(2,1)S(1)}, bf16[8,40,128]{2,1,0:T(8,128)(2,1)S(1)}, u32[]{:S(2)}, u32[]{:S(2)}) collective-permute-start(bf16[8,40,128]{2,1,0:T(8,128)(2,1)S(1)} %get-tuple-element.21), channel_id=1, source_target_pairs={{0,1},{1,0},{2,3},{3,2},{4,5},{5,4},{6,7},{7,6},{8,9},{9,8},{10,11... | collective-permute-start | bytes 245768 | tf_op jit(solution)/shard_map/ppermute | solution.py:303
  18.1 1.2 %collective-permute-start.2 = (f32[4,240]{1,0:T(4,128)S(1)}, f32[4,240]{1,0:T(4,128)S(1)}, u32[]{:S(2)}, u32[]{:S(2)}) collective-permute-start(f32[4,240]{1,0:T(4,128)S(1)} %get-tuple-element.38), channel_id=1, source_target_pairs={{0,1},{1,0},{2,3},{3,2},{4,5},{5,4},{6,7},{7,6},{8,9},{9,8},{10,11... | collective-permute-start | bytes 11528 | tf_op jit(solution)/shard_map/ppermute | solution.py:303

commit v17 on v14

--- a/solution.py
+++ b/solution.py
@@ -53,7 +53,9 @@
 
 def group_order(chips):
     middle = chips // 2
-    return list(range(middle, chips)) + list(range(middle))
+    far, near = list(range(middle, chips)), list(range(middle))
+    cut = middle // 2
+    return far[:cut] + near[:1] + far[cut:] + near[1:]
 
 
 def sibling_columns(chip, owned, core):
@@ -82,25 +84,30 @@
     return jnp.concatenate(kept, axis=0).astype(jnp.bfloat16)
 
 
-def mask_rows(exposure, bits, masked_ref, core, owned, first, last):
-    for pair in range(first // 16, last // 16):
-        flags = [row_flags(2 * pair), row_flags(2 * pair + 1)]
-        for chip in range(masked_ref.shape[1] // owned):
-            masked_ref[16 * pair : 16 * pair + 16, chip * owned : (chip + 1) * owned] = masked_rows(
-                exposure, bits, pair, flags, sibling_columns(chip, owned, core)
+def mask_and_sum(exposure, bits, weights, masked_ref, terms_ref, core):
+    sets = exposure.shape[0]
+    owned = terms_ref.shape[2]
+    for first in range(0, terms_ref.shape[0], 2):
+        rows = []
+        for pair in range(sets // 16):
+            flags = [row_flags(2 * pair), row_flags(2 * pair + 1)]
+            rows.append(
+                jnp.concatenate(
+                    [
+                        masked_rows(
+                            exposure, bits, pair, flags, sibling_columns(chip, owned, core)
+                        )
+                        for chip in (first, first + 1)
+                    ],
+                    axis=1,
+                )
             )
-
-
-def sum_sets(weights, masked_ref, terms_ref):
-    owned = terms_ref.shape[2]
-    for chip in range(0, terms_ref.shape[0], 2):
-        terms = jnp.dot(
-            weights,
-            masked_ref[:, chip * owned : (chip + 2) * owned],
-            preferred_element_type=jnp.float32,
-        ).astype(terms_ref.dtype)
-        terms_ref[chip] = terms[:, :owned]
-        terms_ref[chip + 1] = terms[:, owned:]
+        masked = jnp.concatenate(rows, axis=0)
+        masked_ref[:, first * owned : (first + 2) * owned] = masked
+        terms = jnp.dot(weights, masked, preferred_element_type=jnp.float32)
+        terms = terms.astype(terms_ref.dtype)
+        terms_ref[first] = terms[:, :owned]
+        terms_ref[first + 1] = terms[:, owned:]
 
 
 def first_kernel(
@@ -165,16 +172,6 @@
         exposure_copy(index).start()
     for copy in copies:
         copy.start()
-    for index in range(bits_parts):
-        bits_copy(index).wait()
-
-    other = 1 - lax.axis_index("sets") % 2
-    for index in range(parts):
-        exposure_copy(index).wait()
-        mask_rows(
-            exposure, bits, masked_ref, other, handed_ref.shape[2], index * rows, (index + 1) * rows
-        )
-
     for copy in copies:
         copy.wait()
     used = used_currencies(currencies_ref[...], counts_ref[...])
@@ -188,7 +185,12 @@
         )
     weights = weights.astype(jnp.bfloat16)
     weights_ref[...] = weights
-    sum_sets(weights, masked_ref, handed_ref)
+    for index in range(bits_parts):
+        bits_copy(index).wait()
+    for index in range(parts):
+        exposure_copy(index).wait()
+    other = 1 - lax.axis_index("sets") % 2
+    mask_and_sum(exposure, bits, weights, masked_ref, handed_ref, other)
 
 
 def second_kernel(
@@ -212,8 +214,7 @@
     moved_ref[...] = moved
     carried_ref[...] = moved.astype(jnp.bfloat16)
     own = lax.axis_index("sets") % 2
-    mask_rows(exposure, bits, masked_ref, own, terms_ref.shape[2], 0, exposure.shape[0])
-    sum_sets(weights_ref[...], masked_ref, terms_ref)
+    mask_and_sum(exposure, bits, weights_ref[...], masked_ref, terms_ref, own)
 
 
 def merging_kernel(given_ref, terms_ref, carried_ref, outgoing_ref):

time: 19.2 us -> 19.1 us (level)
  blocking collectives: 12.9 us -> 12.7 us
    all_to_all x1, blocking collectives: 12.9 us -> 12.7 us  [body(): lax.all_to_all(outgoing, 'sets', 0, 0, axis_index_groups=[[2 * chip + cor...]
  transfers between devices with their start and end apart: 2 -> 2, of which waited for: 2 -> 2; matrix products, arithmetic and copies ran while one was open for 0% -> 0% of each run, Pallas kernels for 7% -> 6%
where the time goes in v17:
time: 19.1 us; the launch traced here: 18.9 us
  blocking collectives  12.7 us (66%)
  Pallas kernels  3.94 us (21%)
  waiting for transfers between devices  1 us (5%)
  between operations  0.66 us (3%)
  starting transfers between devices  0.58 us (3%)
    all_to_all x1, blocking collectives, body(): lax.all_to_all(outgoing, 'sets', 0, 0, axis_index_groups=[[2 * chip + cor...  12.7 us
    pallas_call x1, Pallas kernels, body(): pl.pallas_call(first_kernel, out_shape=(pltpu.VMEM((chips,) + block, jnp....  1.86 us
    ppermute x2, waiting for transfers between devices, swapped(): lax.ppermute(value, 'sets', [(peer, peer ^ 1) for peer in range(peers)])  1 us
    pallas_call x1, Pallas kernels, body(): pl.pallas_call(picking_kernel, out_shape=jax.ShapeDtypeStruct((slots, set...  0.88 us
    pallas_call x1, Pallas kernels, body(): pl.pallas_call(functools.partial(adjoint_kernel, dates), out_shape=(jax.S...  0.85 us
    ppermute x2, starting transfers between devices, swapped(): lax.ppermute(value, 'sets', [(peer, peer ^ 1) for peer in range(peers)])  0.58 us
  transfers between devices with their start and end apart: 2, of which 2 were waited for; matrix products, arithmetic and copies ran while one was open for 0% of the time, Pallas kernels for 6%

profile of v17, /device:TPU:0, one launch (start us, length us, event | category | flops | bytes accessed | tf_op | source)
XLA Modules:
  0.0 18.9 jit_solution(1176527100194951119)
XLA Ops:
  0.6 1.9 %first.1 = (bf16[8,40,128]{2,1,0:T(8,128)(2,1)S(1)}, bf16[240,1024]{1,0:T(8,128)(2,1)S(1)}, bf16[240,2048]{1,0:T(8,128)(2,1)S(1)}, s32[16,2048]{1,0:T(8,128)S(1)...) custom-call(bf16[240,2048]{1,0:T(8,128)(2,1)} %exposure_hbm.1, ...), custom_call_target="tpu_custom_call" | custom-call | tf_op jit(solution)/shard_map/first/pallas_call | solution.py:314
  2.5 0.5 %collective-permute-start = (bf16[8,40,128]{2,1,0:T(8,128)(2,1)S(1)}, bf16[8,40,128]{2,1,0:T(8,128)(2,1)S(1)}, u32[]{:S(2)}, u32[]{:S(2)}) collective-permute-start(bf16[8,40,128]{2,1,0:T(8,128)(2,1)S(1)} %get-tuple-element.20), channel_id=1, source_target_pairs={{0,1},{1,0},{2,3},{3,2},{4,5},{5,4},{6,7},{7,6},{8,9},{9,8},{10,11... | collective-permute-start | bytes 245768 | tf_op jit(solution)/shard_map/ppermute | solution.py:312
  3.0 0.3 %second.1 = (bf16[240,1024]{1,0:T(8,128)(2,1)S(1)}, f32[8,40,128]{2,1,0:T(8,128)S(1)}, bf16[40,128]{1,0:T(8,128)(2,1)S(1)}, f32[40,128]{1,0:T(8,128)S(1)}, f32[40,128]{1,0:T(8,128)S(1)}) custom-call(bf16[240,2048]{1,0:T(8,128)(2,1)S(1)} %get-tuple-element.21.exposure, s32[16,2048]{1,0:T(8,128)S(1)} %get-tuple-element.22.bits, ...), custom_call_target="tpu_custom_call" | custom-call | tf_op jit(solution)/shard_map/second/pallas_call | solution.py:350
  3.3 0.6 %collective-permute-done.given_ref = bf16[8,40,128]{2,1,0:T(8,128)(2,1)S(1)} collective-permute-done((bf16[8,40,128]{2,1,0:T(8,128)(2,1)S(1)}, bf16[8,40,128]{2,1,0:T(8,128)(2,1)S(1)}, u32[]{:S(2)}, u32[]{:S(2)}) %collective-permute-start) | collective-permute-done | bytes 81952 | tf_op jit(solution)/shard_map/ppermute | solution.py:312
  4.0 12.7 %all_to_all.5.arrived_ref = bf16[8,80,128]{2,1,0:T(8,128)(2,1)S(1)} all-to-all(bf16[8,80,128]{2,1,0:T(8,128)(2,1)S(1)} %merging.1), channel_id=1, replica_groups={{8,10,0,12,14,2,4,6},{9,11,1,13,15,3,5,7},{24,26,16,28,30,18,20,22},{25..., dimensions={0} | all-to-all | bytes 327680 | tf_op jit(solution)/shard_map/all_to_all | solution.py:372
  16.7 0.1 collective-permute-start.1
  16.8 0.9 %adjoint.1 = (f32[40,128]{1,0:T(8,128)}, f32[40,128]{1,0:T(8,128)}, f32[40,240]{1,0:T(8,128)S(1)}) custom-call(bf16[8,80,128]{2,1,0:T(8,128)(2,1)S(1)} %all_to_all.5.arrived_ref, bf16[8,40,128]{2,1,0:T(8,128)(2,1)S(1)} %unpacking.1.carried_ref, bf16[240,1024]{1,0:T(8,128)(2,1)S(1)} %get-tuple-element.29.masked_own, ...), custom_call_target="tpu_custom_call" | custom-call | tf_op jit(solution)/shard_map/adjoint/pallas_call | solution.py:389
  17.6 0.4 %collective-permute-done.1.carried_ref = bf16[8,40,128]{2,1,0:T(8,128)(2,1)S(1)} collective-permute-done((bf16[8,40,128]{2,1,0:T(8,128)(2,1)S(1)}, bf16[8,40,128]{2,1,0:T(8,128)(2,1)S(1)}, u32[]{:S(2)}, u32[]{:S(2)}) %collective-permute-start.1) | collective-permute-done | bytes 81952 | tf_op jit(solution)/shard_map/ppermute | solution.py:312
  18.0 0.9 %picking.1 = f32[4,240]{1,0:T(4,128)} custom-call(bf16[8,40,128]{2,1,0:T(8,128)(2,1)S(1)} %collective-permute-done.1.carried_ref, bf16[240,1024]{1,0:T(8,128)(2,1)S(1)} %get-tuple-element.34.masked_other, f32[40,240]{1,0:T(8,128)S(1)} %get-tuple-element.35.projected_ref, s32[4,240]{1,0:T(4,128)S(1)} %get-tuple-element.36.used_ref), custom_call_target="tpu_custom_call" | custom-call | tf_op jit(solution)/shard_map/picking/pallas_call | solution.py:401
  (2 shorter events, 0.0 us)
Async XLA Ops:
  2.5 1.4 %collective-permute-start = (bf16[8,40,128]{2,1,0:T(8,128)(2,1)S(1)}, bf16[8,40,128]{2,1,0:T(8,128)(2,1)S(1)}, u32[]{:S(2)}, u32[]{:S(2)}) collective-permute-start(bf16[8,40,128]{2,1,0:T(8,128)(2,1)S(1)} %get-tuple-element.20), channel_id=1, source_target_pairs={{0,1},{1,0},{2,3},{3,2},{4,5},{5,4},{6,7},{7,6},{8,9},{9,8},{10,11... | collective-permute-start | bytes 245768 | tf_op jit(solution)/shard_map/ppermute | solution.py:312
  16.7 1.3 %collective-permute-start.1 = (bf16[8,40,128]{2,1,0:T(8,128)(2,1)S(1)}, bf16[8,40,128]{2,1,0:T(8,128)(2,1)S(1)}, u32[]{:S(2)}, u32[]{:S(2)}) collective-permute-start(bf16[8,40,128]{2,1,0:T(8,128)(2,1)S(1)} %unpacking.1.carried_ref), channel_id=1, source_target_pairs={{0,1},{1,0},{2,3},{3,2},{4,5},{5,4},{6,7},{7,6},{8,9},{9,8},{10,11... | collective-permute-start | bytes 245768 | tf_op jit(solution)/shard_map/ppermute | solution.py:312

commit v18 on v12

--- a/solution.py
+++ b/solution.py
@@ -53,7 +53,9 @@
 
 def group_order(chips):
     middle = chips // 2
-    return list(range(chips - 1, middle - 1, -1)) + list(range(middle))
+    far, near = list(range(middle, chips)), list(range(middle))
+    cut = middle // 2
+    return far[:cut] + near[:1] + far[cut:] + near[1:]
 
 
 def sibling_columns(chip, owned, core):
@@ -82,25 +84,35 @@
     return jnp.concatenate(kept, axis=0).astype(jnp.bfloat16)
 
 
-def mask_blocks(exposure, bits, masked_ref, core, owned, blocks):
-    for pair in range(masked_ref.shape[0] // 16):
-        flags = [row_flags(2 * pair), row_flags(2 * pair + 1)]
-        for chip in blocks:
-            masked_ref[16 * pair : 16 * pair + 16, chip * owned : (chip + 1) * owned] = masked_rows(
-                exposure, bits, pair, flags, chip * owned, sibling_columns(chip, owned, core)
+def mask_and_sum(exposure, bits, weights, masked_ref, terms_ref, core):
+    sets = exposure.shape[0]
+    owned = terms_ref.shape[2]
+    for first in range(0, terms_ref.shape[0], 2):
+        rows = []
+        for pair in range(sets // 16):
+            flags = [row_flags(2 * pair), row_flags(2 * pair + 1)]
+            rows.append(
+                jnp.concatenate(
+                    [
+                        masked_rows(
+                            exposure,
+                            bits,
+                            pair,
+                            flags,
+                            chip * owned,
+                            sibling_columns(chip, owned, core),
+                        )
+                        for chip in (first, first + 1)
+                    ],
+                    axis=1,
+                )
             )
-
-
-def sum_sets(weights, masked_ref, terms_ref):
-    owned = terms_ref.shape[2]
-    for chip in range(0, terms_ref.shape[0], 2):
-        terms = jnp.dot(
-            weights,
-            masked_ref[:, chip * owned : (chip + 2) * owned],
-            preferred_element_type=jnp.float32,
-        ).astype(terms_ref.dtype)
-        terms_ref[chip] = terms[:, :owned]
-        terms_ref[chip + 1] = terms[:, owned:]
+        masked = jnp.concatenate(rows, axis=0)
+        masked_ref[:, first * owned : (first + 2) * owned] = masked
+        terms = jnp.dot(weights, masked, preferred_element_type=jnp.float32)
+        terms = terms.astype(terms_ref.dtype)
+        terms_ref[first] = terms[:, :owned]
+        terms_ref[first + 1] = terms[:, owned:]
 
 
 def block_copies(exposure_hbm, exposure, sems, core, owned):
@@ -131,10 +143,18 @@
     notional_ref,
     sems,
     exposure_sems,
+    bits_sems,
 ):
     sets = exposure.shape[0]
     chips, currency_count, owned = handed_ref.shape
     other = 1 - lax.axis_index("sets") % 2
+    bits_parts = bits_sems.shape[0]
+    bits_width = bits.shape[1] // bits_parts
+
+    def bits_copy(index):
+        part = pl.ds(index * bits_width, bits_width)
+        return pltpu.make_async_copy(bits_hbm.at[:, part], bits.at[:, part], bits_sems.at[index])
+
     copies = [
         pltpu.make_async_copy(source, target, sems.at[index])
         for index, (source, target) in enumerate(
@@ -142,14 +162,15 @@
                 (currencies_hbm, currencies_ref),
                 (counts_hbm, counts_ref),
                 (notional_hbm, notional_ref),
-                (bits_hbm, bits),
             ]
         )
     ]
     exposure_copies = block_copies(exposure_hbm, exposure, exposure_sems, other, owned)
+    for copy in exposure_copies:
+        copy.start()
+    for index in range(bits_parts):
+        bits_copy(index).start()
     for copy in copies:
-        copy.start()
-    for copy in exposure_copies:
         copy.start()
     for copy in copies:
         copy.wait()
@@ -165,12 +186,11 @@
         )
     weights = weights.astype(jnp.bfloat16)
     weights_ref[...] = weights
-    step = 2
-    for first in range(0, chips, step):
-        for copy in exposure_copies[first : first + step]:
-            copy.wait()
-        mask_blocks(exposure, bits, masked_ref, other, owned, range(first, first + step))
-    sum_sets(weights, masked_ref, handed_ref)
+    for index in range(bits_parts):
+        bits_copy(index).wait()
+    for copy in exposure_copies:
+        copy.wait()
+    mask_and_sum(exposure, bits, weights, masked_ref, handed_ref, other)
 
 
 def second_kernel(
@@ -193,7 +213,7 @@
     sems,
     exposure_sems,
 ):
-    chips, currency_count, owned = terms_ref.shape
+    owned = terms_ref.shape[2]
     own = lax.axis_index("sets") % 2
     copies = [
         pltpu.make_async_copy(source, target, sems.at[index])
@@ -202,7 +222,7 @@
         )
     ]
     exposure_copies = block_copies(exposure_hbm, exposure, exposure_sems, own, owned)
-    for copy in copies + exposure_copies:
+    for copy in exposure_copies + copies:
         copy.start()
     for copy in copies:
         copy.wait()
@@ -214,8 +234,7 @@
     carried_ref[...] = moved.astype(jnp.bfloat16)
     for copy in exposure_copies:
         copy.wait()
-    mask_blocks(exposure, bits, masked_ref, own, owned, range(chips))
-    sum_sets(weights_ref[...], masked_ref, terms_ref)
+    mask_and_sum(exposure, bits, weights_ref[...], masked_ref, terms_ref, own)
 
 
 def merging_kernel(given_ref, terms_ref, carried_ref, outgoing_ref):
@@ -329,8 +348,9 @@
             pltpu.VMEM((slots, sets), jnp.int32),
             pltpu.VMEM((1, sets), jnp.int32),
             pltpu.VMEM((slots, sets), jnp.float32),
+            pltpu.SemaphoreType.DMA((3,)),
+            pltpu.SemaphoreType.DMA((chips,)),
             pltpu.SemaphoreType.DMA((4,)),
-            pltpu.SemaphoreType.DMA((chips,)),
         ],
         compiler_params=params,
         name="first",

time: 20 us -> 19.7 us (0.985)
  blocking collectives: 12.9 us -> 12.7 us
where the time goes in v18:
time: 19.7 us; the launch traced here: 19.4 us
  blocking collectives  12.7 us (64%)
  Pallas kernels  5.03 us (26%)
  between operations  0.67 us (3%)
  starting transfers between devices  0.59 us (3%)
  waiting for transfers between devices  0.41 us (2%)
    all_to_all x1, blocking collectives, body(): lax.all_to_all(outgoing, 'sets', 0, 0, axis_index_groups=[[2 * chip + cor...  12.7 us
    pallas_call x1, Pallas kernels, body(): pl.pallas_call(functools.partial(second_kernel, dates), out_shape=(pltpu....  1.68 us
    pallas_call x1, Pallas kernels, body(): pl.pallas_call(first_kernel, out_shape=(pltpu.VMEM((chips,) + block, jnp....  1.58 us
    pallas_call x1, Pallas kernels, body(): pl.pallas_call(picking_kernel, out_shape=jax.ShapeDtypeStruct((slots, set...  0.88 us
    pallas_call x1, Pallas kernels, body(): pl.pallas_call(functools.partial(adjoint_kernel, dates), out_shape=(jax.S...  0.85 us
    ppermute x2, starting transfers between devices, swapped(): lax.ppermute(value, 'sets', [(peer, peer ^ 1) for peer in range(peers)])  0.59 us
    ppermute x2, waiting for transfers between devices, swapped(): lax.ppermute(value, 'sets', [(peer, peer ^ 1) for peer in range(peers)])  0.41 us
  transfers between devices with their start and end apart: 2, of which 1 were waited for; matrix products, arithmetic and copies ran while one was open for 0% of the time, Pallas kernels for 13%

profile of v18, /device:TPU:0, one launch (start us, length us, event | category | flops | bytes accessed | tf_op | source)
XLA Modules:
  0.0 19.4 jit_solution(12430443157642227330)
XLA Ops:
  0.6 1.6 %first.1 = (bf16[8,40,128]{2,1,0:T(8,128)(2,1)S(1)}, bf16[240,1024]{1,0:T(8,128)(2,1)S(1)}, s32[16,2048]{1,0:T(8,128)S(1)}, bf16[40,240]{1,0:T(8,128)(2,1)S(1)}, s32[4,240]{1,0:T(4,128)S(1)}) custom-call(bf16[240,2048]{1,0:T(8,128)(2,1)} %exposure_hbm.3, s32[16,2048]{1,0:T(8,128)} %bits_hbm.1, s32[4,240]{1,0:T(4,128)} %bitcast.6, s32[1,240]{1,0:T(1,128)} %bitcast.9, ...), custom_call_target="tpu_custom_call" | custom-call | tf_op jit(solution)/shard_map/first/pallas_call | solution.py:335
  2.2 0.5 %collective-permute-start = (bf16[8,40,128]{2,1,0:T(8,128)(2,1)S(1)}, bf16[8,40,128]{2,1,0:T(8,128)(2,1)S(1)}, u32[]{:S(2)}, u32[]{:S(2)}) collective-permute-start(bf16[8,40,128]{2,1,0:T(8,128)(2,1)S(1)} %get-tuple-element.16), channel_id=1, source_target_pairs={{0,1},{1,0},{2,3},{3,2},{4,5},{5,4},{6,7},{7,6},{8,9},{9,8},{10,11... | collective-permute-start | bytes 245768 | tf_op jit(solution)/shard_map/ppermute | solution.py:332
  2.7 1.7 %second.1 = (bf16[240,1024]{1,0:T(8,128)(2,1)S(1)}, f32[8,40,128]{2,1,0:T(8,128)S(1)}, bf16[40,128]{1,0:T(8,128)(2,1)S(1)}, f32[40,128]{1,0:T(8,128)S(1)}, f32[40,128]{1,0:T(8,128)S(1)}) custom-call(bf16[240,2048]{1,0:T(8,128)(2,1)} %exposure_hbm.3, f32[40,128]{1,0:T(8,128)} %fx_hbm.1, f32[40,128]{1,0:T(8,128)} %rates_hbm.1, f32[16,40]{1,0:T(8,128)} %bitcast.5, ...), custom_call_target="tpu_custom_call" | custom-call | tf_op jit(solution)/shard_map/second/pallas_call | solution.py:365
  4.4 0.0 collective-permute-done.given_ref
  4.5 12.7 %all_to_all.5.arrived_ref = bf16[8,80,128]{2,1,0:T(8,128)(2,1)S(1)} all-to-all(bf16[8,80,128]{2,1,0:T(8,128)(2,1)S(1)} %merging.1), channel_id=1, replica_groups={{8,10,0,12,14,2,4,6},{9,11,1,13,15,3,5,7},{24,26,16,28,30,18,20,22},{25..., dimensions={0} | all-to-all | bytes 327680 | tf_op jit(solution)/shard_map/all_to_all | solution.py:402
  17.2 0.1 collective-permute-start.1
  17.3 0.9 %adjoint.1 = (f32[40,128]{1,0:T(8,128)}, f32[40,128]{1,0:T(8,128)}, f32[40,240]{1,0:T(8,128)S(1)}) custom-call(bf16[8,80,128]{2,1,0:T(8,128)(2,1)S(1)} %all_to_all.5.arrived_ref, bf16[8,40,128]{2,1,0:T(8,128)(2,1)S(1)} %unpacking.1.carried_ref, bf16[240,1024]{1,0:T(8,128)(2,1)S(1)} %get-tuple-element.21.masked_own, ...), custom_call_target="tpu_custom_call" | custom-call | tf_op jit(solution)/shard_map/adjoint/pallas_call | solution.py:419
  18.1 0.4 %collective-permute-done.1.carried_ref = bf16[8,40,128]{2,1,0:T(8,128)(2,1)S(1)} collective-permute-done((bf16[8,40,128]{2,1,0:T(8,128)(2,1)S(1)}, bf16[8,40,128]{2,1,0:T(8,128)(2,1)S(1)}, u32[]{:S(2)}, u32[]{:S(2)}) %collective-permute-start.1) | collective-permute-done | bytes 81952 | tf_op jit(solution)/shard_map/ppermute | solution.py:332
  18.5 0.9 %picking.1 = f32[4,240]{1,0:T(4,128)} custom-call(bf16[8,40,128]{2,1,0:T(8,128)(2,1)S(1)} %collective-permute-done.1.carried_ref, bf16[240,1024]{1,0:T(8,128)(2,1)S(1)} %get-tuple-element.26.masked_other, f32[40,240]{1,0:T(8,128)S(1)} %get-tuple-element.27.projected_ref, s32[4,240]{1,0:T(4,128)S(1)} %get-tuple-element.28.used_ref), custom_call_target="tpu_custom_call" | custom-call | tf_op jit(solution)/shard_map/picking/pallas_call | solution.py:431
  (2 shorter events, 0.0 us)
Async XLA Ops:
  2.2 2.2 %collective-permute-start = (bf16[8,40,128]{2,1,0:T(8,128)(2,1)S(1)}, bf16[8,40,128]{2,1,0:T(8,128)(2,1)S(1)}, u32[]{:S(2)}, u32[]{:S(2)}) collective-permute-start(bf16[8,40,128]{2,1,0:T(8,128)(2,1)S(1)} %get-tuple-element.16), channel_id=1, source_target_pairs={{0,1},{1,0},{2,3},{3,2},{4,5},{5,4},{6,7},{7,6},{8,9},{9,8},{10,11... | collective-permute-start | bytes 245768 | tf_op jit(solution)/shard_map/ppermute | solution.py:332
  17.2 1.3 %collective-permute-start.1 = (bf16[8,40,128]{2,1,0:T(8,128)(2,1)S(1)}, bf16[8,40,128]{2,1,0:T(8,128)(2,1)S(1)}, u32[]{:S(2)}, u32[]{:S(2)}) collective-permute-start(bf16[8,40,128]{2,1,0:T(8,128)(2,1)S(1)} %unpacking.1.carried_ref), channel_id=1, source_target_pairs={{0,1},{1,0},{2,3},{3,2},{4,5},{5,4},{6,7},{7,6},{8,9},{9,8},{10,11... | collective-permute-start | bytes 245768 | tf_op jit(solution)/shard_map/ppermute | solution.py:332

commit v19 on v18

--- a/solution.py
+++ b/solution.py
@@ -68,17 +68,17 @@
     return jnp.left_shift(jnp.int32(1), shift)
 
 
-def masked_rows(exposure, bits, pair, flags, column, packed_columns):
+def masked_rows(exposure, bits, pair, flags, part):
     row = lax.broadcasted_iota(jnp.int32, (8, lanes), 0)
-    values = exposure[16 * pair : 16 * pair + 16, column : column + lanes].astype(jnp.float32)
+    values = exposure[16 * pair : 16 * pair + 16, part].astype(jnp.float32)
     kept = []
     for half in range(2):
         top = 16 * pair + 8 * half
         group = top // bits_per_row
         left = bits_per_row * (group + 1) - top
-        packed = jnp.broadcast_to(bits[group : group + 1, packed_columns], (8, lanes))
+        packed = jnp.broadcast_to(bits[group : group + 1, part], (8, lanes))
         if left < 8:
-            following = jnp.broadcast_to(bits[group + 1 : group + 2, packed_columns], (8, lanes))
+            following = jnp.broadcast_to(bits[group + 1 : group + 2, part], (8, lanes))
             packed = jnp.where(row < left, packed, following)
         kept.append(jnp.where((packed & flags[half]) != 0, values[8 * half : 8 * half + 8], 0.0))
     return jnp.concatenate(kept, axis=0).astype(jnp.bfloat16)
@@ -95,12 +95,7 @@
                 jnp.concatenate(
                     [
                         masked_rows(
-                            exposure,
-                            bits,
-                            pair,
-                            flags,
-                            chip * owned,
-                            sibling_columns(chip, owned, core),
+                            exposure, bits, pair, flags, sibling_columns(chip, owned, core)
                         )
                         for chip in (first, first + 1)
                     ],
@@ -115,17 +110,6 @@
         terms_ref[first + 1] = terms[:, owned:]
 
 
-def block_copies(exposure_hbm, exposure, sems, core, owned):
-    return [
-        pltpu.make_async_copy(
-            exposure_hbm.at[:, sibling_columns(chip, owned, core)],
-            exposure.at[:, pl.ds(chip * owned, owned)],
-            sems.at[chip],
-        )
-        for chip in range(exposure.shape[1] // owned)
-    ]
-
-
 def first_kernel(
     exposure_hbm,
     bits_hbm,
@@ -134,45 +118,32 @@
     notional_hbm,
     handed_ref,
     masked_ref,
+    exposure,
     bits,
     weights_ref,
     used_ref,
-    exposure,
     currencies_ref,
     counts_ref,
     notional_ref,
     sems,
-    exposure_sems,
-    bits_sems,
 ):
     sets = exposure.shape[0]
-    chips, currency_count, owned = handed_ref.shape
-    other = 1 - lax.axis_index("sets") % 2
-    bits_parts = bits_sems.shape[0]
-    bits_width = bits.shape[1] // bits_parts
-
-    def bits_copy(index):
-        part = pl.ds(index * bits_width, bits_width)
-        return pltpu.make_async_copy(bits_hbm.at[:, part], bits.at[:, part], bits_sems.at[index])
-
+    currency_count = handed_ref.shape[1]
     copies = [
         pltpu.make_async_copy(source, target, sems.at[index])
         for index, (source, target) in enumerate(
             [
+                (exposure_hbm, exposure),
+                (bits_hbm, bits),
                 (currencies_hbm, currencies_ref),
                 (counts_hbm, counts_ref),
                 (notional_hbm, notional_ref),
             ]
         )
     ]
-    exposure_copies = block_copies(exposure_hbm, exposure, exposure_sems, other, owned)
-    for copy in exposure_copies:
-        copy.start()
-    for index in range(bits_parts):
-        bits_copy(index).start()
     for copy in copies:
         copy.start()
-    for copy in copies:
+    for copy in copies[2:]:
         copy.wait()
 
     used = used_currencies(currencies_ref[...], counts_ref[...])
@@ -186,44 +157,40 @@
         )
     weights = weights.astype(jnp.bfloat16)
     weights_ref[...] = weights
-    for index in range(bits_parts):
-        bits_copy(index).wait()
-    for copy in exposure_copies:
+    for copy in copies[:2]:
         copy.wait()
+    other = 1 - lax.axis_index("sets") % 2
     mask_and_sum(exposure, bits, weights, masked_ref, handed_ref, other)
 
 
 def second_kernel(
     dates,
-    exposure_hbm,
+    exposure,
+    bits,
+    weights_ref,
     fx_hbm,
     rates_hbm,
     start_hbm,
-    bits,
-    weights_ref,
     masked_ref,
     terms_ref,
     carried_ref,
     discount_ref,
     moved_ref,
-    exposure,
     fx_ref,
     rates_ref,
     start_ref,
     sems,
-    exposure_sems,
 ):
-    owned = terms_ref.shape[2]
-    own = lax.axis_index("sets") % 2
     copies = [
         pltpu.make_async_copy(source, target, sems.at[index])
         for index, (source, target) in enumerate(
             [(rates_hbm, rates_ref), (start_hbm, start_ref), (fx_hbm, fx_ref)]
         )
     ]
-    exposure_copies = block_copies(exposure_hbm, exposure, exposure_sems, own, owned)
-    for copy in exposure_copies + copies:
+    for copy in copies:
         copy.start()
+    own = lax.axis_index("sets") % 2
+    mask_and_sum(exposure, bits, weights_ref[...], masked_ref, terms_ref, own)
     for copy in copies:
         copy.wait()
     integral = spread_paths(start_ref[...], dates) + step_years * sums_to_date(rates_ref[...], dates)
@@ -232,9 +199,6 @@
     moved = fx_ref[...] * discount
     moved_ref[...] = moved
     carried_ref[...] = moved.astype(jnp.bfloat16)
-    for copy in exposure_copies:
-        copy.wait()
-    mask_and_sum(exposure, bits, weights_ref[...], masked_ref, terms_ref, own)
 
 
 def merging_kernel(given_ref, terms_ref, carried_ref, outgoing_ref):
@@ -331,31 +295,28 @@
     def swapped(value):
         return lax.ppermute(value, "sets", [(peer, peer ^ 1) for peer in range(peers)])
 
-    exposure_adjoint = in_hbm(exposure_adjoint)
-    handed, masked_other, bits, weights, used = pl.pallas_call(
+    handed, masked_other, exposure, bits, weights, used = pl.pallas_call(
         first_kernel,
         out_shape=(
             pltpu.VMEM((chips,) + block, jnp.bfloat16),
             pltpu.VMEM((sets, columns // 2), jnp.bfloat16),
+            pltpu.VMEM((sets, columns), jnp.bfloat16),
             pltpu.VMEM(positive_bits.shape, jnp.int32),
             pltpu.VMEM((currency_count, sets), jnp.bfloat16),
             pltpu.VMEM((slots, sets), jnp.int32),
         ),
         in_specs=[anywhere] * 5,
-        out_specs=(in_vmem,) * 5,
+        out_specs=(in_vmem,) * 6,
         scratch_shapes=[
-            pltpu.VMEM((sets, columns // 2), jnp.bfloat16),
             pltpu.VMEM((slots, sets), jnp.int32),
             pltpu.VMEM((1, sets), jnp.int32),
             pltpu.VMEM((slots, sets), jnp.float32),
-            pltpu.SemaphoreType.DMA((3,)),
-            pltpu.SemaphoreType.DMA((chips,)),
-            pltpu.SemaphoreType.DMA((4,)),
+            pltpu.SemaphoreType.DMA((5,)),
         ],
         compiler_params=params,
         name="first",
     )(
-        exposure_adjoint,
+        in_hbm(exposure_adjoint),
         in_hbm(positive_bits),
         in_hbm(currencies.T),
         in_hbm(mix_count.reshape(1, sets)),
@@ -371,25 +332,23 @@
             pltpu.VMEM(block, jnp.float32),
             pltpu.VMEM(block, jnp.float32),
         ),
-        in_specs=[anywhere] * 4 + [in_vmem] * 2,
+        in_specs=[in_vmem] * 3 + [anywhere] * 3,
         out_specs=(in_vmem,) * 5,
         scratch_shapes=[
-            pltpu.VMEM((sets, columns // 2), jnp.bfloat16),
             pltpu.VMEM(block, jnp.float32),
             pltpu.VMEM(block, jnp.float32),
             pltpu.VMEM((owned // dates, currency_count), jnp.float32),
             pltpu.SemaphoreType.DMA((3,)),
-            pltpu.SemaphoreType.DMA((chips,)),
         ],
         compiler_params=params,
         name="second",
     )(
-        exposure_adjoint,
+        exposure,
+        bits,
+        weights,
         in_hbm(fx_paths),
         in_hbm(short_rates),
         in_hbm(start_integral.T),
-        bits,
-        weights,
     )
     outgoing = pl.pallas_call(
         merging_kernel,

time: 19.7 us -> 19.2 us (0.975)
  Pallas kernels: 5.03 us -> 4.58 us
    pallas_call x1, Pallas kernels: 1.68 us -> 1.23 us  [body(): pl.pallas_call(functools.partial(second_kernel, dates), out_shape=(pltpu....]
  transfers between devices with their start and end apart: 2 -> 2, of which waited for: 1 -> 1; matrix products, arithmetic and copies ran while one was open for 0% -> 0% of each run, Pallas kernels for 13% -> 11%
where the time goes in v19:
time: 19.2 us; the launch traced here: 19 us
  blocking collectives  12.7 us (66%)
  Pallas kernels  4.58 us (24%)
  between operations  0.67 us (3%)
  starting transfers between devices  0.58 us (3%)
  waiting for transfers between devices  0.41 us (2%)
    all_to_all x1, blocking collectives, body(): lax.all_to_all(outgoing, 'sets', 0, 0, axis_index_groups=[[2 * chip + cor...  12.7 us
    pallas_call x1, Pallas kernels, body(): pl.pallas_call(first_kernel, out_shape=(pltpu.VMEM((chips,) + block, jnp....  1.58 us
    pallas_call x1, Pallas kernels, body(): pl.pallas_call(functools.partial(second_kernel, dates), out_shape=(pltpu....  1.23 us
    pallas_call x1, Pallas kernels, body(): pl.pallas_call(picking_kernel, out_shape=jax.ShapeDtypeStruct((slots, set...  0.88 us
    pallas_call x1, Pallas kernels, body(): pl.pallas_call(functools.partial(adjoint_kernel, dates), out_shape=(jax.S...  0.85 us
    ppermute x2, starting transfers between devices, swapped(): lax.ppermute(value, 'sets', [(peer, peer ^ 1) for peer in range(peers)])  0.58 us
    ppermute x2, waiting for transfers between devices, swapped(): lax.ppermute(value, 'sets', [(peer, peer ^ 1) for peer in range(peers)])  0.41 us
  transfers between devices with their start and end apart: 2, of which 1 were waited for; matrix products, arithmetic and copies ran while one was open for 0% of the time, Pallas kernels for 11%

profile of v19, /device:TPU:0, one launch (start us, length us, event | category | flops | bytes accessed | tf_op | source)
XLA Modules:
  0.0 19.0 jit_solution(10646094550785121008)
XLA Ops:
  0.6 1.6 %first.1 = (bf16[8,40,128]{2,1,0:T(8,128)(2,1)S(1)}, bf16[240,1024]{1,0:T(8,128)(2,1)S(1)}, bf16[240,2048]{1,0:T(8,128)(2,1)S(1)}, s32[16,2048]{1,0:T(8,128)S(1)...) custom-call(bf16[240,2048]{1,0:T(8,128)(2,1)} %exposure_hbm.1, s32[16,2048]{1,0:T(8,128)} %bits_hbm.1, ...), custom_call_target="tpu_custom_call" | custom-call | tf_op jit(solution)/shard_map/first/pallas_call | solution.py:298
  2.2 0.5 %collective-permute-start = (bf16[8,40,128]{2,1,0:T(8,128)(2,1)S(1)}, bf16[8,40,128]{2,1,0:T(8,128)(2,1)S(1)}, u32[]{:S(2)}, u32[]{:S(2)}) collective-permute-start(bf16[8,40,128]{2,1,0:T(8,128)(2,1)S(1)} %get-tuple-element.17), channel_id=1, source_target_pairs={{0,1},{1,0},{2,3},{3,2},{4,5},{5,4},{6,7},{7,6},{8,9},{9,8},{10,11... | collective-permute-start | bytes 245768 | tf_op jit(solution)/shard_map/ppermute | solution.py:296
  2.7 1.2 %second.1 = (bf16[240,1024]{1,0:T(8,128)(2,1)S(1)}, f32[8,40,128]{2,1,0:T(8,128)S(1)}, bf16[40,128]{1,0:T(8,128)(2,1)S(1)}, f32[40,128]{1,0:T(8,128)S(1)}, f32[40,128]{1,0:T(8,128)S(1)}) custom-call(bf16[240,2048]{1,0:T(8,128)(2,1)S(1)} %get-tuple-element.18.exposure, s32[16,2048]{1,0:T(8,128)S(1)} %get-tuple-element.19.bits, ...), custom_call_target="tpu_custom_call" | custom-call | tf_op jit(solution)/shard_map/second/pallas_call | solution.py:326
  4.0 0.0 collective-permute-done.given_ref
  4.0 12.7 %all_to_all.5.arrived_ref = bf16[8,80,128]{2,1,0:T(8,128)(2,1)S(1)} all-to-all(bf16[8,80,128]{2,1,0:T(8,128)(2,1)S(1)} %merging.1), channel_id=1, replica_groups={{8,10,0,12,14,2,4,6},{9,11,1,13,15,3,5,7},{24,26,16,28,30,18,20,22},{25..., dimensions={0} | all-to-all | bytes 327680 | tf_op jit(solution)/shard_map/all_to_all | solution.py:361
  16.7 0.1 collective-permute-start.1
  16.8 0.9 %adjoint.1 = (f32[40,128]{1,0:T(8,128)}, f32[40,128]{1,0:T(8,128)}, f32[40,240]{1,0:T(8,128)S(1)}) custom-call(bf16[8,80,128]{2,1,0:T(8,128)(2,1)S(1)} %all_to_all.5.arrived_ref, bf16[8,40,128]{2,1,0:T(8,128)(2,1)S(1)} %unpacking.1.carried_ref, bf16[240,1024]{1,0:T(8,128)(2,1)S(1)} %get-tuple-element.23.masked_own, ...), custom_call_target="tpu_custom_call" | custom-call | tf_op jit(solution)/shard_map/adjoint/pallas_call | solution.py:378
  17.7 0.4 %collective-permute-done.1.carried_ref = bf16[8,40,128]{2,1,0:T(8,128)(2,1)S(1)} collective-permute-done((bf16[8,40,128]{2,1,0:T(8,128)(2,1)S(1)}, bf16[8,40,128]{2,1,0:T(8,128)(2,1)S(1)}, u32[]{:S(2)}, u32[]{:S(2)}) %collective-permute-start.1) | collective-permute-done | bytes 81952 | tf_op jit(solution)/shard_map/ppermute | solution.py:296
  18.1 0.9 %picking.1 = f32[4,240]{1,0:T(4,128)} custom-call(bf16[8,40,128]{2,1,0:T(8,128)(2,1)S(1)} %collective-permute-done.1.carried_ref, bf16[240,1024]{1,0:T(8,128)(2,1)S(1)} %get-tuple-element.28.masked_other, f32[40,240]{1,0:T(8,128)S(1)} %get-tuple-element.29.projected_ref, s32[4,240]{1,0:T(4,128)S(1)} %get-tuple-element.30.used_ref), custom_call_target="tpu_custom_call" | custom-call | tf_op jit(solution)/shard_map/picking/pallas_call | solution.py:390
  (2 shorter events, 0.0 us)
Async XLA Ops:
  2.2 1.8 %collective-permute-start = (bf16[8,40,128]{2,1,0:T(8,128)(2,1)S(1)}, bf16[8,40,128]{2,1,0:T(8,128)(2,1)S(1)}, u32[]{:S(2)}, u32[]{:S(2)}) collective-permute-start(bf16[8,40,128]{2,1,0:T(8,128)(2,1)S(1)} %get-tuple-element.17), channel_id=1, source_target_pairs={{0,1},{1,0},{2,3},{3,2},{4,5},{5,4},{6,7},{7,6},{8,9},{9,8},{10,11... | collective-permute-start | bytes 245768 | tf_op jit(solution)/shard_map/ppermute | solution.py:296
  16.7 1.3 %collective-permute-start.1 = (bf16[8,40,128]{2,1,0:T(8,128)(2,1)S(1)}, bf16[8,40,128]{2,1,0:T(8,128)(2,1)S(1)}, u32[]{:S(2)}, u32[]{:S(2)}) collective-permute-start(bf16[8,40,128]{2,1,0:T(8,128)(2,1)S(1)} %unpacking.1.carried_ref), channel_id=1, source_target_pairs={{0,1},{1,0},{2,3},{3,2},{4,5},{5,4},{6,7},{7,6},{8,9},{9,8},{10,11... | collective-permute-start | bytes 245768 | tf_op jit(solution)/shard_map/ppermute | solution.py:296

commit v20 on v17

--- a/solution.py
+++ b/solution.py
@@ -132,48 +132,29 @@
     counts_ref,
     notional_ref,
     sems,
-    exposure_sems,
-    bits_sems,
 ):
     sets = exposure.shape[0]
-    chips, currency_count = handed_ref.shape[:2]
-    parts = exposure_sems.shape[0]
-    rows = sets // parts
-
-    def exposure_copy(index):
-        part = pl.ds(index * rows, rows)
-        return pltpu.make_async_copy(
-            exposure_hbm.at[part], exposure.at[part], exposure_sems.at[index]
-        )
-
-    bits_parts = bits_sems.shape[0]
-    bits_width = bits.shape[1] // bits_parts
-
-    def bits_copy(index):
-        part = pl.ds(index * bits_width, bits_width)
-        return pltpu.make_async_copy(bits_hbm.at[:, part], bits.at[:, part], bits_sems.at[index])
-
+    currency_count = handed_ref.shape[1]
     copies = [
         pltpu.make_async_copy(source, target, sems.at[index])
         for index, (source, target) in enumerate(
             [
+                (exposure_hbm, exposure),
+                (bits_hbm, bits),
                 (currencies_hbm, currencies_ref),
                 (counts_hbm, counts_ref),
                 (notional_hbm, notional_ref),
+                (fx_hbm, fx_ref),
                 (rates_hbm, rates_ref),
                 (start_hbm, start_ref),
-                (fx_hbm, fx_ref),
             ]
         )
     ]
-    for index in range(bits_parts):
-        bits_copy(index).start()
-    for index in range(parts):
-        exposure_copy(index).start()
     for copy in copies:
         copy.start()
-    for copy in copies:
+    for copy in copies[2:5]:
         copy.wait()
+
     used = used_currencies(currencies_ref[...], counts_ref[...])
     used_ref[...] = used
     notional = notional_ref[...]
@@ -185,12 +166,12 @@
         )
     weights = weights.astype(jnp.bfloat16)
     weights_ref[...] = weights
-    for index in range(bits_parts):
-        bits_copy(index).wait()
-    for index in range(parts):
-        exposure_copy(index).wait()
+    for copy in copies[:2]:
+        copy.wait()
     other = 1 - lax.axis_index("sets") % 2
     mask_and_sum(exposure, bits, weights, masked_ref, handed_ref, other)
+    for copy in copies[5:]:
+        copy.wait()
 
 
 def second_kernel(
@@ -207,14 +188,14 @@
     discount_ref,
     moved_ref,
 ):
+    own = lax.axis_index("sets") % 2
+    mask_and_sum(exposure, bits, weights_ref[...], masked_ref, terms_ref, own)
     integral = spread_paths(start_ref[...], dates) + step_years * sums_to_date(rates_ref[...], dates)
     discount = jnp.exp(-integral)
     discount_ref[...] = discount
     moved = fx_ref[...] * discount
     moved_ref[...] = moved
     carried_ref[...] = moved.astype(jnp.bfloat16)
-    own = lax.axis_index("sets") % 2
-    mask_and_sum(exposure, bits, weights_ref[...], masked_ref, terms_ref, own)
 
 
 def merging_kernel(given_ref, terms_ref, carried_ref, outgoing_ref):
@@ -330,9 +311,7 @@
             pltpu.VMEM((slots, sets), jnp.int32),
             pltpu.VMEM((1, sets), jnp.int32),
             pltpu.VMEM((slots, sets), jnp.float32),
-            pltpu.SemaphoreType.DMA((6,)),
-            pltpu.SemaphoreType.DMA((math.gcd(sets // 16, 5),)),
-            pltpu.SemaphoreType.DMA((4,)),
+            pltpu.SemaphoreType.DMA((8,)),
         ],
         compiler_params=params,
         name="first",
@@ -360,7 +339,14 @@
         out_specs=(in_vmem,) * 5,
         compiler_params=params,
         name="second",
-    )(exposure, bits, weights, fx, rates, start)
+    )(
+        exposure,
+        bits,
+        weights,
+        fx,
+        rates,
+        start,
+    )
     outgoing = pl.pallas_call(
         merging_kernel,
         out_shape=pltpu.VMEM((chips, 2 * currency_count, owned), jnp.bfloat16),

time: 19.1 us -> 18.8 us (0.984)
  Pallas kernels: 3.94 us -> 3.7 us
    pallas_call x1, Pallas kernels: 1.86 us -> 1.61 us  [body(): pl.pallas_call(first_kernel, out_shape=(pltpu.VMEM((chips,) + block, jnp....]
where the time goes in v20:
time: 18.8 us; the launch traced here: 18.7 us
  blocking collectives  12.7 us (68%)
  Pallas kernels  3.7 us (20%)
  waiting for transfers between devices  1.01 us (5%)
  between operations  0.66 us (4%)
  starting transfers between devices  0.58 us (3%)
    all_to_all x1, blocking collectives, body(): lax.all_to_all(outgoing, 'sets', 0, 0, axis_index_groups=[[2 * chip + cor...  12.7 us
    pallas_call x1, Pallas kernels, body(): pl.pallas_call(first_kernel, out_shape=(pltpu.VMEM((chips,) + block, jnp....  1.61 us
    ppermute x2, waiting for transfers between devices, swapped(): lax.ppermute(value, 'sets', [(peer, peer ^ 1) for peer in range(peers)])  1.01 us
    pallas_call x1, Pallas kernels, body(): pl.pallas_call(picking_kernel, out_shape=jax.ShapeDtypeStruct((slots, set...  0.88 us
    pallas_call x1, Pallas kernels, body(): pl.pallas_call(functools.partial(adjoint_kernel, dates), out_shape=(jax.S...  0.85 us
    ppermute x2, starting transfers between devices, swapped(): lax.ppermute(value, 'sets', [(peer, peer ^ 1) for peer in range(peers)])  0.58 us
  transfers between devices with their start and end apart: 2, of which 2 were waited for; matrix products, arithmetic and copies ran while one was open for 0% of the time, Pallas kernels for 6%

profile of v20, /device:TPU:0, one launch (start us, length us, event | category | flops | bytes accessed | tf_op | source)
XLA Modules:
  0.0 18.7 jit_solution(14090800863428412088)
XLA Ops:
  0.6 1.6 %first.1 = (bf16[8,40,128]{2,1,0:T(8,128)(2,1)S(1)}, bf16[240,1024]{1,0:T(8,128)(2,1)S(1)}, bf16[240,2048]{1,0:T(8,128)(2,1)S(1)}, s32[16,2048]{1,0:T(8,128)S(1)...) custom-call(bf16[240,2048]{1,0:T(8,128)(2,1)} %exposure_hbm.1, ...), custom_call_target="tpu_custom_call" | custom-call | tf_op jit(solution)/shard_map/first/pallas_call | solution.py:295
  2.3 0.5 %collective-permute-start = (bf16[8,40,128]{2,1,0:T(8,128)(2,1)S(1)}, bf16[8,40,128]{2,1,0:T(8,128)(2,1)S(1)}, u32[]{:S(2)}, u32[]{:S(2)}) collective-permute-start(bf16[8,40,128]{2,1,0:T(8,128)(2,1)S(1)} %get-tuple-element.20), channel_id=1, source_target_pairs={{0,1},{1,0},{2,3},{3,2},{4,5},{5,4},{6,7},{7,6},{8,9},{9,8},{10,11... | collective-permute-start | bytes 245768 | tf_op jit(solution)/shard_map/ppermute | solution.py:293
  2.8 0.3 %second.1 = (bf16[240,1024]{1,0:T(8,128)(2,1)S(1)}, f32[8,40,128]{2,1,0:T(8,128)S(1)}, bf16[40,128]{1,0:T(8,128)(2,1)S(1)}, f32[40,128]{1,0:T(8,128)S(1)}, f32[40,128]{1,0:T(8,128)S(1)}) custom-call(bf16[240,2048]{1,0:T(8,128)(2,1)S(1)} %get-tuple-element.21.exposure, s32[16,2048]{1,0:T(8,128)S(1)} %get-tuple-element.22.bits, ...), custom_call_target="tpu_custom_call" | custom-call | tf_op jit(solution)/shard_map/second/pallas_call | solution.py:329
  3.1 0.6 %collective-permute-done.given_ref = bf16[8,40,128]{2,1,0:T(8,128)(2,1)S(1)} collective-permute-done((bf16[8,40,128]{2,1,0:T(8,128)(2,1)S(1)}, bf16[8,40,128]{2,1,0:T(8,128)(2,1)S(1)}, u32[]{:S(2)}, u32[]{:S(2)}) %collective-permute-start) | collective-permute-done | bytes 81952 | tf_op jit(solution)/shard_map/ppermute | solution.py:293
  3.7 12.7 %all_to_all.5.arrived_ref = bf16[8,80,128]{2,1,0:T(8,128)(2,1)S(1)} all-to-all(bf16[8,80,128]{2,1,0:T(8,128)(2,1)S(1)} %merging.1), channel_id=1, replica_groups={{8,10,0,12,14,2,4,6},{9,11,1,13,15,3,5,7},{24,26,16,28,30,18,20,22},{25..., dimensions={0} | all-to-all | bytes 327680 | tf_op jit(solution)/shard_map/all_to_all | solution.py:358
  16.5 0.1 collective-permute-start.1
  16.5 0.9 %adjoint.1 = (f32[40,128]{1,0:T(8,128)}, f32[40,128]{1,0:T(8,128)}, f32[40,240]{1,0:T(8,128)S(1)}) custom-call(bf16[8,80,128]{2,1,0:T(8,128)(2,1)S(1)} %all_to_all.5.arrived_ref, bf16[8,40,128]{2,1,0:T(8,128)(2,1)S(1)} %unpacking.1.carried_ref, bf16[240,1024]{1,0:T(8,128)(2,1)S(1)} %get-tuple-element.29.masked_own, ...), custom_call_target="tpu_custom_call" | custom-call | tf_op jit(solution)/shard_map/adjoint/pallas_call | solution.py:375
  17.4 0.4 %collective-permute-done.1.carried_ref = bf16[8,40,128]{2,1,0:T(8,128)(2,1)S(1)} collective-permute-done((bf16[8,40,128]{2,1,0:T(8,128)(2,1)S(1)}, bf16[8,40,128]{2,1,0:T(8,128)(2,1)S(1)}, u32[]{:S(2)}, u32[]{:S(2)}) %collective-permute-start.1) | collective-permute-done | bytes 81952 | tf_op jit(solution)/shard_map/ppermute | solution.py:293
  17.8 0.9 %picking.1 = f32[4,240]{1,0:T(4,128)} custom-call(bf16[8,40,128]{2,1,0:T(8,128)(2,1)S(1)} %collective-permute-done.1.carried_ref, bf16[240,1024]{1,0:T(8,128)(2,1)S(1)} %get-tuple-element.34.masked_other, f32[40,240]{1,0:T(8,128)S(1)} %get-tuple-element.35.projected_ref, s32[4,240]{1,0:T(4,128)S(1)} %get-tuple-element.36.used_ref), custom_call_target="tpu_custom_call" | custom-call | tf_op jit(solution)/shard_map/picking/pallas_call | solution.py:387
  (2 shorter events, 0.0 us)
Async XLA Ops:
  2.3 1.4 %collective-permute-start = (bf16[8,40,128]{2,1,0:T(8,128)(2,1)S(1)}, bf16[8,40,128]{2,1,0:T(8,128)(2,1)S(1)}, u32[]{:S(2)}, u32[]{:S(2)}) collective-permute-start(bf16[8,40,128]{2,1,0:T(8,128)(2,1)S(1)} %get-tuple-element.20), channel_id=1, source_target_pairs={{0,1},{1,0},{2,3},{3,2},{4,5},{5,4},{6,7},{7,6},{8,9},{9,8},{10,11... | collective-permute-start | bytes 245768 | tf_op jit(solution)/shard_map/ppermute | solution.py:293
  16.5 1.3 %collective-permute-start.1 = (bf16[8,40,128]{2,1,0:T(8,128)(2,1)S(1)}, bf16[8,40,128]{2,1,0:T(8,128)(2,1)S(1)}, u32[]{:S(2)}, u32[]{:S(2)}) collective-permute-start(bf16[8,40,128]{2,1,0:T(8,128)(2,1)S(1)} %unpacking.1.carried_ref), channel_id=1, source_target_pairs={{0,1},{1,0},{2,3},{3,2},{4,5},{5,4},{6,7},{7,6},{8,9},{9,8},{10,11... | collective-permute-start | bytes 245768 | tf_op jit(solution)/shard_map/ppermute | solution.py:293

commit v21 on v20

--- a/solution.py
+++ b/solution.py
@@ -51,11 +51,18 @@
     return jnp.where(slot < counts, currencies, -1)
 
 
-def group_order(chips):
+def group_order(chips, core):
     middle = chips // 2
     far, near = list(range(middle, chips)), list(range(middle))
+    if core:
+        return far[::-1] + near
     cut = middle // 2
     return far[:cut] + near[:1] + far[cut:] + near[1:]
+
+
+def chip_at(chips, place):
+    even, odd = (group_order(chips, core)[place] for core in range(2))
+    return jnp.where(lax.axis_index("sets") % 2 == 0, even, odd)
 
 
 def sibling_columns(chip, owned, core):
@@ -200,20 +207,19 @@
 
 def merging_kernel(given_ref, terms_ref, carried_ref, outgoing_ref):
     chips, currency_count, owned = terms_ref.shape
-    order = group_order(chips)
     carried = carried_ref[...]
     for place in range(chips):
+        chip = chip_at(chips, place)
         outgoing_ref[place, 0:currency_count, :] = carried
         outgoing_ref[place, currency_count:, :] = (
-            terms_ref[order[place]] + given_ref[order[place]].astype(jnp.float32)
+            terms_ref[chip] + given_ref[chip].astype(jnp.float32)
         ).astype(jnp.bfloat16)
 
 
 def unpacking_kernel(arrived_ref, carried_ref):
     chips, currency_count, owned = carried_ref.shape
-    order = group_order(chips)
     for place in range(chips):
-        carried_ref[order[place]] = arrived_ref[place, 0:currency_count, :]
+        carried_ref[chip_at(chips, place)] = arrived_ref[place, 0:currency_count, :]
 
 
 def projection(masked, carried_ref):
@@ -360,7 +366,9 @@
         "sets",
         0,
         0,
-        axis_index_groups=[[2 * chip + core for chip in group_order(chips)] for core in range(2)],
+        axis_index_groups=[
+            [2 * chip + core for chip in group_order(chips, core)] for core in range(2)
+        ],
         tiled=True,
     )
     carried_own = pl.pallas_call(

time: 18.8 us -> 19 us (1.011)
  no operation moved by 1% of the time
where the time goes in v21:
time: 19 us; the launch traced here: 18.8 us
  blocking collectives  12.8 us (67%)
  Pallas kernels  3.71 us (20%)
  waiting for transfers between devices  1.01 us (5%)
  between operations  0.66 us (3%)
  starting transfers between devices  0.58 us (3%)
    all_to_all x1, blocking collectives, body(): lax.all_to_all(outgoing, 'sets', 0, 0, axis_index_groups=[[2 * chip + cor...  12.8 us
    pallas_call x1, Pallas kernels, body(): pl.pallas_call(first_kernel, out_shape=(pltpu.VMEM((chips,) + block, jnp....  1.61 us
    ppermute x2, waiting for transfers between devices, swapped(): lax.ppermute(value, 'sets', [(peer, peer ^ 1) for peer in range(peers)])  1.01 us
    pallas_call x1, Pallas kernels, body(): pl.pallas_call(picking_kernel, out_shape=jax.ShapeDtypeStruct((slots, set...  0.88 us
    pallas_call x1, Pallas kernels, body(): pl.pallas_call(functools.partial(adjoint_kernel, dates), out_shape=(jax.S...  0.85 us
    ppermute x2, starting transfers between devices, swapped(): lax.ppermute(value, 'sets', [(peer, peer ^ 1) for peer in range(peers)])  0.58 us
  transfers between devices with their start and end apart: 2, of which 2 were waited for; matrix products, arithmetic and copies ran while one was open for 0% of the time, Pallas kernels for 6%

profile of v21, /device:TPU:0, one launch (start us, length us, event | category | flops | bytes accessed | tf_op | source)
XLA Modules:
  0.0 18.8 jit_solution(10310277006533894166)
XLA Ops:
  0.6 1.6 %first.1 = (bf16[8,40,128]{2,1,0:T(8,128)(2,1)S(1)}, bf16[240,1024]{1,0:T(8,128)(2,1)S(1)}, bf16[240,2048]{1,0:T(8,128)(2,1)S(1)}, s32[16,2048]{1,0:T(8,128)S(1)...) custom-call(bf16[240,2048]{1,0:T(8,128)(2,1)} %exposure_hbm.1, ...), custom_call_target="tpu_custom_call" | custom-call | tf_op jit(solution)/shard_map/first/pallas_call | solution.py:301
  2.3 0.5 %collective-permute-start = (bf16[8,40,128]{2,1,0:T(8,128)(2,1)S(1)}, bf16[8,40,128]{2,1,0:T(8,128)(2,1)S(1)}, u32[]{:S(2)}, u32[]{:S(2)}) collective-permute-start(bf16[8,40,128]{2,1,0:T(8,128)(2,1)S(1)} %get-tuple-element.20), channel_id=1, source_target_pairs={{0,1},{1,0},{2,3},{3,2},{4,5},{5,4},{6,7},{7,6},{8,9},{9,8},{10,11... | collective-permute-start | bytes 245768 | tf_op jit(solution)/shard_map/ppermute | solution.py:299
  2.8 0.3 %second.1 = (bf16[240,1024]{1,0:T(8,128)(2,1)S(1)}, f32[8,40,128]{2,1,0:T(8,128)S(1)}, bf16[40,128]{1,0:T(8,128)(2,1)S(1)}, f32[40,128]{1,0:T(8,128)S(1)}, f32[40,128]{1,0:T(8,128)S(1)}) custom-call(bf16[240,2048]{1,0:T(8,128)(2,1)S(1)} %get-tuple-element.21.exposure, s32[16,2048]{1,0:T(8,128)S(1)} %get-tuple-element.22.bits, ...), custom_call_target="tpu_custom_call" | custom-call | tf_op jit(solution)/shard_map/second/pallas_call | solution.py:335
  3.1 0.6 %collective-permute-done.given_ref = bf16[8,40,128]{2,1,0:T(8,128)(2,1)S(1)} collective-permute-done((bf16[8,40,128]{2,1,0:T(8,128)(2,1)S(1)}, bf16[8,40,128]{2,1,0:T(8,128)(2,1)S(1)}, u32[]{:S(2)}, u32[]{:S(2)}) %collective-permute-start) | collective-permute-done | bytes 81952 | tf_op jit(solution)/shard_map/ppermute | solution.py:299
  3.7 12.8 %all_to_all.5.arrived_ref = bf16[8,80,128]{2,1,0:T(8,128)(2,1)S(1)} all-to-all(bf16[8,80,128]{2,1,0:T(8,128)(2,1)S(1)} %merging.1), channel_id=1, replica_groups={{8,10,0,12,14,2,4,6},{15,13,11,9,1,3,5,7},{24,26,16,28,30,18,20,22},{31..., dimensions={0} | all-to-all | bytes 327680 | tf_op jit(solution)/shard_map/all_to_all | solution.py:364
  16.6 0.1 collective-permute-start.1
  16.7 0.9 %adjoint.1 = (f32[40,128]{1,0:T(8,128)}, f32[40,128]{1,0:T(8,128)}, f32[40,240]{1,0:T(8,128)S(1)}) custom-call(bf16[8,80,128]{2,1,0:T(8,128)(2,1)S(1)} %all_to_all.5.arrived_ref, bf16[8,40,128]{2,1,0:T(8,128)(2,1)S(1)} %unpacking.1.carried_ref, bf16[240,1024]{1,0:T(8,128)(2,1)S(1)} %get-tuple-element.29.masked_own, ...), custom_call_target="tpu_custom_call" | custom-call | tf_op jit(solution)/shard_map/adjoint/pallas_call | solution.py:383
  17.5 0.4 %collective-permute-done.1.carried_ref = bf16[8,40,128]{2,1,0:T(8,128)(2,1)S(1)} collective-permute-done((bf16[8,40,128]{2,1,0:T(8,128)(2,1)S(1)}, bf16[8,40,128]{2,1,0:T(8,128)(2,1)S(1)}, u32[]{:S(2)}, u32[]{:S(2)}) %collective-permute-start.1) | collective-permute-done | bytes 81952 | tf_op jit(solution)/shard_map/ppermute | solution.py:299
  17.9 0.9 %picking.1 = f32[4,240]{1,0:T(4,128)} custom-call(bf16[8,40,128]{2,1,0:T(8,128)(2,1)S(1)} %collective-permute-done.1.carried_ref, bf16[240,1024]{1,0:T(8,128)(2,1)S(1)} %get-tuple-element.34.masked_other, f32[40,240]{1,0:T(8,128)S(1)} %get-tuple-element.35.projected_ref, s32[4,240]{1,0:T(4,128)S(1)} %get-tuple-element.36.used_ref), custom_call_target="tpu_custom_call" | custom-call | tf_op jit(solution)/shard_map/picking/pallas_call | solution.py:395
  (2 shorter events, 0.0 us)
Async XLA Ops:
  2.3 1.4 %collective-permute-start = (bf16[8,40,128]{2,1,0:T(8,128)(2,1)S(1)}, bf16[8,40,128]{2,1,0:T(8,128)(2,1)S(1)}, u32[]{:S(2)}, u32[]{:S(2)}) collective-permute-start(bf16[8,40,128]{2,1,0:T(8,128)(2,1)S(1)} %get-tuple-element.20), channel_id=1, source_target_pairs={{0,1},{1,0},{2,3},{3,2},{4,5},{5,4},{6,7},{7,6},{8,9},{9,8},{10,11... | collective-permute-start | bytes 245768 | tf_op jit(solution)/shard_map/ppermute | solution.py:299
  16.6 1.3 %collective-permute-start.1 = (bf16[8,40,128]{2,1,0:T(8,128)(2,1)S(1)}, bf16[8,40,128]{2,1,0:T(8,128)(2,1)S(1)}, u32[]{:S(2)}, u32[]{:S(2)}) collective-permute-start(bf16[8,40,128]{2,1,0:T(8,128)(2,1)S(1)} %unpacking.1.carried_ref), channel_id=1, source_target_pairs={{0,1},{1,0},{2,3},{3,2},{4,5},{5,4},{6,7},{7,6},{8,9},{9,8},{10,11... | collective-permute-start | bytes 245768 | tf_op jit(solution)/shard_map/ppermute | solution.py:299

commit v22 on v20

--- a/solution.py
+++ b/solution.py
@@ -58,8 +58,18 @@
     return far[:cut] + near[:1] + far[cut:] + near[1:]
 
 
-def sibling_columns(chip, owned, core):
-    return pl.ds(pl.multiple_of((2 * chip + core) * owned, owned), owned)
+def core_in(chips, chip, group):
+    return 1 - group if chip >= chips // 2 else group
+
+
+def own_group(chips):
+    me = lax.axis_index("sets")
+    return jnp.where(me >= chips, 1 - me % 2, me % 2)
+
+
+def group_columns(chips, chip, owned, group):
+    block = 2 * chip + core_in(chips, chip, group)
+    return pl.ds(pl.multiple_of(block * owned, owned), owned)
 
 
 def row_flags(tile):
@@ -84,10 +94,10 @@
     return jnp.concatenate(kept, axis=0).astype(jnp.bfloat16)
 
 
-def mask_and_sum(exposure, bits, weights, masked_ref, terms_ref, core):
+def mask_and_sum(exposure, bits, weights, masked_ref, terms_ref, group):
     sets = exposure.shape[0]
-    owned = terms_ref.shape[2]
-    for first in range(0, terms_ref.shape[0], 2):
+    chips, owned = terms_ref.shape[0], terms_ref.shape[2]
+    for first in range(0, chips, 2):
         rows = []
         for pair in range(sets // 16):
             flags = [row_flags(2 * pair), row_flags(2 * pair + 1)]
@@ -95,7 +105,7 @@
                 jnp.concatenate(
                     [
                         masked_rows(
-                            exposure, bits, pair, flags, sibling_columns(chip, owned, core)
+                            exposure, bits, pair, flags, group_columns(chips, chip, owned, group)
                         )
                         for chip in (first, first + 1)
                     ],
@@ -168,7 +178,7 @@
     weights_ref[...] = weights
     for copy in copies[:2]:
         copy.wait()
-    other = 1 - lax.axis_index("sets") % 2
+    other = 1 - own_group(handed_ref.shape[0])
     mask_and_sum(exposure, bits, weights, masked_ref, handed_ref, other)
     for copy in copies[5:]:
         copy.wait()
@@ -188,7 +198,7 @@
     discount_ref,
     moved_ref,
 ):
-    own = lax.axis_index("sets") % 2
+    own = own_group(terms_ref.shape[0])
     mask_and_sum(exposure, bits, weights_ref[...], masked_ref, terms_ref, own)
     integral = spread_paths(start_ref[...], dates) + step_years * sums_to_date(rates_ref[...], dates)
     discount = jnp.exp(-integral)
@@ -360,7 +370,10 @@
         "sets",
         0,
         0,
-        axis_index_groups=[[2 * chip + core for chip in group_order(chips)] for core in range(2)],
+        axis_index_groups=[
+            [2 * chip + core_in(chips, chip, group) for chip in group_order(chips)]
+            for group in range(2)
+        ],
         tiled=True,
     )
     carried_own = pl.pallas_call(

time: 18.8 us -> 18.3 us (0.973)
  blocking collectives: 12.7 us -> 11.4 us
  starting transfers between devices: 0.58 us -> 1.75 us
  waiting for transfers between devices: 1.01 us -> 0.67 us
    all_to_all x1, blocking collectives: 12.7 us -> 11.4 us  [body(): lax.all_to_all(outgoing, 'sets', 0, 0, axis_index_groups=[[2 * chip + cor...]
    ppermute x2, starting transfers between devices: 0.58 us -> 1.75 us  [swapped(): lax.ppermute(value, 'sets', [(peer, peer ^ 1) for peer in range(peers)])]
    ppermute x2, waiting for transfers between devices: 1.01 us -> 0.67 us  [swapped(): lax.ppermute(value, 'sets', [(peer, peer ^ 1) for peer in range(peers)])]
  transfers between devices with their start and end apart: 2 -> 2, of which waited for: 2 -> 2; matrix products, arithmetic and copies ran while one was open for 0% -> 0% of each run, Pallas kernels for 6% -> 7%
where the time goes in v22:
time: 18.3 us; the launch traced here: 18.1 us
  blocking collectives  11.4 us (62%)
  Pallas kernels  3.69 us (20%)
  starting transfers between devices  1.75 us (10%)
  waiting for transfers between devices  0.67 us (4%)
  between operations  0.65 us (4%)
    all_to_all x1, blocking collectives, body(): lax.all_to_all(outgoing, 'sets', 0, 0, axis_index_groups=[[2 * chip + cor...  11.4 us
    ppermute x2, starting transfers between devices, swapped(): lax.ppermute(value, 'sets', [(peer, peer ^ 1) for peer in range(peers)])  1.75 us
    pallas_call x1, Pallas kernels, body(): pl.pallas_call(first_kernel, out_shape=(pltpu.VMEM((chips,) + block, jnp....  1.61 us
    pallas_call x1, Pallas kernels, body(): pl.pallas_call(picking_kernel, out_shape=jax.ShapeDtypeStruct((slots, set...  0.88 us
    pallas_call x1, Pallas kernels, body(): pl.pallas_call(functools.partial(adjoint_kernel, dates), out_shape=(jax.S...  0.85 us
    ppermute x2, waiting for transfers between devices, swapped(): lax.ppermute(value, 'sets', [(peer, peer ^ 1) for peer in range(peers)])  0.67 us
  transfers between devices with their start and end apart: 2, of which 2 were waited for; matrix products, arithmetic and copies ran while one was open for 0% of the time, Pallas kernels for 7%

profile of v22, /device:TPU:0, one launch (start us, length us, event | category | flops | bytes accessed | tf_op | source)
XLA Modules:
  0.0 18.1 jit_solution(5048459639396438377)
XLA Ops:
  0.6 1.6 %first.1 = (bf16[8,40,128]{2,1,0:T(8,128)(2,1)S(1)}, bf16[240,1024]{1,0:T(8,128)(2,1)S(1)}, bf16[240,2048]{1,0:T(8,128)(2,1)S(1)}, s32[16,2048]{1,0:T(8,128)S(1)...) custom-call(bf16[240,2048]{1,0:T(8,128)(2,1)} %exposure_hbm.1, ...), custom_call_target="tpu_custom_call" | custom-call | tf_op jit(solution)/shard_map/first/pallas_call | solution.py:305
  2.2 0.5 %collective-permute-start = (bf16[8,40,128]{2,1,0:T(8,128)(2,1)S(1)}, bf16[8,40,128]{2,1,0:T(8,128)(2,1)S(1)}, u32[]{:S(2)}, u32[]{:S(2)}) collective-permute-start(bf16[8,40,128]{2,1,0:T(8,128)(2,1)S(1)} %get-tuple-element.20), channel_id=1, source_target_pairs={{0,1},{1,0},{2,3},{3,2},{4,5},{5,4},{6,7},{7,6},{8,9},{9,8},{10,11... | collective-permute-start | bytes 245768 | tf_op jit(solution)/shard_map/ppermute | solution.py:303
  2.8 0.3 %second.1 = (bf16[240,1024]{1,0:T(8,128)(2,1)S(1)}, f32[8,40,128]{2,1,0:T(8,128)S(1)}, bf16[40,128]{1,0:T(8,128)(2,1)S(1)}, f32[40,128]{1,0:T(8,128)S(1)}, f32[40,128]{1,0:T(8,128)S(1)}) custom-call(bf16[240,2048]{1,0:T(8,128)(2,1)S(1)} %get-tuple-element.21.exposure, s32[16,2048]{1,0:T(8,128)S(1)} %get-tuple-element.22.bits, ...), custom_call_target="tpu_custom_call" | custom-call | tf_op jit(solution)/shard_map/second/pallas_call | solution.py:339
  3.1 0.6 %collective-permute-done.given_ref = bf16[8,40,128]{2,1,0:T(8,128)(2,1)S(1)} collective-permute-done((bf16[8,40,128]{2,1,0:T(8,128)(2,1)S(1)}, bf16[8,40,128]{2,1,0:T(8,128)(2,1)S(1)}, u32[]{:S(2)}, u32[]{:S(2)}) %collective-permute-start) | collective-permute-done | bytes 81952 | tf_op jit(solution)/shard_map/ppermute | solution.py:303
  3.7 11.4 %all_to_all.5.arrived_ref = bf16[8,80,128]{2,1,0:T(8,128)(2,1)S(1)} all-to-all(bf16[8,80,128]{2,1,0:T(8,128)(2,1)S(1)} %merging.1), channel_id=1, replica_groups={{9,11,0,13,15,2,4,6},{8,10,1,12,14,3,5,7},{25,27,16,29,31,18,20,22},{24..., dimensions={0} | all-to-all | bytes 327680 | tf_op jit(solution)/shard_map/all_to_all | solution.py:368
  15.1 1.2 %collective-permute-start.1 = (bf16[8,40,128]{2,1,0:T(8,128)(2,1)S(1)}, bf16[8,40,128]{2,1,0:T(8,128)(2,1)S(1)}, u32[]{:S(2)}, u32[]{:S(2)}) collective-permute-start(bf16[8,40,128]{2,1,0:T(8,128)(2,1)S(1)} %unpacking.1.carried_ref), channel_id=1, source_target_pairs={{0,1},{1,0},{2,3},{3,2},{4,5},{5,4},{6,7},{7,6},{8,9},{9,8},{10,11... | collective-permute-start | bytes 245768 | tf_op jit(solution)/shard_map/ppermute | solution.py:303
  16.3 0.9 %adjoint.1 = (f32[40,128]{1,0:T(8,128)}, f32[40,128]{1,0:T(8,128)}, f32[40,240]{1,0:T(8,128)S(1)}) custom-call(bf16[8,80,128]{2,1,0:T(8,128)(2,1)S(1)} %all_to_all.5.arrived_ref, bf16[8,40,128]{2,1,0:T(8,128)(2,1)S(1)} %unpacking.1.carried_ref, bf16[240,1024]{1,0:T(8,128)(2,1)S(1)} %get-tuple-element.29.masked_own, ...), custom_call_target="tpu_custom_call" | custom-call | tf_op jit(solution)/shard_map/adjoint/pallas_call | solution.py:388
  17.2 0.1 collective-permute-done.1.carried_ref
  17.3 0.9 %picking.1 = f32[4,240]{1,0:T(4,128)} custom-call(bf16[8,40,128]{2,1,0:T(8,128)(2,1)S(1)} %collective-permute-done.1.carried_ref, bf16[240,1024]{1,0:T(8,128)(2,1)S(1)} %get-tuple-element.34.masked_other, f32[40,240]{1,0:T(8,128)S(1)} %get-tuple-element.35.projected_ref, s32[4,240]{1,0:T(4,128)S(1)} %get-tuple-element.36.used_ref), custom_call_target="tpu_custom_call" | custom-call | tf_op jit(solution)/shard_map/picking/pallas_call | solution.py:400
  (2 shorter events, 0.0 us)
Async XLA Ops:
  2.2 1.4 %collective-permute-start = (bf16[8,40,128]{2,1,0:T(8,128)(2,1)S(1)}, bf16[8,40,128]{2,1,0:T(8,128)(2,1)S(1)}, u32[]{:S(2)}, u32[]{:S(2)}) collective-permute-start(bf16[8,40,128]{2,1,0:T(8,128)(2,1)S(1)} %get-tuple-element.20), channel_id=1, source_target_pairs={{0,1},{1,0},{2,3},{3,2},{4,5},{5,4},{6,7},{7,6},{8,9},{9,8},{10,11... | collective-permute-start | bytes 245768 | tf_op jit(solution)/shard_map/ppermute | solution.py:303
  15.1 2.2 %collective-permute-start.1 = (bf16[8,40,128]{2,1,0:T(8,128)(2,1)S(1)}, bf16[8,40,128]{2,1,0:T(8,128)(2,1)S(1)}, u32[]{:S(2)}, u32[]{:S(2)}) collective-permute-start(bf16[8,40,128]{2,1,0:T(8,128)(2,1)S(1)} %unpacking.1.carried_ref), channel_id=1, source_target_pairs={{0,1},{1,0},{2,3},{3,2},{4,5},{5,4},{6,7},{7,6},{8,9},{9,8},{10,11... | collective-permute-start | bytes 245768 | tf_op jit(solution)/shard_map/ppermute | solution.py:303

commit v23 on v21

--- a/solution.py
+++ b/solution.py
@@ -51,22 +51,32 @@
     return jnp.where(slot < counts, currencies, -1)
 
 
-def group_order(chips, core):
+def core_in(chip, group):
+    return 1 - group if chip % 2 else group
+
+
+def own_group():
+    me = lax.axis_index("sets")
+    return (me + me // 2) % 2
+
+
+def group_order(chips, group):
     middle = chips // 2
     far, near = list(range(middle, chips)), list(range(middle))
-    if core:
-        return far[::-1] + near
+    if group == 0 and middle % 2 == 0:
+        far = [chip ^ 1 for chip in far]
     cut = middle // 2
     return far[:cut] + near[:1] + far[cut:] + near[1:]
 
 
 def chip_at(chips, place):
-    even, odd = (group_order(chips, core)[place] for core in range(2))
-    return jnp.where(lax.axis_index("sets") % 2 == 0, even, odd)
-
-
-def sibling_columns(chip, owned, core):
-    return pl.ds(pl.multiple_of((2 * chip + core) * owned, owned), owned)
+    chosen = [group_order(chips, group)[place] for group in range(2)]
+    return jnp.where(own_group() == 0, chosen[0], chosen[1])
+
+
+def group_columns(chip, owned, group):
+    block = 2 * chip + core_in(chip, group)
+    return pl.ds(pl.multiple_of(block * owned, owned), owned)
 
 
 def row_flags(tile):
@@ -91,10 +101,10 @@
     return jnp.concatenate(kept, axis=0).astype(jnp.bfloat16)
 
 
-def mask_and_sum(exposure, bits, weights, masked_ref, terms_ref, core):
+def mask_and_sum(exposure, bits, weights, masked_ref, terms_ref, group):
     sets = exposure.shape[0]
-    owned = terms_ref.shape[2]
-    for first in range(0, terms_ref.shape[0], 2):
+    chips, owned = terms_ref.shape[0], terms_ref.shape[2]
+    for first in range(0, chips, 2):
         rows = []
         for pair in range(sets // 16):
             flags = [row_flags(2 * pair), row_flags(2 * pair + 1)]
@@ -102,7 +112,7 @@
                 jnp.concatenate(
                     [
                         masked_rows(
-                            exposure, bits, pair, flags, sibling_columns(chip, owned, core)
+                            exposure, bits, pair, flags, group_columns(chip, owned, group)
                         )
                         for chip in (first, first + 1)
                     ],
@@ -175,7 +185,7 @@
     weights_ref[...] = weights
     for copy in copies[:2]:
         copy.wait()
-    other = 1 - lax.axis_index("sets") % 2
+    other = 1 - own_group()
     mask_and_sum(exposure, bits, weights, masked_ref, handed_ref, other)
     for copy in copies[5:]:
         copy.wait()
@@ -195,7 +205,7 @@
     discount_ref,
     moved_ref,
 ):
-    own = lax.axis_index("sets") % 2
+    own = own_group()
     mask_and_sum(exposure, bits, weights_ref[...], masked_ref, terms_ref, own)
     integral = spread_paths(start_ref[...], dates) + step_years * sums_to_date(rates_ref[...], dates)
     discount = jnp.exp(-integral)
@@ -367,7 +377,8 @@
         0,
         0,
         axis_index_groups=[
-            [2 * chip + core for chip in group_order(chips, core)] for core in range(2)
+            [2 * chip + core_in(chip, group) for chip in group_order(chips, group)]
+            for group in range(2)
         ],
         tiled=True,
     )

time: 19 us -> 17.8 us (0.937)
  blocking collectives: 12.8 us -> 11.4 us
  starting transfers between devices: 0.58 us -> 1.19 us
  waiting for transfers between devices: 1.01 us -> 0.66 us
    all_to_all x1, blocking collectives: 12.8 us -> 11.4 us  [body(): lax.all_to_all(outgoing, 'sets', 0, 0, axis_index_groups=[[2 * chip + cor...]
    ppermute x2, starting transfers between devices: 0.58 us -> 1.19 us  [swapped(): lax.ppermute(value, 'sets', [(peer, peer ^ 1) for peer in range(peers)])]
    ppermute x2, waiting for transfers between devices: 1.01 us -> 0.66 us  [swapped(): lax.ppermute(value, 'sets', [(peer, peer ^ 1) for peer in range(peers)])]
  transfers between devices with their start and end apart: 2 -> 2, of which waited for: 2 -> 2; matrix products, arithmetic and copies ran while one was open for 0% -> 0% of each run, Pallas kernels for 6% -> 7%
where the time goes in v23:
time: 17.8 us; the launch traced here: 17.6 us
  blocking collectives  11.4 us (64%)
  Pallas kernels  3.71 us (21%)
  starting transfers between devices  1.19 us (7%)
  waiting for transfers between devices  0.66 us (4%)
  between operations  0.65 us (4%)
    all_to_all x1, blocking collectives, body(): lax.all_to_all(outgoing, 'sets', 0, 0, axis_index_groups=[[2 * chip + cor...  11.4 us
    pallas_call x1, Pallas kernels, body(): pl.pallas_call(first_kernel, out_shape=(pltpu.VMEM((chips,) + block, jnp....  1.61 us
    ppermute x2, starting transfers between devices, swapped(): lax.ppermute(value, 'sets', [(peer, peer ^ 1) for peer in range(peers)])  1.19 us
    pallas_call x1, Pallas kernels, body(): pl.pallas_call(picking_kernel, out_shape=jax.ShapeDtypeStruct((slots, set...  0.88 us
    pallas_call x1, Pallas kernels, body(): pl.pallas_call(functools.partial(adjoint_kernel, dates), out_shape=(jax.S...  0.85 us
    ppermute x2, waiting for transfers between devices, swapped(): lax.ppermute(value, 'sets', [(peer, peer ^ 1) for peer in range(peers)])  0.66 us
  transfers between devices with their start and end apart: 2, of which 2 were waited for; matrix products, arithmetic and copies ran while one was open for 0% of the time, Pallas kernels for 7%

profile of v23, /device:TPU:0, one launch (start us, length us, event | category | flops | bytes accessed | tf_op | source)
XLA Modules:
  0.0 17.6 jit_solution(7433734231656848423)
XLA Ops:
  0.6 1.6 %first.1 = (bf16[8,40,128]{2,1,0:T(8,128)(2,1)S(1)}, bf16[240,1024]{1,0:T(8,128)(2,1)S(1)}, bf16[240,2048]{1,0:T(8,128)(2,1)S(1)}, s32[16,2048]{1,0:T(8,128)S(1)...) custom-call(bf16[240,2048]{1,0:T(8,128)(2,1)} %exposure_hbm.1, ...), custom_call_target="tpu_custom_call" | custom-call | tf_op jit(solution)/shard_map/first/pallas_call | solution.py:311
  2.2 0.5 %collective-permute-start = (bf16[8,40,128]{2,1,0:T(8,128)(2,1)S(1)}, bf16[8,40,128]{2,1,0:T(8,128)(2,1)S(1)}, u32[]{:S(2)}, u32[]{:S(2)}) collective-permute-start(bf16[8,40,128]{2,1,0:T(8,128)(2,1)S(1)} %get-tuple-element.20), channel_id=1, source_target_pairs={{0,1},{1,0},{2,3},{3,2},{4,5},{5,4},{6,7},{7,6},{8,9},{9,8},{10,11... | collective-permute-start | bytes 245768 | tf_op jit(solution)/shard_map/ppermute | solution.py:309
  2.8 0.3 %second.1 = (bf16[240,1024]{1,0:T(8,128)(2,1)S(1)}, f32[8,40,128]{2,1,0:T(8,128)S(1)}, bf16[40,128]{1,0:T(8,128)(2,1)S(1)}, f32[40,128]{1,0:T(8,128)S(1)}, f32[40,128]{1,0:T(8,128)S(1)}) custom-call(bf16[240,2048]{1,0:T(8,128)(2,1)S(1)} %get-tuple-element.21.exposure, s32[16,2048]{1,0:T(8,128)S(1)} %get-tuple-element.22.bits, ...), custom_call_target="tpu_custom_call" | custom-call | tf_op jit(solution)/shard_map/second/pallas_call | solution.py:345
  3.1 0.6 %collective-permute-done.given_ref = bf16[8,40,128]{2,1,0:T(8,128)(2,1)S(1)} collective-permute-done((bf16[8,40,128]{2,1,0:T(8,128)(2,1)S(1)}, bf16[8,40,128]{2,1,0:T(8,128)(2,1)S(1)}, u32[]{:S(2)}, u32[]{:S(2)}) %collective-permute-start) | collective-permute-done | bytes 81952 | tf_op jit(solution)/shard_map/ppermute | solution.py:309
  3.7 11.4 %all_to_all.5.arrived_ref = bf16[8,80,128]{2,1,0:T(8,128)(2,1)S(1)} all-to-all(bf16[8,80,128]{2,1,0:T(8,128)(2,1)S(1)} %merging.1), channel_id=1, replica_groups={{11,8,0,15,12,3,4,7},{9,10,1,13,14,2,5,6},{27,24,16,31,28,19,20,23},{25..., dimensions={0} | all-to-all | bytes 327680 | tf_op jit(solution)/shard_map/all_to_all | solution.py:374
  15.2 0.7 %collective-permute-start.1 = (bf16[8,40,128]{2,1,0:T(8,128)(2,1)S(1)}, bf16[8,40,128]{2,1,0:T(8,128)(2,1)S(1)}, u32[]{:S(2)}, u32[]{:S(2)}) collective-permute-start(bf16[8,40,128]{2,1,0:T(8,128)(2,1)S(1)} %unpacking.1.carried_ref), channel_id=1, source_target_pairs={{0,1},{1,0},{2,3},{3,2},{4,5},{5,4},{6,7},{7,6},{8,9},{9,8},{10,11... | collective-permute-start | bytes 245768 | tf_op jit(solution)/shard_map/ppermute | solution.py:309
  15.8 0.9 %adjoint.1 = (f32[40,128]{1,0:T(8,128)}, f32[40,128]{1,0:T(8,128)}, f32[40,240]{1,0:T(8,128)S(1)}) custom-call(bf16[8,80,128]{2,1,0:T(8,128)(2,1)S(1)} %all_to_all.5.arrived_ref, bf16[8,40,128]{2,1,0:T(8,128)(2,1)S(1)} %unpacking.1.carried_ref, bf16[240,1024]{1,0:T(8,128)(2,1)S(1)} %get-tuple-element.29.masked_own, ...), custom_call_target="tpu_custom_call" | custom-call | tf_op jit(solution)/shard_map/adjoint/pallas_call | solution.py:394
  16.7 0.1 collective-permute-done.1.carried_ref
  16.8 0.9 %picking.1 = f32[4,240]{1,0:T(4,128)} custom-call(bf16[8,40,128]{2,1,0:T(8,128)(2,1)S(1)} %collective-permute-done.1.carried_ref, bf16[240,1024]{1,0:T(8,128)(2,1)S(1)} %get-tuple-element.34.masked_other, f32[40,240]{1,0:T(8,128)S(1)} %get-tuple-element.35.projected_ref, s32[4,240]{1,0:T(4,128)S(1)} %get-tuple-element.36.used_ref), custom_call_target="tpu_custom_call" | custom-call | tf_op jit(solution)/shard_map/picking/pallas_call | solution.py:406
  (2 shorter events, 0.0 us)
Async XLA Ops:
  2.2 1.4 %collective-permute-start = (bf16[8,40,128]{2,1,0:T(8,128)(2,1)S(1)}, bf16[8,40,128]{2,1,0:T(8,128)(2,1)S(1)}, u32[]{:S(2)}, u32[]{:S(2)}) collective-permute-start(bf16[8,40,128]{2,1,0:T(8,128)(2,1)S(1)} %get-tuple-element.20), channel_id=1, source_target_pairs={{0,1},{1,0},{2,3},{3,2},{4,5},{5,4},{6,7},{7,6},{8,9},{9,8},{10,11... | collective-permute-start | bytes 245768 | tf_op jit(solution)/shard_map/ppermute | solution.py:309
  15.2 1.6 %collective-permute-start.1 = (bf16[8,40,128]{2,1,0:T(8,128)(2,1)S(1)}, bf16[8,40,128]{2,1,0:T(8,128)(2,1)S(1)}, u32[]{:S(2)}, u32[]{:S(2)}) collective-permute-start(bf16[8,40,128]{2,1,0:T(8,128)(2,1)S(1)} %unpacking.1.carried_ref), channel_id=1, source_target_pairs={{0,1},{1,0},{2,3},{3,2},{4,5},{5,4},{6,7},{7,6},{8,9},{9,8},{10,11... | collective-permute-start | bytes 245768 | tf_op jit(solution)/shard_map/ppermute | solution.py:309

commit v24 on v23

--- a/solution.py
+++ b/solution.py
@@ -85,11 +85,11 @@
     return jnp.left_shift(jnp.int32(1), shift)
 
 
-def masked_rows(exposure, bits, pair, flags, part):
+def masked_rows(exposure, bits, pair, flags, chip, part):
     row = lax.broadcasted_iota(jnp.int32, (8, lanes), 0)
-    values = exposure[16 * pair : 16 * pair + 16, part].astype(jnp.float32)
     kept = []
     for half in range(2):
+        values = exposure[chip % 2, 2 * pair + half, chip // 2].astype(jnp.float32)
         top = 16 * pair + 8 * half
         group = top // bits_per_row
         left = bits_per_row * (group + 1) - top
@@ -97,12 +97,12 @@
         if left < 8:
             following = jnp.broadcast_to(bits[group + 1 : group + 2, part], (8, lanes))
             packed = jnp.where(row < left, packed, following)
-        kept.append(jnp.where((packed & flags[half]) != 0, values[8 * half : 8 * half + 8], 0.0))
+        kept.append(jnp.where((packed & flags[half]) != 0, values, 0.0))
     return jnp.concatenate(kept, axis=0).astype(jnp.bfloat16)
 
 
 def mask_and_sum(exposure, bits, weights, masked_ref, terms_ref, group):
-    sets = exposure.shape[0]
+    sets = 8 * exposure.shape[1]
     chips, owned = terms_ref.shape[0], terms_ref.shape[2]
     for first in range(0, chips, 2):
         rows = []
@@ -112,7 +112,7 @@
                 jnp.concatenate(
                     [
                         masked_rows(
-                            exposure, bits, pair, flags, group_columns(chip, owned, group)
+                            exposure, bits, pair, flags, chip, group_columns(chip, owned, group)
                         )
                         for chip in (first, first + 1)
                     ],
@@ -138,7 +138,7 @@
     start_hbm,
     handed_ref,
     masked_ref,
-    exposure,
+    exposure_own,
     bits,
     weights_ref,
     used_ref,
@@ -148,15 +148,18 @@
     currencies_ref,
     counts_ref,
     notional_ref,
+    exposure_other,
     sems,
+    tile_sems,
 ):
-    sets = exposure.shape[0]
+    sets = 8 * exposure_own.shape[1]
+    own = own_group()
+    other = 1 - own
     currency_count = handed_ref.shape[1]
     copies = [
         pltpu.make_async_copy(source, target, sems.at[index])
         for index, (source, target) in enumerate(
             [
-                (exposure_hbm, exposure),
                 (bits_hbm, bits),
                 (currencies_hbm, currencies_ref),
                 (counts_hbm, counts_ref),
@@ -167,9 +170,20 @@
             ]
         )
     ]
-    for copy in copies:
+    tile_copies = [
+        [
+            pltpu.make_async_copy(
+                exposure_hbm.at[:, :, parity, core_in(parity, group)],
+                target.at[parity],
+                tile_sems.at[2 * index + parity],
+            )
+            for parity in range(2)
+        ]
+        for index, (group, target) in enumerate([(other, exposure_other), (own, exposure_own)])
+    ]
+    for copy in copies[:1] + tile_copies[0] + copies[1:4] + tile_copies[1] + copies[4:]:
         copy.start()
-    for copy in copies[2:5]:
+    for copy in copies[1:4]:
         copy.wait()
 
     used = used_currencies(currencies_ref[...], counts_ref[...])
@@ -183,11 +197,10 @@
         )
     weights = weights.astype(jnp.bfloat16)
     weights_ref[...] = weights
-    for copy in copies[:2]:
+    for copy in copies[:1] + tile_copies[0]:
         copy.wait()
-    other = 1 - own_group()
-    mask_and_sum(exposure, bits, weights, masked_ref, handed_ref, other)
-    for copy in copies[5:]:
+    mask_and_sum(exposure_other, bits, weights, masked_ref, handed_ref, other)
+    for copy in tile_copies[1] + copies[4:]:
         copy.wait()
 
 
@@ -305,6 +318,10 @@
     def in_hbm(value):
         return pltpu.with_memory_space_constraint(value, pltpu.HBM)
 
+    tiles = exposure_adjoint.reshape(sets // 8, 8, chips // 2, 2, 2, owned)
+    tiles = tiles.transpose(0, 2, 3, 4, 1, 5)
+    half_tiles = (2, sets // 8, chips // 2, 8, owned)
+
     def swapped(value):
         return lax.ppermute(value, "sets", [(peer, peer ^ 1) for peer in range(peers)])
 
@@ -313,7 +330,7 @@
         out_shape=(
             pltpu.VMEM((chips,) + block, jnp.bfloat16),
             pltpu.VMEM((sets, columns // 2), jnp.bfloat16),
-            pltpu.VMEM((sets, columns), jnp.bfloat16),
+            pltpu.VMEM(half_tiles, jnp.bfloat16),
             pltpu.VMEM(positive_bits.shape, jnp.int32),
             pltpu.VMEM((currency_count, sets), jnp.bfloat16),
             pltpu.VMEM((slots, sets), jnp.int32),
@@ -327,12 +344,14 @@
             pltpu.VMEM((slots, sets), jnp.int32),
             pltpu.VMEM((1, sets), jnp.int32),
             pltpu.VMEM((slots, sets), jnp.float32),
-            pltpu.SemaphoreType.DMA((8,)),
+            pltpu.VMEM(half_tiles, jnp.bfloat16),
+            pltpu.SemaphoreType.DMA((7,)),
+            pltpu.SemaphoreType.DMA((4,)),
         ],
         compiler_params=params,
         name="first",
     )(
-        in_hbm(exposure_adjoint),
+        in_hbm(tiles),
         in_hbm(positive_bits),
         in_hbm(currencies.T),
         in_hbm(mix_count.reshape(1, sets)),

time: 17.8 us -> 17.9 us (level)
  no operation moved by 1% of the time
where the time goes in v24:
time: 17.9 us; the launch traced here: 17.7 us
  blocking collectives  11.4 us (64%)
  Pallas kernels  3.77 us (21%)
  starting transfers between devices  1.19 us (7%)
  waiting for transfers between devices  0.66 us (4%)
  between operations  0.65 us (4%)
    all_to_all x1, blocking collectives, body(): lax.all_to_all(outgoing, 'sets', 0, 0, axis_index_groups=[[2 * chip + cor...  11.4 us
    pallas_call x1, Pallas kernels, body(): pl.pallas_call(first_kernel, out_shape=(pltpu.VMEM((chips,) + block, jnp....  1.66 us
    ppermute x2, starting transfers between devices, swapped(): lax.ppermute(value, 'sets', [(peer, peer ^ 1) for peer in range(peers)])  1.19 us
    pallas_call x1, Pallas kernels, body(): pl.pallas_call(picking_kernel, out_shape=jax.ShapeDtypeStruct((slots, set...  0.88 us
    pallas_call x1, Pallas kernels, body(): pl.pallas_call(functools.partial(adjoint_kernel, dates), out_shape=(jax.S...  0.85 us
    ppermute x2, waiting for transfers between devices, swapped(): lax.ppermute(value, 'sets', [(peer, peer ^ 1) for peer in range(peers)])  0.66 us
  transfers between devices with their start and end apart: 2, of which 2 were waited for; matrix products, arithmetic and copies ran while one was open for 0% of the time, Pallas kernels for 7%

profile of v24, /device:TPU:0, one launch (start us, length us, event | category | flops | bytes accessed | tf_op | source)
XLA Modules:
  0.0 17.7 jit_solution(10324219387969293171)
XLA Ops:
  0.6 1.7 %first.1 = (bf16[8,40,128]{2,1,0:T(8,128)(2,1)S(1)}, bf16[240,1024]{1,0:T(8,128)(2,1)S(1)}, bf16[2,30,4,8,128]{4,3,2,1,0:T(8,128)(2,1)S(1)}, s32[16,2048]{1,0:T(...) custom-call(bf16[30,4,2,2,8,128]{5,4,3,2,1,0:T(8,128)(2,1)} %bitcast, ...), custom_call_target="tpu_custom_call" | custom-call | tf_op jit(solution)/shard_map/first/pallas_call | solution.py:328
  2.3 0.5 %collective-permute-start = (bf16[8,40,128]{2,1,0:T(8,128)(2,1)S(1)}, bf16[8,40,128]{2,1,0:T(8,128)(2,1)S(1)}, u32[]{:S(2)}, u32[]{:S(2)}) collective-permute-start(bf16[8,40,128]{2,1,0:T(8,128)(2,1)S(1)} %get-tuple-element.20), channel_id=1, source_target_pairs={{0,1},{1,0},{2,3},{3,2},{4,5},{5,4},{6,7},{7,6},{8,9},{9,8},{10,11... | collective-permute-start | bytes 245768 | tf_op jit(solution)/shard_map/ppermute | solution.py:326
  2.8 0.3 %second.1 = (bf16[240,1024]{1,0:T(8,128)(2,1)S(1)}, f32[8,40,128]{2,1,0:T(8,128)S(1)}, bf16[40,128]{1,0:T(8,128)(2,1)S(1)}, f32[40,128]{1,0:T(8,128)S(1)}, f32[40,128]{1,0:T(8,128)S(1)}) custom-call(bf16[2,30,4,8,128]{4,3,2,1,0:T(8,128)(2,1)S(1)} %get-tuple-element.21.exposure, s32[16,2048]{1,0:T(8,128)S(1)} %get-tuple-element.22.bits, ...), custom_call_target="tpu_custom_call" | custom-call | tf_op jit(solution)/shard_map/second/pallas_call | solution.py:364
  3.2 0.6 %collective-permute-done.given_ref = bf16[8,40,128]{2,1,0:T(8,128)(2,1)S(1)} collective-permute-done((bf16[8,40,128]{2,1,0:T(8,128)(2,1)S(1)}, bf16[8,40,128]{2,1,0:T(8,128)(2,1)S(1)}, u32[]{:S(2)}, u32[]{:S(2)}) %collective-permute-start) | collective-permute-done | bytes 81952 | tf_op jit(solution)/shard_map/ppermute | solution.py:326
  3.8 11.4 %all_to_all.5.arrived_ref = bf16[8,80,128]{2,1,0:T(8,128)(2,1)S(1)} all-to-all(bf16[8,80,128]{2,1,0:T(8,128)(2,1)S(1)} %merging.1), channel_id=1, replica_groups={{11,8,0,15,12,3,4,7},{9,10,1,13,14,2,5,6},{27,24,16,31,28,19,20,23},{25..., dimensions={0} | all-to-all | bytes 327680 | tf_op jit(solution)/shard_map/all_to_all | solution.py:393
  15.2 0.7 %collective-permute-start.1 = (bf16[8,40,128]{2,1,0:T(8,128)(2,1)S(1)}, bf16[8,40,128]{2,1,0:T(8,128)(2,1)S(1)}, u32[]{:S(2)}, u32[]{:S(2)}) collective-permute-start(bf16[8,40,128]{2,1,0:T(8,128)(2,1)S(1)} %unpacking.1.carried_ref), channel_id=1, source_target_pairs={{0,1},{1,0},{2,3},{3,2},{4,5},{5,4},{6,7},{7,6},{8,9},{9,8},{10,11... | collective-permute-start | bytes 245768 | tf_op jit(solution)/shard_map/ppermute | solution.py:326
  15.9 0.8 %adjoint.1 = (f32[40,128]{1,0:T(8,128)}, f32[40,128]{1,0:T(8,128)}, f32[40,240]{1,0:T(8,128)S(1)}) custom-call(bf16[8,80,128]{2,1,0:T(8,128)(2,1)S(1)} %all_to_all.5.arrived_ref, bf16[8,40,128]{2,1,0:T(8,128)(2,1)S(1)} %unpacking.1.carried_ref, bf16[240,1024]{1,0:T(8,128)(2,1)S(1)} %get-tuple-element.29.masked_own, ...), custom_call_target="tpu_custom_call" | custom-call | tf_op jit(solution)/shard_map/adjoint/pallas_call | solution.py:413
  16.7 0.1 collective-permute-done.1.carried_ref
  16.8 0.9 %picking.1 = f32[4,240]{1,0:T(4,128)} custom-call(bf16[8,40,128]{2,1,0:T(8,128)(2,1)S(1)} %collective-permute-done.1.carried_ref, bf16[240,1024]{1,0:T(8,128)(2,1)S(1)} %get-tuple-element.34.masked_other, f32[40,240]{1,0:T(8,128)S(1)} %get-tuple-element.35.projected_ref, s32[4,240]{1,0:T(4,128)S(1)} %get-tuple-element.36.used_ref), custom_call_target="tpu_custom_call" | custom-call | tf_op jit(solution)/shard_map/picking/pallas_call | solution.py:425
  (2 shorter events, 0.0 us)
Async XLA Ops:
  2.3 1.4 %collective-permute-start = (bf16[8,40,128]{2,1,0:T(8,128)(2,1)S(1)}, bf16[8,40,128]{2,1,0:T(8,128)(2,1)S(1)}, u32[]{:S(2)}, u32[]{:S(2)}) collective-permute-start(bf16[8,40,128]{2,1,0:T(8,128)(2,1)S(1)} %get-tuple-element.20), channel_id=1, source_target_pairs={{0,1},{1,0},{2,3},{3,2},{4,5},{5,4},{6,7},{7,6},{8,9},{9,8},{10,11... | collective-permute-start | bytes 245768 | tf_op jit(solution)/shard_map/ppermute | solution.py:326
  15.2 1.6 %collective-permute-start.1 = (bf16[8,40,128]{2,1,0:T(8,128)(2,1)S(1)}, bf16[8,40,128]{2,1,0:T(8,128)(2,1)S(1)}, u32[]{:S(2)}, u32[]{:S(2)}) collective-permute-start(bf16[8,40,128]{2,1,0:T(8,128)(2,1)S(1)} %unpacking.1.carried_ref), channel_id=1, source_target_pairs={{0,1},{1,0},{2,3},{3,2},{4,5},{5,4},{6,7},{7,6},{8,9},{9,8},{10,11... | collective-permute-start | bytes 245768 | tf_op jit(solution)/shard_map/ppermute | solution.py:326

commit v25 on v23

--- a/solution.py
+++ b/solution.py
@@ -52,12 +52,12 @@
 
 
 def core_in(chip, group):
-    return 1 - group if chip % 2 else group
+    return 1 - group if (chip + chip // 2) % 2 else group
 
 
 def own_group():
     me = lax.axis_index("sets")
-    return (me + me // 2) % 2
+    return (me + me // 2 + me // 4) % 2
 
 
 def group_order(chips, group):
@@ -199,11 +199,13 @@
     fx_ref,
     rates_ref,
     start_ref,
+    masked_other,
     masked_ref,
     terms_ref,
     carried_ref,
     discount_ref,
     moved_ref,
+    turned_ref,
 ):
     own = own_group()
     mask_and_sum(exposure, bits, weights_ref[...], masked_ref, terms_ref, own)
@@ -213,6 +215,8 @@
     moved = fx_ref[...] * discount
     moved_ref[...] = moved
     carried_ref[...] = moved.astype(jnp.bfloat16)
+    for column in range(0, masked_other.shape[1], lanes):
+        turned_ref[column : column + lanes, :] = masked_other[:, column : column + lanes].T
 
 
 def merging_kernel(given_ref, terms_ref, carried_ref, outgoing_ref):
@@ -268,10 +272,19 @@
     projected_ref[...] = projection(masked_own, carried_ref)
 
 
-def picking_kernel(carried_ref, masked_other, projected_ref, used_ref, notional_adjoint_ref):
-    sets, half = masked_other.shape
+def picking_kernel(carried_ref, turned_ref, projected_ref, used_ref, notional_adjoint_ref):
+    half, sets = turned_ref.shape
     currency_count = carried_ref.shape[1]
-    projected = projected_ref[...] + projection(masked_other, carried_ref)
+    chips, _, owned = carried_ref.shape
+    here = min(chips, 8)
+    projected = projected_ref[...]
+    for first in range(0, chips, here):
+        carried = jnp.concatenate([carried_ref[first + chip] for chip in range(here)], axis=1)
+        projected = projected + jnp.dot(
+            carried,
+            turned_ref[first * owned : (first + here) * owned, :],
+            preferred_element_type=jnp.float32,
+        )
     used = used_ref[...]
     currency = lax.broadcasted_iota(jnp.int32, (currency_count, sets), 0)
     for slot in range(used.shape[0]):
@@ -342,7 +355,7 @@
         in_hbm(start_integral.T),
     )
     given = swapped(handed)
-    masked_own, terms, carried, discount, moved = pl.pallas_call(
+    masked_own, terms, carried, discount, moved, turned = pl.pallas_call(
         functools.partial(second_kernel, dates),
         out_shape=(
             pltpu.VMEM((sets, columns // 2), jnp.bfloat16),
@@ -350,9 +363,10 @@
             pltpu.VMEM(block, jnp.bfloat16),
             pltpu.VMEM(block, jnp.float32),
             pltpu.VMEM(block, jnp.float32),
+            pltpu.VMEM((columns // 2, sets), jnp.bfloat16),
         ),
-        in_specs=[in_vmem] * 6,
-        out_specs=(in_vmem,) * 5,
+        in_specs=[in_vmem] * 7,
+        out_specs=(in_vmem,) * 6,
         compiler_params=params,
         name="second",
     )(
@@ -362,6 +376,7 @@
         fx,
         rates,
         start,
+        masked_other,
     )
     outgoing = pl.pallas_call(
         merging_kernel,
@@ -410,7 +425,7 @@
         out_specs=in_vmem,
         compiler_params=params,
         name="picking",
-    )(carried_other, masked_other, projected, used)
+    )(carried_other, turned, projected, used)
     return fx_adjoint, rate_adjoint, notional_adjoint.T
 
 

time: 17.8 us -> 17.7 us (level)
  no operation moved by 1% of the time
where the time goes in v25:
time: 17.7 us; the launch traced here: 17.6 us
  blocking collectives  11.3 us (64%)
  Pallas kernels  3.72 us (21%)
  starting transfers between devices  1.29 us (7%)
  between operations  0.66 us (4%)
  waiting for transfers between devices  0.6 us (3%)
    all_to_all x1, blocking collectives, body(): lax.all_to_all(outgoing, 'sets', 0, 0, axis_index_groups=[[2 * chip + cor...  11.3 us
    pallas_call x1, Pallas kernels, body(): pl.pallas_call(first_kernel, out_shape=(pltpu.VMEM((chips,) + block, jnp....  1.61 us
    ppermute x2, starting transfers between devices, swapped(): lax.ppermute(value, 'sets', [(peer, peer ^ 1) for peer in range(peers)])  1.29 us
    pallas_call x1, Pallas kernels, body(): pl.pallas_call(functools.partial(adjoint_kernel, dates), out_shape=(jax.S...  0.85 us
    pallas_call x1, Pallas kernels, body(): pl.pallas_call(picking_kernel, out_shape=jax.ShapeDtypeStruct((slots, set...  0.82 us
    ppermute x2, waiting for transfers between devices, swapped(): lax.ppermute(value, 'sets', [(peer, peer ^ 1) for peer in range(peers)])  0.6 us
    pallas_call x1, Pallas kernels, body(): pl.pallas_call(functools.partial(second_kernel, dates), out_shape=(pltpu....  0.39 us
  transfers between devices with their start and end apart: 2, of which 2 were waited for; matrix products, arithmetic and copies ran while one was open for 0% of the time, Pallas kernels for 7%

profile of v25, /device:TPU:0, one launch (start us, length us, event | category | flops | bytes accessed | tf_op | source)
XLA Modules:
  0.0 17.6 jit_solution(12284688796379139869)
XLA Ops:
  0.6 1.6 %first.1 = (bf16[8,40,128]{2,1,0:T(8,128)(2,1)S(1)}, bf16[240,1024]{1,0:T(8,128)(2,1)S(1)}, bf16[240,2048]{1,0:T(8,128)(2,1)S(1)}, s32[16,2048]{1,0:T(8,128)S(1)...) custom-call(bf16[240,2048]{1,0:T(8,128)(2,1)} %exposure_hbm.1, ...), custom_call_target="tpu_custom_call" | custom-call | tf_op jit(solution)/shard_map/first/pallas_call | solution.py:324
  2.3 0.5 %collective-permute-start = (bf16[8,40,128]{2,1,0:T(8,128)(2,1)S(1)}, bf16[8,40,128]{2,1,0:T(8,128)(2,1)S(1)}, u32[]{:S(2)}, u32[]{:S(2)}) collective-permute-start(bf16[8,40,128]{2,1,0:T(8,128)(2,1)S(1)} %get-tuple-element.21), channel_id=1, source_target_pairs={{0,1},{1,0},{2,3},{3,2},{4,5},{5,4},{6,7},{7,6},{8,9},{9,8},{10,11... | collective-permute-start | bytes 245768 | tf_op jit(solution)/shard_map/ppermute | solution.py:322
  2.8 0.4 %second.1 = (bf16[240,1024]{1,0:T(8,128)(2,1)S(1)}, f32[8,40,128]{2,1,0:T(8,128)S(1)}, bf16[40,128]{1,0:T(8,128)(2,1)S(1)}, f32[40,128]{1,0:T(8,128)S(1)}, f32[4...) custom-call(bf16[240,2048]{1,0:T(8,128)(2,1)S(1)} %get-tuple-element.22.exposure, s32[16,2048]{1,0:T(8,128)S(1)} %get-tuple-element.23.bits, ...), custom_call_target="tpu_custom_call" | custom-call | tf_op jit(solution)/shard_map/second/pallas_call | solution.py:358
  3.2 0.5 %collective-permute-done.given_ref = bf16[8,40,128]{2,1,0:T(8,128)(2,1)S(1)} collective-permute-done((bf16[8,40,128]{2,1,0:T(8,128)(2,1)S(1)}, bf16[8,40,128]{2,1,0:T(8,128)(2,1)S(1)}, u32[]{:S(2)}, u32[]{:S(2)}) %collective-permute-start) | collective-permute-done | bytes 81952 | tf_op jit(solution)/shard_map/ppermute | solution.py:322
  3.7 11.3 %all_to_all.5.arrived_ref = bf16[8,80,128]{2,1,0:T(8,128)(2,1)S(1)} all-to-all(bf16[8,80,128]{2,1,0:T(8,128)(2,1)S(1)} %merging.1), channel_id=1, replica_groups={{11,8,0,14,13,3,5,6},{9,10,1,12,15,2,4,7},{27,24,16,30,29,19,21,22},{25..., dimensions={0} | all-to-all | bytes 327680 | tf_op jit(solution)/shard_map/all_to_all | solution.py:389
  15.0 0.8 %collective-permute-start.1 = (bf16[8,40,128]{2,1,0:T(8,128)(2,1)S(1)}, bf16[8,40,128]{2,1,0:T(8,128)(2,1)S(1)}, u32[]{:S(2)}, u32[]{:S(2)}) collective-permute-start(bf16[8,40,128]{2,1,0:T(8,128)(2,1)S(1)} %unpacking.1.carried_ref), channel_id=1, source_target_pairs={{0,1},{1,0},{2,3},{3,2},{4,5},{5,4},{6,7},{7,6},{8,9},{9,8},{10,11... | collective-permute-start | bytes 245768 | tf_op jit(solution)/shard_map/ppermute | solution.py:322
  15.8 0.8 %adjoint.1 = (f32[40,128]{1,0:T(8,128)}, f32[40,128]{1,0:T(8,128)}, f32[40,240]{1,0:T(8,128)S(1)}) custom-call(bf16[8,80,128]{2,1,0:T(8,128)(2,1)S(1)} %all_to_all.5.arrived_ref, bf16[8,40,128]{2,1,0:T(8,128)(2,1)S(1)} %unpacking.1.carried_ref, bf16[240,1024]{1,0:T(8,128)(2,1)S(1)} %get-tuple-element.31.masked_own, ...), custom_call_target="tpu_custom_call" | custom-call | tf_op jit(solution)/shard_map/adjoint/pallas_call | solution.py:409
  16.7 0.1 collective-permute-done.1.carried_ref
  16.7 0.8 %picking.1 = f32[4,240]{1,0:T(4,128)} custom-call(bf16[8,40,128]{2,1,0:T(8,128)(2,1)S(1)} %collective-permute-done.1.carried_ref, bf16[1024,240]{1,0:T(8,128)(2,1)S(1)} %get-tuple-element.36.turned_ref, f32[40,240]{1,0:T(8,128)S(1)} %get-tuple-element.37.projected_ref, s32[4,240]{1,0:T(4,128)S(1)} %get-tuple-element.38.used_ref), custom_call_target="tpu_custom_call" | custom-call | tf_op jit(solution)/shard_map/picking/pallas_call | solution.py:421
  (2 shorter events, 0.0 us)
Async XLA Ops:
  2.3 1.4 %collective-permute-start = (bf16[8,40,128]{2,1,0:T(8,128)(2,1)S(1)}, bf16[8,40,128]{2,1,0:T(8,128)(2,1)S(1)}, u32[]{:S(2)}, u32[]{:S(2)}) collective-permute-start(bf16[8,40,128]{2,1,0:T(8,128)(2,1)S(1)} %get-tuple-element.21), channel_id=1, source_target_pairs={{0,1},{1,0},{2,3},{3,2},{4,5},{5,4},{6,7},{7,6},{8,9},{9,8},{10,11... | collective-permute-start | bytes 245768 | tf_op jit(solution)/shard_map/ppermute | solution.py:322
  15.0 1.7 %collective-permute-start.1 = (bf16[8,40,128]{2,1,0:T(8,128)(2,1)S(1)}, bf16[8,40,128]{2,1,0:T(8,128)(2,1)S(1)}, u32[]{:S(2)}, u32[]{:S(2)}) collective-permute-start(bf16[8,40,128]{2,1,0:T(8,128)(2,1)S(1)} %unpacking.1.carried_ref), channel_id=1, source_target_pairs={{0,1},{1,0},{2,3},{3,2},{4,5},{5,4},{6,7},{7,6},{8,9},{9,8},{10,11... | collective-permute-start | bytes 245768 | tf_op jit(solution)/shard_map/ppermute | solution.py:322

commit v26 on v25

--- a/solution.py
+++ b/solution.py
@@ -63,10 +63,8 @@
 def group_order(chips, group):
     middle = chips // 2
     far, near = list(range(middle, chips)), list(range(middle))
-    if group == 0 and middle % 2 == 0:
-        far = [chip ^ 1 for chip in far]
-    cut = middle // 2
-    return far[:cut] + near[:1] + far[cut:] + near[1:]
+    lead = [chip for chip in near[middle // 2 :] if core_in(chip, group)][:1]
+    return lead + far + [chip for chip in near if chip not in lead]
 
 
 def chip_at(chips, place):

time: 17.7 us -> 19.4 us (1.096)
  blocking collectives: 11.3 us -> 13.3 us
  starting transfers between devices: 1.29 us -> 0.59 us
  waiting for transfers between devices: 0.6 us -> 0.94 us
    all_to_all x1, blocking collectives: 11.3 us -> 13.3 us  [body(): lax.all_to_all(outgoing, 'sets', 0, 0, axis_index_groups=[[2 * chip + cor...]
    ppermute x2, starting transfers between devices: 1.29 us -> 0.59 us  [swapped(): lax.ppermute(value, 'sets', [(peer, peer ^ 1) for peer in range(peers)])]
    ppermute x2, waiting for transfers between devices: 0.6 us -> 0.94 us  [swapped(): lax.ppermute(value, 'sets', [(peer, peer ^ 1) for peer in range(peers)])]
  transfers between devices with their start and end apart: 2 -> 2, of which waited for: 2 -> 2; matrix products, arithmetic and copies ran while one was open for 0% -> 0% of each run, Pallas kernels for 7% -> 6%
where the time goes in v26:
time: 19.4 us; the launch traced here: 19.3 us
  blocking collectives  13.3 us (69%)
  Pallas kernels  3.72 us (19%)
  waiting for transfers between devices  0.94 us (5%)
  between operations  0.67 us (3%)
  starting transfers between devices  0.59 us (3%)
    all_to_all x1, blocking collectives, body(): lax.all_to_all(outgoing, 'sets', 0, 0, axis_index_groups=[[2 * chip + cor...  13.3 us
    pallas_call x1, Pallas kernels, body(): pl.pallas_call(first_kernel, out_shape=(pltpu.VMEM((chips,) + block, jnp....  1.61 us
    ppermute x2, waiting for transfers between devices, swapped(): lax.ppermute(value, 'sets', [(peer, peer ^ 1) for peer in range(peers)])  0.94 us
    pallas_call x1, Pallas kernels, body(): pl.pallas_call(functools.partial(adjoint_kernel, dates), out_shape=(jax.S...  0.85 us
    pallas_call x1, Pallas kernels, body(): pl.pallas_call(picking_kernel, out_shape=jax.ShapeDtypeStruct((slots, set...  0.82 us
    ppermute x2, starting transfers between devices, swapped(): lax.ppermute(value, 'sets', [(peer, peer ^ 1) for peer in range(peers)])  0.59 us
    pallas_call x1, Pallas kernels, body(): pl.pallas_call(functools.partial(second_kernel, dates), out_shape=(pltpu....  0.39 us
  transfers between devices with their start and end apart: 2, of which 2 were waited for; matrix products, arithmetic and copies ran while one was open for 0% of the time, Pallas kernels for 6%

profile of v26, /device:TPU:0, one launch (start us, length us, event | category | flops | bytes accessed | tf_op | source)
XLA Modules:
  0.0 19.3 jit_solution(1631348311461604408)
XLA Ops:
  0.6 1.6 %first.1 = (bf16[8,40,128]{2,1,0:T(8,128)(2,1)S(1)}, bf16[240,1024]{1,0:T(8,128)(2,1)S(1)}, bf16[240,2048]{1,0:T(8,128)(2,1)S(1)}, s32[16,2048]{1,0:T(8,128)S(1)...) custom-call(bf16[240,2048]{1,0:T(8,128)(2,1)} %exposure_hbm.1, ...), custom_call_target="tpu_custom_call" | custom-call | tf_op jit(solution)/shard_map/first/pallas_call | solution.py:322
  2.3 0.5 %collective-permute-start = (bf16[8,40,128]{2,1,0:T(8,128)(2,1)S(1)}, bf16[8,40,128]{2,1,0:T(8,128)(2,1)S(1)}, u32[]{:S(2)}, u32[]{:S(2)}) collective-permute-start(bf16[8,40,128]{2,1,0:T(8,128)(2,1)S(1)} %get-tuple-element.21), channel_id=1, source_target_pairs={{0,1},{1,0},{2,3},{3,2},{4,5},{5,4},{6,7},{7,6},{8,9},{9,8},{10,11... | collective-permute-start | bytes 245768 | tf_op jit(solution)/shard_map/ppermute | solution.py:320
  2.8 0.4 %second.1 = (bf16[240,1024]{1,0:T(8,128)(2,1)S(1)}, f32[8,40,128]{2,1,0:T(8,128)S(1)}, bf16[40,128]{1,0:T(8,128)(2,1)S(1)}, f32[40,128]{1,0:T(8,128)S(1)}, f32[4...) custom-call(bf16[240,2048]{1,0:T(8,128)(2,1)S(1)} %get-tuple-element.22.exposure, s32[16,2048]{1,0:T(8,128)S(1)} %get-tuple-element.23.bits, ...), custom_call_target="tpu_custom_call" | custom-call | tf_op jit(solution)/shard_map/second/pallas_call | solution.py:356
  3.2 0.5 %collective-permute-done.given_ref = bf16[8,40,128]{2,1,0:T(8,128)(2,1)S(1)} collective-permute-done((bf16[8,40,128]{2,1,0:T(8,128)(2,1)S(1)}, bf16[8,40,128]{2,1,0:T(8,128)(2,1)S(1)}, u32[]{:S(2)}, u32[]{:S(2)}) %collective-permute-start) | collective-permute-done | bytes 81952 | tf_op jit(solution)/shard_map/ppermute | solution.py:320
  3.7 13.3 %all_to_all.5.arrived_ref = bf16[8,80,128]{2,1,0:T(8,128)(2,1)S(1)} all-to-all(bf16[8,80,128]{2,1,0:T(8,128)(2,1)S(1)} %merging.1), channel_id=1, replica_groups={{5,8,11,13,14,0,3,6},{7,9,10,12,15,1,2,4},{21,24,27,29,30,16,19,22},{23..., dimensions={0} | all-to-all | bytes 327680 | tf_op jit(solution)/shard_map/all_to_all | solution.py:387
  17.1 0.1 collective-permute-start.1
  17.2 0.9 %adjoint.1 = (f32[40,128]{1,0:T(8,128)}, f32[40,128]{1,0:T(8,128)}, f32[40,240]{1,0:T(8,128)S(1)}) custom-call(bf16[8,80,128]{2,1,0:T(8,128)(2,1)S(1)} %all_to_all.5.arrived_ref, bf16[8,40,128]{2,1,0:T(8,128)(2,1)S(1)} %unpacking.1.carried_ref, bf16[240,1024]{1,0:T(8,128)(2,1)S(1)} %get-tuple-element.31.masked_own, ...), custom_call_target="tpu_custom_call" | custom-call | tf_op jit(solution)/shard_map/adjoint/pallas_call | solution.py:407
  18.0 0.4 %collective-permute-done.1.carried_ref = bf16[8,40,128]{2,1,0:T(8,128)(2,1)S(1)} collective-permute-done((bf16[8,40,128]{2,1,0:T(8,128)(2,1)S(1)}, bf16[8,40,128]{2,1,0:T(8,128)(2,1)S(1)}, u32[]{:S(2)}, u32[]{:S(2)}) %collective-permute-start.1) | collective-permute-done | bytes 81952 | tf_op jit(solution)/shard_map/ppermute | solution.py:320
  18.4 0.8 %picking.1 = f32[4,240]{1,0:T(4,128)} custom-call(bf16[8,40,128]{2,1,0:T(8,128)(2,1)S(1)} %collective-permute-done.1.carried_ref, bf16[1024,240]{1,0:T(8,128)(2,1)S(1)} %get-tuple-element.36.turned_ref, f32[40,240]{1,0:T(8,128)S(1)} %get-tuple-element.37.projected_ref, s32[4,240]{1,0:T(4,128)S(1)} %get-tuple-element.38.used_ref), custom_call_target="tpu_custom_call" | custom-call | tf_op jit(solution)/shard_map/picking/pallas_call | solution.py:419
  (2 shorter events, 0.0 us)
Async XLA Ops:
  2.3 1.4 %collective-permute-start = (bf16[8,40,128]{2,1,0:T(8,128)(2,1)S(1)}, bf16[8,40,128]{2,1,0:T(8,128)(2,1)S(1)}, u32[]{:S(2)}, u32[]{:S(2)}) collective-permute-start(bf16[8,40,128]{2,1,0:T(8,128)(2,1)S(1)} %get-tuple-element.21), channel_id=1, source_target_pairs={{0,1},{1,0},{2,3},{3,2},{4,5},{5,4},{6,7},{7,6},{8,9},{9,8},{10,11... | collective-permute-start | bytes 245768 | tf_op jit(solution)/shard_map/ppermute | solution.py:320
  17.1 1.3 %collective-permute-start.1 = (bf16[8,40,128]{2,1,0:T(8,128)(2,1)S(1)}, bf16[8,40,128]{2,1,0:T(8,128)(2,1)S(1)}, u32[]{:S(2)}, u32[]{:S(2)}) collective-permute-start(bf16[8,40,128]{2,1,0:T(8,128)(2,1)S(1)} %unpacking.1.carried_ref), channel_id=1, source_target_pairs={{0,1},{1,0},{2,3},{3,2},{4,5},{5,4},{6,7},{7,6},{8,9},{9,8},{10,11... | collective-permute-start | bytes 245768 | tf_op jit(solution)/shard_map/ppermute | solution.py:320

commit v27 on v25

--- a/solution.py
+++ b/solution.py
@@ -62,7 +62,7 @@
 
 def group_order(chips, group):
     middle = chips // 2
-    far, near = list(range(middle, chips)), list(range(middle))
+    far, near = list(range(chips - 1, middle - 1, -1)), list(range(middle))
     if group == 0 and middle % 2 == 0:
         far = [chip ^ 1 for chip in far]
     cut = middle // 2

time: 17.7 us -> 18 us (1.017)
  starting transfers between devices: 1.29 us -> 0.59 us
  blocking collectives: 11.3 us -> 11.9 us
  waiting for transfers between devices: 0.6 us -> 0.94 us
    ppermute x2, starting transfers between devices: 1.29 us -> 0.59 us  [swapped(): lax.ppermute(value, 'sets', [(peer, peer ^ 1) for peer in range(peers)])]
    all_to_all x1, blocking collectives: 11.3 us -> 11.9 us  [body(): lax.all_to_all(outgoing, 'sets', 0, 0, axis_index_groups=[[2 * chip + cor...]
    ppermute x2, waiting for transfers between devices: 0.6 us -> 0.94 us  [swapped(): lax.ppermute(value, 'sets', [(peer, peer ^ 1) for peer in range(peers)])]
where the time goes in v27:
time: 18 us; the launch traced here: 17.8 us
  blocking collectives  11.9 us (66%)
  Pallas kernels  3.72 us (21%)
  waiting for transfers between devices  0.94 us (5%)
  between operations  0.67 us (4%)
  starting transfers between devices  0.59 us (3%)
    all_to_all x1, blocking collectives, body(): lax.all_to_all(outgoing, 'sets', 0, 0, axis_index_groups=[[2 * chip + cor...  11.9 us
    pallas_call x1, Pallas kernels, body(): pl.pallas_call(first_kernel, out_shape=(pltpu.VMEM((chips,) + block, jnp....  1.61 us
    ppermute x2, waiting for transfers between devices, swapped(): lax.ppermute(value, 'sets', [(peer, peer ^ 1) for peer in range(peers)])  0.94 us
    pallas_call x1, Pallas kernels, body(): pl.pallas_call(functools.partial(adjoint_kernel, dates), out_shape=(jax.S...  0.85 us
    pallas_call x1, Pallas kernels, body(): pl.pallas_call(picking_kernel, out_shape=jax.ShapeDtypeStruct((slots, set...  0.82 us
    ppermute x2, starting transfers between devices, swapped(): lax.ppermute(value, 'sets', [(peer, peer ^ 1) for peer in range(peers)])  0.59 us
    pallas_call x1, Pallas kernels, body(): pl.pallas_call(functools.partial(second_kernel, dates), out_shape=(pltpu....  0.39 us
  transfers between devices with their start and end apart: 2, of which 2 were waited for; matrix products, arithmetic and copies ran while one was open for 0% of the time, Pallas kernels for 7%

profile of v27, /device:TPU:0, one launch (start us, length us, event | category | flops | bytes accessed | tf_op | source)
XLA Modules:
  0.0 17.8 jit_solution(3857334329660026936)
XLA Ops:
  0.6 1.6 %first.1 = (bf16[8,40,128]{2,1,0:T(8,128)(2,1)S(1)}, bf16[240,1024]{1,0:T(8,128)(2,1)S(1)}, bf16[240,2048]{1,0:T(8,128)(2,1)S(1)}, s32[16,2048]{1,0:T(8,128)S(1)...) custom-call(bf16[240,2048]{1,0:T(8,128)(2,1)} %exposure_hbm.1, ...), custom_call_target="tpu_custom_call" | custom-call | tf_op jit(solution)/shard_map/first/pallas_call | solution.py:324
  2.3 0.5 %collective-permute-start = (bf16[8,40,128]{2,1,0:T(8,128)(2,1)S(1)}, bf16[8,40,128]{2,1,0:T(8,128)(2,1)S(1)}, u32[]{:S(2)}, u32[]{:S(2)}) collective-permute-start(bf16[8,40,128]{2,1,0:T(8,128)(2,1)S(1)} %get-tuple-element.21), channel_id=1, source_target_pairs={{0,1},{1,0},{2,3},{3,2},{4,5},{5,4},{6,7},{7,6},{8,9},{9,8},{10,11... | collective-permute-start | bytes 245768 | tf_op jit(solution)/shard_map/ppermute | solution.py:322
  2.8 0.4 %second.1 = (bf16[240,1024]{1,0:T(8,128)(2,1)S(1)}, f32[8,40,128]{2,1,0:T(8,128)S(1)}, bf16[40,128]{1,0:T(8,128)(2,1)S(1)}, f32[40,128]{1,0:T(8,128)S(1)}, f32[4...) custom-call(bf16[240,2048]{1,0:T(8,128)(2,1)S(1)} %get-tuple-element.22.exposure, s32[16,2048]{1,0:T(8,128)S(1)} %get-tuple-element.23.bits, ...), custom_call_target="tpu_custom_call" | custom-call | tf_op jit(solution)/shard_map/second/pallas_call | solution.py:358
  3.2 0.5 %collective-permute-done.given_ref = bf16[8,40,128]{2,1,0:T(8,128)(2,1)S(1)} collective-permute-done((bf16[8,40,128]{2,1,0:T(8,128)(2,1)S(1)}, bf16[8,40,128]{2,1,0:T(8,128)(2,1)S(1)}, u32[]{:S(2)}, u32[]{:S(2)}) %collective-permute-start) | collective-permute-done | bytes 81952 | tf_op jit(solution)/shard_map/ppermute | solution.py:322
  3.7 11.9 %all_to_all.5.arrived_ref = bf16[8,80,128]{2,1,0:T(8,128)(2,1)S(1)} all-to-all(bf16[8,80,128]{2,1,0:T(8,128)(2,1)S(1)} %merging.1), channel_id=1, replica_groups={{13,14,0,8,11,3,5,6},{15,12,1,10,9,2,4,7},{29,30,16,24,27,19,21,22},{31..., dimensions={0} | all-to-all | bytes 327680 | tf_op jit(solution)/shard_map/all_to_all | solution.py:389
  15.7 0.1 collective-permute-start.1
  15.7 0.9 %adjoint.1 = (f32[40,128]{1,0:T(8,128)}, f32[40,128]{1,0:T(8,128)}, f32[40,240]{1,0:T(8,128)S(1)}) custom-call(bf16[8,80,128]{2,1,0:T(8,128)(2,1)S(1)} %all_to_all.5.arrived_ref, bf16[8,40,128]{2,1,0:T(8,128)(2,1)S(1)} %unpacking.1.carried_ref, bf16[240,1024]{1,0:T(8,128)(2,1)S(1)} %get-tuple-element.31.masked_own, ...), custom_call_target="tpu_custom_call" | custom-call | tf_op jit(solution)/shard_map/adjoint/pallas_call | solution.py:409
  16.6 0.4 %collective-permute-done.1.carried_ref = bf16[8,40,128]{2,1,0:T(8,128)(2,1)S(1)} collective-permute-done((bf16[8,40,128]{2,1,0:T(8,128)(2,1)S(1)}, bf16[8,40,128]{2,1,0:T(8,128)(2,1)S(1)}, u32[]{:S(2)}, u32[]{:S(2)}) %collective-permute-start.1) | collective-permute-done | bytes 81952 | tf_op jit(solution)/shard_map/ppermute | solution.py:322
  17.0 0.8 %picking.1 = f32[4,240]{1,0:T(4,128)} custom-call(bf16[8,40,128]{2,1,0:T(8,128)(2,1)S(1)} %collective-permute-done.1.carried_ref, bf16[1024,240]{1,0:T(8,128)(2,1)S(1)} %get-tuple-element.36.turned_ref, f32[40,240]{1,0:T(8,128)S(1)} %get-tuple-element.37.projected_ref, s32[4,240]{1,0:T(4,128)S(1)} %get-tuple-element.38.used_ref), custom_call_target="tpu_custom_call" | custom-call | tf_op jit(solution)/shard_map/picking/pallas_call | solution.py:421
  (2 shorter events, 0.0 us)
Async XLA Ops:
  2.3 1.4 %collective-permute-start = (bf16[8,40,128]{2,1,0:T(8,128)(2,1)S(1)}, bf16[8,40,128]{2,1,0:T(8,128)(2,1)S(1)}, u32[]{:S(2)}, u32[]{:S(2)}) collective-permute-start(bf16[8,40,128]{2,1,0:T(8,128)(2,1)S(1)} %get-tuple-element.21), channel_id=1, source_target_pairs={{0,1},{1,0},{2,3},{3,2},{4,5},{5,4},{6,7},{7,6},{8,9},{9,8},{10,11... | collective-permute-start | bytes 245768 | tf_op jit(solution)/shard_map/ppermute | solution.py:322
  15.7 1.3 %collective-permute-start.1 = (bf16[8,40,128]{2,1,0:T(8,128)(2,1)S(1)}, bf16[8,40,128]{2,1,0:T(8,128)(2,1)S(1)}, u32[]{:S(2)}, u32[]{:S(2)}) collective-permute-start(bf16[8,40,128]{2,1,0:T(8,128)(2,1)S(1)} %unpacking.1.carried_ref), channel_id=1, source_target_pairs={{0,1},{1,0},{2,3},{3,2},{4,5},{5,4},{6,7},{7,6},{8,9},{9,8},{10,11... | collective-permute-start | bytes 245768 | tf_op jit(solution)/shard_map/ppermute | solution.py:322

commit v28 on v25

--- a/solution.py
+++ b/solution.py
@@ -63,7 +63,9 @@
 def group_order(chips, group):
     middle = chips // 2
     far, near = list(range(middle, chips)), list(range(middle))
-    if group == 0 and middle % 2 == 0:
+    if group:
+        far = far[::-1]
+    elif middle % 2 == 0:
         far = [chip ^ 1 for chip in far]
     cut = middle // 2
     return far[:cut] + near[:1] + far[cut:] + near[1:]

time: 17.7 us -> 18 us (1.017)
  blocking collectives: 11.3 us -> 11.9 us
  starting transfers between devices: 1.29 us -> 0.8 us
    all_to_all x1, blocking collectives: 11.3 us -> 11.9 us  [body(): lax.all_to_all(outgoing, 'sets', 0, 0, axis_index_groups=[[2 * chip + cor...]
    ppermute x2, starting transfers between devices: 1.29 us -> 0.8 us  [swapped(): lax.ppermute(value, 'sets', [(peer, peer ^ 1) for peer in range(peers)])]
where the time goes in v28:
time: 18 us; the launch traced here: 17.8 us
  blocking collectives  11.9 us (66%)
  Pallas kernels  3.72 us (21%)
  starting transfers between devices  0.8 us (4%)
  waiting for transfers between devices  0.74 us (4%)
  between operations  0.66 us (4%)
    all_to_all x1, blocking collectives, body(): lax.all_to_all(outgoing, 'sets', 0, 0, axis_index_groups=[[2 * chip + cor...  11.9 us
    pallas_call x1, Pallas kernels, body(): pl.pallas_call(first_kernel, out_shape=(pltpu.VMEM((chips,) + block, jnp....  1.61 us
    pallas_call x1, Pallas kernels, body(): pl.pallas_call(functools.partial(adjoint_kernel, dates), out_shape=(jax.S...  0.85 us
    pallas_call x1, Pallas kernels, body(): pl.pallas_call(picking_kernel, out_shape=jax.ShapeDtypeStruct((slots, set...  0.82 us
    ppermute x2, starting transfers between devices, swapped(): lax.ppermute(value, 'sets', [(peer, peer ^ 1) for peer in range(peers)])  0.8 us
    ppermute x2, waiting for transfers between devices, swapped(): lax.ppermute(value, 'sets', [(peer, peer ^ 1) for peer in range(peers)])  0.74 us
    pallas_call x1, Pallas kernels, body(): pl.pallas_call(functools.partial(second_kernel, dates), out_shape=(pltpu....  0.39 us
  transfers between devices with their start and end apart: 2, of which 2 were waited for; matrix products, arithmetic and copies ran while one was open for 0% of the time, Pallas kernels for 7%

profile of v28, /device:TPU:0, one launch (start us, length us, event | category | flops | bytes accessed | tf_op | source)
XLA Modules:
  0.0 17.8 jit_solution(7189887815413545527)
XLA Ops:
  0.6 1.6 %first.1 = (bf16[8,40,128]{2,1,0:T(8,128)(2,1)S(1)}, bf16[240,1024]{1,0:T(8,128)(2,1)S(1)}, bf16[240,2048]{1,0:T(8,128)(2,1)S(1)}, s32[16,2048]{1,0:T(8,128)S(1)...) custom-call(bf16[240,2048]{1,0:T(8,128)(2,1)} %exposure_hbm.1, ...), custom_call_target="tpu_custom_call" | custom-call | tf_op jit(solution)/shard_map/first/pallas_call | solution.py:326
  2.3 0.5 %collective-permute-start = (bf16[8,40,128]{2,1,0:T(8,128)(2,1)S(1)}, bf16[8,40,128]{2,1,0:T(8,128)(2,1)S(1)}, u32[]{:S(2)}, u32[]{:S(2)}) collective-permute-start(bf16[8,40,128]{2,1,0:T(8,128)(2,1)S(1)} %get-tuple-element.21), channel_id=1, source_target_pairs={{0,1},{1,0},{2,3},{3,2},{4,5},{5,4},{6,7},{7,6},{8,9},{9,8},{10,11... | collective-permute-start | bytes 245768 | tf_op jit(solution)/shard_map/ppermute | solution.py:324
  2.8 0.4 %second.1 = (bf16[240,1024]{1,0:T(8,128)(2,1)S(1)}, f32[8,40,128]{2,1,0:T(8,128)S(1)}, bf16[40,128]{1,0:T(8,128)(2,1)S(1)}, f32[40,128]{1,0:T(8,128)S(1)}, f32[4...) custom-call(bf16[240,2048]{1,0:T(8,128)(2,1)S(1)} %get-tuple-element.22.exposure, s32[16,2048]{1,0:T(8,128)S(1)} %get-tuple-element.23.bits, ...), custom_call_target="tpu_custom_call" | custom-call | tf_op jit(solution)/shard_map/second/pallas_call | solution.py:360
  3.2 0.5 %collective-permute-done.given_ref = bf16[8,40,128]{2,1,0:T(8,128)(2,1)S(1)} collective-permute-done((bf16[8,40,128]{2,1,0:T(8,128)(2,1)S(1)}, bf16[8,40,128]{2,1,0:T(8,128)(2,1)S(1)}, u32[]{:S(2)}, u32[]{:S(2)}) %collective-permute-start) | collective-permute-done | bytes 81952 | tf_op jit(solution)/shard_map/ppermute | solution.py:324
  3.7 11.9 %all_to_all.5.arrived_ref = bf16[8,80,128]{2,1,0:T(8,128)(2,1)S(1)} all-to-all(bf16[8,80,128]{2,1,0:T(8,128)(2,1)S(1)} %merging.1), channel_id=1, replica_groups={{11,8,0,14,13,3,5,6},{15,12,1,10,9,2,4,7},{27,24,16,30,29,19,21,22},{31..., dimensions={0} | all-to-all | bytes 327680 | tf_op jit(solution)/shard_map/all_to_all | solution.py:391
  15.6 0.3 %collective-permute-start.1 = (bf16[8,40,128]{2,1,0:T(8,128)(2,1)S(1)}, bf16[8,40,128]{2,1,0:T(8,128)(2,1)S(1)}, u32[]{:S(2)}, u32[]{:S(2)}) collective-permute-start(bf16[8,40,128]{2,1,0:T(8,128)(2,1)S(1)} %unpacking.1.carried_ref), channel_id=1, source_target_pairs={{0,1},{1,0},{2,3},{3,2},{4,5},{5,4},{6,7},{7,6},{8,9},{9,8},{10,11... | collective-permute-start | bytes 245768 | tf_op jit(solution)/shard_map/ppermute | solution.py:324
  15.9 0.8 %adjoint.1 = (f32[40,128]{1,0:T(8,128)}, f32[40,128]{1,0:T(8,128)}, f32[40,240]{1,0:T(8,128)S(1)}) custom-call(bf16[8,80,128]{2,1,0:T(8,128)(2,1)S(1)} %all_to_all.5.arrived_ref, bf16[8,40,128]{2,1,0:T(8,128)(2,1)S(1)} %unpacking.1.carried_ref, bf16[240,1024]{1,0:T(8,128)(2,1)S(1)} %get-tuple-element.31.masked_own, ...), custom_call_target="tpu_custom_call" | custom-call | tf_op jit(solution)/shard_map/adjoint/pallas_call | solution.py:411
  16.8 0.2 %collective-permute-done.1.carried_ref = bf16[8,40,128]{2,1,0:T(8,128)(2,1)S(1)} collective-permute-done((bf16[8,40,128]{2,1,0:T(8,128)(2,1)S(1)}, bf16[8,40,128]{2,1,0:T(8,128)(2,1)S(1)}, u32[]{:S(2)}, u32[]{:S(2)}) %collective-permute-start.1) | collective-permute-done | bytes 81952 | tf_op jit(solution)/shard_map/ppermute | solution.py:324
  17.0 0.8 %picking.1 = f32[4,240]{1,0:T(4,128)} custom-call(bf16[8,40,128]{2,1,0:T(8,128)(2,1)S(1)} %collective-permute-done.1.carried_ref, bf16[1024,240]{1,0:T(8,128)(2,1)S(1)} %get-tuple-element.36.turned_ref, f32[40,240]{1,0:T(8,128)S(1)} %get-tuple-element.37.projected_ref, s32[4,240]{1,0:T(4,128)S(1)} %get-tuple-element.38.used_ref), custom_call_target="tpu_custom_call" | custom-call | tf_op jit(solution)/shard_map/picking/pallas_call | solution.py:423
  (2 shorter events, 0.0 us)
Async XLA Ops:
  2.3 1.4 %collective-permute-start = (bf16[8,40,128]{2,1,0:T(8,128)(2,1)S(1)}, bf16[8,40,128]{2,1,0:T(8,128)(2,1)S(1)}, u32[]{:S(2)}, u32[]{:S(2)}) collective-permute-start(bf16[8,40,128]{2,1,0:T(8,128)(2,1)S(1)} %get-tuple-element.21), channel_id=1, source_target_pairs={{0,1},{1,0},{2,3},{3,2},{4,5},{5,4},{6,7},{7,6},{8,9},{9,8},{10,11... | collective-permute-start | bytes 245768 | tf_op jit(solution)/shard_map/ppermute | solution.py:324
  15.6 1.3 %collective-permute-start.1 = (bf16[8,40,128]{2,1,0:T(8,128)(2,1)S(1)}, bf16[8,40,128]{2,1,0:T(8,128)(2,1)S(1)}, u32[]{:S(2)}, u32[]{:S(2)}) collective-permute-start(bf16[8,40,128]{2,1,0:T(8,128)(2,1)S(1)} %unpacking.1.carried_ref), channel_id=1, source_target_pairs={{0,1},{1,0},{2,3},{3,2},{4,5},{5,4},{6,7},{7,6},{8,9},{9,8},{10,11... | collective-permute-start | bytes 245768 | tf_op jit(solution)/shard_map/ppermute | solution.py:324

commit v29 on v25

--- a/solution.py
+++ b/solution.py
@@ -101,10 +101,10 @@
     return jnp.concatenate(kept, axis=0).astype(jnp.bfloat16)
 
 
-def mask_and_sum(exposure, bits, weights, masked_ref, terms_ref, group):
+def mask_and_sum(exposure, bits, weights, masked_ref, terms_ref, group, chips):
     sets = exposure.shape[0]
-    chips, owned = terms_ref.shape[0], terms_ref.shape[2]
-    for first in range(0, chips, 2):
+    owned = terms_ref.shape[2]
+    for first in chips[::2]:
         rows = []
         for pair in range(sets // 16):
             flags = [row_flags(2 * pair), row_flags(2 * pair + 1)]
@@ -151,12 +151,14 @@
     sems,
 ):
     sets = exposure.shape[0]
-    currency_count = handed_ref.shape[1]
+    chips, currency_count = handed_ref.shape[:2]
+    half = exposure.shape[1] // 2
     copies = [
         pltpu.make_async_copy(source, target, sems.at[index])
         for index, (source, target) in enumerate(
             [
-                (exposure_hbm, exposure),
+                (exposure_hbm.at[:, :half], exposure.at[:, :half]),
+                (exposure_hbm.at[:, half:], exposure.at[:, half:]),
                 (bits_hbm, bits),
                 (currencies_hbm, currencies_ref),
                 (counts_hbm, counts_ref),
@@ -169,7 +171,7 @@
     ]
     for copy in copies:
         copy.start()
-    for copy in copies[2:5]:
+    for copy in copies[3:6]:
         copy.wait()
 
     used = used_currencies(currencies_ref[...], counts_ref[...])
@@ -183,11 +185,13 @@
         )
     weights = weights.astype(jnp.bfloat16)
     weights_ref[...] = weights
-    for copy in copies[:2]:
-        copy.wait()
     other = 1 - own_group()
-    mask_and_sum(exposure, bits, weights, masked_ref, handed_ref, other)
-    for copy in copies[5:]:
+    copies[2].wait()
+    for index in range(2):
+        copies[index].wait()
+        part = range(index * chips // 2, (index + 1) * chips // 2)
+        mask_and_sum(exposure, bits, weights, masked_ref, handed_ref, other, part)
+    for copy in copies[6:]:
         copy.wait()
 
 
@@ -208,7 +212,9 @@
     turned_ref,
 ):
     own = own_group()
-    mask_and_sum(exposure, bits, weights_ref[...], masked_ref, terms_ref, own)
+    mask_and_sum(
+        exposure, bits, weights_ref[...], masked_ref, terms_ref, own, range(terms_ref.shape[0])
+    )
     integral = spread_paths(start_ref[...], dates) + step_years * sums_to_date(rates_ref[...], dates)
     discount = jnp.exp(-integral)
     discount_ref[...] = discount
@@ -340,7 +346,7 @@
             pltpu.VMEM((slots, sets), jnp.int32),
             pltpu.VMEM((1, sets), jnp.int32),
             pltpu.VMEM((slots, sets), jnp.float32),
-            pltpu.SemaphoreType.DMA((8,)),
+            pltpu.SemaphoreType.DMA((9,)),
         ],
         compiler_params=params,
         name="first",

time: 17.7 us -> 17.9 us (1.011)
  no operation moved by 1% of the time
where the time goes in v29:
time: 17.9 us; the launch traced here: 17.7 us
  blocking collectives  11.3 us (63%)
  Pallas kernels  3.84 us (21%)
  starting transfers between devices  1.28 us (7%)
  between operations  0.66 us (4%)
  waiting for transfers between devices  0.6 us (3%)
    all_to_all x1, blocking collectives, body(): lax.all_to_all(outgoing, 'sets', 0, 0, axis_index_groups=[[2 * chip + cor...  11.3 us
    pallas_call x1, Pallas kernels, body(): pl.pallas_call(first_kernel, out_shape=(pltpu.VMEM((chips,) + block, jnp....  1.73 us
    ppermute x2, starting transfers between devices, swapped(): lax.ppermute(value, 'sets', [(peer, peer ^ 1) for peer in range(peers)])  1.28 us
    pallas_call x1, Pallas kernels, body(): pl.pallas_call(functools.partial(adjoint_kernel, dates), out_shape=(jax.S...  0.85 us
    pallas_call x1, Pallas kernels, body(): pl.pallas_call(picking_kernel, out_shape=jax.ShapeDtypeStruct((slots, set...  0.82 us
    ppermute x2, waiting for transfers between devices, swapped(): lax.ppermute(value, 'sets', [(peer, peer ^ 1) for peer in range(peers)])  0.6 us
    pallas_call x1, Pallas kernels, body(): pl.pallas_call(functools.partial(second_kernel, dates), out_shape=(pltpu....  0.39 us
  transfers between devices with their start and end apart: 2, of which 2 were waited for; matrix products, arithmetic and copies ran while one was open for 0% of the time, Pallas kernels for 7%

profile of v29, /device:TPU:0, one launch (start us, length us, event | category | flops | bytes accessed | tf_op | source)
XLA Modules:
  0.0 17.7 jit_solution(8490630996795388224)
XLA Ops:
  0.6 1.7 %first.1 = (bf16[8,40,128]{2,1,0:T(8,128)(2,1)S(1)}, bf16[240,1024]{1,0:T(8,128)(2,1)S(1)}, bf16[240,2048]{1,0:T(8,128)(2,1)S(1)}, s32[16,2048]{1,0:T(8,128)S(1)...) custom-call(bf16[240,2048]{1,0:T(8,128)(2,1)} %exposure_hbm.1, ...), custom_call_target="tpu_custom_call" | custom-call | tf_op jit(solution)/shard_map/first/pallas_call | solution.py:330
  2.4 0.5 %collective-permute-start = (bf16[8,40,128]{2,1,0:T(8,128)(2,1)S(1)}, bf16[8,40,128]{2,1,0:T(8,128)(2,1)S(1)}, u32[]{:S(2)}, u32[]{:S(2)}) collective-permute-start(bf16[8,40,128]{2,1,0:T(8,128)(2,1)S(1)} %get-tuple-element.21), channel_id=1, source_target_pairs={{0,1},{1,0},{2,3},{3,2},{4,5},{5,4},{6,7},{7,6},{8,9},{9,8},{10,11... | collective-permute-start | bytes 245768 | tf_op jit(solution)/shard_map/ppermute | solution.py:328
  2.9 0.4 %second.1 = (bf16[240,1024]{1,0:T(8,128)(2,1)S(1)}, f32[8,40,128]{2,1,0:T(8,128)S(1)}, bf16[40,128]{1,0:T(8,128)(2,1)S(1)}, f32[40,128]{1,0:T(8,128)S(1)}, f32[4...) custom-call(bf16[240,2048]{1,0:T(8,128)(2,1)S(1)} %get-tuple-element.22.exposure, s32[16,2048]{1,0:T(8,128)S(1)} %get-tuple-element.23.bits, ...), custom_call_target="tpu_custom_call" | custom-call | tf_op jit(solution)/shard_map/second/pallas_call | solution.py:364
  3.3 0.5 %collective-permute-done.given_ref = bf16[8,40,128]{2,1,0:T(8,128)(2,1)S(1)} collective-permute-done((bf16[8,40,128]{2,1,0:T(8,128)(2,1)S(1)}, bf16[8,40,128]{2,1,0:T(8,128)(2,1)S(1)}, u32[]{:S(2)}, u32[]{:S(2)}) %collective-permute-start) | collective-permute-done | bytes 81952 | tf_op jit(solution)/shard_map/ppermute | solution.py:328
  3.9 11.3 %all_to_all.5.arrived_ref = bf16[8,80,128]{2,1,0:T(8,128)(2,1)S(1)} all-to-all(bf16[8,80,128]{2,1,0:T(8,128)(2,1)S(1)} %merging.1), channel_id=1, replica_groups={{11,8,0,14,13,3,5,6},{9,10,1,12,15,2,4,7},{27,24,16,30,29,19,21,22},{25..., dimensions={0} | all-to-all | bytes 327680 | tf_op jit(solution)/shard_map/all_to_all | solution.py:395
  15.2 0.8 %collective-permute-start.1 = (bf16[8,40,128]{2,1,0:T(8,128)(2,1)S(1)}, bf16[8,40,128]{2,1,0:T(8,128)(2,1)S(1)}, u32[]{:S(2)}, u32[]{:S(2)}) collective-permute-start(bf16[8,40,128]{2,1,0:T(8,128)(2,1)S(1)} %unpacking.1.carried_ref), channel_id=1, source_target_pairs={{0,1},{1,0},{2,3},{3,2},{4,5},{5,4},{6,7},{7,6},{8,9},{9,8},{10,11... | collective-permute-start | bytes 245768 | tf_op jit(solution)/shard_map/ppermute | solution.py:328
  15.9 0.8 %adjoint.1 = (f32[40,128]{1,0:T(8,128)}, f32[40,128]{1,0:T(8,128)}, f32[40,240]{1,0:T(8,128)S(1)}) custom-call(bf16[8,80,128]{2,1,0:T(8,128)(2,1)S(1)} %all_to_all.5.arrived_ref, bf16[8,40,128]{2,1,0:T(8,128)(2,1)S(1)} %unpacking.1.carried_ref, bf16[240,1024]{1,0:T(8,128)(2,1)S(1)} %get-tuple-element.31.masked_own, ...), custom_call_target="tpu_custom_call" | custom-call | tf_op jit(solution)/shard_map/adjoint/pallas_call | solution.py:415
  16.8 0.1 collective-permute-done.1.carried_ref
  16.9 0.8 %picking.1 = f32[4,240]{1,0:T(4,128)} custom-call(bf16[8,40,128]{2,1,0:T(8,128)(2,1)S(1)} %collective-permute-done.1.carried_ref, bf16[1024,240]{1,0:T(8,128)(2,1)S(1)} %get-tuple-element.36.turned_ref, f32[40,240]{1,0:T(8,128)S(1)} %get-tuple-element.37.projected_ref, s32[4,240]{1,0:T(4,128)S(1)} %get-tuple-element.38.used_ref), custom_call_target="tpu_custom_call" | custom-call | tf_op jit(solution)/shard_map/picking/pallas_call | solution.py:427
  (2 shorter events, 0.0 us)
Async XLA Ops:
  2.4 1.4 %collective-permute-start = (bf16[8,40,128]{2,1,0:T(8,128)(2,1)S(1)}, bf16[8,40,128]{2,1,0:T(8,128)(2,1)S(1)}, u32[]{:S(2)}, u32[]{:S(2)}) collective-permute-start(bf16[8,40,128]{2,1,0:T(8,128)(2,1)S(1)} %get-tuple-element.21), channel_id=1, source_target_pairs={{0,1},{1,0},{2,3},{3,2},{4,5},{5,4},{6,7},{7,6},{8,9},{9,8},{10,11... | collective-permute-start | bytes 245768 | tf_op jit(solution)/shard_map/ppermute | solution.py:328
  15.2 1.7 %collective-permute-start.1 = (bf16[8,40,128]{2,1,0:T(8,128)(2,1)S(1)}, bf16[8,40,128]{2,1,0:T(8,128)(2,1)S(1)}, u32[]{:S(2)}, u32[]{:S(2)}) collective-permute-start(bf16[8,40,128]{2,1,0:T(8,128)(2,1)S(1)} %unpacking.1.carried_ref), channel_id=1, source_target_pairs={{0,1},{1,0},{2,3},{3,2},{4,5},{5,4},{6,7},{7,6},{8,9},{9,8},{10,11... | collective-permute-start | bytes 245768 | tf_op jit(solution)/shard_map/ppermute | solution.py:328
